TPU v7x, 256 devices: a whole 4x4x8 slice. The times are simulated.
256 devices in a mesh: section: 8 (over y, x_lo), ts: 32 (over z, x_hi, core).
Axes of the slice: x: 4 (x_hi: 2, x_lo: 2; x = x_hi * 2 + x_lo), y: 4, z: 8, core: 2. Of those that a mesh axis runs over, the one named last changes fastest.
Arguments:
- upstream: bfloat16 [8, 4096, 8192], P('section', None, 'ts'), as said below
- stashed: bfloat16 [8, 4096, 8192], P('section', None, 'ts'), as said below
- returning: bfloat16 [8, 4096, 8192], P('section', None, 'ts'), may hold values from -3 to 3
- key_cotangent: bfloat16 [8, 4096, 1024], P('section', 'ts'), as said below
- key_weight: bfloat16 [8, 8192, 1024], P('section', 'ts'), as said below
- norm_gain: float32 [8, 8192], P('section', 'ts'), may hold values from 0.1 to 1.9
- lengths: int32 [8], P('section'), may hold values from 512 to 4096, as said below
Outputs:
- new_keys: bfloat16 [8, 4096, 1024], P('section', 'ts')
- input_grad: bfloat16 [8, 4096, 8192], P('section', None, 'ts')
- weight_grad: float32 [8, 8192, 1024], P('section', 'ts')
- gain_grad: float32 [8, 8192], P('section', 'ts')
Inputs may be any that keep to these rules, and one draw needn't show every extreme that they name: `lengths`: some section has all 4096 tokens live in every draw. `upstream`: float entries; every token row has positive mean square. `stashed`: float entries; every token row has positive mean square. `key_cotangent`: float entries. `key_weight`: float entries.
All inputs are finite; a program needn't handle non-finite values.
Results may differ from a plain program's by a relative error of at most 0.023.
Values may be sent and summed in bfloat16 or wider, within the bound.
No kernel may reach another device: no remote copies, remote signals or barrier semaphores. Data moves between devices by JAX's collectives and lax.ppermute only.
A program may use at most 128 MiB of HBM per device.

v0:
```python
import jax
import jax.numpy as jnp
from jax import lax
from jax.sharding import PartitionSpec as P

eps = 1e-05


def from_behind(block, axis, distance):
    devices = range(lax.axis_size(axis))
    route = [((i - distance) % len(devices), i) for i in devices]
    return lax.ppermute(block, axis, route)


def partner(value, axis, apart):
    return lax.ppermute(value, axis, [(i, i ^ 1 << apart) for i in range(lax.axis_size(axis))])


def shards(upstream, stashed, returning, key_cotangent, key_weight, norm_gain, lengths):
    inbound = from_behind(upstream[0], "section", 1)
    downstream = from_behind(returning[0], "section", -1)
    sections = lax.axis_size("section")
    levels = sections.bit_length() - 1
    older = stashed[0]
    for bit in range(levels):
        older = partner(older, "section", bit)
    lanes = lax.axis_size("ts")
    tokens = inbound.shape[0]
    width = inbound.shape[1] * lanes
    tok_rows = tokens // lanes
    gain_row = norm_gain[0]
    weights = key_weight[0]
    inbound_wide = inbound.astype(jnp.float32)
    older_wide = older.astype(jnp.float32)
    fresh_sq, older_sq = (
        lax.psum(jnp.sum(inbound_wide * inbound_wide, axis=1).astype(jnp.bfloat16), "ts").astype(
            jnp.float32
        ),
        lax.psum(jnp.sum(older_wide * older_wide, axis=1).astype(jnp.bfloat16), "ts").astype(
            jnp.float32
        ),
    )
    fresh_rate = lax.rsqrt(fresh_sq / width + eps)
    older_rate = lax.rsqrt(older_sq / width + eps)
    scaled = (inbound_wide * gain_row).astype(jnp.bfloat16)
    older_scaled = (older_wide * gain_row).astype(jnp.bfloat16)
    full_term = jnp.dot(scaled, weights, preferred_element_type=jnp.float32)
    column_share = lax.psum_scatter(
        full_term.astype(jnp.bfloat16), "ts", scatter_dimension=1, tiled=True
    ).astype(jnp.float32)
    summed = lax.all_to_all(
        column_share.astype(jnp.bfloat16), "ts", split_axis=0, concat_axis=1, tiled=True
    ).astype(column_share.dtype)
    own_rate = lax.dynamic_slice_in_dim(fresh_rate, lax.axis_index("ts") * tok_rows, tok_rows, 0)
    new_keys = (summed * own_rate[:, None]).astype(jnp.bfloat16)
    limit = lengths[0]
    piece = lax.all_gather(key_cotangent[0], "ts", axis=0, tiled=True)
    count = piece.shape[0]
    positions = jnp.arange(count, dtype=jnp.int32)
    live = (positions < limit).astype(jnp.float32)
    graded = (piece.astype(jnp.float32) * (live * older_rate)[:, None]).astype(jnp.bfloat16)
    weight_total = lax.dot_general(
        older_scaled, graded, (((0,), (0,)), ((), ())), preferred_element_type=jnp.float32
    )
    back_rows = lax.dot_general(
        graded, weights, (((1,), (1,)), ((), ())), preferred_element_type=jnp.float32
    )
    partial_curve = jnp.sum(back_rows * older_scaled.astype(jnp.float32), axis=1)
    curvature = lax.psum(partial_curve, "ts")
    total = (
        downstream.astype(jnp.float32)
        + gain_row * back_rows
        - (older_rate * older_rate / width * curvature)[:, None] * older_wide
    )
    input_grad = total.astype(jnp.bfloat16)
    gain_grad = jnp.sum(back_rows * older_wide, axis=0)
    return (new_keys[None], input_grad[None], weight_total[None], gain_grad[None])


def solution(mesh):
    return jax.shard_map(
        shards,
        mesh=mesh,
        in_specs=(
            P("section", None, "ts"),
            P("section", None, "ts"),
            P("section", None, "ts"),
            P("section", "ts", None),
            P("section", "ts", None),
            P("section", "ts"),
            P("section"),
        ),
        out_specs=(
            P("section", "ts", None),
            P("section", None, "ts"),
            P("section", "ts", None),
            P("section", "ts"),
        ),
        check_vma=False,
    )
```

profile of v0, /device:TPU:1, one launch (start us, length us, event | category | flops | bytes accessed | tf_op | source)
XLA Modules:
  0.0 530.0 jit_solution(10997214116587729469)
XLA Ops:
  7.2 0.0 copy-start
  7.2 0.0 reduce-scatter.2.cloned.1.call-start
  7.2 2.1 collective-permute-start
  9.3 46.0 %collective-permute-done = bf16[4096,256]{1,0:T(8,128)(2,1)S(1)} collective-permute-done((bf16[4096,256]{1,0:T(8,128)(2,1)}, bf16[4096,256]{1,0:T(8,128)(2,1)S(1)}, u32[]{:S(2)}, u32[]{:S(2)}) %collective-permute-start) | collective-permute-done | bytes 2097184 | tf_op jit(solution)/shard_map/ppermute | solution.py:12
  55.3 0.0 copy-done
  55.3 6.3 %convolution_convert_fusion = bf16[4096,1024]{0,1:T(8,128)(2,1)} fusion(bf16[4096,256]{1,0:T(8,128)(2,1)S(1)} %collective-permute-done, f32[256]{0:T(256)} %bitcast.40, bf16[1,256,1024]{2,1,0:T(8,128)(2,1)S(1)} %copy-done), kind=kOutput, calls=%fused_computation.2 | convolution fusion | flops 2154823680 | bytes 11011072 | tf_op jit(solution)/shard_map/dot_general | solution.py:47
  61.6 0.0 reduce-scatter.2.cloned.1.call-update
  61.7 0.0 copy-start.2
  61.7 0.0 all-gather.3.cloned.1.call-start
  61.7 0.7 all-gather.3.cloned.1.call-update
  62.4 0.5 collective-permute-start.2
  62.9 43.7 %collective-permute-done.2 = bf16[4096,256]{1,0:T(8,128)(2,1)S(1)} collective-permute-done((bf16[4096,256]{1,0:T(8,128)(2,1)}, bf16[4096,256]{1,0:T(8,128)(2,1)S(1)}, u32[]{:S(2)}, u32[]{:S(2)}) %collective-permute-start.2) | collective-permute-done | bytes 2097184 | tf_op jit(solution)/shard_map/ppermute | solution.py:16
  106.6 3.4 collective-permute-start.3
  110.0 43.5 %collective-permute-done.3 = bf16[4096,256]{1,0:T(8,128)(2,1)} collective-permute-done((bf16[4096,256]{1,0:T(8,128)(2,1)S(1)}, bf16[4096,256]{1,0:T(8,128)(2,1)}, u32[]{:S(2)}, u32[]{:S(2)}) %collective-permute-start.3) | collective-permute-done | bytes 2097184 | tf_op jit(solution)/shard_map/ppermute | solution.py:16
  153.5 2.9 collective-permute-start.4
  156.3 0.9 collective-permute-start.1
  157.8 0.6 fusion.2
  158.5 70.8 %reduce-scatter.2.cloned.1.call-done = bf16[4096,32]{0,1:T(8,128)(2,1)} async-done(((bf16[4096,1024]{0,1:T(8,128)(2,1)}), bf16[4096,32]{0,1:T(8,128)(2,1)}) %reduce-scatter.2.cloned.1.call-update) | async-done | bytes 262160 | tf_op jit(solution)/shard_map/reduce_scatter | solution.py:48
  229.3 1.7 copy_bitcast_fusion
  231.0 10.3 %all-to-all-start = ((bf16[32,128,32]{1,2,0:T(8,128)(2,1)}), bf16[32,128,32]{1,2,0:T(8,128)(2,1)S(1)}, u32[]{:S(2)}, u32[]{:S(2)}) async-start(bf16[32,128,32]{1,2,0:T(8,128)(2,1)} %copy_bitcast_fusion), calls=%async_computation.1 | async-start | bytes 524288 | tf_op jit(solution)/shard_map/all_to_all | solution.py:51
  241.4 0.0 collective-permute-done.4
  241.4 2.2 fusion.3
  243.6 128.8 %all-reduce = (bf16[4096]{0:T(1024)(128)(2,1)S(1)}, bf16[4096]{0:T(1024)(128)(2,1)S(1)}) all-reduce(bf16[4096]{0:T(1024)(128)(2,1)S(1)} %fusion.2, bf16[4096]{0:T(1024)(128)(2,1)S(1)} %fusion.3), channel_id=1, replica_groups=mesh['section'=8,'ts'=32] {'ts'}, use_global_device_ids=true, to_apply=%region_2.0 | all-reduce | flops 8192 | bytes 32768 | tf_op jit(solution)/shard_map/psum | solution.py:36
  372.4 0.1 fusion.27
  372.4 0.0 all-to-all-done
  372.5 0.1 convert_element_type.90
  372.6 0.9 copy.13
  373.4 9.6 %fusion.7 = (f32[256]{0:T(256)}, f32[4096]{0:T(1024)S(1)}, f32[4096,256]{1,0:T(8,128)}) fusion(bf16[4096,256]{1,0:T(8,128)(2,1)} %collective-permute-done.4, f32[256]{0:T(256)S(1)} %bitcast.41, bf16[1,256,1024]{2,1,0:T(8,128)(2,1)S(1)} %copy-done, bf16[1,4096,1024]{2,1,0:T(8,128)(2,1)} %all-gather.3.cloned.1.call-done, f32[4096]{0:T(1024)S(1)} %fusion.24), kind=kOutput, calls=%fused_computation.15 | convolution fusion | flops 2168450816 | bytes 15239168 | tf_op jit(solution)/shard_map/dot_general | solution.py:65
  383.1 128.6 %psum.23 = f32[4096]{0:T(1024)S(1)} all-reduce(f32[4096]{0:T(1024)S(1)} %get-tuple-element.9), channel_id=1, replica_groups=mesh['section'=8,'ts'=32] {'ts'}, use_global_device_ids=true, to_apply=%region_6.0 | all-reduce | flops 4096 | bytes 32768 | tf_op jit(solution)/shard_map/psum | solution.py:69
  511.7 7.7 %fusion.16 = f32[1,256,1024]{2,1,0:T(8,128)} fusion(bf16[1,4096,1024]{2,1,0:T(8,128)(2,1)} %all-gather.3.cloned.1.call-done, f32[4096]{0:T(1024)S(1)} %fusion.24, bf16[4096,256]{1,0:T(8,128)(2,1)} %collective-permute-done.4, f32[256]{0:T(256)S(1)} %bitcast.42), kind=kOutput, calls=%fused_computation.21 | convolution fusion | flops 2163212288 | bytes 11551744 | tf_op jit(solution)/shard_map/dot_general | solution.py:62
  519.5 0.0 collective-permute-done.1
  519.5 3.7 fusion.12
  (7 shorter events, 0.1 us)
Async XLA Ops:
  7.2 48.2 %copy-start = (bf16[1,256,1024]{2,1,0:T(8,128)(2,1)S(1)}, bf16[1,256,1024]{2,1,0:T(8,128)(2,1)}, u32[]{:S(2)}) copy-start(bf16[1,256,1024]{2,1,0:T(8,128)(2,1)} %param.11) | copy-start | bytes 1572868
  7.2 222.1 %reduce-scatter.2.cloned.1.call-start = ((), (), s32[]{:S(2)}) async-start(), calls=%async_computation.2 | async-start | bytes 8650752 | tf_op jit(solution)/shard_map/reduce_scatter | solution.py:48
  7.2 48.1 %collective-permute-start = (bf16[4096,256]{1,0:T(8,128)(2,1)}, bf16[4096,256]{1,0:T(8,128)(2,1)S(1)}, u32[]{:S(2)}, u32[]{:S(2)}) collective-permute-start(bf16[4096,256]{1,0:T(8,128)(2,1)} %bitcast.44), channel_id=1, source_target_pairs={{224,0},{0,32},{32,64},{64,96},{96,128},{128,160},{160,192},{192,2... | collective-permute-start | bytes 6291464 | tf_op jit(solution)/shard_map/ppermute | solution.py:12
  61.7 311.8 %copy-start.2 = (f32[1,256]{1,0:T(1,128)S(1)}, f32[1,256]{1,0:T(1,128)}, u32[]{:S(2)}) copy-start(f32[1,256]{1,0:T(1,128)} %param.12) | copy-start | bytes 3076
  61.7 311.7 %all-gather.3.cloned.1.call-start = ((), (), s32[]{:S(2)}) async-start(), calls=%async_computation.3 | async-start | bytes 8650752 | tf_op jit(solution)/shard_map/all_gather | solution.py:57
  62.4 44.2 %collective-permute-start.2 = (bf16[4096,256]{1,0:T(8,128)(2,1)}, bf16[4096,256]{1,0:T(8,128)(2,1)S(1)}, u32[]{:S(2)}, u32[]{:S(2)}) collective-permute-start(bf16[4096,256]{1,0:T(8,128)(2,1)} %bitcast.45), channel_id=1, source_target_pairs={{0,32},{32,0},{64,96},{96,64},{128,160},{160,128},{192,224},{224,1... | collective-permute-start | bytes 6291464 | tf_op jit(solution)/shard_map/ppermute | solution.py:16
  106.6 46.9 %collective-permute-start.3 = (bf16[4096,256]{1,0:T(8,128)(2,1)S(1)}, bf16[4096,256]{1,0:T(8,128)(2,1)}, u32[]{:S(2)}, u32[]{:S(2)}) collective-permute-start(bf16[4096,256]{1,0:T(8,128)(2,1)S(1)} %collective-permute-done.2), channel_id=1, source_target_pairs={{0,64},{32,96},{64,0},{96,32},{128,192},{160,224},{192,128},{224,1... | collective-permute-start | bytes 6291464 | tf_op jit(solution)/shard_map/ppermute | solution.py:16
  153.5 87.9 %collective-permute-start.4 = (bf16[4096,256]{1,0:T(8,128)(2,1)}, bf16[4096,256]{1,0:T(8,128)(2,1)}, u32[]{:S(2)}, u32[]{:S(2)}) collective-permute-start(bf16[4096,256]{1,0:T(8,128)(2,1)} %collective-permute-done.3), channel_id=1, source_target_pairs={{0,128},{32,160},{64,192},{96,224},{128,0},{160,32},{192,64},{224,... | collective-permute-start | bytes 6291464 | tf_op jit(solution)/shard_map/ppermute | solution.py:16
  156.3 363.1 %collective-permute-start.1 = (bf16[4096,256]{1,0:T(8,128)(2,1)}, bf16[4096,256]{1,0:T(8,128)(2,1)}, u32[]{:S(2)}, u32[]{:S(2)}) collective-permute-start(bf16[4096,256]{1,0:T(8,128)(2,1)} %bitcast.46), channel_id=1, source_target_pairs={{32,0},{64,32},{96,64},{128,96},{160,128},{192,160},{224,192},{0,2... | collective-permute-start | bytes 6291464 | tf_op jit(solution)/shard_map/ppermute | solution.py:12
  231.0 141.4 %all-to-all-start = ((bf16[32,128,32]{1,2,0:T(8,128)(2,1)}), bf16[32,128,32]{1,2,0:T(8,128)(2,1)S(1)}, u32[]{:S(2)}, u32[]{:S(2)}) async-start(bf16[32,128,32]{1,2,0:T(8,128)(2,1)} %copy_bitcast_fusion), calls=%async_computation.1 | async-start | bytes 524288 | tf_op jit(solution)/shard_map/all_to_all | solution.py:51
  511.7 7.8 %copy-start.1 = (f32[4096,256]{1,0:T(8,128)S(1)}, f32[4096,256]{1,0:T(8,128)}, u32[]{:S(2)}) copy-start(f32[4096,256]{1,0:T(8,128)} %get-tuple-element.12) | copy-start | bytes 12582916
Sparse Core Ops, SparseCore 0:
  61.8 167.4 reduce-scatter.1
  232.1 104.3 all-gather.2
where the time goes:
time: 540 us; the launch traced here: 530 us
  blocking collectives  257 us (48%)
  waiting for transfers between devices  205 us (38%)
  matrix products  23.7 us (4%)
  starting transfers between devices  20.1 us (4%)
  between operations  14.8 us (3%)
  other arithmetic  6.74 us (1%)
    psum x1, blocking collectives, shards(): lax.psum(jnp.sum(inbound_wide * inbound_wide, axis=1).astype(jnp.bfloat16...  129 us
    psum x1, blocking collectives, shards(): curvature = lax.psum(partial_curve, 'ts')  129 us
    ppermute x3, waiting for transfers between devices, partner(): lax.ppermute(value, axis, [(i, i ^ 1 << apart) for i in range(lax.axis_si...  87.2 us
    reduce_scatter x1, waiting for transfers between devices, shards(): lax.psum_scatter(full_term.astype(jnp.bfloat16), 'ts', scatter_dimension=...  70.8 us
    ppermute x2, waiting for transfers between devices, from_behind(): return lax.ppermute(block, axis, route)  46 us
  transfers between devices with their start and end apart: 8, of which 4 were waited for; matrix products, arithmetic and copies ran while one was open for 4% of the time, Pallas kernels for 0%

commit v1 on v0

v1 whole, which is shorter than its diff:
```python
import jax
import jax.numpy as jnp
from jax import lax
from jax.experimental import pallas as pl
from jax.experimental.pallas import tpu as pltpu
from jax.sharding import PartitionSpec as P

eps = 1e-05
BF = jnp.bfloat16
F32 = jnp.float32
N_S = 8
N_T = 32
N_Z = 8
TOK = 4096
OWN = TOK // N_T
WIDTH = 8192
LANE = WIDTH // N_T
KEYS = 1024
Z_STEP = 4
PACK = LANE + 16
AXES = ("section", "ts")


def move(value, target, cores=(0, 1)):
    pairs = []
    for s in range(N_S):
        for t in [t for t in range(N_T) if t % 2 in cores]:
            to_s, to_t = target(s, t)
            pairs.append((s * N_T + t, to_s * N_T + to_t))
    return lax.ppermute(value, AXES, pairs)


def to_next(s, t):
    return (s + 1) % N_S, t


def to_previous(s, t):
    return (s - 1) % N_S, t


def to_mirror(s, t):
    return N_S - 1 - s, t


def to_other_core(s, t):
    return s, t ^ 1


def to_other_half(s, t):
    return s, t ^ 2


def to_next_other_half(s, t):
    return (s + 1) % N_S, t ^ 2


def z_up(s, t):
    return s, (t + 4) % N_T


def z_down(s, t):
    return s, (t - 4) % N_T


def pick(value, index):
    return lax.dynamic_index_in_dim(value, index, 0, keepdims=False)


def after(value, *others):
    return lax.optimization_barrier((value,) + others)[0]


def add(a, b):
    return (a.astype(F32) + b.astype(F32)).astype(BF)


def call(kernel, grid, in_specs, out_specs, out_shape, flops, size, aliases=None):
    return pl.pallas_call(
        kernel,
        grid_spec=pltpu.PrefetchScalarGridSpec(
            num_scalar_prefetch=1, grid=grid, in_specs=in_specs, out_specs=out_specs
        ),
        out_shape=out_shape,
        input_output_aliases=aliases or {},
        compiler_params=pltpu.CompilerParams(vmem_limit_bytes=56 * 1024 * 1024),
        cost_estimate=pl.CostEstimate(flops=flops, bytes_accessed=size, transcendentals=0),
    )


def pack_kernel(place, weights, gain, out):
    out[:LANE, :] = weights[...]
    value = gain[...]
    high = value.astype(BF)
    middle = (value - high.astype(F32)).astype(BF)
    low = (value - high.astype(F32) - middle.astype(F32)).astype(BF)
    row = jnp.concatenate([high, middle, low, jnp.zeros((1, LANE), BF)], axis=1)
    out[LANE:, :] = jnp.broadcast_to(row, (PACK - LANE, KEYS))


def pack(place, weights, gain):
    return call(
        pack_kernel,
        (1,),
        [
            pl.BlockSpec((LANE, KEYS), lambda i, place: (0, 0)),
            pl.BlockSpec((1, LANE), lambda i, place: (0, 0)),
        ],
        pl.BlockSpec((PACK, KEYS), lambda i, place: (0, 0)),
        jax.ShapeDtypeStruct((PACK, KEYS), BF),
        0,
        2 * PACK * KEYS * 2,
    )(place, weights, gain)


def forward_kernel(place, rows_mine, rows_other, packed_mine, packed_other, out):
    rows = out.shape[0] * OWN
    total = None
    for block, packed in ((rows_mine, packed_mine), (rows_other, packed_other)):
        pieces = packed[LANE : LANE + 1, :].astype(F32)
        gains = pieces[:, :LANE] + pieces[:, LANE : 2 * LANE] + pieces[:, 2 * LANE : 3 * LANE]
        left = (block[...].reshape(rows, LANE).astype(F32) * gains).astype(BF)
        term = jnp.dot(left, packed[:LANE, :], preferred_element_type=F32)
        total = term if total is None else total + term
    out[...] = total.astype(BF).reshape(out.shape)


def forward(place, fresh, rows_other, packed_mine, packed_other):
    step = 4
    return call(
        forward_kernel,
        (N_T // 2 // step,),
        [
            pl.BlockSpec((step, 1, OWN, LANE), lambda i, place: (i, place[1], 0, 0)),
            pl.BlockSpec((step, OWN, LANE), lambda i, place: (i, 0, 0)),
            pl.BlockSpec((PACK, KEYS), lambda i, place: (0, 0)),
            pl.BlockSpec((PACK, KEYS), lambda i, place: (0, 0)),
        ],
        pl.BlockSpec((step, OWN, KEYS), lambda i, place: (i, 0, 0)),
        jax.ShapeDtypeStruct((N_T // 2, OWN, KEYS), BF),
        2 * TOK // 2 * 2 * LANE * KEYS,
        7 * 1024 * 1024,
    )(place, fresh, rows_other, packed_mine, packed_other)


def column(value):
    return value.reshape(value.shape[0] * OWN)[:, None]


def backward_kernel(place, cot, weights, older, gain, scale, *refs):
    *before, base, curve, weight_sum, gain_sum = refs
    first = (pl.program_id(0) == 0) & (pl.program_id(1) == 0)

    @pl.when(first)
    def _():
        if before:
            weight_sum[...] = before[2][...]
            gain_sum[...] = before[3][...]
        else:
            weight_sum[...] = jnp.zeros_like(weight_sum)
            gain_sum[...] = jnp.zeros_like(gain_sum)

    rows = Z_STEP * OWN
    keys = cot[...].reshape(rows, KEYS)
    wide = older[...].reshape(rows, LANE).astype(F32)
    row_scale = column(scale[...].reshape(Z_STEP, OWN))
    gains = gain[...]
    grad = row_scale * lax.dot_general(
        keys, weights[...], (((1,), (1,)), ((), ())), preferred_element_type=F32
    )
    scaled = wide * gains
    curve[...] = jnp.sum(
        (grad * scaled.astype(BF).astype(F32)).reshape(Z_STEP, OWN, LANE), axis=-1
    ).reshape(curve.shape)
    gain_sum[...] += jnp.sum(grad * wide, axis=0, keepdims=True)
    base[...] = (grad * gains).reshape(base.shape)
    weight_sum[...] += lax.dot_general(
        (scaled * row_scale).astype(BF), keys, (((0,), (0,)), ((), ())), preferred_element_type=F32
    )


def backward(place, cot, weights, older, gain, scale, which, before):
    def tokens(a, i, place):
        return (i, a, place[1] ^ which, 0, 0)

    def whole(a, i, place):
        return (0, 0)

    in_specs = [
        pl.BlockSpec((Z_STEP, 1, OWN, KEYS), lambda a, i, place: (i, a, 0, 0)),
        pl.BlockSpec((LANE, KEYS), whole),
        pl.BlockSpec((Z_STEP, 1, 1, OWN, LANE), tokens),
        pl.BlockSpec((1, LANE), whole),
        pl.BlockSpec((Z_STEP, 1, 1, 1, OWN), tokens),
    ]
    aliases = {}
    if before:
        in_specs += [
            pl.BlockSpec(memory_space=pl.ANY),
            pl.BlockSpec(memory_space=pl.ANY),
            pl.BlockSpec((LANE, KEYS), whole),
            pl.BlockSpec((1, LANE), whole),
        ]
        aliases = {6: 0, 7: 1}
    return call(
        backward_kernel,
        (2, N_Z // Z_STEP),
        in_specs,
        [
            pl.BlockSpec((Z_STEP, 1, 1, OWN, LANE), tokens),
            pl.BlockSpec((Z_STEP, 1, 1, 1, OWN), tokens),
            pl.BlockSpec((LANE, KEYS), whole),
            pl.BlockSpec((1, LANE), whole),
        ],
        [
            jax.ShapeDtypeStruct((N_Z, 2, 2, OWN, LANE), F32),
            jax.ShapeDtypeStruct((N_Z, 2, 2, 1, OWN), F32),
            jax.ShapeDtypeStruct((LANE, KEYS), F32),
            jax.ShapeDtypeStruct((1, LANE), F32),
        ],
        4 * (TOK // 2) * LANE * KEYS,
        9 * 1024 * 1024,
        aliases,
    )(place, cot, weights, older, gain, scale, *before)


def finish_kernel(place, early, late, base, older, pull, out):
    bent = base[...] - column(pull[0]) * older[...].astype(F32)
    down = jnp.where(pl.program_id(0) < N_Z // 2, early[...].astype(F32), late[...].astype(F32))
    out[...] = (down + bent).astype(BF)


def finish(place, early, late, base, older, pull):
    rows = TOK // N_Z
    mid = N_Z // 2
    block = pl.BlockSpec((rows, LANE), lambda i, place: (i, 0))
    return call(
        finish_kernel,
        (N_Z,),
        [
            pl.BlockSpec((rows, LANE), lambda i, place: (jnp.minimum(i, mid - 1), 0)),
            pl.BlockSpec((rows, LANE), lambda i, place: (jnp.maximum(i - mid, 0), 0)),
            block,
            block,
            pl.BlockSpec((1, rows // OWN, OWN), lambda i, place: (i, 0, 0)),
        ],
        block,
        jax.ShapeDtypeStruct((TOK, LANE), BF),
        0,
        10 * 1024 * 1024,
    )(place, early, late, base, older, pull)


def shards(upstream, stashed, returning, key_cotangent, key_weight, norm_gain, lengths):
    lane = lax.axis_index("ts")
    core = lane % 2
    half = (lane // 2) % 2
    z = lane // 4
    place = jnp.stack([half, core, z]).astype(jnp.int32)
    weights = key_weight[0]
    fresh = upstream[0]
    saved = stashed[0]

    packed = move(pack(place, weights, norm_gain), to_previous)

    lanes = [[q * 2 + c for q in range(N_T // 2)] for c in range(2)]
    cot_mine = lax.all_gather(key_cotangent[0], "ts", axis=0, axis_index_groups=lanes, tiled=True)

    fresh_wide = fresh.astype(F32)
    saved_wide = saved.astype(F32)
    fresh_part = jnp.sum(fresh_wide * fresh_wide, axis=1).reshape(N_Z, 2, 2, OWN)
    saved_part = jnp.sum(saved_wide * saved_wide, axis=1).reshape(1, N_T, OWN)
    squares = jnp.concatenate(
        [
            fresh_part.reshape(N_T, 1, OWN),
            fresh_part[:, ::-1].reshape(N_T, 1, OWN),
            jnp.broadcast_to(saved_part, (N_T, N_T, OWN)),
        ],
        axis=1,
    )
    squares = jnp.sum(lax.all_to_all(squares, "ts", 0, 0, tiled=True), axis=0)
    fresh_rate = lax.rsqrt(squares[:2] / WIDTH + eps)
    older_sq = move(squares[2:], to_mirror)

    older = move(after(saved, packed), to_mirror)
    early, late = lax.optimization_barrier((returning[0, : TOK // 2], returning[0, TOK // 2 :]))
    early = move(after(early, older, older_sq), to_previous)
    late = move(after(late, older, older_sq), to_previous)

    rows = fresh.reshape(N_T // 2, 2, OWN, LANE)
    rows_other = move(lax.dynamic_index_in_dim(rows, 1 - core, 1, keepdims=False), to_other_core)
    packed_other = move(packed, to_other_core)
    partial = forward(place, rows, rows_other, packed, after(packed_other, squares))

    def block(distance):
        return lax.dynamic_slice_in_dim(partial, ((z + distance) % N_Z) * 2, 2, 0)

    older_rate = lax.rsqrt(older_sq / WIDTH + eps)
    live = (jnp.arange(TOK, dtype=jnp.int32) < lengths[0]).astype(F32).reshape(N_T, OWN)
    scale = (live * older_rate).reshape(N_Z, 2, 2, 1, OWN)
    older_parts = older.reshape(N_Z, 2, 2, OWN, LANE)
    cot_mine = after(cot_mine, older, older_sq, partial)
    cot_other = move(cot_mine, to_other_core)
    cots = [value.reshape(N_Z, 2, OWN, KEYS) for value in (cot_mine, cot_other)]
    sums = backward(place, cots[0], weights, older_parts, norm_gain, scale, 0, [])
    base, curve, weight_total, gain_grad = backward(
        place, cots[1], weights, older_parts, norm_gain, scale, 1, sums
    )

    up = move(after(block(4), older), z_up, (0,))
    down = move(after(block(4), older), z_down, (1,))
    up, down = lax.optimization_barrier((up, down))
    up = move(add(block(3), up), z_up)
    down = move(add(block(-3), down), z_down)
    up, down = lax.optimization_barrier((up, down, sums[1], early))[:2]
    up = move(add(block(2), up), z_up)
    down = move(add(block(-2), down), z_down)
    up, down = lax.optimization_barrier((up, down, curve))[:2]
    up = move(add(block(1), up), z_up)
    down = move(add(block(-1), down), z_down)

    curve = jnp.broadcast_to(curve.astype(BF).reshape(1, N_T, OWN), (N_T, N_T, OWN))
    curve = jnp.sum(lax.all_to_all(curve, "ts", 0, 0, tiled=True).astype(F32), axis=0)
    pull = (older_rate * older_rate / WIDTH * curve).reshape(N_Z, N_T // N_Z, OWN)

    summed = block(0).astype(F32) + up.astype(F32) + after(down, pull, late).astype(F32)
    straight = move((pick(summed, half) * fresh_rate[0][:, None]).astype(BF), to_next)
    crossed = move((pick(summed, 1 - half) * fresh_rate[1][:, None]).astype(BF), to_next_other_half)
    new_keys = (straight.astype(F32) + crossed.astype(F32)).astype(BF)

    input_grad = finish(place, early, late, base.reshape(TOK, LANE), older, pull)
    return (new_keys[None], input_grad[None], weight_total[None], gain_grad)


def solution(mesh):
    return jax.shard_map(
        shards,
        mesh=mesh,
        in_specs=(
            P("section", None, "ts"),
            P("section", None, "ts"),
            P("section", None, "ts"),
            P("section", "ts", None),
            P("section", "ts", None),
            P("section", "ts"),
            P("section"),
        ),
        out_specs=(
            P("section", "ts", None),
            P("section", None, "ts"),
            P("section", "ts", None),
            P("section", "ts"),
        ),
        check_vma=False,
    )
```

time: 540 us -> 241 us (0.45); the launches traced: 530 us -> 239 us
  blocking collectives: 257 us -> 0 us
  waiting for transfers between devices: 205 us -> 112 us
  Pallas kernels: 0 us -> 40 us
  starting transfers between devices: 20.1 us -> 49 us
  matrix products: 23.7 us -> 0 us
  other arithmetic: 6.74 us -> 18.2 us
    psum x2 -> x0, blocking collectives: 257 us -> none  [the longest x1 129 us: shards(): lax.psum(jnp.sum(inbound_wide * inbound_wide, axis=1).astype(jnp.bfloat16...]
    ppermute x5 -> x18, waiting for transfers between devices: 133 us -> 30.1 us  [move(): return lax.ppermute(value, AXES, pairs)]
    reduce_scatter x1 -> x0, waiting for transfers between devices: 70.8 us -> none  [shards(): lax.psum_scatter(full_term.astype(jnp.bfloat16), 'ts', scatter_dimension=...]
    all_to_all x1 -> x2, waiting for transfers between devices: 0.01 us -> 58.6 us  [the longest x1 50.5 us: shards(): squares = jnp.sum(lax.all_to_all(squares, 'ts', 0, 0, tiled=True), axis=0)]
    pallas_call x0 -> x5, Pallas kernels: none -> 40 us  [the longest x2 20.1 us: backward(): call(backward_kernel, (2, N_Z // Z_STEP), in_specs, [pl.BlockSpec((Z_STEP...]
    dot_general x3 -> x0, matrix products: 23.7 us -> none  [the longest x1 9.64 us: shards(): lax.dot_general(graded, weights, (((1,), (1,)), ((), ())), preferred_elem...]
    all_gather x1, waiting for transfers between devices: 0.01 us -> 22.3 us  [shards(): lax.all_gather(key_cotangent[0], 'ts', axis=0, axis_index_groups=lanes, t...]
    ppermute x5 -> x18, starting transfers between devices: 9.71 us -> 26.3 us  [move(): return lax.ppermute(value, AXES, pairs)]
  transfers between devices with their start and end apart: 8 -> 21, of which waited for: 4 -> 11; matrix products, arithmetic and copies ran while one was open for 4% -> 9% of each run, Pallas kernels for 0% -> 17%
where the time goes in v1:
time: 241 us; the launch traced here: 239 us
  waiting for transfers between devices  112 us (46%)
  starting transfers between devices  49 us (20%)
  Pallas kernels  40 us (17%)
  other arithmetic  18.2 us (8%)
  between operations  15 us (6%)
  local copies, waits for them, and re-layouts  4.85 us (2%)
    all_to_all x1, waiting for transfers between devices, shards(): squares = jnp.sum(lax.all_to_all(squares, 'ts', 0, 0, tiled=True), axis=0)  50.5 us
    ppermute x18, waiting for transfers between devices, move(): return lax.ppermute(value, AXES, pairs)  30.1 us
    ppermute x18, starting transfers between devices, move(): return lax.ppermute(value, AXES, pairs)  26.3 us
    all_gather x1, waiting for transfers between devices, shards(): lax.all_gather(key_cotangent[0], 'ts', axis=0, axis_index_groups=lanes, t...  22.3 us
    pallas_call x2, Pallas kernels, backward(): call(backward_kernel, (2, N_Z // Z_STEP), in_specs, [pl.BlockSpec((Z_STEP...  20.1 us
    all_to_all x1, starting transfers between devices, shards(): squares = jnp.sum(lax.all_to_all(squares, 'ts', 0, 0, tiled=True), axis=0)  15.4 us
    pallas_call x1, Pallas kernels, finish(): call(finish_kernel, (N_Z,), [pl.BlockSpec((rows, LANE), lambda i, place:...  10.4 us
    all_to_all x1, waiting for transfers between devices, shards(): lax.all_to_all(curve, 'ts', 0, 0, tiled=True).astype(F32)  8.08 us
  transfers between devices with their start and end apart: 21, of which 11 were waited for; matrix products, arithmetic and copies ran while one was open for 9% of the time, Pallas kernels for 17%

profile of v1, /device:TPU:1, one launch (start us, length us, event | category | flops | bytes accessed | tf_op | source)
XLA Modules:
  0.0 238.7 jit_solution(13093222890512507279)
XLA Ops:
  8.6 2.7 %shard_map.102 = bf16[272,1024]{1,0:T(8,128)(2,1)} custom-call(s32[3]{0:T(128)} %pad_add_fusion.place, bf16[256,1024]{1,0:T(8,128)(2,1)} %bitcast.46, f32[1,256]{1,0:T(1,128)} %gain.5), custom_call_target="tpu_custom_call" | custom-call | bytes 1114112 | tf_op jit(solution)/shard_map/pallas_call | solution.py:101
  11.3 4.5 %collective-permute-start.1 = (bf16[272,1024]{1,0:T(8,128)(2,1)}, bf16[272,1024]{1,0:T(8,128)(2,1)S(1)}, u32[]{:S(2)}, u32[]{:S(2)}) collective-permute-start(bf16[272,1024]{1,0:T(8,128)(2,1)} %shard_map.102), channel_id=1, source_target_pairs={{0,224},{1,225},{2,226},{3,227},{4,228},{5,229},{6,230},{7,231},{8... | collective-permute-start | bytes 1671176 | tf_op jit(solution)/shard_map/ppermute | solution.py:30
  15.8 11.6 %collective-permute-done.1.packed_mine = bf16[272,1024]{1,0:T(8,128)(2,1)S(1)} collective-permute-done((bf16[272,1024]{1,0:T(8,128)(2,1)}, bf16[272,1024]{1,0:T(8,128)(2,1)S(1)}, u32[]{:S(2)}, u32[]{:S(2)}) %collective-permute-start.1) | collective-permute-done | bytes 557088 | tf_op jit(solution)/shard_map/ppermute | solution.py:30
  27.4 4.2 %collective-permute-start.3 = (bf16[4096,256]{1,0:T(8,128)(2,1)}, bf16[4096,256]{1,0:T(8,128)(2,1)}, u32[]{:S(2)}, u32[]{:S(2)}) collective-permute-start(bf16[4096,256]{1,0:T(8,128)(2,1)} %bitcast.49), channel_id=1, source_target_pairs={{0,224},{1,225},{2,226},{3,227},{4,228},{5,229},{6,230},{7,231},{8... | collective-permute-start | bytes 6291464 | tf_op jit(solution)/shard_map/ppermute | solution.py:30
  31.6 2.2 multiply_reduce_fusion.1
  33.8 2.2 multiply_reduce_fusion
  37.0 15.4 %all-to-all-start = ((f32[32,34,128]{2,1,0:T(8,128)}), f32[32,34,128]{2,1,0:T(8,128)S(1)}, u32[]{:S(2)}, u32[]{:S(2)}) async-start(f32[32,34,128]{2,1,0:T(8,128)} %pad_maximum_fusion), calls=%async_computation | async-start | bytes 1310720 | tf_op jit(solution)/shard_map/all_to_all | solution.py:280
  54.0 50.5 %all-to-all-done = f32[32,34,128]{2,1,0:T(8,128)S(1)} async-done(((f32[32,34,128]{2,1,0:T(8,128)}), f32[32,34,128]{2,1,0:T(8,128)S(1)}, u32[]{:S(2)}, u32[]{:S(2)}) %all-to-all-start) | async-done | bytes 557088 | tf_op jit(solution)/shard_map/all_to_all | solution.py:280
  104.7 6.8 %shard_map.103 = bf16[16,128,1024]{2,1,0:T(8,128)(2,1)} custom-call(s32[3]{0:T(128)} %pad_add_fusion.place, bf16[16,2,128,256]{3,2,1,0:T(8,128)(2,1)} %bitcast.44, bf16[16,128,256]{2,1,0:T(8,128)(2,1)} %collective-permute-done.rows_other, bf16[272,1024]{1,0:T(8,128)(2,1)} %copy-done.3, bf16[272,1024]{1,0:T(8,128)(2,1)} %collective-permute-done.2.packed_other), custom_call_target="tpu_custom_call" | custom-call | flops 2147483648 | bytes 7340032 | tf_op jit(solution)/shard_map/pallas_call | solution.py:129
  111.5 22.3 %all-gather.3.cloned.1.call-done = bf16[1,2048,1024]{2,1,0:T(8,128)(2,1)} async-done(((bf16[1,128,1024]{2,1,0:T(8,128)(2,1)}), bf16[1,2048,1024]{2,1,0:T(8,128)(2,1)}) %all-gather.3.cloned.1.call-update) | async-done | bytes 4194320 | tf_op jit(solution)/shard_map/all_gather | solution.py:266
  133.8 4.5 %collective-permute-start.12 = (bf16[2048,1024]{1,0:T(8,128)(2,1)}, bf16[2048,1024]{1,0:T(8,128)(2,1)}, u32[]{:S(2)}, u32[]{:S(2)}) collective-permute-start(bf16[2048,1024]{1,0:T(8,128)(2,1)} %bitcast.59), channel_id=1, source_target_pairs={{0,1},{1,0},{2,3},{3,2},{4,5},{5,4},{6,7},{7,6},{8,9},{9,8},{10,11... | collective-permute-start | bytes 12582920 | tf_op jit(solution)/shard_map/ppermute | solution.py:30
  138.3 1.9 constant_dynamic-slice_fusion
  140.1 2.7 %collective-permute-start.5 = (bf16[2,128,1024]{2,1,0:T(8,128)(2,1)}, bf16[2,128,1024]{2,1,0:T(8,128)(2,1)}, u32[]{:S(2)}, u32[]{:S(2)}) collective-permute-start(bf16[2,128,1024]{2,1,0:T(8,128)(2,1)} %constant_dynamic-slice_fusion), channel_id=1, source_target_pairs={{1,29},{3,31},{5,1},{7,3},{9,5},{11,7},{13,9},{15,11},{17,13},{19,... | collective-permute-start | bytes 1572872 | tf_op jit(solution)/shard_map/ppermute | solution.py:30
  142.9 1.5 collective-permute-start.4
  145.5 5.2 %collective-permute-done.5 = bf16[2,128,1024]{2,1,0:T(8,128)(2,1)} collective-permute-done((bf16[2,128,1024]{2,1,0:T(8,128)(2,1)}, bf16[2,128,1024]{2,1,0:T(8,128)(2,1)}, u32[]{:S(2)}, u32[]{:S(2)}) %collective-permute-start.5) | collective-permute-done | bytes 524320 | tf_op jit(solution)/shard_map/ppermute | solution.py:30
  150.7 2.7 %add_convert_fusion.4 = (bf16[2,128,1024]{2,1,0:T(8,128)(2,1)}, bf16[2,128,1024]{2,1,0:T(8,128)(2,1)S(1)}) fusion(bf16[2,128,1024]{2,1,0:T(8,128)(2,1)} %collective-permute-done.5, bf16[16,128,1024]{2,1,0:T(8,128)(2,1)} %shard_map.103, s32[]{:T(128)S(6)} %select_n.104, bf16[2,128,1024]{2,1,0:T(8,128)(2,1)} %collective-permute-done.4, s32[]{:T(128)S(6)} %select_n.100), kind=kLoop, calls=%fused_computation.9 | loop fusion | flops 2097152 | bytes 3145736 | tf_op jit(solution)/shard_map/convert_element_type | solution.py:74
  153.4 1.8 collective-permute-start.7
  156.4 9.9 %shard_map.104 = (f32[8,2,2,128,256]{4,3,2,1,0:T(8,128)}, f32[8,2,2,1,128]{4,3,2,1,0:T(1,128)}, f32[256,1024]{1,0:T(8,128)}, f32[1,256]{1,0:T(1,128)}) custom-call(s32[3]{0:T(128)} %pad_add_fusion.place, bf16[8,2,128,1024]{3,2,1,0:T(8,128)(2,1)} %bitcast.60, bf16[256,1024]{1,0:T(8,128)(2,1)} %bitcast.47, bf16[8,2,2,128,256]{4,3,2,1,0:T(8,128)(2,1)} %bitcast.13.older, ...), custom_call_target="tpu_custom_call" | custom-call | flops 2147483648 | bytes 9437184 | tf_op jit(solution)/shard_map/pallas_call | solution.py:204
  166.3 1.7 collective-permute-done.6
  168.1 2.4 collective-permute-done.9.early
  170.4 3.1 %add_convert_fusion.2 = (bf16[2,128,1024]{2,1,0:T(8,128)(2,1)}, bf16[2,128,1024]{2,1,0:T(8,128)(2,1)S(1)}) fusion(bf16[2,128,1024]{2,1,0:T(8,128)(2,1)} %collective-permute-done.7, bf16[16,128,1024]{2,1,0:T(8,128)(2,1)} %shard_map.103, s32[]{:T(128)S(6)} %select_n.106, bf16[2,128,1024]{2,1,0:T(8,128)(2,1)} %collective-permute-done.6, s32[]{:T(128)S(6)} %select_n.98), kind=kLoop, calls=%fused_computation.5 | loop fusion | flops 2097152 | bytes 3145736 | tf_op jit(solution)/shard_map/convert_element_type | solution.py:74
  175.0 1.7 collective-permute-start.15
  176.7 10.3 %shard_map.105 = (f32[8,2,2,128,256]{4,3,2,1,0:T(8,128)}, f32[8,2,2,1,128]{4,3,2,1,0:T(1,128)}, f32[256,1024]{1,0:T(8,128)}, f32[1,256]{1,0:T(1,128)}) custom-call(s32[3]{0:T(128)} %pad_add_fusion.place, bf16[8,2,128,1024]{3,2,1,0:T(8,128)(2,1)} %bitcast.18.cot, bf16[256,1024]{1,0:T(8,128)(2,1)} %bitcast.48, ...), custom_call_target="tpu_custom_call", output_to_operand_aliasing={{0}: (6, {}), {1}: (7, {})} | custom-call | flops 2147483648 | bytes 9437184 | tf_op jit(solution)/shard_map/pallas_call | solution.py:204
  188.4 7.3 %all-to-all-start.1 = ((bf16[32,32,128]{2,1,0:T(8,128)(2,1)}), bf16[32,32,128]{2,1,0:T(8,128)(2,1)S(1)}, u32[]{:S(2)}, u32[]{:S(2)}) async-start(bf16[32,32,128]{2,1,0:T(8,128)(2,1)} %broadcast_in_dim.26), calls=%async_computation.1 | async-start | bytes 524288 | tf_op jit(solution)/shard_map/all_to_all | solution.py:322
  195.7 1.9 add_convert_fusion.1
  197.7 1.5 collective-permute-start.13
  199.1 1.4 collective-permute-start.14
  200.5 8.1 %all-to-all-done.1 = bf16[32,32,128]{2,1,0:T(8,128)(2,1)S(1)} async-done(((bf16[32,32,128]{2,1,0:T(8,128)(2,1)}), bf16[32,32,128]{2,1,0:T(8,128)(2,1)S(1)}, u32[]{:S(2)}, u32[]{:S(2)}) %all-to-all-start.1) | async-done | bytes 262176 | tf_op jit(solution)/shard_map/all_to_all | solution.py:322
  209.3 5.6 %collective-permute-done.14 = bf16[2,128,1024]{2,1,0:T(8,128)(2,1)} collective-permute-done((bf16[2,128,1024]{2,1,0:T(8,128)(2,1)S(1)}, bf16[2,128,1024]{2,1,0:T(8,128)(2,1)}, u32[]{:S(2)}, u32[]{:S(2)}) %collective-permute-start.14) | collective-permute-done | bytes 524320 | tf_op jit(solution)/shard_map/ppermute | solution.py:30
  216.1 1.5 convert_add_fusion
  218.4 10.4 %shard_map.106 = bf16[4096,256]{1,0:T(8,128)(2,1)} custom-call(s32[3]{0:T(128)} %pad_add_fusion.place, bf16[2048,256]{1,0:T(8,128)(2,1)} %copy-done.2, bf16[2048,256]{1,0:T(8,128)(2,1)} %collective-permute-done.15.late, f32[4096,256]{1,0:T(8,128)} %bitcast.43, bf16[4096,256]{1,0:T(8,128)(2,1)} %collective-permute-done.3.older, f32[8,4,128]{2,1,0:T(4,128)} %bitcast.53), custom_call_target="tpu_custom_call" | custom-call | bytes 10485760 | tf_op jit(solution)/shard_map/pallas_call | solution.py:236
  228.7 1.6 collective-permute-done.16
  (49 shorter events, 13.0 us)
Async XLA Ops:
  7.2 126.7 %all-gather.3.cloned.1.call-start = ((), (), s32[]{:S(2)}) async-start(), calls=%async_computation.2 | async-start | bytes 4456448 | tf_op jit(solution)/shard_map/all_gather | solution.py:266
  8.6 43.8 %copy-start = (bf16[1,4096,256]{2,1,0:T(8,128)(2,1)S(1)}, bf16[1,4096,256]{2,1,0:T(8,128)(2,1)}, u32[]{:S(2)}) copy-start(bf16[1,4096,256]{2,1,0:T(8,128)(2,1)} %param.7) | copy-start | bytes 6291460
  11.3 16.1 %collective-permute-start.1 = (bf16[272,1024]{1,0:T(8,128)(2,1)}, bf16[272,1024]{1,0:T(8,128)(2,1)S(1)}, u32[]{:S(2)}, u32[]{:S(2)}) collective-permute-start(bf16[272,1024]{1,0:T(8,128)(2,1)} %shard_map.102), channel_id=1, source_target_pairs={{0,224},{1,225},{2,226},{3,227},{4,228},{5,229},{6,230},{7,231},{8... | collective-permute-start | bytes 1671176 | tf_op jit(solution)/shard_map/ppermute | solution.py:30
  27.4 26.3 %copy-start.3 = (bf16[272,1024]{1,0:T(8,128)(2,1)}, bf16[272,1024]{1,0:T(8,128)(2,1)S(1)}, u32[]{:S(2)}) copy-start(bf16[272,1024]{1,0:T(8,128)(2,1)S(1)} %collective-permute-done.1.packed_mine) | copy-start | bytes 1671172
  27.4 84.1 %collective-permute-start.3 = (bf16[4096,256]{1,0:T(8,128)(2,1)}, bf16[4096,256]{1,0:T(8,128)(2,1)}, u32[]{:S(2)}, u32[]{:S(2)}) collective-permute-start(bf16[4096,256]{1,0:T(8,128)(2,1)} %bitcast.49), channel_id=1, source_target_pairs={{0,224},{1,225},{2,226},{3,227},{4,228},{5,229},{6,230},{7,231},{8... | collective-permute-start | bytes 6291464 | tf_op jit(solution)/shard_map/ppermute | solution.py:30
  37.0 67.4 %all-to-all-start = ((f32[32,34,128]{2,1,0:T(8,128)}), f32[32,34,128]{2,1,0:T(8,128)S(1)}, u32[]{:S(2)}, u32[]{:S(2)}) async-start(f32[32,34,128]{2,1,0:T(8,128)} %pad_maximum_fusion), calls=%async_computation | async-start | bytes 1310720 | tf_op jit(solution)/shard_map/all_to_all | solution.py:280
  53.5 51.2 %collective-permute-start = (bf16[16,128,256]{2,1,0:T(8,128)(2,1)}, bf16[16,128,256]{2,1,0:T(8,128)(2,1)}, u32[]{:S(2)}, u32[]{:S(2)}) collective-permute-start(bf16[16,128,256]{2,1,0:T(8,128)(2,1)} %dynamic-slice_bitcast_fusion), channel_id=1, source_target_pairs={{0,1},{1,0},{2,3},{3,2},{4,5},{5,4},{6,7},{7,6},{8,9},{9,8},{10,11... | collective-permute-start | bytes 3145736 | tf_op jit(solution)/shard_map/ppermute | solution.py:30
  53.7 50.9 %collective-permute-start.2 = (bf16[272,1024]{1,0:T(8,128)(2,1)S(1)}, bf16[272,1024]{1,0:T(8,128)(2,1)}, u32[]{:S(2)}, u32[]{:S(2)}) collective-permute-start(bf16[272,1024]{1,0:T(8,128)(2,1)S(1)} %collective-permute-done.1.packed_mine), channel_id=1, source_target_pairs={{0,1},{1,0},{2,3},{3,2},{4,5},{5,4},{6,7},{7,6},{8,9},{9,8},{10,11... | collective-permute-start | bytes 1671176 | tf_op jit(solution)/shard_map/ppermute | solution.py:30
  104.5 39.8 %copy-start.1 = (bf16[1,4096,256]{2,1,0:T(8,128)(2,1)S(1)}, bf16[1,4096,256]{2,1,0:T(8,128)(2,1)}, u32[]{:S(2)}) copy-start(bf16[1,4096,256]{2,1,0:T(8,128)(2,1)} %param.9) | copy-start | bytes 6291460
  104.5 6.9 %collective-permute-start.8 = (f32[32,128]{1,0:T(8,128)S(1)}, f32[32,128]{1,0:T(8,128)S(1)}, u32[]{:S(2)}, u32[]{:S(2)}) collective-permute-start(f32[32,128]{1,0:T(8,128)S(1)} %slice.24), channel_id=1, source_target_pairs={{0,224},{1,225},{2,226},{3,227},{4,228},{5,229},{6,230},{7,231},{8... | collective-permute-start | bytes 49160 | tf_op jit(solution)/shard_map/ppermute | solution.py:30
  133.8 42.8 %collective-permute-start.12 = (bf16[2048,1024]{1,0:T(8,128)(2,1)}, bf16[2048,1024]{1,0:T(8,128)(2,1)}, u32[]{:S(2)}, u32[]{:S(2)}) collective-permute-start(bf16[2048,1024]{1,0:T(8,128)(2,1)} %bitcast.59), channel_id=1, source_target_pairs={{0,1},{1,0},{2,3},{3,2},{4,5},{5,4},{6,7},{7,6},{8,9},{9,8},{10,11... | collective-permute-start | bytes 12582920 | tf_op jit(solution)/shard_map/ppermute | solution.py:30
  140.1 10.5 %collective-permute-start.5 = (bf16[2,128,1024]{2,1,0:T(8,128)(2,1)}, bf16[2,128,1024]{2,1,0:T(8,128)(2,1)}, u32[]{:S(2)}, u32[]{:S(2)}) collective-permute-start(bf16[2,128,1024]{2,1,0:T(8,128)(2,1)} %constant_dynamic-slice_fusion), channel_id=1, source_target_pairs={{1,29},{3,31},{5,1},{7,3},{9,5},{11,7},{13,9},{15,11},{17,13},{19,... | collective-permute-start | bytes 1572872 | tf_op jit(solution)/shard_map/ppermute | solution.py:30
  142.9 7.8 %collective-permute-start.4 = (bf16[2,128,1024]{2,1,0:T(8,128)(2,1)}, bf16[2,128,1024]{2,1,0:T(8,128)(2,1)}, u32[]{:S(2)}, u32[]{:S(2)}) collective-permute-start(bf16[2,128,1024]{2,1,0:T(8,128)(2,1)} %constant_dynamic-slice_fusion), channel_id=1, source_target_pairs={{0,4},{2,6},{4,8},{6,10},{8,12},{10,14},{12,16},{14,18},{16,20},{1... | collective-permute-start | bytes 1572872 | tf_op jit(solution)/shard_map/ppermute | solution.py:30
  145.5 25.0 %collective-permute-start.9 = (bf16[2048,256]{1,0:T(8,128)(2,1)}, bf16[2048,256]{1,0:T(8,128)(2,1)S(1)}, u32[]{:S(2)}, u32[]{:S(2)}) collective-permute-start(bf16[2048,256]{1,0:T(8,128)(2,1)} %get-tuple-element.35), channel_id=1, source_target_pairs={{0,224},{1,225},{2,226},{3,227},{4,228},{5,229},{6,230},{7,231},{8... | collective-permute-start | bytes 3145736 | tf_op jit(solution)/shard_map/ppermute | solution.py:30
  153.4 12.9 %collective-permute-start.7 = (bf16[2,128,1024]{2,1,0:T(8,128)(2,1)}, bf16[2,128,1024]{2,1,0:T(8,128)(2,1)}, u32[]{:S(2)}, u32[]{:S(2)}) collective-permute-start(bf16[2,128,1024]{2,1,0:T(8,128)(2,1)} %get-tuple-element.54), channel_id=1, source_target_pairs={{0,28},{1,29},{2,30},{3,31},{4,0},{5,1},{6,2},{7,3},{8,4},{9,5},{1... | collective-permute-start | bytes 1572872 | tf_op jit(solution)/shard_map/ppermute | solution.py:30
  155.2 12.9 %collective-permute-start.6 = (bf16[2,128,1024]{2,1,0:T(8,128)(2,1)S(1)}, bf16[2,128,1024]{2,1,0:T(8,128)(2,1)}, u32[]{:S(2)}, u32[]{:S(2)}) collective-permute-start(bf16[2,128,1024]{2,1,0:T(8,128)(2,1)S(1)} %get-tuple-element.55), channel_id=1, source_target_pairs={{0,4},{1,5},{2,6},{3,7},{4,8},{5,9},{6,10},{7,11},{8,12},{9,13},{1... | collective-permute-start | bytes 1572872 | tf_op jit(solution)/shard_map/ppermute | solution.py:30
  170.4 16.5 %copy-start.2 = (bf16[2048,256]{1,0:T(8,128)(2,1)}, bf16[2048,256]{1,0:T(8,128)(2,1)S(1)}, u32[]{:S(2)}) copy-start(bf16[2048,256]{1,0:T(8,128)(2,1)S(1)} %collective-permute-done.9.early) | copy-start | bytes 3145732
  173.5 22.2 %collective-permute-start.11 = (bf16[2,128,1024]{2,1,0:T(8,128)(2,1)}, bf16[2,128,1024]{2,1,0:T(8,128)(2,1)}, u32[]{:S(2)}, u32[]{:S(2)}) collective-permute-start(bf16[2,128,1024]{2,1,0:T(8,128)(2,1)} %get-tuple-element.52), channel_id=1, source_target_pairs={{0,28},{1,29},{2,30},{3,31},{4,0},{5,1},{6,2},{7,3},{8,4},{9,5},{1... | collective-permute-start | bytes 1572872 | tf_op jit(solution)/shard_map/ppermute | solution.py:30
  173.8 22.0 %collective-permute-start.10 = (bf16[2,128,1024]{2,1,0:T(8,128)(2,1)S(1)}, bf16[2,128,1024]{2,1,0:T(8,128)(2,1)}, u32[]{:S(2)}, u32[]{:S(2)}) collective-permute-start(bf16[2,128,1024]{2,1,0:T(8,128)(2,1)S(1)} %get-tuple-element.53), channel_id=1, source_target_pairs={{0,4},{1,5},{2,6},{3,7},{4,8},{5,9},{6,10},{7,11},{8,12},{9,13},{1... | collective-permute-start | bytes 1572872 | tf_op jit(solution)/shard_map/ppermute | solution.py:30
  175.0 34.3 %collective-permute-start.15 = (bf16[2048,256]{1,0:T(8,128)(2,1)S(1)}, bf16[2048,256]{1,0:T(8,128)(2,1)}, u32[]{:S(2)}, u32[]{:S(2)}) collective-permute-start(bf16[2048,256]{1,0:T(8,128)(2,1)S(1)} %get-tuple-element.45), channel_id=1, source_target_pairs={{0,224},{1,225},{2,226},{3,227},{4,228},{5,229},{6,230},{7,231},{8... | collective-permute-start | bytes 3145736 | tf_op jit(solution)/shard_map/ppermute | solution.py:30
  188.4 20.2 %all-to-all-start.1 = ((bf16[32,32,128]{2,1,0:T(8,128)(2,1)}), bf16[32,32,128]{2,1,0:T(8,128)(2,1)S(1)}, u32[]{:S(2)}, u32[]{:S(2)}) async-start(bf16[32,32,128]{2,1,0:T(8,128)(2,1)} %broadcast_in_dim.26), calls=%async_computation.1 | async-start | bytes 524288 | tf_op jit(solution)/shard_map/all_to_all | solution.py:322
  197.7 18.4 %collective-permute-start.13 = (bf16[2,128,1024]{2,1,0:T(8,128)(2,1)S(1)}, bf16[2,128,1024]{2,1,0:T(8,128)(2,1)S(1)}, u32[]{:S(2)}, u32[]{:S(2)}) collective-permute-start(bf16[2,128,1024]{2,1,0:T(8,128)(2,1)S(1)} %get-tuple-element.50), channel_id=1, source_target_pairs={{0,4},{1,5},{2,6},{3,7},{4,8},{5,9},{6,10},{7,11},{8,12},{9,13},{1... | collective-permute-start | bytes 1572872 | tf_op jit(solution)/shard_map/ppermute | solution.py:30
  199.1 15.8 %collective-permute-start.14 = (bf16[2,128,1024]{2,1,0:T(8,128)(2,1)S(1)}, bf16[2,128,1024]{2,1,0:T(8,128)(2,1)}, u32[]{:S(2)}, u32[]{:S(2)}) collective-permute-start(bf16[2,128,1024]{2,1,0:T(8,128)(2,1)S(1)} %get-tuple-element.51), channel_id=1, source_target_pairs={{0,28},{1,29},{2,30},{3,31},{4,0},{5,1},{6,2},{7,3},{8,4},{9,5},{1... | collective-permute-start | bytes 1572872 | tf_op jit(solution)/shard_map/ppermute | solution.py:30
  217.7 12.6 %collective-permute-start.16 = (bf16[128,1024]{1,0:T(8,128)(2,1)S(1)}, bf16[128,1024]{1,0:T(8,128)(2,1)S(1)}, u32[]{:S(2)}, u32[]{:S(2)}) collective-permute-start(bf16[128,1024]{1,0:T(8,128)(2,1)S(1)} %get-tuple-element.58), channel_id=1, source_target_pairs={{0,32},{1,33},{2,34},{3,35},{4,36},{5,37},{6,38},{7,39},{8,40},{9,... | collective-permute-start | bytes 786440 | tf_op jit(solution)/shard_map/ppermute | solution.py:30
  217.8 13.3 %collective-permute-start.17 = (bf16[128,1024]{1,0:T(8,128)(2,1)S(1)}, bf16[128,1024]{1,0:T(8,128)(2,1)S(1)}, u32[]{:S(2)}, u32[]{:S(2)}) collective-permute-start(bf16[128,1024]{1,0:T(8,128)(2,1)S(1)} %get-tuple-element.59), channel_id=1, source_target_pairs={{0,34},{1,35},{2,32},{3,33},{4,38},{5,39},{6,36},{7,37},{8,42},{9,... | collective-permute-start | bytes 786440 | tf_op jit(solution)/shard_map/ppermute | solution.py:30
Sparse Core Ops, SparseCore 0:
  10.6 123.1 all-gather.2

commit v2 on v1

v2 whole, which is shorter than its diff:
```python
import jax
import jax.numpy as jnp
from jax import lax
from jax.experimental import pallas as pl
from jax.experimental.pallas import tpu as pltpu
from jax.sharding import PartitionSpec as P

eps = 1e-05
BF = jnp.bfloat16
F32 = jnp.float32
N_S = 8
N_T = 32
N_Z = 8
TOK = 4096
OWN = TOK // N_T
WIDTH = 8192
LANE = WIDTH // N_T
KEYS = 1024
PACK = LANE + 16
SPLIT = TOK // 2
AXES = ("section", "ts")


def move(value, target, cores=(0, 1)):
    pairs = []
    for s in range(N_S):
        for t in [t for t in range(N_T) if t % 2 in cores]:
            to_s, to_t = target(s, t)
            pairs.append((s * N_T + t, to_s * N_T + to_t))
    return lax.ppermute(value, AXES, pairs)


def to_next(s, t):
    return (s + 1) % N_S, t


def to_previous(s, t):
    return (s - 1) % N_S, t


def to_mirror(s, t):
    return N_S - 1 - s, t


def to_mirror_other_half(s, t):
    return N_S - 1 - s, t ^ 2


def to_other_core(s, t):
    return s, t ^ 1


def to_other_half(s, t):
    return s, t ^ 2


def to_next_other_half(s, t):
    return (s + 1) % N_S, t ^ 2


def z_up(s, t):
    return s, (t + 4) % N_T


def z_down(s, t):
    return s, (t - 4) % N_T


def pick(value, index):
    return lax.dynamic_index_in_dim(value, index, 0, keepdims=False)


def after(value, *others):
    return lax.optimization_barrier((value,) + others)[0]


def add(a, b):
    return (a.astype(F32) + b.astype(F32)).astype(BF)


def call(kernel, grid, in_specs, out_specs, out_shape, flops, size, scratch=()):
    return pl.pallas_call(
        kernel,
        grid_spec=pltpu.PrefetchScalarGridSpec(
            num_scalar_prefetch=1,
            grid=grid,
            in_specs=in_specs,
            out_specs=out_specs,
            scratch_shapes=scratch,
        ),
        out_shape=out_shape,
        compiler_params=pltpu.CompilerParams(vmem_limit_bytes=24 * 1024 * 1024),
        cost_estimate=pl.CostEstimate(flops=flops, bytes_accessed=size, transcendentals=0),
    )


def pack_kernel(place, weights, gain, out):
    out[:LANE, :] = weights[...]
    value = gain[...]
    high = value.astype(BF)
    middle = (value - high.astype(F32)).astype(BF)
    low = (value - high.astype(F32) - middle.astype(F32)).astype(BF)
    row = jnp.concatenate([high, middle, low, jnp.zeros((1, LANE), BF)], axis=1)
    out[LANE:, :] = jnp.broadcast_to(row, (PACK - LANE, KEYS))


def pack(place, weights, gain):
    return call(
        pack_kernel,
        (1,),
        [
            pl.BlockSpec((LANE, KEYS), lambda i, place: (0, 0)),
            pl.BlockSpec((1, LANE), lambda i, place: (0, 0)),
        ],
        pl.BlockSpec((PACK, KEYS), lambda i, place: (0, 0)),
        jax.ShapeDtypeStruct((PACK, KEYS), BF),
        0,
        2 * PACK * KEYS * 2,
    )(place, weights, gain)


def forward_kernel(place, rows_mine, rows_other, packed_mine, packed_other, out, weights):
    rows = out.shape[0] * OWN

    @pl.when(pl.program_id(0) == 0)
    def _():
        weights[:LANE, :] = packed_mine[:LANE, :]
        weights[LANE:, :] = packed_other[:LANE, :]

    left = []
    for block, packed in ((rows_mine, packed_mine), (rows_other, packed_other)):
        pieces = packed[LANE : LANE + 1, :].astype(F32)
        gains = pieces[:, :LANE] + pieces[:, LANE : 2 * LANE] + pieces[:, 2 * LANE : 3 * LANE]
        left.append((block[...].reshape(rows, LANE).astype(F32) * gains).astype(BF))
    total = jnp.dot(jnp.concatenate(left, axis=1), weights[...], preferred_element_type=F32)
    out[...] = total.astype(BF).reshape(out.shape)


def forward(place, fresh, rows_other, packed_mine, packed_other):
    step = 4
    return call(
        forward_kernel,
        (N_T // 2 // step,),
        [
            pl.BlockSpec((step, 1, OWN, LANE), lambda i, place: (i, place[0], 0, 0)),
            pl.BlockSpec((step, OWN, LANE), lambda i, place: (i, 0, 0)),
            pl.BlockSpec((PACK, KEYS), lambda i, place: (0, 0)),
            pl.BlockSpec((PACK, KEYS), lambda i, place: (0, 0)),
        ],
        pl.BlockSpec((step, OWN, KEYS), lambda i, place: (i, 0, 0)),
        jax.ShapeDtypeStruct((N_T // 2, OWN, KEYS), BF),
        2 * TOK // 2 * 2 * LANE * KEYS,
        7 * 1024 * 1024,
        [pltpu.VMEM((2 * LANE, KEYS), BF)],
    )(place, fresh, rows_other, packed_mine, packed_other)


def shards(upstream, stashed, returning, key_cotangent, key_weight, norm_gain, lengths):
    lane = lax.axis_index("ts")
    core = lane % 2
    half = (lane // 2) % 2
    z = lane // 4
    place = core.astype(jnp.int32)[None]
    gain = norm_gain[0]
    weights = key_weight[0]
    fresh = upstream[0]
    saved = stashed[0]

    def by_core(value):
        parts = value.reshape(N_T // 2, 2, OWN, *value.shape[1:])
        return [
            lax.dynamic_index_in_dim(parts, index, 1, keepdims=False).reshape(
                TOK // 2, *value.shape[1:]
            )
            for index in (core, 1 - core)
        ]

    fresh_wide = fresh.astype(F32)
    saved_wide = saved.astype(F32)
    fresh_part = jnp.sum(fresh_wide * fresh_wide, axis=1).reshape(N_Z, 2, 2, OWN)
    saved_part = jnp.sum(saved_wide * saved_wide, axis=1).reshape(1, N_T, OWN)
    squares = jnp.concatenate(
        [
            fresh_part.reshape(N_T, 1, OWN).astype(BF),
            fresh_part[:, ::-1].reshape(N_T, 1, OWN).astype(BF),
            jnp.broadcast_to(saved_part.astype(BF), (N_T, N_T, OWN)),
        ],
        axis=1,
    )
    squares = lax.all_to_all(squares, "ts", 0, 0, tiled=True)

    packed = move(after(pack(place, weights, norm_gain), squares), to_previous)
    squares = jnp.sum(squares.astype(F32), axis=0)
    fresh_rate = lax.rsqrt(squares[:2] / WIDTH + eps)
    older_sq = move(squares[2:], to_mirror)

    cot_own = key_cotangent[0]
    cot_half = move(cot_own, to_other_half)
    cot_pair = jnp.stack(
        [jnp.where(half == 0, cot_own, cot_half), jnp.where(half == 0, cot_half, cot_own)]
    )
    lanes = [[q * 4 + j for q in range(N_Z)] for j in range(4)]
    cot_mine = lax.all_gather(cot_pair, "ts", axis=0, axis_index_groups=lanes, tiled=True)
    cot_mine = cot_mine.reshape(TOK // 2, KEYS)

    older = move(after(saved, squares), to_mirror)

    rows = fresh.reshape(N_T // 2, 2, OWN, LANE)
    rows_other = move(lax.dynamic_index_in_dim(rows, 1 - core, 1, keepdims=False), to_other_core)
    packed_other = move(packed, to_other_core)
    partial = forward(place, rows, rows_other, packed, packed_other)

    def block(distance):
        return lax.dynamic_slice_in_dim(partial, ((z + distance) % N_Z) * 2, 2, 0)

    up = move(block(4), z_up, (0,))
    down = move(block(4), z_down, (1,))
    up, down = lax.optimization_barrier((up, down))
    up = move(add(block(3), up), z_up)
    down = move(add(block(-3), down), z_down)
    up, down = lax.optimization_barrier((up, down, older))[:2]
    up = add(block(2), up)
    down = add(block(-2), down)

    cot_mine, older_sq = lax.optimization_barrier((cot_mine, older_sq, up, down, older))[:2]
    early = move(after(returning[0, :SPLIT], older, older_sq), to_previous)
    late = move(after(returning[0, SPLIT:], older, older_sq), to_previous)
    up = move(up, z_up)
    down = move(down, z_down)
    cots = [cot_mine, after(move(cot_mine, to_other_core), early)]
    older_rate = lax.rsqrt(older_sq / WIDTH + eps).reshape(TOK)
    live = (jnp.arange(TOK, dtype=jnp.int32) < lengths[0]).astype(F32)
    scales = by_core(live * older_rate)
    raw = [
        lax.dot_general(cot, weights, (((1,), (1,)), ((), ())), preferred_element_type=F32)
        for cot in cots
    ]
    up, down, raw[0] = lax.optimization_barrier((up, down, raw[0]))
    up = move(add(block(1), up), z_up)
    down = move(add(block(-1), down), z_down)
    grads = []
    curves = []
    weight_total = jnp.zeros((LANE, KEYS), F32)
    gain_grad = jnp.zeros((LANE,), F32)
    for cot, product, rows, scale in zip(cots, raw, by_core(older), scales):
        wide = rows.astype(F32)
        grad = scale[:, None] * product
        grads.append(grad)
        curves.append(jnp.sum(grad * (wide * gain).astype(BF).astype(F32), axis=1))
        gain_grad = gain_grad + jnp.sum(grad * wide, axis=0)
        weight_total = weight_total + lax.dot_general(
            (wide * gain * scale[:, None]).astype(BF),
            cot,
            (((0,), (0,)), ((), ())),
            preferred_element_type=F32,
        )

    mine = (jnp.arange(2) == core)[None, :, None]
    curve = [part.reshape(N_T // 2, 1, OWN) for part in curves]
    curve = jnp.where(mine, curve[0], curve[1])
    curve = jnp.broadcast_to(curve.reshape(1, N_T, OWN).astype(BF), (N_T, N_T, OWN))
    curve = lax.all_to_all(curve, "ts", 0, 0, tiled=True)
    up, down = lax.optimization_barrier((up, down, curve, late))[:2]
    curve = jnp.sum(curve.astype(F32), axis=0).reshape(TOK)
    pull = older_rate * older_rate / WIDTH * curve

    summed = block(0).astype(F32) + up.astype(F32) + down.astype(F32)
    straight = move((pick(summed, half) * fresh_rate[0][:, None]).astype(BF), to_next)
    crossed = move(
        (pick(summed, 1 - half) * fresh_rate[1][:, None]).astype(BF), to_next_other_half
    )
    new_keys = (straight.astype(F32) + crossed.astype(F32)).astype(BF)

    base = [(gain * grad).reshape(N_T // 2, 1, OWN, LANE) for grad in grads]
    base = jnp.where(mine[..., None], base[0], base[1]).reshape(TOK, LANE)
    downstream = jnp.concatenate([early, late], axis=0)
    total = downstream.astype(F32) + base - pull[:, None] * older.astype(F32)
    return (
        new_keys[None],
        total.astype(BF)[None],
        weight_total[None],
        gain_grad[None],
    )


def solution(mesh):
    return jax.shard_map(
        shards,
        mesh=mesh,
        in_specs=(
            P("section", None, "ts"),
            P("section", None, "ts"),
            P("section", None, "ts"),
            P("section", "ts", None),
            P("section", "ts", None),
            P("section", "ts"),
            P("section"),
        ),
        out_specs=(
            P("section", "ts", None),
            P("section", None, "ts"),
            P("section", "ts", None),
            P("section", "ts"),
        ),
        check_vma=False,
    )
```

time: 241 us -> 208 us (0.86)
  Pallas kernels: 40 us -> 5.17 us
  waiting for transfers between devices: 112 us -> 91.1 us
  matrix products: 0 us -> 13.2 us
  starting transfers between devices: 49 us -> 53.8 us
  other arithmetic: 18.2 us -> 21.2 us
  local copies, waits for them, and re-layouts: 4.85 us -> 7.83 us
    ppermute x18 -> x19, waiting for transfers between devices: 30.1 us -> 69.5 us  [move(): return lax.ppermute(value, AXES, pairs)]
    all_to_all x2, waiting for transfers between devices: 58.6 us -> 21.6 us  [the longest x1 15.8 us: shards(): squares = lax.all_to_all(squares, 'ts', 0, 0, tiled=True)]
    pallas_call x3 -> x0, Pallas kernels: 30.5 us -> none  [the longest x2 20.1 us: backward(): call(backward_kernel, (2, N_Z // Z_STEP), in_specs, [pl.BlockSpec((Z_STEP...]
    all_gather x1, waiting for transfers between devices: 22.3 us -> 0.02 us  [shards(): lax.all_gather(cot_pair, 'ts', axis=0, axis_index_groups=lanes, tiled=True)]
    dot_general x0 -> x4, matrix products: none -> 13.2 us  [the longest x2 6.82 us: shards(): lax.dot_general(cot, weights, (((1,), (1,)), ((), ())), preferred_element...]
    ppermute x18 -> x19, starting transfers between devices: 26.3 us -> 31.5 us  [move(): return lax.ppermute(value, AXES, pairs)]
    convert_element_type x1 -> x2, other arithmetic: 0.73 us -> 5.28 us  [the longest x1 5.2 us: shards(): total.astype(BF)[None]]
    unnamed x9 -> x26, local copies, waits for them, and re-layouts: 0.03 us -> 2.85 us
  transfers between devices with their start and end apart: 21 -> 22, of which waited for: 11 -> 11; matrix products, arithmetic and copies ran while one was open for 9% -> 17% of each run, Pallas kernels for 17% -> 2%
where the time goes in v2:
time: 208 us
  waiting for transfers between devices  91.1 us (44%)
  starting transfers between devices  53.8 us (26%)
  other arithmetic  21.2 us (10%)
  between operations  15.1 us (7%)
  matrix products  13.2 us (6%)
  local copies, waits for them, and re-layouts  7.83 us (4%)
  Pallas kernels  5.17 us (2%)
    ppermute x19, waiting for transfers between devices, move(): return lax.ppermute(value, AXES, pairs)  69.5 us
    ppermute x19, starting transfers between devices, move(): return lax.ppermute(value, AXES, pairs)  31.5 us
    all_to_all x1, waiting for transfers between devices, shards(): squares = lax.all_to_all(squares, 'ts', 0, 0, tiled=True)  15.8 us
    all_to_all x1, starting transfers between devices, shards(): squares = lax.all_to_all(squares, 'ts', 0, 0, tiled=True)  13.5 us
    all_to_all x1, starting transfers between devices, shards(): curve = lax.all_to_all(curve, 'ts', 0, 0, tiled=True)  8.83 us
    convert_element_type x3, other arithmetic, add(): return (a.astype(F32) + b.astype(F32)).astype(BF)  6.94 us
    dot_general x2, matrix products, shards(): lax.dot_general(cot, weights, (((1,), (1,)), ((), ())), preferred_element...  6.82 us
    dot_general x2, matrix products, shards(): lax.dot_general((wide * gain * scale[:, None]).astype(BF), cot, (((0,), (...  6.4 us
  transfers between devices with their start and end apart: 22, of which 11 were waited for; matrix products, arithmetic and copies ran while one was open for 17% of the time, Pallas kernels for 2%

profile of v2, /device:TPU:1, one launch (start us, length us, event | category | flops | bytes accessed | tf_op | source)
XLA Modules:
  0.0 207.5 jit_solution(10543037794696385678)
XLA Ops:
  7.2 3.7 %collective-permute-start.10 = (bf16[128,1024]{1,0:T(8,128)(2,1)}, bf16[128,1024]{1,0:T(8,128)(2,1)S(1)}, u32[]{:S(2)}, u32[]{:S(2)}) collective-permute-start(bf16[128,1024]{1,0:T(8,128)(2,1)} %bitcast.103), channel_id=1, source_target_pairs={{0,2},{1,3},{2,0},{3,1},{4,6},{5,7},{6,4},{7,5},{8,10},{9,11},{10,... | collective-permute-start | bytes 786440 | tf_op jit(solution)/shard_map/ppermute | solution.py:30
  10.9 5.3 %collective-permute-done.10 = bf16[128,1024]{1,0:T(8,128)(2,1)S(1)} collective-permute-done((bf16[128,1024]{1,0:T(8,128)(2,1)}, bf16[128,1024]{1,0:T(8,128)(2,1)S(1)}, u32[]{:S(2)}, u32[]{:S(2)}) %collective-permute-start.10) | collective-permute-done | bytes 262176 | tf_op jit(solution)/shard_map/ppermute | solution.py:30
  18.8 2.3 %multiply_reduce_fusion = bf16[4096]{0:T(1024)(128)(2,1)S(1)} fusion(bf16[1,4096,256]{2,1,0:T(8,128)(2,1)} %param.8), kind=kLoop, calls=%fused_computation.4 | loop fusion | flops 3141632 | bytes 2105344 | tf_op jit(solution)/shard_map/reduce_sum | solution.py:181
  22.0 13.5 %all-to-all-start = ((bf16[32,34,128]{2,1,0:T(8,128)(2,1)}), bf16[32,34,128]{2,1,0:T(8,128)(2,1)S(1)}, u32[]{:S(2)}, u32[]{:S(2)}) async-start(bf16[32,34,128]{2,1,0:T(8,128)(2,1)} %pad_maximum_fusion.1), calls=%async_computation | async-start | bytes 655360 | tf_op jit(solution)/shard_map/all_to_all | solution.py:190
  36.4 15.8 %all-to-all-done = bf16[32,34,128]{2,1,0:T(8,128)(2,1)S(1)} async-done(((bf16[32,34,128]{2,1,0:T(8,128)(2,1)}), bf16[32,34,128]{2,1,0:T(8,128)(2,1)S(1)}, u32[]{:S(2)}, u32[]{:S(2)}) %all-to-all-start) | async-done | bytes 278560 | tf_op jit(solution)/shard_map/all_to_all | solution.py:190
  52.2 2.3 %collective-permute-start.1 = (bf16[272,1024]{1,0:T(8,128)(2,1)}, bf16[272,1024]{1,0:T(8,128)(2,1)}, u32[]{:S(2)}, u32[]{:S(2)}) collective-permute-start(bf16[272,1024]{1,0:T(8,128)(2,1)} %shard_map.102), channel_id=1, source_target_pairs={{0,224},{1,225},{2,226},{3,227},{4,228},{5,229},{6,230},{7,231},{8... | collective-permute-start | bytes 1671176 | tf_op jit(solution)/shard_map/ppermute | solution.py:30
  55.6 2.1 collective-permute-start
  57.6 7.8 %collective-permute-done.1.packed_mine = bf16[272,1024]{1,0:T(8,128)(2,1)} collective-permute-done((bf16[272,1024]{1,0:T(8,128)(2,1)}, bf16[272,1024]{1,0:T(8,128)(2,1)}, u32[]{:S(2)}, u32[]{:S(2)}) %collective-permute-start.1) | collective-permute-done | bytes 557088 | tf_op jit(solution)/shard_map/ppermute | solution.py:30
  65.5 2.3 %collective-permute-start.2 = (bf16[272,1024]{1,0:T(8,128)(2,1)}, bf16[272,1024]{1,0:T(8,128)(2,1)}, u32[]{:S(2)}, u32[]{:S(2)}) collective-permute-start(bf16[272,1024]{1,0:T(8,128)(2,1)} %collective-permute-done.1.packed_mine), channel_id=1, source_target_pairs={{0,1},{1,0},{2,3},{3,2},{4,5},{5,4},{6,7},{7,6},{8,9},{9,8},{10,11... | collective-permute-start | bytes 1671176 | tf_op jit(solution)/shard_map/ppermute | solution.py:30
  67.8 4.4 %collective-permute-start.7 = (bf16[4096,256]{1,0:T(8,128)(2,1)}, bf16[4096,256]{1,0:T(8,128)(2,1)}, u32[]{:S(2)}, u32[]{:S(2)}) collective-permute-start(bf16[4096,256]{1,0:T(8,128)(2,1)} %bitcast.7), channel_id=1, source_target_pairs={{0,224},{1,225},{2,226},{3,227},{4,228},{5,229},{6,230},{7,231},{8... | collective-permute-start | bytes 6291464 | tf_op jit(solution)/shard_map/ppermute | solution.py:30
  72.2 4.3 %shard_map.103 = bf16[16,128,1024]{2,1,0:T(8,128)(2,1)S(1)} custom-call(s32[1]{0:T(128)} %bitcast.place, bf16[16,2,128,256]{3,2,1,0:T(8,128)(2,1)S(1)} %bitcast.93, bf16[16,128,256]{2,1,0:T(8,128)(2,1)S(1)} %collective-permute-done.rows_other, bf16[272,1024]{1,0:T(8,128)(2,1)} %collective-permute-done.1.packed_mine, ...), custom_call_target="tpu_custom_call" | custom-call | flops 2147483648 | bytes 7340032 | tf_op jit(solution)/shard_map/pallas_call | solution.py:141
  76.5 2.0 copy-done
  78.5 3.2 %collective-permute-start.4 = (bf16[2,128,1024]{2,1,0:T(8,128)(2,1)S(1)}, bf16[2,128,1024]{2,1,0:T(8,128)(2,1)S(1)}, u32[]{:S(2)}, u32[]{:S(2)}) collective-permute-start(bf16[2,128,1024]{2,1,0:T(8,128)(2,1)S(1)} %constant_dynamic-slice_fusion.4), channel_id=1, source_target_pairs={{1,29},{3,31},{5,1},{7,3},{9,5},{11,7},{13,9},{15,11},{17,13},{19,... | collective-permute-start | bytes 1572872 | tf_op jit(solution)/shard_map/ppermute | solution.py:30
  82.5 6.4 %collective-permute-done.4 = bf16[2,128,1024]{2,1,0:T(8,128)(2,1)S(1)} collective-permute-done((bf16[2,128,1024]{2,1,0:T(8,128)(2,1)S(1)}, bf16[2,128,1024]{2,1,0:T(8,128)(2,1)S(1)}, u32[]{:S(2)}, u32[]{:S(2)}) %collective-permute-start.4) | collective-permute-done | bytes 524320 | tf_op jit(solution)/shard_map/ppermute | solution.py:30
  88.9 2.4 %add_convert_fusion.4 = (bf16[2,128,1024]{2,1,0:T(8,128)(2,1)}, bf16[2,128,1024]{2,1,0:T(8,128)(2,1)S(1)}) fusion(bf16[2,128,1024]{2,1,0:T(8,128)(2,1)S(1)} %collective-permute-done.4, bf16[16,128,1024]{2,1,0:T(8,128)(2,1)} %copy-done, s32[]{:T(128)S(6)} %select_n.135, bf16[2,128,1024]{2,1,0:T(8,128)(2,1)S(1)} %collective-permute-done.3, s32[]{:T(128)S(6)} %select_n.131), kind=kLoop, calls=%fused_computation.37 | loop fusion | flops 2097152 | bytes 3145736 | tf_op jit(solution)/shard_map/convert_element_type | solution.py:78
  91.3 2.5 %collective-permute-start.6 = (bf16[2,128,1024]{2,1,0:T(8,128)(2,1)}, bf16[2,128,1024]{2,1,0:T(8,128)(2,1)S(1)}, u32[]{:S(2)}, u32[]{:S(2)}) collective-permute-start(bf16[2,128,1024]{2,1,0:T(8,128)(2,1)} %get-tuple-element.44), channel_id=1, source_target_pairs={{0,28},{1,29},{2,30},{3,31},{4,0},{5,1},{6,2},{7,3},{8,4},{9,5},{1... | collective-permute-start | bytes 1572872 | tf_op jit(solution)/shard_map/ppermute | solution.py:30
  93.8 2.4 %collective-permute-start.11 = (f32[32,128]{1,0:T(8,128)S(1)}, f32[32,128]{1,0:T(8,128)S(1)}, u32[]{:S(2)}, u32[]{:S(2)}) collective-permute-start(f32[32,128]{1,0:T(8,128)S(1)} %slice.24), channel_id=1, source_target_pairs={{0,224},{1,225},{2,226},{3,227},{4,228},{5,229},{6,230},{7,231},{8... | collective-permute-start | bytes 49160 | tf_op jit(solution)/shard_map/ppermute | solution.py:30
  96.2 22.3 %collective-permute-done.7 = bf16[4096,256]{1,0:T(8,128)(2,1)} collective-permute-done((bf16[4096,256]{1,0:T(8,128)(2,1)}, bf16[4096,256]{1,0:T(8,128)(2,1)}, u32[]{:S(2)}, u32[]{:S(2)}) %collective-permute-start.7) | collective-permute-done | bytes 2097184 | tf_op jit(solution)/shard_map/ppermute | solution.py:30
  119.3 1.9 add_convert_fusion.2
  127.5 3.8 %collective-permute-start.15 = (bf16[2048,256]{1,0:T(8,128)(2,1)S(1)}, bf16[2048,256]{1,0:T(8,128)(2,1)S(1)}, u32[]{:S(2)}, u32[]{:S(2)}) collective-permute-start(bf16[2048,256]{1,0:T(8,128)(2,1)S(1)} %get-tuple-element.31), channel_id=1, source_target_pairs={{0,224},{1,225},{2,226},{3,227},{4,228},{5,229},{6,230},{7,231},{8... | collective-permute-start | bytes 3145736 | tf_op jit(solution)/shard_map/ppermute | solution.py:30
  132.8 5.0 %collective-permute-done.9 = bf16[2,128,1024]{2,1,0:T(8,128)(2,1)S(1)} collective-permute-done((bf16[2,128,1024]{2,1,0:T(8,128)(2,1)S(1)}, bf16[2,128,1024]{2,1,0:T(8,128)(2,1)S(1)}, u32[]{:S(2)}, u32[]{:S(2)}) %collective-permute-start.9) | collective-permute-done | bytes 524320 | tf_op jit(solution)/shard_map/ppermute | solution.py:30
  137.7 2.2 %collective-permute-done.8 = bf16[2,128,1024]{2,1,0:T(8,128)(2,1)S(1)} collective-permute-done((bf16[2,128,1024]{2,1,0:T(8,128)(2,1)S(1)}, bf16[2,128,1024]{2,1,0:T(8,128)(2,1)S(1)}, u32[]{:S(2)}, u32[]{:S(2)}) %collective-permute-start.8) | collective-permute-done | bytes 524320 | tf_op jit(solution)/shard_map/ppermute | solution.py:30
  139.9 2.6 %add_convert_fusion = (bf16[2,128,1024]{2,1,0:T(8,128)(2,1)}, bf16[2,128,1024]{2,1,0:T(8,128)(2,1)}) fusion(bf16[2,128,1024]{2,1,0:T(8,128)(2,1)S(1)} %collective-permute-done.9, bf16[16,128,1024]{2,1,0:T(8,128)(2,1)} %copy-done, s32[]{:T(128)S(6)} %select_n.144, bf16[2,128,1024]{2,1,0:T(8,128)(2,1)S(1)} %collective-permute-done.8, s32[]{:T(128)S(6)} %select_n.127), kind=kLoop, calls=%fused_computation.33 | loop fusion | flops 2097152 | bytes 3145736 | tf_op jit(solution)/shard_map/convert_element_type | solution.py:78
  144.1 9.1 %collective-permute-done.15 = bf16[2048,256]{1,0:T(8,128)(2,1)S(1)} collective-permute-done((bf16[2048,256]{1,0:T(8,128)(2,1)S(1)}, bf16[2048,256]{1,0:T(8,128)(2,1)S(1)}, u32[]{:S(2)}, u32[]{:S(2)}) %collective-permute-start.15) | collective-permute-done | bytes 1048608 | tf_op jit(solution)/shard_map/ppermute | solution.py:30
  153.2 5.5 %fusion.10 = (f32[256]{0:T(256)S(1)}, bf16[2048]{0:T(1024)(128)(2,1)S(1)}, f32[2048,256]{1,0:T(8,128)S(1)}, f32[2048,256]{1,0:T(8,128)}, bf16[2048]{0:T(1024)(128)(2,1)S(1)}, /*index=5*/f32[256]{0:T(256)S(1)}) fusion(bf16[16,1,128,256]{3,2,1,0:T(8,128)(2,1)S(1)} %get-tuple-element.50, f32[256]{0:T(256)S(1)} %bitcast.95, f32[2048,256]{1,0:T(8,128)S(1)} %fusion.25, ...), kind=kOutput, calls=%fused_computation.18 | convolution fusion | flops 1084222976 | bytes 13134848 | tf_op jit(solution)/shard_map/dot_general | solution.py:235
  159.5 8.8 %all-to-all-start.1 = ((bf16[32,32,128]{2,1,0:T(8,128)(2,1)}), bf16[32,32,128]{2,1,0:T(8,128)(2,1)S(1)}, u32[]{:S(2)}, u32[]{:S(2)}) async-start(bf16[32,32,128]{2,1,0:T(8,128)(2,1)} %broadcast_in_dim.108), calls=%async_computation.1 | async-start | bytes 524288 | tf_op jit(solution)/shard_map/all_to_all | solution.py:262
  168.4 4.0 %fusion.13 = f32[256,1024]{1,0:T(8,128)S(1)} fusion(bf16[2048,1024]{1,0:T(8,128)(2,1)} %collective-permute-done.14, bf16[2048,256]{1,0:T(8,128)(2,1)} %bitcast.102, f32[2048]{0:T(1024)S(1)} %bitcast.114, f32[256]{0:T(256)S(1)} %bitcast.96), kind=kOutput, calls=%fused_computation.24 | convolution fusion | flops 1075838976 | bytes 6300672 | tf_op jit(solution)/shard_map/dot_general | solution.py:251
  173.0 2.4 %fusion.11 = f32[1,256,1024]{2,1,0:T(8,128)} fusion(f32[256,1024]{1,0:T(8,128)S(1)} %fusion.13, bf16[2048,1024]{1,0:T(8,128)(2,1)S(1)} %bitcast.120, bf16[2048,256]{1,0:T(8,128)(2,1)S(1)} %bitcast.101, f32[256]{0:T(256)S(1)} %bitcast.97, f32[2048]{0:T(1024)S(1)} %bitcast.112), kind=kOutput, calls=%fused_computation.23 | convolution fusion | flops 1076101120 | bytes 7349248 | tf_op jit(solution)/shard_map/dot_general | solution.py:251
  175.3 2.6 %collective-permute-done.16 = bf16[2048,256]{1,0:T(8,128)(2,1)} collective-permute-done((bf16[2048,256]{1,0:T(8,128)(2,1)}, bf16[2048,256]{1,0:T(8,128)(2,1)}, u32[]{:S(2)}, u32[]{:S(2)}) %collective-permute-start.16) | collective-permute-done | bytes 1048608 | tf_op jit(solution)/shard_map/ppermute | solution.py:30
  178.0 5.8 %all-to-all-done.1 = bf16[32,32,128]{2,1,0:T(8,128)(2,1)S(1)} async-done(((bf16[32,32,128]{2,1,0:T(8,128)(2,1)}), bf16[32,32,128]{2,1,0:T(8,128)(2,1)S(1)}, u32[]{:S(2)}, u32[]{:S(2)}) %all-to-all-start.1) | async-done | bytes 262176 | tf_op jit(solution)/shard_map/all_to_all | solution.py:262
  185.9 5.2 %fusion.2 = bf16[4096,256]{1,0:T(8,128)(2,1)} fusion(bf16[4096,256]{1,0:T(8,128)(2,1)} %collective-permute-done.7, bf16[2048,256]{1,0:T(8,128)(2,1)} %collective-permute-done.16, bf16[2048,256]{1,0:T(8,128)(2,1)S(1)} %collective-permute-done.15, f32[4096]{0:T(1024)S(1)} %multiply_bitcast_fusion, f32[16,128,256]{2,1,0:T(8,128)S(1)} %bitcast.98, ...), kind=kLoop, calls=%fused_computation.3 | loop fusion | flops 10485760 | bytes 10506240 | tf_op jit(solution)/shard_map/convert_element_type | solution.py:280
  191.1 8.8 %collective-permute-done.17 = bf16[128,1024]{1,0:T(8,128)(2,1)S(1)} collective-permute-done((bf16[128,1024]{1,0:T(8,128)(2,1)S(1)}, bf16[128,1024]{1,0:T(8,128)(2,1)S(1)}, u32[]{:S(2)}, u32[]{:S(2)}) %collective-permute-start.17) | collective-permute-done | bytes 262176 | tf_op jit(solution)/shard_map/ppermute | solution.py:30
  (84 shorter events, 19.8 us)
Async XLA Ops:
  7.2 10.9 %copy-start.1 = (bf16[1,4096,256]{2,1,0:T(8,128)(2,1)S(1)}, bf16[1,4096,256]{2,1,0:T(8,128)(2,1)}, u32[]{:S(2)}) copy-start(bf16[1,4096,256]{2,1,0:T(8,128)(2,1)} %param.7) | copy-start | bytes 6291460
  7.2 114.1 %all-gather.2.cloned.1.call-start = ((), (), s32[]{:S(2)}) async-start(), calls=%async_computation.2 | async-start | bytes 4718592 | tf_op jit(solution)/shard_map/all_gather | solution.py:203
  7.2 8.9 %collective-permute-start.10 = (bf16[128,1024]{1,0:T(8,128)(2,1)}, bf16[128,1024]{1,0:T(8,128)(2,1)S(1)}, u32[]{:S(2)}, u32[]{:S(2)}) collective-permute-start(bf16[128,1024]{1,0:T(8,128)(2,1)} %bitcast.103), channel_id=1, source_target_pairs={{0,2},{1,3},{2,0},{3,1},{4,6},{5,7},{6,4},{7,5},{8,10},{9,11},{10,... | collective-permute-start | bytes 786440 | tf_op jit(solution)/shard_map/ppermute | solution.py:30
  18.7 16.8 %copy-start.2 = (bf16[1,256,1024]{2,1,0:T(8,128)(2,1)S(1)}, bf16[1,256,1024]{2,1,0:T(8,128)(2,1)}, u32[]{:S(2)}) copy-start(bf16[1,256,1024]{2,1,0:T(8,128)(2,1)} %param.11) | copy-start | bytes 1572868
  18.7 16.8 %copy-start.4 = (f32[1,256]{1,0:T(1,128)S(1)}, f32[1,256]{1,0:T(1,128)}, u32[]{:S(2)}) copy-start(f32[1,256]{1,0:T(1,128)} %gain.1) | copy-start | bytes 3076
  22.0 30.2 %all-to-all-start = ((bf16[32,34,128]{2,1,0:T(8,128)(2,1)}), bf16[32,34,128]{2,1,0:T(8,128)(2,1)S(1)}, u32[]{:S(2)}, u32[]{:S(2)}) async-start(bf16[32,34,128]{2,1,0:T(8,128)(2,1)} %pad_maximum_fusion.1), calls=%async_computation | async-start | bytes 655360 | tf_op jit(solution)/shard_map/all_to_all | solution.py:190
  52.2 13.2 %collective-permute-start.1 = (bf16[272,1024]{1,0:T(8,128)(2,1)}, bf16[272,1024]{1,0:T(8,128)(2,1)}, u32[]{:S(2)}, u32[]{:S(2)}) collective-permute-start(bf16[272,1024]{1,0:T(8,128)(2,1)} %shard_map.102), channel_id=1, source_target_pairs={{0,224},{1,225},{2,226},{3,227},{4,228},{5,229},{6,230},{7,231},{8... | collective-permute-start | bytes 1671176 | tf_op jit(solution)/shard_map/ppermute | solution.py:30
  55.6 16.6 %collective-permute-start = (bf16[16,128,256]{2,1,0:T(8,128)(2,1)}, bf16[16,128,256]{2,1,0:T(8,128)(2,1)S(1)}, u32[]{:S(2)}, u32[]{:S(2)}) collective-permute-start(bf16[16,128,256]{2,1,0:T(8,128)(2,1)} %dynamic-slice_bitcast_fusion), channel_id=1, source_target_pairs={{0,1},{1,0},{2,3},{3,2},{4,5},{5,4},{6,7},{7,6},{8,9},{9,8},{10,11... | collective-permute-start | bytes 3145736 | tf_op jit(solution)/shard_map/ppermute | solution.py:30
  65.5 6.7 %collective-permute-start.2 = (bf16[272,1024]{1,0:T(8,128)(2,1)}, bf16[272,1024]{1,0:T(8,128)(2,1)}, u32[]{:S(2)}, u32[]{:S(2)}) collective-permute-start(bf16[272,1024]{1,0:T(8,128)(2,1)} %collective-permute-done.1.packed_mine), channel_id=1, source_target_pairs={{0,1},{1,0},{2,3},{3,2},{4,5},{5,4},{6,7},{7,6},{8,9},{9,8},{10,11... | collective-permute-start | bytes 1671176 | tf_op jit(solution)/shard_map/ppermute | solution.py:30
  67.8 50.7 %collective-permute-start.7 = (bf16[4096,256]{1,0:T(8,128)(2,1)}, bf16[4096,256]{1,0:T(8,128)(2,1)}, u32[]{:S(2)}, u32[]{:S(2)}) collective-permute-start(bf16[4096,256]{1,0:T(8,128)(2,1)} %bitcast.7), channel_id=1, source_target_pairs={{0,224},{1,225},{2,226},{3,227},{4,228},{5,229},{6,230},{7,231},{8... | collective-permute-start | bytes 6291464 | tf_op jit(solution)/shard_map/ppermute | solution.py:30
  78.5 10.3 %collective-permute-start.4 = (bf16[2,128,1024]{2,1,0:T(8,128)(2,1)S(1)}, bf16[2,128,1024]{2,1,0:T(8,128)(2,1)S(1)}, u32[]{:S(2)}, u32[]{:S(2)}) collective-permute-start(bf16[2,128,1024]{2,1,0:T(8,128)(2,1)S(1)} %constant_dynamic-slice_fusion.4), channel_id=1, source_target_pairs={{1,29},{3,31},{5,1},{7,3},{9,5},{11,7},{13,9},{15,11},{17,13},{19,... | collective-permute-start | bytes 1572872 | tf_op jit(solution)/shard_map/ppermute | solution.py:30
  81.8 7.1 %collective-permute-start.3 = (bf16[2,128,1024]{2,1,0:T(8,128)(2,1)S(1)}, bf16[2,128,1024]{2,1,0:T(8,128)(2,1)S(1)}, u32[]{:S(2)}, u32[]{:S(2)}) collective-permute-start(bf16[2,128,1024]{2,1,0:T(8,128)(2,1)S(1)} %constant_dynamic-slice_fusion.4), channel_id=1, source_target_pairs={{0,4},{2,6},{4,8},{6,10},{8,12},{10,14},{12,16},{14,18},{16,20},{1... | collective-permute-start | bytes 1572872 | tf_op jit(solution)/shard_map/ppermute | solution.py:30
  91.3 31.7 %copy-start.6 = (bf16[1,4096,256]{2,1,0:T(8,128)(2,1)S(1)}, bf16[1,4096,256]{2,1,0:T(8,128)(2,1)}, u32[]{:S(2)}) copy-start(bf16[1,4096,256]{2,1,0:T(8,128)(2,1)} %param.9) | copy-start | bytes 6291460
  91.3 27.2 %collective-permute-start.6 = (bf16[2,128,1024]{2,1,0:T(8,128)(2,1)}, bf16[2,128,1024]{2,1,0:T(8,128)(2,1)S(1)}, u32[]{:S(2)}, u32[]{:S(2)}) collective-permute-start(bf16[2,128,1024]{2,1,0:T(8,128)(2,1)} %get-tuple-element.44), channel_id=1, source_target_pairs={{0,28},{1,29},{2,30},{3,31},{4,0},{5,1},{6,2},{7,3},{8,4},{9,5},{1... | collective-permute-start | bytes 1572872 | tf_op jit(solution)/shard_map/ppermute | solution.py:30
  93.8 25.5 %collective-permute-start.5 = (bf16[2,128,1024]{2,1,0:T(8,128)(2,1)S(1)}, bf16[2,128,1024]{2,1,0:T(8,128)(2,1)}, u32[]{:S(2)}, u32[]{:S(2)}) collective-permute-start(bf16[2,128,1024]{2,1,0:T(8,128)(2,1)S(1)} %get-tuple-element.45), channel_id=1, source_target_pairs={{0,4},{1,5},{2,6},{3,7},{4,8},{5,9},{6,10},{7,11},{8,12},{9,13},{1... | collective-permute-start | bytes 1572872 | tf_op jit(solution)/shard_map/ppermute | solution.py:30
  93.8 27.4 %collective-permute-start.11 = (f32[32,128]{1,0:T(8,128)S(1)}, f32[32,128]{1,0:T(8,128)S(1)}, u32[]{:S(2)}, u32[]{:S(2)}) collective-permute-start(f32[32,128]{1,0:T(8,128)S(1)} %slice.24), channel_id=1, source_target_pairs={{0,224},{1,225},{2,226},{3,227},{4,228},{5,229},{6,230},{7,231},{8... | collective-permute-start | bytes 49160 | tf_op jit(solution)/shard_map/ppermute | solution.py:30
  121.3 31.9 %collective-permute-start.14 = (bf16[2048,1024]{1,0:T(8,128)(2,1)}, bf16[2048,1024]{1,0:T(8,128)(2,1)}, u32[]{:S(2)}, u32[]{:S(2)}) collective-permute-start(bf16[2048,1024]{1,0:T(8,128)(2,1)} %bitcast.118), channel_id=1, source_target_pairs={{0,1},{1,0},{2,3},{3,2},{4,5},{5,4},{6,7},{7,6},{8,9},{9,8},{10,11... | collective-permute-start | bytes 12582920 | tf_op jit(solution)/shard_map/ppermute | solution.py:30
  123.0 8.4 %copy-start.11 = (bf16[16,128,1024]{2,1,0:T(8,128)(2,1)S(1)}, bf16[16,128,1024]{2,1,0:T(8,128)(2,1)}, u32[]{:S(2)}) copy-start(bf16[16,128,1024]{2,1,0:T(8,128)(2,1)} %all-gather.2.cloned.1.call-done) | copy-start | bytes 12582916
  124.2 13.6 %collective-permute-start.9 = (bf16[2,128,1024]{2,1,0:T(8,128)(2,1)S(1)}, bf16[2,128,1024]{2,1,0:T(8,128)(2,1)S(1)}, u32[]{:S(2)}, u32[]{:S(2)}) collective-permute-start(bf16[2,128,1024]{2,1,0:T(8,128)(2,1)S(1)} %get-tuple-element.42), channel_id=1, source_target_pairs={{0,28},{1,29},{2,30},{3,31},{4,0},{5,1},{6,2},{7,3},{8,4},{9,5},{1... | collective-permute-start | bytes 1572872 | tf_op jit(solution)/shard_map/ppermute | solution.py:30
  125.5 14.4 %collective-permute-start.8 = (bf16[2,128,1024]{2,1,0:T(8,128)(2,1)S(1)}, bf16[2,128,1024]{2,1,0:T(8,128)(2,1)S(1)}, u32[]{:S(2)}, u32[]{:S(2)}) collective-permute-start(bf16[2,128,1024]{2,1,0:T(8,128)(2,1)S(1)} %get-tuple-element.43), channel_id=1, source_target_pairs={{0,4},{1,5},{2,6},{3,7},{4,8},{5,9},{6,10},{7,11},{8,12},{9,13},{1... | collective-permute-start | bytes 1572872 | tf_op jit(solution)/shard_map/ppermute | solution.py:30
  125.7 5.7 %copy-start.3 = (bf16[1,256,1024]{2,1,0:T(8,128)(2,1)S(1)}, bf16[1,256,1024]{2,1,0:T(8,128)(2,1)}, u32[]{:S(2)}) copy-start(bf16[1,256,1024]{2,1,0:T(8,128)(2,1)} %param.11) | copy-start | bytes 1572868
  127.5 25.7 %copy-start.7 = (bf16[16,1,128,256]{3,2,1,0:T(8,128)(2,1)}, bf16[16,1,128,256]{3,2,1,0:T(8,128)(2,1)S(1)}, u32[]{:S(2)}) copy-start(bf16[16,1,128,256]{3,2,1,0:T(8,128)(2,1)S(1)} %get-tuple-element.51) | copy-start | bytes 3145732
  127.5 25.7 %copy-start.9 = (bf16[16,1,128,256]{3,2,1,0:T(8,128)(2,1)}, bf16[16,1,128,256]{3,2,1,0:T(8,128)(2,1)S(1)}, u32[]{:S(2)}) copy-start(bf16[16,1,128,256]{3,2,1,0:T(8,128)(2,1)S(1)} %get-tuple-element.50) | copy-start | bytes 3145732
  127.5 25.7 %collective-permute-start.15 = (bf16[2048,256]{1,0:T(8,128)(2,1)S(1)}, bf16[2048,256]{1,0:T(8,128)(2,1)S(1)}, u32[]{:S(2)}, u32[]{:S(2)}) collective-permute-start(bf16[2048,256]{1,0:T(8,128)(2,1)S(1)} %get-tuple-element.31), channel_id=1, source_target_pairs={{0,224},{1,225},{2,226},{3,227},{4,228},{5,229},{6,230},{7,231},{8... | collective-permute-start | bytes 3145736 | tf_op jit(solution)/shard_map/ppermute | solution.py:30
  131.3 46.7 %collective-permute-start.16 = (bf16[2048,256]{1,0:T(8,128)(2,1)}, bf16[2048,256]{1,0:T(8,128)(2,1)}, u32[]{:S(2)}, u32[]{:S(2)}) collective-permute-start(bf16[2048,256]{1,0:T(8,128)(2,1)} %get-tuple-element.33), channel_id=1, source_target_pairs={{0,224},{1,225},{2,226},{3,227},{4,228},{5,229},{6,230},{7,231},{8... | collective-permute-start | bytes 3145736 | tf_op jit(solution)/shard_map/ppermute | solution.py:30
  142.5 32.8 %collective-permute-start.13 = (bf16[2,128,1024]{2,1,0:T(8,128)(2,1)}, bf16[2,128,1024]{2,1,0:T(8,128)(2,1)}, u32[]{:S(2)}, u32[]{:S(2)}) collective-permute-start(bf16[2,128,1024]{2,1,0:T(8,128)(2,1)} %get-tuple-element.40), channel_id=1, source_target_pairs={{0,28},{1,29},{2,30},{3,31},{4,0},{5,1},{6,2},{7,3},{8,4},{9,5},{1... | collective-permute-start | bytes 1572872 | tf_op jit(solution)/shard_map/ppermute | solution.py:30
  142.9 32.5 %collective-permute-start.12 = (bf16[2,128,1024]{2,1,0:T(8,128)(2,1)}, bf16[2,128,1024]{2,1,0:T(8,128)(2,1)}, u32[]{:S(2)}, u32[]{:S(2)}) collective-permute-start(bf16[2,128,1024]{2,1,0:T(8,128)(2,1)} %get-tuple-element.41), channel_id=1, source_target_pairs={{0,4},{1,5},{2,6},{3,7},{4,8},{5,9},{6,10},{7,11},{8,12},{9,13},{1... | collective-permute-start | bytes 1572872 | tf_op jit(solution)/shard_map/ppermute | solution.py:30
  159.5 24.2 %all-to-all-start.1 = ((bf16[32,32,128]{2,1,0:T(8,128)(2,1)}), bf16[32,32,128]{2,1,0:T(8,128)(2,1)S(1)}, u32[]{:S(2)}, u32[]{:S(2)}) async-start(bf16[32,32,128]{2,1,0:T(8,128)(2,1)} %broadcast_in_dim.108), calls=%async_computation.1 | async-start | bytes 524288 | tf_op jit(solution)/shard_map/all_to_all | solution.py:262
  168.3 4.6 %copy-start.8 = (bf16[16,1,128,256]{3,2,1,0:T(8,128)(2,1)S(1)}, bf16[16,1,128,256]{3,2,1,0:T(8,128)(2,1)}, u32[]{:S(2)}) copy-start(bf16[16,1,128,256]{3,2,1,0:T(8,128)(2,1)} %copy-done.7) | copy-start | bytes 3145732
  168.4 4.6 %copy-start.12 = (bf16[16,128,1024]{2,1,0:T(8,128)(2,1)S(1)}, bf16[16,128,1024]{2,1,0:T(8,128)(2,1)}, u32[]{:S(2)}) copy-start(bf16[16,128,1024]{2,1,0:T(8,128)(2,1)} %all-gather.2.cloned.1.call-done) | copy-start | bytes 12582916
  185.6 14.3 %collective-permute-start.17 = (bf16[128,1024]{1,0:T(8,128)(2,1)S(1)}, bf16[128,1024]{1,0:T(8,128)(2,1)S(1)}, u32[]{:S(2)}, u32[]{:S(2)}) collective-permute-start(bf16[128,1024]{1,0:T(8,128)(2,1)S(1)} %get-tuple-element.52), channel_id=1, source_target_pairs={{0,32},{1,33},{2,34},{3,35},{4,36},{5,37},{6,38},{7,39},{8,40},{9,... | collective-permute-start | bytes 786440 | tf_op jit(solution)/shard_map/ppermute | solution.py:30
  185.7 14.2 %collective-permute-start.18 = (bf16[128,1024]{1,0:T(8,128)(2,1)S(1)}, bf16[128,1024]{1,0:T(8,128)(2,1)S(1)}, u32[]{:S(2)}, u32[]{:S(2)}) collective-permute-start(bf16[128,1024]{1,0:T(8,128)(2,1)S(1)} %get-tuple-element.53), channel_id=1, source_target_pairs={{0,34},{1,35},{2,32},{3,33},{4,38},{5,39},{6,36},{7,37},{8,42},{9,... | collective-permute-start | bytes 786440 | tf_op jit(solution)/shard_map/ppermute | solution.py:30
  (3 other events, 5.0 us)
Sparse Core Ops, SparseCore 0:
  18.2 66.5 all-gather.1

commit v3 on v2

--- a/solution.py
+++ b/solution.py
@@ -17,7 +17,7 @@
 LANE = WIDTH // N_T
 KEYS = 1024
 PACK = LANE + 16
-SPLIT = TOK // 2
+SPLIT = (TOK // 4, 5 * TOK // 8)
 AXES = ("section", "ts")
 
 
@@ -175,60 +175,76 @@
             for index in (core, 1 - core)
         ]
 
+    packed = pack(place, weights, norm_gain)
+    packed, fresh_rows = lax.optimization_barrier((packed, fresh))
+    packed = move(packed, to_previous)
+
+    cot_own = key_cotangent[0]
+    cot_half = move(cot_own, to_other_half)
+    cot_pair = jnp.stack(
+        [jnp.where(half == 0, cot_own, cot_half), jnp.where(half == 0, cot_half, cot_own)]
+    )
+    lanes = [[q * 4 + j for q in range(N_Z)] for j in range(4)]
+    cot_mine = lax.all_gather(cot_pair, "ts", axis=0, axis_index_groups=lanes, tiled=True)
+    cot_mine = cot_mine.reshape(TOK // 2, KEYS)
+
+    older_first = move(after(saved[: TOK // 2], cot_half), to_mirror)
+
+    rows = fresh.reshape(N_T // 2, 2, OWN, LANE)
+    rows_other = fresh_rows.reshape(N_T // 2, 2, OWN, LANE)
+    rows_other = move(
+        lax.dynamic_index_in_dim(rows_other, 1 - core, 1, keepdims=False), to_other_core
+    )
+
     fresh_wide = fresh.astype(F32)
     saved_wide = saved.astype(F32)
     fresh_part = jnp.sum(fresh_wide * fresh_wide, axis=1).reshape(N_Z, 2, 2, OWN)
     saved_part = jnp.sum(saved_wide * saved_wide, axis=1).reshape(1, N_T, OWN)
     squares = jnp.concatenate(
         [
-            fresh_part.reshape(N_T, 1, OWN).astype(BF),
-            fresh_part[:, ::-1].reshape(N_T, 1, OWN).astype(BF),
-            jnp.broadcast_to(saved_part.astype(BF), (N_T, N_T, OWN)),
+            fresh_part.transpose(0, 2, 1, 3).reshape(N_T // 2, 2, OWN).astype(BF),
+            jnp.broadcast_to(saved_part.astype(BF), (N_T // 2, N_T, OWN)),
         ],
         axis=1,
     )
-    squares = lax.all_to_all(squares, "ts", 0, 0, tiled=True)
-
-    packed = move(after(pack(place, weights, norm_gain), squares), to_previous)
+    halves = [[q * 4 + h * 2 + c for q in range(N_Z) for c in range(2)] for h in range(2)]
+    squares = lax.all_to_all(
+        after(squares, rows_other), "ts", 0, 0, axis_index_groups=halves, tiled=True
+    )
+    squares_raw = squares
     squares = jnp.sum(squares.astype(F32), axis=0)
-    fresh_rate = lax.rsqrt(squares[:2] / WIDTH + eps)
-    older_sq = move(squares[2:], to_mirror)
-
-    cot_own = key_cotangent[0]
-    cot_half = move(cot_own, to_other_half)
-    cot_pair = jnp.stack(
-        [jnp.where(half == 0, cot_own, cot_half), jnp.where(half == 0, cot_half, cot_own)]
-    )
-    lanes = [[q * 4 + j for q in range(N_Z)] for j in range(4)]
-    cot_mine = lax.all_gather(cot_pair, "ts", axis=0, axis_index_groups=lanes, tiled=True)
-    cot_mine = cot_mine.reshape(TOK // 2, KEYS)
-
-    older = move(after(saved, squares), to_mirror)
-
-    rows = fresh.reshape(N_T // 2, 2, OWN, LANE)
-    rows_other = move(lax.dynamic_index_in_dim(rows, 1 - core, 1, keepdims=False), to_other_core)
+    older_sq = [move(squares[2:], to_mirror), move(squares[2:], to_mirror_other_half)]
+    fresh_other = move(after(squares[:2], *older_sq), to_other_half)
+
+    older_second = move(after(saved[TOK // 2 :], *older_sq), to_mirror)
+
+    parts = [
+        move(after(returning[0, begin:end], *older_sq), to_previous)
+        for begin, end in zip((0,) + SPLIT, SPLIT + (TOK,))
+    ]
+
     packed_other = move(packed, to_other_core)
     partial = forward(place, rows, rows_other, packed, packed_other)
 
     def block(distance):
         return lax.dynamic_slice_in_dim(partial, ((z + distance) % N_Z) * 2, 2, 0)
 
-    up = move(block(4), z_up, (0,))
-    down = move(block(4), z_down, (1,))
-    up, down = lax.optimization_barrier((up, down))
+    far = after(block(4), squares_raw)
+    up = move(far, z_up, (0,))
+    down = move(far, z_down, (1,))
+    up, down = lax.optimization_barrier((up, down, older_first))[:2]
     up = move(add(block(3), up), z_up)
     down = move(add(block(-3), down), z_down)
-    up, down = lax.optimization_barrier((up, down, older))[:2]
+    up, down = lax.optimization_barrier((up, down, older_second, parts[0]))[:2]
     up = add(block(2), up)
     down = add(block(-2), down)
 
-    cot_mine, older_sq = lax.optimization_barrier((cot_mine, older_sq, up, down, older))[:2]
-    early = move(after(returning[0, :SPLIT], older, older_sq), to_previous)
-    late = move(after(returning[0, SPLIT:], older, older_sq), to_previous)
+    older = jnp.concatenate([older_first, older_second], axis=0)
+    cot_mine, *older_sq = lax.optimization_barrier((cot_mine, *older_sq, up, down))[:3]
     up = move(up, z_up)
     down = move(down, z_down)
-    cots = [cot_mine, after(move(cot_mine, to_other_core), early)]
-    older_rate = lax.rsqrt(older_sq / WIDTH + eps).reshape(TOK)
+    cots = [cot_mine, move(cot_mine, to_other_core)]
+    older_rate = lax.rsqrt((older_sq[0] + older_sq[1]) / WIDTH + eps).reshape(TOK)
     live = (jnp.arange(TOK, dtype=jnp.int32) < lengths[0]).astype(F32)
     scales = by_core(live * older_rate)
     raw = [
@@ -236,6 +252,7 @@
         for cot in cots
     ]
     up, down, raw[0] = lax.optimization_barrier((up, down, raw[0]))
+    up, down = lax.optimization_barrier((up, down, parts[1]))[:2]
     up = move(add(block(1), up), z_up)
     down = move(add(block(-1), down), z_down)
     grads = []
@@ -260,20 +277,25 @@
     curve = jnp.where(mine, curve[0], curve[1])
     curve = jnp.broadcast_to(curve.reshape(1, N_T, OWN).astype(BF), (N_T, N_T, OWN))
     curve = lax.all_to_all(curve, "ts", 0, 0, tiled=True)
-    up, down = lax.optimization_barrier((up, down, curve, late))[:2]
+    up, down, fresh_other = lax.optimization_barrier((up, down, fresh_other, curve, parts[2]))[:3]
+    fresh_rate = lax.rsqrt((squares[:2] + fresh_other) / WIDTH + eps)
     curve = jnp.sum(curve.astype(F32), axis=0).reshape(TOK)
     pull = older_rate * older_rate / WIDTH * curve
 
     summed = block(0).astype(F32) + up.astype(F32) + down.astype(F32)
-    straight = move((pick(summed, half) * fresh_rate[0][:, None]).astype(BF), to_next)
+    straight = move((pick(summed, half) * pick(fresh_rate, half)[:, None]).astype(BF), to_next)
     crossed = move(
-        (pick(summed, 1 - half) * fresh_rate[1][:, None]).astype(BF), to_next_other_half
+        (pick(summed, 1 - half) * pick(fresh_rate, 1 - half)[:, None]).astype(BF), to_next_other_half
     )
     new_keys = (straight.astype(F32) + crossed.astype(F32)).astype(BF)
 
-    base = [(gain * grad).reshape(N_T // 2, 1, OWN, LANE) for grad in grads]
-    base = jnp.where(mine[..., None], base[0], base[1]).reshape(TOK, LANE)
-    downstream = jnp.concatenate([early, late], axis=0)
+    base = jnp.zeros((N_T // 2, 2, OWN, LANE), F32)
+    for index, grad in zip((core, 1 - core), grads):
+        base = lax.dynamic_update_index_in_dim(
+            base, (gain * grad).reshape(N_T // 2, OWN, LANE), index, 1
+        )
+    base = base.reshape(TOK, LANE)
+    downstream = jnp.concatenate(parts, axis=0)
     total = downstream.astype(F32) + base - pull[:, None] * older.astype(F32)
     return (
         new_keys[None],

time: 208 us -> 195 us (0.938)
  waiting for transfers between devices: 91.1 us -> 58.1 us
  starting transfers between devices: 53.8 us -> 62.8 us
  local copies, waits for them, and re-layouts: 7.83 us -> 15.3 us
  other arithmetic: 21.2 us -> 24.2 us
    ppermute x19 -> x23, waiting for transfers between devices: 69.5 us -> 52.5 us  [move(): return lax.ppermute(value, AXES, pairs)]
    ppermute x19 -> x23, starting transfers between devices: 31.5 us -> 46.2 us  [move(): return lax.ppermute(value, AXES, pairs)]
    all_to_all x1, waiting for transfers between devices: 15.8 us -> 5.23 us  [shards(): lax.all_to_all(after(squares, rows_other), 'ts', 0, 0, axis_index_groups=...]
    all_to_all x1, waiting for transfers between devices: 5.75 us -> 0.35 us  [shards(): curve = lax.all_to_all(curve, 'ts', 0, 0, tiled=True)]
    all_to_all x1, starting transfers between devices: 13.5 us -> 8.76 us  [shards(): lax.all_to_all(after(squares, rows_other), 'ts', 0, 0, axis_index_groups=...]
    dynamic_update_slice x0 -> x2, local copies, waits for them, and re-layouts: none -> 3.1 us  [shards(): lax.dynamic_update_index_in_dim(base, (gain * grad).reshape(N_T // 2, OWN...]
    broadcast_in_dim x3 -> x2, local copies, waits for them, and re-layouts: 0.14 us -> 2.47 us  [the longest x1 2.45 us: shards(): base = jnp.zeros((N_T // 2, 2, OWN, LANE), F32)]
    convert_element_type x1, other arithmetic: 5.2 us -> 7.29 us  [shards(): total.astype(BF)[None]]
  transfers between devices with their start and end apart: 22 -> 26, of which waited for: 11 -> 12; matrix products, arithmetic and copies ran while one was open for 17% -> 23% of each run, Pallas kernels for 2% -> 3%
where the time goes in v3:
time: 195 us; the launch traced here: 194 us
  starting transfers between devices  62.8 us (32%)
  waiting for transfers between devices  58.1 us (30%)
  other arithmetic  24.2 us (12%)
  local copies, waits for them, and re-layouts  15.3 us (8%)
  between operations  15.2 us (8%)
  matrix products  13.2 us (7%)
  Pallas kernels  5.19 us (3%)
    ppermute x23, waiting for transfers between devices, move(): return lax.ppermute(value, AXES, pairs)  52.5 us
    ppermute x23, starting transfers between devices, move(): return lax.ppermute(value, AXES, pairs)  46.2 us
    all_to_all x1, starting transfers between devices, shards(): lax.all_to_all(after(squares, rows_other), 'ts', 0, 0, axis_index_groups=...  8.76 us
    convert_element_type x3, other arithmetic, add(): return (a.astype(F32) + b.astype(F32)).astype(BF)  8.26 us
    all_to_all x1, starting transfers between devices, shards(): curve = lax.all_to_all(curve, 'ts', 0, 0, tiled=True)  7.84 us
    convert_element_type x1, other arithmetic, shards(): total.astype(BF)[None]  7.29 us
    dot_general x2, matrix products, shards(): lax.dot_general(cot, weights, (((1,), (1,)), ((), ())), preferred_element...  6.76 us
    dot_general x2, matrix products, shards(): lax.dot_general((wide * gain * scale[:, None]).astype(BF), cot, (((0,), (...  6.41 us
  transfers between devices with their start and end apart: 26, of which 12 were waited for; matrix products, arithmetic and copies ran while one was open for 23% of the time, Pallas kernels for 3%

profile of v3, /device:TPU:1, one launch (start us, length us, event | category | flops | bytes accessed | tf_op | source)
XLA Modules:
  0.0 194.0 jit_solution(6218968380969636631)
XLA Ops:
  7.2 3.7 %collective-permute-start.5 = (bf16[128,1024]{1,0:T(8,128)(2,1)}, bf16[128,1024]{1,0:T(8,128)(2,1)S(1)}, u32[]{:S(2)}, u32[]{:S(2)}) collective-permute-start(bf16[128,1024]{1,0:T(8,128)(2,1)} %bitcast.112), channel_id=1, source_target_pairs={{0,2},{1,3},{2,0},{3,1},{4,6},{5,7},{6,4},{7,5},{8,10},{9,11},{10,... | collective-permute-start | bytes 786440 | tf_op jit(solution)/shard_map/ppermute | solution.py:30
  10.9 5.3 %collective-permute-done.5 = bf16[128,1024]{1,0:T(8,128)(2,1)S(1)} collective-permute-done((bf16[128,1024]{1,0:T(8,128)(2,1)}, bf16[128,1024]{1,0:T(8,128)(2,1)S(1)}, u32[]{:S(2)}, u32[]{:S(2)}) %collective-permute-start.5) | collective-permute-done | bytes 262176 | tf_op jit(solution)/shard_map/ppermute | solution.py:30
  19.0 4.5 %collective-permute-start.1 = (bf16[272,1024]{1,0:T(8,128)(2,1)}, bf16[272,1024]{1,0:T(8,128)(2,1)}, u32[]{:S(2)}, u32[]{:S(2)}) collective-permute-start(bf16[272,1024]{1,0:T(8,128)(2,1)} %shard_map.102), channel_id=1, source_target_pairs={{0,224},{1,225},{2,226},{3,227},{4,228},{5,229},{6,230},{7,231},{8... | collective-permute-start | bytes 1671176 | tf_op jit(solution)/shard_map/ppermute | solution.py:30
  24.5 1.8 collective-permute-start
  27.9 6.3 %collective-permute-done.1.packed_mine = bf16[272,1024]{1,0:T(8,128)(2,1)} collective-permute-done((bf16[272,1024]{1,0:T(8,128)(2,1)}, bf16[272,1024]{1,0:T(8,128)(2,1)}, u32[]{:S(2)}, u32[]{:S(2)}) %collective-permute-start.1) | collective-permute-done | bytes 557088 | tf_op jit(solution)/shard_map/ppermute | solution.py:30
  34.2 2.5 %collective-permute-start.2 = (bf16[272,1024]{1,0:T(8,128)(2,1)}, bf16[272,1024]{1,0:T(8,128)(2,1)}, u32[]{:S(2)}, u32[]{:S(2)}) collective-permute-start(bf16[272,1024]{1,0:T(8,128)(2,1)} %collective-permute-done.1.packed_mine), channel_id=1, source_target_pairs={{0,1},{1,0},{2,3},{3,2},{4,5},{5,4},{6,7},{7,6},{8,9},{9,8},{10,11... | collective-permute-start | bytes 1671176 | tf_op jit(solution)/shard_map/ppermute | solution.py:30
  37.3 4.4 %collective-permute-start.6 = (bf16[2048,256]{1,0:T(8,128)(2,1)}, bf16[2048,256]{1,0:T(8,128)(2,1)}, u32[]{:S(2)}, u32[]{:S(2)}) collective-permute-start(bf16[2048,256]{1,0:T(8,128)(2,1)} %get-tuple-element.33), channel_id=1, source_target_pairs={{0,224},{1,225},{2,226},{3,227},{4,228},{5,229},{6,230},{7,231},{8... | collective-permute-start | bytes 3145736 | tf_op jit(solution)/shard_map/ppermute | solution.py:30
  43.1 8.8 %all-to-all-start = ((bf16[16,34,128]{2,1,0:T(8,128)(2,1)}), bf16[16,34,128]{2,1,0:T(8,128)(2,1)S(1)}, u32[]{:S(2)}, u32[]{:S(2)}) async-start(bf16[16,34,128]{2,1,0:T(8,128)(2,1)} %pad_maximum_fusion.2), calls=%async_computation | async-start | bytes 327680 | tf_op jit(solution)/shard_map/all_to_all | solution.py:211
  51.9 4.3 %shard_map.103 = bf16[16,128,1024]{2,1,0:T(8,128)(2,1)S(1)} custom-call(s32[1]{0:T(128)} %bitcast.place, bf16[16,2,128,256]{3,2,1,0:T(8,128)(2,1)S(1)} %bitcast.100, bf16[16,128,256]{2,1,0:T(8,128)(2,1)S(1)} %collective-permute-done.rows_other, bf16[272,1024]{1,0:T(8,128)(2,1)} %collective-permute-done.1.packed_mine, ...), custom_call_target="tpu_custom_call" | custom-call | flops 2147483648 | bytes 7340032 | tf_op jit(solution)/shard_map/pallas_call | solution.py:141
  56.2 2.0 %copy-done = bf16[16,128,1024]{2,1,0:T(8,128)(2,1)} copy-done((bf16[16,128,1024]{2,1,0:T(8,128)(2,1)}, bf16[16,128,1024]{2,1,0:T(8,128)(2,1)S(1)}, u32[]{:S(2)}) %copy-start) | copy-done | bytes 4194328
  58.2 5.2 %all-to-all-done = bf16[16,34,128]{2,1,0:T(8,128)(2,1)S(1)} async-done(((bf16[16,34,128]{2,1,0:T(8,128)(2,1)}), bf16[16,34,128]{2,1,0:T(8,128)(2,1)S(1)}, u32[]{:S(2)}, u32[]{:S(2)}) %all-to-all-start) | async-done | bytes 139296 | tf_op jit(solution)/shard_map/all_to_all | solution.py:211
  64.2 2.0 %collective-permute-start.4 = (bf16[2,128,1024]{2,1,0:T(8,128)(2,1)S(1)}, bf16[2,128,1024]{2,1,0:T(8,128)(2,1)S(1)}, u32[]{:S(2)}, u32[]{:S(2)}) collective-permute-start(bf16[2,128,1024]{2,1,0:T(8,128)(2,1)S(1)} %constant_dynamic-slice_fusion.6), channel_id=1, source_target_pairs={{1,29},{3,31},{5,1},{7,3},{9,5},{11,7},{13,9},{15,11},{17,13},{19,... | collective-permute-start | bytes 1572872 | tf_op jit(solution)/shard_map/ppermute | solution.py:30
  67.5 3.1 %collective-permute-start.9 = (f32[32,128]{1,0:T(8,128)S(1)}, f32[32,128]{1,0:T(8,128)S(1)}, u32[]{:S(2)}, u32[]{:S(2)}) collective-permute-start(f32[32,128]{1,0:T(8,128)S(1)} %slice.38), channel_id=1, source_target_pairs={{0,224},{1,225},{2,226},{3,227},{4,228},{5,229},{6,230},{7,231},{8... | collective-permute-start | bytes 49160 | tf_op jit(solution)/shard_map/ppermute | solution.py:30
  72.5 2.8 %collective-permute-start.11 = (bf16[2048,256]{1,0:T(8,128)(2,1)}, bf16[2048,256]{1,0:T(8,128)(2,1)S(1)}, u32[]{:S(2)}, u32[]{:S(2)}) collective-permute-start(bf16[2048,256]{1,0:T(8,128)(2,1)} %get-tuple-element.36), channel_id=1, source_target_pairs={{0,224},{1,225},{2,226},{3,227},{4,228},{5,229},{6,230},{7,231},{8... | collective-permute-start | bytes 3145736 | tf_op jit(solution)/shard_map/ppermute | solution.py:30
  75.3 1.9 slice_bitcast_fusion.4
  77.9 6.9 %collective-permute-done.4 = bf16[2,128,1024]{2,1,0:T(8,128)(2,1)S(1)} collective-permute-done((bf16[2,128,1024]{2,1,0:T(8,128)(2,1)S(1)}, bf16[2,128,1024]{2,1,0:T(8,128)(2,1)S(1)}, u32[]{:S(2)}, u32[]{:S(2)}) %collective-permute-start.4) | collective-permute-done | bytes 524320 | tf_op jit(solution)/shard_map/ppermute | solution.py:30
  84.9 2.6 %add_convert_fusion.4 = (bf16[2,128,1024]{2,1,0:T(8,128)(2,1)}, bf16[2,128,1024]{2,1,0:T(8,128)(2,1)}) fusion(bf16[2,128,1024]{2,1,0:T(8,128)(2,1)S(1)} %collective-permute-done.4, bf16[16,128,1024]{2,1,0:T(8,128)(2,1)} %copy-done, s32[]{:T(128)S(6)} %select_n.133, bf16[2,128,1024]{2,1,0:T(8,128)(2,1)S(1)} %collective-permute-done.3, s32[]{:T(128)S(6)} %select_n.129), kind=kLoop, calls=%fused_computation.34 | loop fusion | flops 2097152 | bytes 3145736 | tf_op jit(solution)/shard_map/convert_element_type | solution.py:78
  87.6 2.5 %collective-permute-start.8 = (bf16[2,128,1024]{2,1,0:T(8,128)(2,1)}, bf16[2,128,1024]{2,1,0:T(8,128)(2,1)}, u32[]{:S(2)}, u32[]{:S(2)}) collective-permute-start(bf16[2,128,1024]{2,1,0:T(8,128)(2,1)} %get-tuple-element.62), channel_id=1, source_target_pairs={{0,28},{1,29},{2,30},{3,31},{4,0},{5,1},{6,2},{7,3},{8,4},{9,5},{1... | collective-permute-start | bytes 1572872 | tf_op jit(solution)/shard_map/ppermute | solution.py:30
  90.1 18.0 %collective-permute-done.12 = bf16[1024,256]{1,0:T(8,128)(2,1)} collective-permute-done((bf16[1024,256]{1,0:T(8,128)(2,1)}, bf16[1024,256]{1,0:T(8,128)(2,1)}, u32[]{:S(2)}, u32[]{:S(2)}) %collective-permute-start.12) | collective-permute-done | bytes 524320 | tf_op jit(solution)/shard_map/ppermute | solution.py:30
  108.1 2.9 %add_convert_fusion.2 = (bf16[2,128,1024]{2,1,0:T(8,128)(2,1)}, bf16[2,128,1024]{2,1,0:T(8,128)(2,1)}) fusion(bf16[2,128,1024]{2,1,0:T(8,128)(2,1)} %collective-permute-done.8, bf16[16,128,1024]{2,1,0:T(8,128)(2,1)} %copy-done, s32[]{:T(128)S(6)} %select_n.135, bf16[2,128,1024]{2,1,0:T(8,128)(2,1)} %collective-permute-done.7, s32[]{:T(128)S(6)} %select_n.127), kind=kLoop, calls=%fused_computation.31 | loop fusion | flops 2097152 | bytes 3145736 | tf_op jit(solution)/shard_map/convert_element_type | solution.py:78
  111.0 2.1 %collective-permute-start.19 = (bf16[2048,1024]{1,0:T(8,128)(2,1)}, bf16[2048,1024]{1,0:T(8,128)(2,1)}, u32[]{:S(2)}, u32[]{:S(2)}) collective-permute-start(bf16[2048,1024]{1,0:T(8,128)(2,1)} %bitcast.126), channel_id=1, source_target_pairs={{0,1},{1,0},{2,3},{3,2},{4,5},{5,4},{6,7},{7,6},{8,9},{9,8},{10,11... | collective-permute-start | bytes 12582920 | tf_op jit(solution)/shard_map/ppermute | solution.py:30
  115.0 4.3 %collective-permute-start.15 = (bf16[1536,256]{1,0:T(8,128)(2,1)S(1)}, bf16[1536,256]{1,0:T(8,128)(2,1)S(1)}, u32[]{:S(2)}, u32[]{:S(2)}) collective-permute-start(bf16[1536,256]{1,0:T(8,128)(2,1)S(1)} %get-tuple-element.43), channel_id=1, source_target_pairs={{0,224},{1,225},{2,226},{3,227},{4,228},{5,229},{6,230},{7,231},{8... | collective-permute-start | bytes 2359304 | tf_op jit(solution)/shard_map/ppermute | solution.py:30
  126.2 7.6 %collective-permute-done.13 = bf16[2,128,1024]{2,1,0:T(8,128)(2,1)S(1)} collective-permute-done((bf16[2,128,1024]{2,1,0:T(8,128)(2,1)S(1)}, bf16[2,128,1024]{2,1,0:T(8,128)(2,1)S(1)}, u32[]{:S(2)}, u32[]{:S(2)}) %collective-permute-start.13) | collective-permute-done | bytes 524320 | tf_op jit(solution)/shard_map/ppermute | solution.py:30
  136.3 2.8 %add_convert_fusion = (bf16[2,128,1024]{2,1,0:T(8,128)(2,1)}, bf16[2,128,1024]{2,1,0:T(8,128)(2,1)}) fusion(bf16[2,128,1024]{2,1,0:T(8,128)(2,1)S(1)} %collective-permute-done.14, bf16[16,128,1024]{2,1,0:T(8,128)(2,1)} %copy-done, s32[]{:T(128)S(6)} %select_n.142, bf16[2,128,1024]{2,1,0:T(8,128)(2,1)S(1)} %collective-permute-done.13, s32[]{:T(128)S(6)} %select_n.125), kind=kLoop, calls=%fused_computation.29 | loop fusion | flops 2097152 | bytes 3145736 | tf_op jit(solution)/shard_map/convert_element_type | solution.py:78
  141.8 5.5 %fusion.7 = (f32[256]{0:T(256)S(1)}, bf16[2048]{0:T(1024)(128)(2,1)S(1)}, f32[2048,256]{1,0:T(8,128)S(1)}, f32[2048,256]{1,0:T(8,128)}, bf16[2048]{0:T(1024)(128)(2,1)S(1)}, /*index=5*/f32[256]{0:T(256)S(1)}) fusion(bf16[16,1,128,256]{3,2,1,0:T(8,128)(2,1)S(1)} %get-tuple-element.68, f32[256]{0:T(256)S(1)} %bitcast.102, f32[2048,256]{1,0:T(8,128)S(1)} %fusion.22, ...), kind=kOutput, calls=%fused_computation.15 | convolution fusion | flops 1084222976 | bytes 13134848 | tf_op jit(solution)/shard_map/dot_general | solution.py:251
  148.1 7.8 %all-to-all-start.1 = ((bf16[32,32,128]{2,1,0:T(8,128)(2,1)}), bf16[32,32,128]{2,1,0:T(8,128)(2,1)S(1)}, u32[]{:S(2)}, u32[]{:S(2)}) async-start(bf16[32,32,128]{2,1,0:T(8,128)(2,1)} %broadcast_in_dim.82), calls=%async_computation.1 | async-start | bytes 524288 | tf_op jit(solution)/shard_map/all_to_all | solution.py:279
  156.0 4.0 %fusion.10 = f32[256,1024]{1,0:T(8,128)S(1)} fusion(bf16[2048,1024]{1,0:T(8,128)(2,1)} %collective-permute-done.19, bf16[2048,256]{1,0:T(8,128)(2,1)} %bitcast.110, f32[2048]{0:T(1024)S(1)} %bitcast.122, f32[256]{0:T(256)S(1)} %bitcast.103), kind=kOutput, calls=%fused_computation.22 | convolution fusion | flops 1075838976 | bytes 6300672 | tf_op jit(solution)/shard_map/dot_general | solution.py:268
  160.1 2.4 %fusion.8 = f32[1,256,1024]{2,1,0:T(8,128)} fusion(f32[256,1024]{1,0:T(8,128)S(1)} %fusion.10, bf16[2048,1024]{1,0:T(8,128)(2,1)S(1)} %bitcast.128, bf16[2048,256]{1,0:T(8,128)(2,1)S(1)} %bitcast.109, f32[256]{0:T(256)S(1)} %bitcast.104, f32[2048]{0:T(1024)S(1)} %bitcast.120), kind=kOutput, calls=%fused_computation.21 | convolution fusion | flops 1076101120 | bytes 7349248 | tf_op jit(solution)/shard_map/dot_general | solution.py:268
  162.5 2.4 %broadcast_in_dim.84 = f32[16,2,128,256]{3,2,1,0:T(8,128)} broadcast(f32[]{:T(128)} %constant.136.clone.1), dimensions={} | broadcast | bytes 4194308 | tf_op jit(solution)/shard_map/broadcast_in_dim | solution.py:292
  171.4 2.1 %collective-permute-start.22 = (bf16[128,1024]{1,0:T(8,128)(2,1)S(1)}, bf16[128,1024]{1,0:T(8,128)(2,1)S(1)}, u32[]{:S(2)}, u32[]{:S(2)}) collective-permute-start(bf16[128,1024]{1,0:T(8,128)(2,1)S(1)} %get-tuple-element.73), channel_id=1, source_target_pairs={{0,34},{1,35},{2,32},{3,33},{4,38},{5,39},{6,36},{7,37},{8,42},{9,... | collective-permute-start | bytes 786440 | tf_op jit(solution)/shard_map/ppermute | solution.py:30
  173.5 7.3 %subtract_convert_fusion = bf16[1,4096,256]{2,1,0:T(8,128)(2,1)} fusion(f32[1,4096,256]{2,1,0:T(8,128)} %bitcast.43, bf16[1,1536,256]{2,1,0:T(8,128)(2,1)} %bitcast.38, bf16[1,1536,256]{2,1,0:T(8,128)(2,1)S(1)} %bitcast.111, bf16[1,1024,256]{2,1,0:T(8,128)(2,1)} %bitcast.36, bf16[1,2048,256]{2,1,0:T(8,128)(2,1)S(1)} %bitcast.106, ...), kind=kLoop, calls=%fused_computation | loop fusion | flops 14680064 | bytes 10502144 | tf_op jit(solution)/shard_map/convert_element_type | solution.py:302
  180.7 3.8 %collective-permute-done.21 = bf16[128,1024]{1,0:T(8,128)(2,1)S(1)} collective-permute-done((bf16[128,1024]{1,0:T(8,128)(2,1)S(1)}, bf16[128,1024]{1,0:T(8,128)(2,1)S(1)}, u32[]{:S(2)}, u32[]{:S(2)}) %collective-permute-start.21) | collective-permute-done | bytes 262176 | tf_op jit(solution)/shard_map/ppermute | solution.py:30
  (104 shorter events, 35.3 us)
Async XLA Ops:
  7.2 10.9 %copy-start.2 = (bf16[1,256,1024]{2,1,0:T(8,128)(2,1)S(1)}, bf16[1,256,1024]{2,1,0:T(8,128)(2,1)}, u32[]{:S(2)}) copy-start(bf16[1,256,1024]{2,1,0:T(8,128)(2,1)} %param.11) | copy-start | bytes 1572868
  7.2 10.9 %copy-start.4 = (f32[1,256]{1,0:T(1,128)S(1)}, f32[1,256]{1,0:T(1,128)}, u32[]{:S(2)}) copy-start(f32[1,256]{1,0:T(1,128)} %gain.1) | copy-start | bytes 3076
  7.2 16.3 %copy-start.1 = (bf16[1,4096,256]{2,1,0:T(8,128)(2,1)S(1)}, bf16[1,4096,256]{2,1,0:T(8,128)(2,1)}, u32[]{:S(2)}) copy-start(bf16[1,4096,256]{2,1,0:T(8,128)(2,1)} %param.7) | copy-start | bytes 6291460
  7.2 103.8 %all-gather.2.cloned.1.call-start = ((), (), s32[]{:S(2)}) async-start(), calls=%async_computation.2 | async-start | bytes 4718592 | tf_op jit(solution)/shard_map/all_gather | solution.py:188
  7.2 8.9 %collective-permute-start.5 = (bf16[128,1024]{1,0:T(8,128)(2,1)}, bf16[128,1024]{1,0:T(8,128)(2,1)S(1)}, u32[]{:S(2)}, u32[]{:S(2)}) collective-permute-start(bf16[128,1024]{1,0:T(8,128)(2,1)} %bitcast.112), channel_id=1, source_target_pairs={{0,2},{1,3},{2,0},{3,1},{4,6},{5,7},{6,4},{7,5},{8,10},{9,11},{10,... | collective-permute-start | bytes 786440 | tf_op jit(solution)/shard_map/ppermute | solution.py:30
  19.0 15.2 %collective-permute-start.1 = (bf16[272,1024]{1,0:T(8,128)(2,1)}, bf16[272,1024]{1,0:T(8,128)(2,1)}, u32[]{:S(2)}, u32[]{:S(2)}) collective-permute-start(bf16[272,1024]{1,0:T(8,128)(2,1)} %shard_map.102), channel_id=1, source_target_pairs={{0,224},{1,225},{2,226},{3,227},{4,228},{5,229},{6,230},{7,231},{8... | collective-permute-start | bytes 1671176 | tf_op jit(solution)/shard_map/ppermute | solution.py:30
  24.5 18.6 %collective-permute-start = (bf16[16,128,256]{2,1,0:T(8,128)(2,1)}, bf16[16,128,256]{2,1,0:T(8,128)(2,1)S(1)}, u32[]{:S(2)}, u32[]{:S(2)}) collective-permute-start(bf16[16,128,256]{2,1,0:T(8,128)(2,1)} %dynamic-slice_bitcast_fusion), channel_id=1, source_target_pairs={{0,1},{1,0},{2,3},{3,2},{4,5},{5,4},{6,7},{7,6},{8,9},{9,8},{10,11... | collective-permute-start | bytes 3145736 | tf_op jit(solution)/shard_map/ppermute | solution.py:30
  34.2 17.7 %collective-permute-start.2 = (bf16[272,1024]{1,0:T(8,128)(2,1)}, bf16[272,1024]{1,0:T(8,128)(2,1)}, u32[]{:S(2)}, u32[]{:S(2)}) collective-permute-start(bf16[272,1024]{1,0:T(8,128)(2,1)} %collective-permute-done.1.packed_mine), channel_id=1, source_target_pairs={{0,1},{1,0},{2,3},{3,2},{4,5},{5,4},{6,7},{7,6},{8,9},{9,8},{10,11... | collective-permute-start | bytes 1671176 | tf_op jit(solution)/shard_map/ppermute | solution.py:30
  37.3 40.7 %collective-permute-start.6 = (bf16[2048,256]{1,0:T(8,128)(2,1)}, bf16[2048,256]{1,0:T(8,128)(2,1)}, u32[]{:S(2)}, u32[]{:S(2)}) collective-permute-start(bf16[2048,256]{1,0:T(8,128)(2,1)} %get-tuple-element.33), channel_id=1, source_target_pairs={{0,224},{1,225},{2,226},{3,227},{4,228},{5,229},{6,230},{7,231},{8... | collective-permute-start | bytes 3145736 | tf_op jit(solution)/shard_map/ppermute | solution.py:30
  43.1 20.4 %all-to-all-start = ((bf16[16,34,128]{2,1,0:T(8,128)(2,1)}), bf16[16,34,128]{2,1,0:T(8,128)(2,1)S(1)}, u32[]{:S(2)}, u32[]{:S(2)}) async-start(bf16[16,34,128]{2,1,0:T(8,128)(2,1)} %pad_maximum_fusion.2), calls=%async_computation | async-start | bytes 327680 | tf_op jit(solution)/shard_map/all_to_all | solution.py:211
  63.5 14.5 %collective-permute-start.3 = (bf16[2,128,1024]{2,1,0:T(8,128)(2,1)S(1)}, bf16[2,128,1024]{2,1,0:T(8,128)(2,1)S(1)}, u32[]{:S(2)}, u32[]{:S(2)}) collective-permute-start(bf16[2,128,1024]{2,1,0:T(8,128)(2,1)S(1)} %constant_dynamic-slice_fusion.6), channel_id=1, source_target_pairs={{0,4},{2,6},{4,8},{6,10},{8,12},{10,14},{12,16},{14,18},{16,20},{1... | collective-permute-start | bytes 1572872 | tf_op jit(solution)/shard_map/ppermute | solution.py:30
  64.2 20.7 %collective-permute-start.4 = (bf16[2,128,1024]{2,1,0:T(8,128)(2,1)S(1)}, bf16[2,128,1024]{2,1,0:T(8,128)(2,1)S(1)}, u32[]{:S(2)}, u32[]{:S(2)}) collective-permute-start(bf16[2,128,1024]{2,1,0:T(8,128)(2,1)S(1)} %constant_dynamic-slice_fusion.6), channel_id=1, source_target_pairs={{1,29},{3,31},{5,1},{7,3},{9,5},{11,7},{13,9},{15,11},{17,13},{19,... | collective-permute-start | bytes 1572872 | tf_op jit(solution)/shard_map/ppermute | solution.py:30
  66.2 6.2 %collective-permute-start.10 = (f32[32,128]{1,0:T(8,128)S(1)}, f32[32,128]{1,0:T(8,128)S(1)}, u32[]{:S(2)}, u32[]{:S(2)}) collective-permute-start(f32[32,128]{1,0:T(8,128)S(1)} %slice.38), channel_id=1, source_target_pairs={{0,226},{1,227},{2,224},{3,225},{4,230},{5,231},{6,228},{7,229},{8... | collective-permute-start | bytes 49160 | tf_op jit(solution)/shard_map/ppermute | solution.py:30
  67.5 5.0 %collective-permute-start.9 = (f32[32,128]{1,0:T(8,128)S(1)}, f32[32,128]{1,0:T(8,128)S(1)}, u32[]{:S(2)}, u32[]{:S(2)}) collective-permute-start(f32[32,128]{1,0:T(8,128)S(1)} %slice.38), channel_id=1, source_target_pairs={{0,224},{1,225},{2,226},{3,227},{4,228},{5,229},{6,230},{7,231},{8... | collective-permute-start | bytes 49160 | tf_op jit(solution)/shard_map/ppermute | solution.py:30
  72.5 35.6 %collective-permute-start.11 = (bf16[2048,256]{1,0:T(8,128)(2,1)}, bf16[2048,256]{1,0:T(8,128)(2,1)S(1)}, u32[]{:S(2)}, u32[]{:S(2)}) collective-permute-start(bf16[2048,256]{1,0:T(8,128)(2,1)} %get-tuple-element.36), channel_id=1, source_target_pairs={{0,224},{1,225},{2,226},{3,227},{4,228},{5,229},{6,230},{7,231},{8... | collective-permute-start | bytes 3145736 | tf_op jit(solution)/shard_map/ppermute | solution.py:30
  77.2 31.0 %collective-permute-start.12 = (bf16[1024,256]{1,0:T(8,128)(2,1)}, bf16[1024,256]{1,0:T(8,128)(2,1)}, u32[]{:S(2)}, u32[]{:S(2)}) collective-permute-start(bf16[1024,256]{1,0:T(8,128)(2,1)} %slice_bitcast_fusion.4), channel_id=1, source_target_pairs={{0,224},{1,225},{2,226},{3,227},{4,228},{5,229},{6,230},{7,231},{8... | collective-permute-start | bytes 1572872 | tf_op jit(solution)/shard_map/ppermute | solution.py:30
  87.5 26.5 %copy-start.6 = (bf16[1,4096,256]{2,1,0:T(8,128)(2,1)S(1)}, bf16[1,4096,256]{2,1,0:T(8,128)(2,1)}, u32[]{:S(2)}) copy-start(bf16[1,4096,256]{2,1,0:T(8,128)(2,1)} %param.9) | copy-start | bytes 6291460
  87.5 20.7 %collective-permute-start.7 = (bf16[2,128,1024]{2,1,0:T(8,128)(2,1)}, bf16[2,128,1024]{2,1,0:T(8,128)(2,1)}, u32[]{:S(2)}, u32[]{:S(2)}) collective-permute-start(bf16[2,128,1024]{2,1,0:T(8,128)(2,1)} %get-tuple-element.63), channel_id=1, source_target_pairs={{0,4},{1,5},{2,6},{3,7},{4,8},{5,9},{6,10},{7,11},{8,12},{9,13},{1... | collective-permute-start | bytes 1572872 | tf_op jit(solution)/shard_map/ppermute | solution.py:30
  87.6 20.5 %collective-permute-start.8 = (bf16[2,128,1024]{2,1,0:T(8,128)(2,1)}, bf16[2,128,1024]{2,1,0:T(8,128)(2,1)}, u32[]{:S(2)}, u32[]{:S(2)}) collective-permute-start(bf16[2,128,1024]{2,1,0:T(8,128)(2,1)} %get-tuple-element.62), channel_id=1, source_target_pairs={{0,28},{1,29},{2,30},{3,31},{4,0},{5,1},{6,2},{7,3},{8,4},{9,5},{1... | collective-permute-start | bytes 1572872 | tf_op jit(solution)/shard_map/ppermute | solution.py:30
  111.0 30.7 %collective-permute-start.19 = (bf16[2048,1024]{1,0:T(8,128)(2,1)}, bf16[2048,1024]{1,0:T(8,128)(2,1)}, u32[]{:S(2)}, u32[]{:S(2)}) collective-permute-start(bf16[2048,1024]{1,0:T(8,128)(2,1)} %bitcast.126), channel_id=1, source_target_pairs={{0,1},{1,0},{2,3},{3,2},{4,5},{5,4},{6,7},{7,6},{8,9},{9,8},{10,11... | collective-permute-start | bytes 12582920 | tf_op jit(solution)/shard_map/ppermute | solution.py:30
  115.0 21.3 %collective-permute-start.15 = (bf16[1536,256]{1,0:T(8,128)(2,1)S(1)}, bf16[1536,256]{1,0:T(8,128)(2,1)S(1)}, u32[]{:S(2)}, u32[]{:S(2)}) collective-permute-start(bf16[1536,256]{1,0:T(8,128)(2,1)S(1)} %get-tuple-element.43), channel_id=1, source_target_pairs={{0,224},{1,225},{2,226},{3,227},{4,228},{5,229},{6,230},{7,231},{8... | collective-permute-start | bytes 2359304 | tf_op jit(solution)/shard_map/ppermute | solution.py:30
  119.3 49.7 %collective-permute-start.20 = (bf16[1536,256]{1,0:T(8,128)(2,1)}, bf16[1536,256]{1,0:T(8,128)(2,1)}, u32[]{:S(2)}, u32[]{:S(2)}) collective-permute-start(bf16[1536,256]{1,0:T(8,128)(2,1)} %get-tuple-element.50), channel_id=1, source_target_pairs={{0,224},{1,225},{2,226},{3,227},{4,228},{5,229},{6,230},{7,231},{8... | collective-permute-start | bytes 2359304 | tf_op jit(solution)/shard_map/ppermute | solution.py:30
  119.4 14.4 %collective-permute-start.13 = (bf16[2,128,1024]{2,1,0:T(8,128)(2,1)S(1)}, bf16[2,128,1024]{2,1,0:T(8,128)(2,1)S(1)}, u32[]{:S(2)}, u32[]{:S(2)}) collective-permute-start(bf16[2,128,1024]{2,1,0:T(8,128)(2,1)S(1)} %copy-done.14), channel_id=1, source_target_pairs={{0,4},{1,5},{2,6},{3,7},{4,8},{5,9},{6,10},{7,11},{8,12},{9,13},{1... | collective-permute-start | bytes 1572872 | tf_op jit(solution)/shard_map/ppermute | solution.py:30
  120.9 14.6 %collective-permute-start.14 = (bf16[2,128,1024]{2,1,0:T(8,128)(2,1)S(1)}, bf16[2,128,1024]{2,1,0:T(8,128)(2,1)S(1)}, u32[]{:S(2)}, u32[]{:S(2)}) collective-permute-start(bf16[2,128,1024]{2,1,0:T(8,128)(2,1)S(1)} %copy-done.13), channel_id=1, source_target_pairs={{0,28},{1,29},{2,30},{3,31},{4,0},{5,1},{6,2},{7,3},{8,4},{9,5},{1... | collective-permute-start | bytes 1572872 | tf_op jit(solution)/shard_map/ppermute | solution.py:30
  124.9 16.9 %copy-start.8 = (bf16[16,1,128,256]{3,2,1,0:T(8,128)(2,1)}, bf16[16,1,128,256]{3,2,1,0:T(8,128)(2,1)S(1)}, u32[]{:S(2)}) copy-start(bf16[16,1,128,256]{3,2,1,0:T(8,128)(2,1)S(1)} %get-tuple-element.69) | copy-start | bytes 3145732
  124.9 16.9 %copy-start.10 = (bf16[16,1,128,256]{3,2,1,0:T(8,128)(2,1)}, bf16[16,1,128,256]{3,2,1,0:T(8,128)(2,1)S(1)}, u32[]{:S(2)}) copy-start(bf16[16,1,128,256]{3,2,1,0:T(8,128)(2,1)S(1)} %get-tuple-element.68) | copy-start | bytes 3145732
  133.8 35.2 %collective-permute-start.18 = (f32[2,128]{1,0:T(2,128)S(1)}, f32[2,128]{1,0:T(2,128)S(1)}, u32[]{:S(2)}, u32[]{:S(2)}) collective-permute-start(f32[2,128]{1,0:T(2,128)S(1)} %slice.39), channel_id=1, source_target_pairs={{0,2},{1,3},{2,0},{3,1},{4,6},{5,7},{6,4},{7,5},{8,10},{9,11},{10,... | collective-permute-start | bytes 3080 | tf_op jit(solution)/shard_map/ppermute | solution.py:30
  139.0 30.0 %collective-permute-start.16 = (bf16[2,128,1024]{2,1,0:T(8,128)(2,1)}, bf16[2,128,1024]{2,1,0:T(8,128)(2,1)}, u32[]{:S(2)}, u32[]{:S(2)}) collective-permute-start(bf16[2,128,1024]{2,1,0:T(8,128)(2,1)} %get-tuple-element.59), channel_id=1, source_target_pairs={{0,4},{1,5},{2,6},{3,7},{4,8},{5,9},{6,10},{7,11},{8,12},{9,13},{1... | collective-permute-start | bytes 1572872 | tf_op jit(solution)/shard_map/ppermute | solution.py:30
  140.6 28.5 %collective-permute-start.17 = (bf16[2,128,1024]{2,1,0:T(8,128)(2,1)}, bf16[2,128,1024]{2,1,0:T(8,128)(2,1)}, u32[]{:S(2)}, u32[]{:S(2)}) collective-permute-start(bf16[2,128,1024]{2,1,0:T(8,128)(2,1)} %get-tuple-element.58), channel_id=1, source_target_pairs={{0,28},{1,29},{2,30},{3,31},{4,0},{5,1},{6,2},{7,3},{8,4},{9,5},{1... | collective-permute-start | bytes 1572872 | tf_op jit(solution)/shard_map/ppermute | solution.py:30
  148.1 20.8 %all-to-all-start.1 = ((bf16[32,32,128]{2,1,0:T(8,128)(2,1)}), bf16[32,32,128]{2,1,0:T(8,128)(2,1)S(1)}, u32[]{:S(2)}, u32[]{:S(2)}) async-start(bf16[32,32,128]{2,1,0:T(8,128)(2,1)} %broadcast_in_dim.82), calls=%async_computation.1 | async-start | bytes 524288 | tf_op jit(solution)/shard_map/all_to_all | solution.py:279
  170.9 13.7 %collective-permute-start.21 = (bf16[128,1024]{1,0:T(8,128)(2,1)S(1)}, bf16[128,1024]{1,0:T(8,128)(2,1)S(1)}, u32[]{:S(2)}, u32[]{:S(2)}) collective-permute-start(bf16[128,1024]{1,0:T(8,128)(2,1)S(1)} %get-tuple-element.72), channel_id=1, source_target_pairs={{0,32},{1,33},{2,34},{3,35},{4,36},{5,37},{6,38},{7,39},{8,40},{9,... | collective-permute-start | bytes 786440 | tf_op jit(solution)/shard_map/ppermute | solution.py:30
  171.4 15.0 %collective-permute-start.22 = (bf16[128,1024]{1,0:T(8,128)(2,1)S(1)}, bf16[128,1024]{1,0:T(8,128)(2,1)S(1)}, u32[]{:S(2)}, u32[]{:S(2)}) collective-permute-start(bf16[128,1024]{1,0:T(8,128)(2,1)S(1)} %get-tuple-element.73), channel_id=1, source_target_pairs={{0,34},{1,35},{2,32},{3,33},{4,38},{5,39},{6,36},{7,37},{8,42},{9,... | collective-permute-start | bytes 786440 | tf_op jit(solution)/shard_map/ppermute | solution.py:30
  (11 other events, 41.5 us)
Sparse Core Ops, SparseCore 0:
  18.2 68.5 all-gather.1

commit v4 on v3

--- a/solution.py
+++ b/solution.py
@@ -17,7 +17,8 @@
 LANE = WIDTH // N_T
 KEYS = 1024
 PACK = LANE + 16
-SPLIT = (TOK // 4, 5 * TOK // 8)
+CUT = 3 * TOK // 4
+SPLIT = TOK // 4
 AXES = ("section", "ts")
 
 
@@ -188,7 +189,7 @@
     cot_mine = lax.all_gather(cot_pair, "ts", axis=0, axis_index_groups=lanes, tiled=True)
     cot_mine = cot_mine.reshape(TOK // 2, KEYS)
 
-    older_first = move(after(saved[: TOK // 2], cot_half), to_mirror)
+    older_first = move(after(saved[:CUT], cot_half), to_mirror)
 
     rows = fresh.reshape(N_T // 2, 2, OWN, LANE)
     rows_other = fresh_rows.reshape(N_T // 2, 2, OWN, LANE)
@@ -209,19 +210,17 @@
     )
     halves = [[q * 4 + h * 2 + c for q in range(N_Z) for c in range(2)] for h in range(2)]
     squares = lax.all_to_all(
-        after(squares, rows_other), "ts", 0, 0, axis_index_groups=halves, tiled=True
+        after(squares, packed), "ts", 0, 0, axis_index_groups=halves, tiled=True
     )
     squares_raw = squares
     squares = jnp.sum(squares.astype(F32), axis=0)
     older_sq = [move(squares[2:], to_mirror), move(squares[2:], to_mirror_other_half)]
     fresh_other = move(after(squares[:2], *older_sq), to_other_half)
 
-    older_second = move(after(saved[TOK // 2 :], *older_sq), to_mirror)
-
-    parts = [
-        move(after(returning[0, begin:end], *older_sq), to_previous)
-        for begin, end in zip((0,) + SPLIT, SPLIT + (TOK,))
-    ]
+    older_second = move(after(saved[CUT:], *older_sq), to_mirror)
+
+    early = move(after(returning[0, :SPLIT], *older_sq), to_previous)
+    late = returning[0, SPLIT:]
 
     packed_other = move(packed, to_other_core)
     partial = forward(place, rows, rows_other, packed, packed_other)
@@ -229,35 +228,44 @@
     def block(distance):
         return lax.dynamic_slice_in_dim(partial, ((z + distance) % N_Z) * 2, 2, 0)
 
-    far = after(block(4), squares_raw)
-    up = move(far, z_up, (0,))
-    down = move(far, z_down, (1,))
-    up, down = lax.optimization_barrier((up, down, older_first))[:2]
-    up = move(add(block(3), up), z_up)
-    down = move(add(block(-3), down), z_down)
-    up, down = lax.optimization_barrier((up, down, older_second, parts[0]))[:2]
-    up = add(block(2), up)
-    down = add(block(-2), down)
-
-    older = jnp.concatenate([older_first, older_second], axis=0)
-    cot_mine, *older_sq = lax.optimization_barrier((cot_mine, *older_sq, up, down))[:3]
+    up = move(block(4), z_up, (0,))
+    down = move(block(4), z_down, (1,))
+    base = jnp.zeros((N_T // 2, 2, OWN, LANE), F32)
+    up, down, base, late = lax.optimization_barrier(
+        (up, down, base, late, squares_raw, older_first, *older_sq)
+    )[:4]
+    late = move(after(late, early), to_previous)
+    up = add(block(3), up)
+    down = add(block(-3), down)
     up = move(up, z_up)
     down = move(down, z_down)
+    up, down, cot_mine = lax.optimization_barrier((up, down, cot_mine, older_second, early))[:3]
+
     cots = [cot_mine, move(cot_mine, to_other_core)]
-    older_rate = lax.rsqrt((older_sq[0] + older_sq[1]) / WIDTH + eps).reshape(TOK)
-    live = (jnp.arange(TOK, dtype=jnp.int32) < lengths[0]).astype(F32)
-    scales = by_core(live * older_rate)
     raw = [
         lax.dot_general(cot, weights, (((1,), (1,)), ((), ())), preferred_element_type=F32)
         for cot in cots
     ]
-    up, down, raw[0] = lax.optimization_barrier((up, down, raw[0]))
-    up, down = lax.optimization_barrier((up, down, parts[1]))[:2]
-    up = move(add(block(1), up), z_up)
-    down = move(add(block(-1), down), z_down)
+    up = add(block(2), up)
+    down = add(block(-2), down)
+    older_first, older_second, *older_sq = lax.optimization_barrier(
+        (older_first, older_second, *older_sq, up, down)
+    )[:4]
+    up = move(up, z_up)
+    down = move(down, z_down)
+    up, down, *raw = lax.optimization_barrier((up, down, *raw))
+    up = add(block(1), up)
+    down = add(block(-1), down)
+    up, down, *raw = lax.optimization_barrier((up, down, *raw))
+    up = move(up, z_up)
+    down = move(down, z_down)
+    older = jnp.concatenate([older_first, older_second], axis=0)
+    older_rate = lax.rsqrt((older_sq[0] + older_sq[1]) / WIDTH + eps).reshape(TOK)
+    live = (jnp.arange(TOK, dtype=jnp.int32) < lengths[0]).astype(F32)
+    scales = by_core(live * older_rate)
     grads = []
     curves = []
-    weight_total = jnp.zeros((LANE, KEYS), F32)
+    lefts = []
     gain_grad = jnp.zeros((LANE,), F32)
     for cot, product, rows, scale in zip(cots, raw, by_core(older), scales):
         wide = rows.astype(F32)
@@ -265,37 +273,38 @@
         grads.append(grad)
         curves.append(jnp.sum(grad * (wide * gain).astype(BF).astype(F32), axis=1))
         gain_grad = gain_grad + jnp.sum(grad * wide, axis=0)
-        weight_total = weight_total + lax.dot_general(
-            (wide * gain * scale[:, None]).astype(BF),
-            cot,
-            (((0,), (0,)), ((), ())),
-            preferred_element_type=F32,
-        )
+        lefts.append(wide * gain * scale[:, None])
 
     mine = (jnp.arange(2) == core)[None, :, None]
     curve = [part.reshape(N_T // 2, 1, OWN) for part in curves]
     curve = jnp.where(mine, curve[0], curve[1])
     curve = jnp.broadcast_to(curve.reshape(1, N_T, OWN).astype(BF), (N_T, N_T, OWN))
     curve = lax.all_to_all(curve, "ts", 0, 0, tiled=True)
-    up, down, fresh_other = lax.optimization_barrier((up, down, fresh_other, curve, parts[2]))[:3]
+    up, down, fresh_other = lax.optimization_barrier((up, down, fresh_other, curve))[:3]
     fresh_rate = lax.rsqrt((squares[:2] + fresh_other) / WIDTH + eps)
     curve = jnp.sum(curve.astype(F32), axis=0).reshape(TOK)
     pull = older_rate * older_rate / WIDTH * curve
 
     summed = block(0).astype(F32) + up.astype(F32) + down.astype(F32)
-    straight = move((pick(summed, half) * pick(fresh_rate, half)[:, None]).astype(BF), to_next)
-    crossed = move(
-        (pick(summed, 1 - half) * pick(fresh_rate, 1 - half)[:, None]).astype(BF), to_next_other_half
-    )
+    straight = (pick(summed, half) * pick(fresh_rate, half)[:, None]).astype(BF)
+    crossed = (pick(summed, 1 - half) * pick(fresh_rate, 1 - half)[:, None]).astype(BF)
+    *cots, pull = lax.optimization_barrier((*cots, pull, straight, crossed))[:3]
+    straight = move(straight, to_next)
+    crossed = move(crossed, to_next_other_half)
     new_keys = (straight.astype(F32) + crossed.astype(F32)).astype(BF)
 
-    base = jnp.zeros((N_T // 2, 2, OWN, LANE), F32)
+    weight_total = sum(
+        lax.dot_general(
+            left.astype(BF), cot, (((0,), (0,)), ((), ())), preferred_element_type=F32
+        )
+        for left, cot in zip(lefts, cots)
+    )
     for index, grad in zip((core, 1 - core), grads):
         base = lax.dynamic_update_index_in_dim(
             base, (gain * grad).reshape(N_T // 2, OWN, LANE), index, 1
         )
     base = base.reshape(TOK, LANE)
-    downstream = jnp.concatenate(parts, axis=0)
+    downstream = jnp.concatenate([early, late], axis=0)
     total = downstream.astype(F32) + base - pull[:, None] * older.astype(F32)
     return (
         new_keys[None],

time: 195 us -> 195 us (level)
  waiting for transfers between devices: 58.1 us -> 53.1 us
  starting transfers between devices: 62.8 us -> 65.7 us
    all_to_all x1, waiting for transfers between devices: 5.23 us -> 0.01 us  [shards(): lax.all_to_all(after(squares, packed), 'ts', 0, 0, axis_index_groups=halv...]
    reduce_sum x0 -> x1, other arithmetic: none -> 2.91 us  [shards(): gain_grad = gain_grad + jnp.sum(grad * wide, axis=0)]
    convert_element_type x3, other arithmetic: 8.26 us -> 5.75 us  [add(): return (a.astype(F32) + b.astype(F32)).astype(BF)]
    slice x1 -> x2, local copies, waits for them, and re-layouts: 1.51 us -> 3.73 us  [the longest x1 2.65 us: shards(): older_first = move(after(saved[:CUT], cot_half), to_mirror)]
    ppermute x23 -> x22, starting transfers between devices: 46.2 us -> 48.3 us  [move(): return lax.ppermute(value, AXES, pairs)]
    ppermute x23 -> x22, waiting for transfers between devices: 52.5 us -> 53.1 us  [move(): return lax.ppermute(value, AXES, pairs)]
  transfers between devices with their start and end apart: 26 -> 25, of which waited for: 12 -> 10; matrix products, arithmetic and copies ran while one was open for 23% -> 22% of each run, Pallas kernels for 3% -> 3%
where the time goes in v4:
time: 195 us; the launch traced here: 193 us
  starting transfers between devices  65.7 us (34%)
  waiting for transfers between devices  53.1 us (27%)
  other arithmetic  24.6 us (13%)
  local copies, waits for them, and re-layouts  15.8 us (8%)
  between operations  15.2 us (8%)
  matrix products  13.4 us (7%)
  Pallas kernels  5.23 us (3%)
    ppermute x22, waiting for transfers between devices, move(): return lax.ppermute(value, AXES, pairs)  53.1 us
    ppermute x22, starting transfers between devices, move(): return lax.ppermute(value, AXES, pairs)  48.3 us
    all_to_all x1, starting transfers between devices, shards(): curve = lax.all_to_all(curve, 'ts', 0, 0, tiled=True)  8.85 us
    all_to_all x1, starting transfers between devices, shards(): lax.all_to_all(after(squares, packed), 'ts', 0, 0, axis_index_groups=halv...  8.59 us
    dot_general x2, matrix products, shards(): lax.dot_general(cot, weights, (((1,), (1,)), ((), ())), preferred_element...  7.39 us
    dot_general x2, matrix products, shards(): lax.dot_general(left.astype(BF), cot, (((0,), (0,)), ((), ())), preferred...  5.99 us
    convert_element_type x3, other arithmetic, add(): return (a.astype(F32) + b.astype(F32)).astype(BF)  5.75 us
    convert_element_type x1, other arithmetic, shards(): total.astype(BF)[None]  5.47 us
  transfers between devices with their start and end apart: 25, of which 10 were waited for; matrix products, arithmetic and copies ran while one was open for 22% of the time, Pallas kernels for 3%

profile of v4, /device:TPU:1, one launch (start us, length us, event | category | flops | bytes accessed | tf_op | source)
XLA Modules:
  0.0 193.1 jit_solution(7402078647304601804)
XLA Ops:
  7.2 3.7 %collective-permute-start.5 = (bf16[128,1024]{1,0:T(8,128)(2,1)}, bf16[128,1024]{1,0:T(8,128)(2,1)S(1)}, u32[]{:S(2)}, u32[]{:S(2)}) collective-permute-start(bf16[128,1024]{1,0:T(8,128)(2,1)} %bitcast.106), channel_id=1, source_target_pairs={{0,2},{1,3},{2,0},{3,1},{4,6},{5,7},{6,4},{7,5},{8,10},{9,11},{10,... | collective-permute-start | bytes 786440 | tf_op jit(solution)/shard_map/ppermute | solution.py:31
  10.9 5.3 %collective-permute-done.5 = bf16[128,1024]{1,0:T(8,128)(2,1)S(1)} collective-permute-done((bf16[128,1024]{1,0:T(8,128)(2,1)}, bf16[128,1024]{1,0:T(8,128)(2,1)S(1)}, u32[]{:S(2)}, u32[]{:S(2)}) %collective-permute-start.5) | collective-permute-done | bytes 262176 | tf_op jit(solution)/shard_map/ppermute | solution.py:31
  20.0 2.5 %collective-permute-start = (bf16[16,128,256]{2,1,0:T(8,128)(2,1)}, bf16[16,128,256]{2,1,0:T(8,128)(2,1)S(1)}, u32[]{:S(2)}, u32[]{:S(2)}) collective-permute-start(bf16[16,128,256]{2,1,0:T(8,128)(2,1)} %dynamic-slice_bitcast_fusion), channel_id=1, source_target_pairs={{0,1},{1,0},{2,3},{3,2},{4,5},{5,4},{6,7},{7,6},{8,9},{9,8},{10,11... | collective-permute-start | bytes 3145736 | tf_op jit(solution)/shard_map/ppermute | solution.py:31
  22.5 3.6 %collective-permute-start.1 = (bf16[272,1024]{1,0:T(8,128)(2,1)}, bf16[272,1024]{1,0:T(8,128)(2,1)}, u32[]{:S(2)}, u32[]{:S(2)}) collective-permute-start(bf16[272,1024]{1,0:T(8,128)(2,1)} %shard_map.102), channel_id=1, source_target_pairs={{0,224},{1,225},{2,226},{3,227},{4,228},{5,229},{6,230},{7,231},{8... | collective-permute-start | bytes 1671176 | tf_op jit(solution)/shard_map/ppermute | solution.py:31
  26.1 2.7 %slice_bitcast_fusion = bf16[3072,256]{1,0:T(8,128)(2,1)} fusion(bf16[1,4096,256]{2,1,0:T(8,128)(2,1)} %param.8), kind=kLoop, calls=%fused_computation.20 | loop fusion | bytes 3145728 | tf_op jit(solution)/shard_map/slice | solution.py:192
  29.4 2.4 %multiply_reduce_fusion = bf16[4096]{0:T(1024)(128)(2,1)S(1)} fusion(bf16[1,4096,256]{2,1,0:T(8,128)(2,1)} %param.8), kind=kLoop, calls=%fused_computation.1 | loop fusion | flops 3141632 | bytes 2105344 | tf_op jit(solution)/shard_map/reduce_sum | solution.py:203
  32.8 5.7 %collective-permute-done.1.packed_mine = bf16[272,1024]{1,0:T(8,128)(2,1)} collective-permute-done((bf16[272,1024]{1,0:T(8,128)(2,1)}, bf16[272,1024]{1,0:T(8,128)(2,1)}, u32[]{:S(2)}, u32[]{:S(2)}) %collective-permute-start.1) | collective-permute-done | bytes 557088 | tf_op jit(solution)/shard_map/ppermute | solution.py:31
  40.9 8.6 %all-to-all-start = ((bf16[16,34,128]{2,1,0:T(8,128)(2,1)}), bf16[16,34,128]{2,1,0:T(8,128)(2,1)S(1)}, u32[]{:S(2)}, u32[]{:S(2)}) async-start(bf16[16,34,128]{2,1,0:T(8,128)(2,1)} %pad_maximum_fusion.2), calls=%async_computation | async-start | bytes 327680 | tf_op jit(solution)/shard_map/all_to_all | solution.py:212
  49.5 4.3 %shard_map.103 = bf16[16,128,1024]{2,1,0:T(8,128)(2,1)S(1)} custom-call(s32[1]{0:T(128)} %bitcast.place, bf16[16,2,128,256]{3,2,1,0:T(8,128)(2,1)S(1)} %bitcast.95, bf16[16,128,256]{2,1,0:T(8,128)(2,1)S(1)} %collective-permute-done.rows_other, bf16[272,1024]{1,0:T(8,128)(2,1)} %collective-permute-done.1.packed_mine, ...), custom_call_target="tpu_custom_call" | custom-call | flops 2147483648 | bytes 7340032 | tf_op jit(solution)/shard_map/pallas_call | solution.py:142
  53.8 2.0 %copy-done = bf16[16,128,1024]{2,1,0:T(8,128)(2,1)} copy-done((bf16[16,128,1024]{2,1,0:T(8,128)(2,1)}, bf16[16,128,1024]{2,1,0:T(8,128)(2,1)S(1)}, u32[]{:S(2)}) %copy-start) | copy-done | bytes 4194328
  56.6 4.5 %collective-permute-start.4 = (bf16[2,128,1024]{2,1,0:T(8,128)(2,1)S(1)}, bf16[2,128,1024]{2,1,0:T(8,128)(2,1)S(1)}, u32[]{:S(2)}, u32[]{:S(2)}) collective-permute-start(bf16[2,128,1024]{2,1,0:T(8,128)(2,1)S(1)} %constant_dynamic-slice_fusion.6), channel_id=1, source_target_pairs={{1,29},{3,31},{5,1},{7,3},{9,5},{11,7},{13,9},{15,11},{17,13},{19,... | collective-permute-start | bytes 1572872 | tf_op jit(solution)/shard_map/ppermute | solution.py:31
  62.3 4.4 %collective-permute-start.7 = (f32[32,128]{1,0:T(8,128)S(1)}, f32[32,128]{1,0:T(8,128)S(1)}, u32[]{:S(2)}, u32[]{:S(2)}) collective-permute-start(f32[32,128]{1,0:T(8,128)S(1)} %slice.34), channel_id=1, source_target_pairs={{0,224},{1,225},{2,226},{3,227},{4,228},{5,229},{6,230},{7,231},{8... | collective-permute-start | bytes 49160 | tf_op jit(solution)/shard_map/ppermute | solution.py:31
  69.2 4.4 %collective-permute-done.7 = f32[32,128]{1,0:T(8,128)S(1)} collective-permute-done((f32[32,128]{1,0:T(8,128)S(1)}, f32[32,128]{1,0:T(8,128)S(1)}, u32[]{:S(2)}, u32[]{:S(2)}) %collective-permute-start.7) | collective-permute-done | bytes 16416 | tf_op jit(solution)/shard_map/ppermute | solution.py:31
  73.5 3.6 %collective-permute-start.11 = (bf16[1024,256]{1,0:T(8,128)(2,1)S(1)}, bf16[1024,256]{1,0:T(8,128)(2,1)S(1)}, u32[]{:S(2)}, u32[]{:S(2)}) collective-permute-start(bf16[1024,256]{1,0:T(8,128)(2,1)S(1)} %slice_bitcast_fusion.3), channel_id=1, source_target_pairs={{0,224},{1,225},{2,226},{3,227},{4,228},{5,229},{6,230},{7,231},{8... | collective-permute-start | bytes 1572872 | tf_op jit(solution)/shard_map/ppermute | solution.py:31
  81.2 3.5 %collective-permute-start.10 = (bf16[2,128,1024]{2,1,0:T(8,128)(2,1)S(1)}, bf16[2,128,1024]{2,1,0:T(8,128)(2,1)S(1)}, u32[]{:S(2)}, u32[]{:S(2)}) collective-permute-start(bf16[2,128,1024]{2,1,0:T(8,128)(2,1)S(1)} %get-tuple-element.78), channel_id=1, source_target_pairs={{0,28},{1,29},{2,30},{3,31},{4,0},{5,1},{6,2},{7,3},{8,4},{9,5},{1... | collective-permute-start | bytes 1572872 | tf_op jit(solution)/shard_map/ppermute | solution.py:31
  84.8 3.3 %collective-permute-done.11 = bf16[1024,256]{1,0:T(8,128)(2,1)S(1)} collective-permute-done((bf16[1024,256]{1,0:T(8,128)(2,1)S(1)}, bf16[1024,256]{1,0:T(8,128)(2,1)S(1)}, u32[]{:S(2)}, u32[]{:S(2)}) %collective-permute-start.11) | collective-permute-done | bytes 524320 | tf_op jit(solution)/shard_map/ppermute | solution.py:31
  88.1 10.8 %collective-permute-done.12 = bf16[1024,256]{1,0:T(8,128)(2,1)} collective-permute-done((bf16[1024,256]{1,0:T(8,128)(2,1)S(1)}, bf16[1024,256]{1,0:T(8,128)(2,1)}, u32[]{:S(2)}, u32[]{:S(2)}) %collective-permute-start.12) | collective-permute-done | bytes 524320 | tf_op jit(solution)/shard_map/ppermute | solution.py:31
  104.9 4.0 %collective-permute-start.14 = (bf16[2,128,1024]{2,1,0:T(8,128)(2,1)S(1)}, bf16[2,128,1024]{2,1,0:T(8,128)(2,1)S(1)}, u32[]{:S(2)}, u32[]{:S(2)}) collective-permute-start(bf16[2,128,1024]{2,1,0:T(8,128)(2,1)S(1)} %get-tuple-element.76), channel_id=1, source_target_pairs={{0,28},{1,29},{2,30},{3,31},{4,0},{5,1},{6,2},{7,3},{8,4},{9,5},{1... | collective-permute-start | bytes 1572872 | tf_op jit(solution)/shard_map/ppermute | solution.py:31
  109.0 3.5 %fusion.23 = f32[2048,256]{1,0:T(8,128)S(1)} fusion(bf16[2048,1024]{1,0:T(8,128)(2,1)} %bitcast.121, bf16[1,256,1024]{2,1,0:T(8,128)(2,1)S(1)} %copy-done.3), kind=kOutput, calls=%fused_computation.71 | convolution fusion | flops 1073741824 | bytes 6815744 | tf_op jit(solution)/shard_map/dot_general | solution.py:246
  114.3 3.9 %fusion.21 = f32[2048,256]{1,0:T(8,128)S(1)} fusion(bf16[2048,1024]{1,0:T(8,128)(2,1)} %collective-permute-done.15, bf16[1,256,1024]{2,1,0:T(8,128)(2,1)S(1)} %copy-done.3), kind=kOutput, calls=%fused_computation.69 | convolution fusion | flops 1073741824 | bytes 6815744 | tf_op jit(solution)/shard_map/dot_general | solution.py:246
  118.2 2.9 %collective-permute-done.13 = bf16[2,128,1024]{2,1,0:T(8,128)(2,1)S(1)} collective-permute-done((bf16[2,128,1024]{2,1,0:T(8,128)(2,1)S(1)}, bf16[2,128,1024]{2,1,0:T(8,128)(2,1)S(1)}, u32[]{:S(2)}, u32[]{:S(2)}) %collective-permute-start.13) | collective-permute-done | bytes 524320 | tf_op jit(solution)/shard_map/ppermute | solution.py:31
  121.0 2.5 %add_convert_fusion = (bf16[2,128,1024]{2,1,0:T(8,128)(2,1)}, bf16[2,128,1024]{2,1,0:T(8,128)(2,1)}) fusion(bf16[2,128,1024]{2,1,0:T(8,128)(2,1)S(1)} %collective-permute-done.14, bf16[16,128,1024]{2,1,0:T(8,128)(2,1)} %copy-done, s32[]{:T(128)S(6)} %select_n.145, bf16[2,128,1024]{2,1,0:T(8,128)(2,1)S(1)} %collective-permute-done.13, s32[]{:T(128)S(6)} %select_n.128), kind=kLoop, calls=%fused_computation.30 | loop fusion | flops 2097152 | bytes 3145736 | tf_op jit(solution)/shard_map/convert_element_type | solution.py:79
  123.6 2.9 %fusion.7 = (f32[256]{0:T(256)S(1)}, bf16[2048]{0:T(1024)(128)(2,1)S(1)}, f32[2048,256]{1,0:T(8,128)S(1)}, f32[2048,256]{1,0:T(8,128)}, bf16[2048]{0:T(1024)(128)(2,1)S(1)}, /*index=5*/f32[256]{0:T(256)S(1)}) fusion(f32[2048,256]{1,0:T(8,128)S(1)} %fusion.21, bf16[16,1,128,256]{3,2,1,0:T(8,128)(2,1)S(1)} %get-tuple-element.82, f32[2048]{0:T(1024)S(1)} %bitcast.115, ...), kind=kLoop, calls=%fused_computation.14 | loop fusion | flops 10481152 | bytes 10513408 | tf_op jit(solution)/shard_map/reduce_sum | solution.py:275
  127.3 8.8 %all-to-all-start.1 = ((bf16[32,32,128]{2,1,0:T(8,128)(2,1)}), bf16[32,32,128]{2,1,0:T(8,128)(2,1)S(1)}, u32[]{:S(2)}, u32[]{:S(2)}) async-start(bf16[32,32,128]{2,1,0:T(8,128)(2,1)} %broadcast_in_dim.83), calls=%async_computation.1 | async-start | bytes 524288 | tf_op jit(solution)/shard_map/all_to_all | solution.py:282
  136.2 3.0 %collective-permute-start.18 = (f32[2,128]{1,0:T(2,128)S(1)}, f32[2,128]{1,0:T(2,128)S(1)}, u32[]{:S(2)}, u32[]{:S(2)}) collective-permute-start(f32[2,128]{1,0:T(2,128)S(1)} %slice.35), channel_id=1, source_target_pairs={{0,2},{1,3},{2,0},{3,1},{4,6},{5,7},{6,4},{7,5},{8,10},{9,11},{10,... | collective-permute-start | bytes 3080 | tf_op jit(solution)/shard_map/ppermute | solution.py:31
  139.2 3.8 %collective-permute-start.21 = (bf16[3072,256]{1,0:T(8,128)(2,1)}, bf16[3072,256]{1,0:T(8,128)(2,1)}, u32[]{:S(2)}, u32[]{:S(2)}) collective-permute-start(bf16[3072,256]{1,0:T(8,128)(2,1)} %slice_bitcast_fusion.1), channel_id=1, source_target_pairs={{0,224},{1,225},{2,226},{3,227},{4,228},{5,229},{6,230},{7,231},{8... | collective-permute-start | bytes 4718600 | tf_op jit(solution)/shard_map/ppermute | solution.py:31
  145.7 2.4 %broadcast_in_dim.72 = f32[16,2,128,256]{3,2,1,0:T(8,128)} broadcast(f32[]{:T(128)} %constant.138.clone.1), dimensions={} | broadcast | bytes 4194308 | tf_op jit(solution)/shard_map/broadcast_in_dim | solution.py:233
  151.9 5.7 %collective-permute-done.16 = bf16[2,128,1024]{2,1,0:T(8,128)(2,1)} collective-permute-done((bf16[2,128,1024]{2,1,0:T(8,128)(2,1)}, bf16[2,128,1024]{2,1,0:T(8,128)(2,1)}, u32[]{:S(2)}, u32[]{:S(2)}) %collective-permute-start.16) | collective-permute-done | bytes 524320 | tf_op jit(solution)/shard_map/ppermute | solution.py:31
  159.9 3.6 %fusion.10 = f32[256,1024]{1,0:T(8,128)S(1)} fusion(bf16[2048,1024]{1,0:T(8,128)(2,1)} %collective-permute-done.15, bf16[2048,256]{1,0:T(8,128)(2,1)S(1)} %bitcast.104, f32[2048]{0:T(1024)S(1)} %bitcast.116, f32[256]{0:T(256)S(1)} %bitcast.98), kind=kOutput, calls=%fused_computation.24 | convolution fusion | flops 1075838976 | bytes 6300672 | tf_op jit(solution)/shard_map/dot_general | solution.py:297
  163.5 13.5 %collective-permute-done.21 = bf16[3072,256]{1,0:T(8,128)(2,1)} collective-permute-done((bf16[3072,256]{1,0:T(8,128)(2,1)}, bf16[3072,256]{1,0:T(8,128)(2,1)}, u32[]{:S(2)}, u32[]{:S(2)}) %collective-permute-start.21) | collective-permute-done | bytes 1572896 | tf_op jit(solution)/shard_map/ppermute | solution.py:31
  177.0 5.5 %subtract_convert_fusion = bf16[1,4096,256]{2,1,0:T(8,128)(2,1)} fusion(f32[1,4096,256]{2,1,0:T(8,128)} %bitcast.41, bf16[1,3072,256]{2,1,0:T(8,128)(2,1)} %bitcast.36, bf16[1,1024,256]{2,1,0:T(8,128)(2,1)} %bitcast.35, bf16[1,1024,256]{2,1,0:T(8,128)(2,1)S(1)} %bitcast.105, bf16[1,3072,256]{2,1,0:T(8,128)(2,1)} %bitcast.43, f32[4096]{0:T(1024)S(1)} %multiply_bitcast_fusion), kind=kLoop, calls=%fused_computation | loop fusion | flops 12582912 | bytes 10502144 | tf_op jit(solution)/shard_map/convert_element_type | solution.py:311
  182.5 2.4 %fusion.8 = f32[1,256,1024]{2,1,0:T(8,128)} fusion(f32[256,1024]{1,0:T(8,128)S(1)} %fusion.10, bf16[2048,1024]{1,0:T(8,128)(2,1)S(1)} %bitcast.122, bf16[2048,256]{1,0:T(8,128)(2,1)S(1)} %bitcast.103, f32[256]{0:T(256)S(1)} %bitcast.99, f32[2048]{0:T(1024)S(1)} %bitcast.114), kind=kOutput, calls=%fused_computation.23 | convolution fusion | flops 1076101120 | bytes 7349248 | tf_op jit(solution)/shard_map/dot_general | solution.py:297
  (94 shorter events, 34.2 us)
Async XLA Ops:
  7.2 10.9 %copy-start.2 = (bf16[1,256,1024]{2,1,0:T(8,128)(2,1)S(1)}, bf16[1,256,1024]{2,1,0:T(8,128)(2,1)}, u32[]{:S(2)}) copy-start(bf16[1,256,1024]{2,1,0:T(8,128)(2,1)} %param.11) | copy-start | bytes 1572868
  7.2 10.9 %copy-start.4 = (f32[1,256]{1,0:T(1,128)S(1)}, f32[1,256]{1,0:T(1,128)}, u32[]{:S(2)}) copy-start(f32[1,256]{1,0:T(1,128)} %gain.1) | copy-start | bytes 3076
  7.2 11.8 %copy-start.1 = (bf16[1,4096,256]{2,1,0:T(8,128)(2,1)S(1)}, bf16[1,4096,256]{2,1,0:T(8,128)(2,1)}, u32[]{:S(2)}) copy-start(bf16[1,4096,256]{2,1,0:T(8,128)(2,1)} %param.7) | copy-start | bytes 6291460
  7.2 91.7 %all-gather.2.cloned.1.call-start = ((), (), s32[]{:S(2)}) async-start(), calls=%async_computation.2 | async-start | bytes 4718592 | tf_op jit(solution)/shard_map/all_gather | solution.py:189
  7.2 8.9 %collective-permute-start.5 = (bf16[128,1024]{1,0:T(8,128)(2,1)}, bf16[128,1024]{1,0:T(8,128)(2,1)S(1)}, u32[]{:S(2)}, u32[]{:S(2)}) collective-permute-start(bf16[128,1024]{1,0:T(8,128)(2,1)} %bitcast.106), channel_id=1, source_target_pairs={{0,2},{1,3},{2,0},{3,1},{4,6},{5,7},{6,4},{7,5},{8,10},{9,11},{10,... | collective-permute-start | bytes 786440 | tf_op jit(solution)/shard_map/ppermute | solution.py:31
  20.0 29.5 %collective-permute-start = (bf16[16,128,256]{2,1,0:T(8,128)(2,1)}, bf16[16,128,256]{2,1,0:T(8,128)(2,1)S(1)}, u32[]{:S(2)}, u32[]{:S(2)}) collective-permute-start(bf16[16,128,256]{2,1,0:T(8,128)(2,1)} %dynamic-slice_bitcast_fusion), channel_id=1, source_target_pairs={{0,1},{1,0},{2,3},{3,2},{4,5},{5,4},{6,7},{7,6},{8,9},{9,8},{10,11... | collective-permute-start | bytes 3145736 | tf_op jit(solution)/shard_map/ppermute | solution.py:31
  22.5 16.0 %collective-permute-start.1 = (bf16[272,1024]{1,0:T(8,128)(2,1)}, bf16[272,1024]{1,0:T(8,128)(2,1)}, u32[]{:S(2)}, u32[]{:S(2)}) collective-permute-start(bf16[272,1024]{1,0:T(8,128)(2,1)} %shard_map.102), channel_id=1, source_target_pairs={{0,224},{1,225},{2,226},{3,227},{4,228},{5,229},{6,230},{7,231},{8... | collective-permute-start | bytes 1671176 | tf_op jit(solution)/shard_map/ppermute | solution.py:31
  29.4 10.2 %copy-start.8 = (bf16[1,4096,256]{2,1,0:T(8,128)(2,1)S(1)}, bf16[1,4096,256]{2,1,0:T(8,128)(2,1)}, u32[]{:S(2)}) copy-start(bf16[1,4096,256]{2,1,0:T(8,128)(2,1)} %param.9) | copy-start | bytes 6291460
  32.5 45.6 %collective-permute-start.6 = (bf16[3072,256]{1,0:T(8,128)(2,1)}, bf16[3072,256]{1,0:T(8,128)(2,1)}, u32[]{:S(2)}, u32[]{:S(2)}) collective-permute-start(bf16[3072,256]{1,0:T(8,128)(2,1)} %slice_bitcast_fusion), channel_id=1, source_target_pairs={{0,224},{1,225},{2,226},{3,227},{4,228},{5,229},{6,230},{7,231},{8... | collective-permute-start | bytes 4718600 | tf_op jit(solution)/shard_map/ppermute | solution.py:31
  38.5 11.0 %collective-permute-start.2 = (bf16[272,1024]{1,0:T(8,128)(2,1)}, bf16[272,1024]{1,0:T(8,128)(2,1)}, u32[]{:S(2)}, u32[]{:S(2)}) collective-permute-start(bf16[272,1024]{1,0:T(8,128)(2,1)} %collective-permute-done.1.packed_mine), channel_id=1, source_target_pairs={{0,1},{1,0},{2,3},{3,2},{4,5},{5,4},{6,7},{7,6},{8,9},{9,8},{10,11... | collective-permute-start | bytes 1671176 | tf_op jit(solution)/shard_map/ppermute | solution.py:31
  40.9 21.3 %all-to-all-start = ((bf16[16,34,128]{2,1,0:T(8,128)(2,1)}), bf16[16,34,128]{2,1,0:T(8,128)(2,1)S(1)}, u32[]{:S(2)}, u32[]{:S(2)}) async-start(bf16[16,34,128]{2,1,0:T(8,128)(2,1)} %pad_maximum_fusion.2), calls=%async_computation | async-start | bytes 327680 | tf_op jit(solution)/shard_map/all_to_all | solution.py:212
  55.9 21.3 %collective-permute-start.3 = (bf16[2,128,1024]{2,1,0:T(8,128)(2,1)S(1)}, bf16[2,128,1024]{2,1,0:T(8,128)(2,1)S(1)}, u32[]{:S(2)}, u32[]{:S(2)}) collective-permute-start(bf16[2,128,1024]{2,1,0:T(8,128)(2,1)S(1)} %constant_dynamic-slice_fusion.6), channel_id=1, source_target_pairs={{0,4},{2,6},{4,8},{6,10},{8,12},{10,14},{12,16},{14,18},{16,20},{1... | collective-permute-start | bytes 1572872 | tf_op jit(solution)/shard_map/ppermute | solution.py:31
  56.6 21.5 %collective-permute-start.4 = (bf16[2,128,1024]{2,1,0:T(8,128)(2,1)S(1)}, bf16[2,128,1024]{2,1,0:T(8,128)(2,1)S(1)}, u32[]{:S(2)}, u32[]{:S(2)}) collective-permute-start(bf16[2,128,1024]{2,1,0:T(8,128)(2,1)S(1)} %constant_dynamic-slice_fusion.6), channel_id=1, source_target_pairs={{1,29},{3,31},{5,1},{7,3},{9,5},{11,7},{13,9},{15,11},{17,13},{19,... | collective-permute-start | bytes 1572872 | tf_op jit(solution)/shard_map/ppermute | solution.py:31
  62.3 11.2 %collective-permute-start.7 = (f32[32,128]{1,0:T(8,128)S(1)}, f32[32,128]{1,0:T(8,128)S(1)}, u32[]{:S(2)}, u32[]{:S(2)}) collective-permute-start(f32[32,128]{1,0:T(8,128)S(1)} %slice.34), channel_id=1, source_target_pairs={{0,224},{1,225},{2,226},{3,227},{4,228},{5,229},{6,230},{7,231},{8... | collective-permute-start | bytes 49160 | tf_op jit(solution)/shard_map/ppermute | solution.py:31
  66.7 6.9 %collective-permute-start.8 = (f32[32,128]{1,0:T(8,128)S(1)}, f32[32,128]{1,0:T(8,128)S(1)}, u32[]{:S(2)}, u32[]{:S(2)}) collective-permute-start(f32[32,128]{1,0:T(8,128)S(1)} %slice.34), channel_id=1, source_target_pairs={{0,226},{1,227},{2,224},{3,225},{4,230},{5,231},{6,228},{7,229},{8... | collective-permute-start | bytes 49160 | tf_op jit(solution)/shard_map/ppermute | solution.py:31
  73.5 14.6 %collective-permute-start.11 = (bf16[1024,256]{1,0:T(8,128)(2,1)S(1)}, bf16[1024,256]{1,0:T(8,128)(2,1)S(1)}, u32[]{:S(2)}, u32[]{:S(2)}) collective-permute-start(bf16[1024,256]{1,0:T(8,128)(2,1)S(1)} %slice_bitcast_fusion.3), channel_id=1, source_target_pairs={{0,224},{1,225},{2,226},{3,227},{4,228},{5,229},{6,230},{7,231},{8... | collective-permute-start | bytes 1572872 | tf_op jit(solution)/shard_map/ppermute | solution.py:31
  77.1 21.8 %collective-permute-start.12 = (bf16[1024,256]{1,0:T(8,128)(2,1)S(1)}, bf16[1024,256]{1,0:T(8,128)(2,1)}, u32[]{:S(2)}, u32[]{:S(2)}) collective-permute-start(bf16[1024,256]{1,0:T(8,128)(2,1)S(1)} %slice_bitcast_fusion.2), channel_id=1, source_target_pairs={{0,224},{1,225},{2,226},{3,227},{4,228},{5,229},{6,230},{7,231},{8... | collective-permute-start | bytes 1572872 | tf_op jit(solution)/shard_map/ppermute | solution.py:31
  79.8 29.2 %copy-start.3 = (bf16[1,256,1024]{2,1,0:T(8,128)(2,1)S(1)}, bf16[1,256,1024]{2,1,0:T(8,128)(2,1)}, u32[]{:S(2)}) copy-start(bf16[1,256,1024]{2,1,0:T(8,128)(2,1)} %param.11) | copy-start | bytes 1572868
  79.8 19.1 %collective-permute-start.9 = (bf16[2,128,1024]{2,1,0:T(8,128)(2,1)S(1)}, bf16[2,128,1024]{2,1,0:T(8,128)(2,1)S(1)}, u32[]{:S(2)}, u32[]{:S(2)}) collective-permute-start(bf16[2,128,1024]{2,1,0:T(8,128)(2,1)S(1)} %get-tuple-element.79), channel_id=1, source_target_pairs={{0,4},{1,5},{2,6},{3,7},{4,8},{5,9},{6,10},{7,11},{8,12},{9,13},{1... | collective-permute-start | bytes 1572872 | tf_op jit(solution)/shard_map/ppermute | solution.py:31
  81.2 17.7 %collective-permute-start.10 = (bf16[2,128,1024]{2,1,0:T(8,128)(2,1)S(1)}, bf16[2,128,1024]{2,1,0:T(8,128)(2,1)S(1)}, u32[]{:S(2)}, u32[]{:S(2)}) collective-permute-start(bf16[2,128,1024]{2,1,0:T(8,128)(2,1)S(1)} %get-tuple-element.78), channel_id=1, source_target_pairs={{0,28},{1,29},{2,30},{3,31},{4,0},{5,1},{6,2},{7,3},{8,4},{9,5},{1... | collective-permute-start | bytes 1572872 | tf_op jit(solution)/shard_map/ppermute | solution.py:31
  88.1 24.4 %copy-start.9 = (bf16[1024,256]{1,0:T(8,128)(2,1)}, bf16[1024,256]{1,0:T(8,128)(2,1)S(1)}, u32[]{:S(2)}) copy-start(bf16[1024,256]{1,0:T(8,128)(2,1)S(1)} %collective-permute-done.11) | copy-start | bytes 1572868
  98.9 15.4 %collective-permute-start.15 = (bf16[2048,1024]{1,0:T(8,128)(2,1)}, bf16[2048,1024]{1,0:T(8,128)(2,1)}, u32[]{:S(2)}, u32[]{:S(2)}) collective-permute-start(bf16[2048,1024]{1,0:T(8,128)(2,1)} %bitcast.120), channel_id=1, source_target_pairs={{0,1},{1,0},{2,3},{3,2},{4,5},{5,4},{6,7},{7,6},{8,9},{9,8},{10,11... | collective-permute-start | bytes 12582920 | tf_op jit(solution)/shard_map/ppermute | solution.py:31
  103.0 18.0 %collective-permute-start.13 = (bf16[2,128,1024]{2,1,0:T(8,128)(2,1)S(1)}, bf16[2,128,1024]{2,1,0:T(8,128)(2,1)S(1)}, u32[]{:S(2)}, u32[]{:S(2)}) collective-permute-start(bf16[2,128,1024]{2,1,0:T(8,128)(2,1)S(1)} %get-tuple-element.77), channel_id=1, source_target_pairs={{0,4},{1,5},{2,6},{3,7},{4,8},{5,9},{6,10},{7,11},{8,12},{9,13},{1... | collective-permute-start | bytes 1572872 | tf_op jit(solution)/shard_map/ppermute | solution.py:31
  104.9 16.1 %collective-permute-start.14 = (bf16[2,128,1024]{2,1,0:T(8,128)(2,1)S(1)}, bf16[2,128,1024]{2,1,0:T(8,128)(2,1)S(1)}, u32[]{:S(2)}, u32[]{:S(2)}) collective-permute-start(bf16[2,128,1024]{2,1,0:T(8,128)(2,1)S(1)} %get-tuple-element.76), channel_id=1, source_target_pairs={{0,28},{1,29},{2,30},{3,31},{4,0},{5,1},{6,2},{7,3},{8,4},{9,5},{1... | collective-permute-start | bytes 1572872 | tf_op jit(solution)/shard_map/ppermute | solution.py:31
  127.3 24.5 %all-to-all-start.1 = ((bf16[32,32,128]{2,1,0:T(8,128)(2,1)}), bf16[32,32,128]{2,1,0:T(8,128)(2,1)S(1)}, u32[]{:S(2)}, u32[]{:S(2)}) async-start(bf16[32,32,128]{2,1,0:T(8,128)(2,1)} %broadcast_in_dim.83), calls=%async_computation.1 | async-start | bytes 524288 | tf_op jit(solution)/shard_map/all_to_all | solution.py:282
  136.2 15.6 %collective-permute-start.18 = (f32[2,128]{1,0:T(2,128)S(1)}, f32[2,128]{1,0:T(2,128)S(1)}, u32[]{:S(2)}, u32[]{:S(2)}) collective-permute-start(f32[2,128]{1,0:T(2,128)S(1)} %slice.35), channel_id=1, source_target_pairs={{0,2},{1,3},{2,0},{3,1},{4,6},{5,7},{6,4},{7,5},{8,10},{9,11},{10,... | collective-permute-start | bytes 3080 | tf_op jit(solution)/shard_map/ppermute | solution.py:31
  139.2 37.8 %collective-permute-start.21 = (bf16[3072,256]{1,0:T(8,128)(2,1)}, bf16[3072,256]{1,0:T(8,128)(2,1)}, u32[]{:S(2)}, u32[]{:S(2)}) collective-permute-start(bf16[3072,256]{1,0:T(8,128)(2,1)} %slice_bitcast_fusion.1), channel_id=1, source_target_pairs={{0,224},{1,225},{2,226},{3,227},{4,228},{5,229},{6,230},{7,231},{8... | collective-permute-start | bytes 4718600 | tf_op jit(solution)/shard_map/ppermute | solution.py:31
  143.0 14.6 %collective-permute-start.16 = (bf16[2,128,1024]{2,1,0:T(8,128)(2,1)}, bf16[2,128,1024]{2,1,0:T(8,128)(2,1)}, u32[]{:S(2)}, u32[]{:S(2)}) collective-permute-start(bf16[2,128,1024]{2,1,0:T(8,128)(2,1)} %get-tuple-element.52), channel_id=1, source_target_pairs={{0,4},{1,5},{2,6},{3,7},{4,8},{5,9},{6,10},{7,11},{8,12},{9,13},{1... | collective-permute-start | bytes 1572872 | tf_op jit(solution)/shard_map/ppermute | solution.py:31
  144.2 13.4 %collective-permute-start.17 = (bf16[2,128,1024]{2,1,0:T(8,128)(2,1)}, bf16[2,128,1024]{2,1,0:T(8,128)(2,1)}, u32[]{:S(2)}, u32[]{:S(2)}) collective-permute-start(bf16[2,128,1024]{2,1,0:T(8,128)(2,1)} %get-tuple-element.53), channel_id=1, source_target_pairs={{0,28},{1,29},{2,30},{3,31},{4,0},{5,1},{6,2},{7,3},{8,4},{9,5},{1... | collective-permute-start | bytes 1572872 | tf_op jit(solution)/shard_map/ppermute | solution.py:31
  159.5 25.4 %collective-permute-start.20 = (bf16[128,1024]{1,0:T(8,128)(2,1)S(1)}, bf16[128,1024]{1,0:T(8,128)(2,1)S(1)}, u32[]{:S(2)}, u32[]{:S(2)}) collective-permute-start(bf16[128,1024]{1,0:T(8,128)(2,1)S(1)} %get-tuple-element.85), channel_id=1, source_target_pairs={{0,34},{1,35},{2,32},{3,33},{4,38},{5,39},{6,36},{7,37},{8,42},{9,... | collective-permute-start | bytes 786440 | tf_op jit(solution)/shard_map/ppermute | solution.py:31
  159.7 25.7 %collective-permute-start.19 = (bf16[128,1024]{1,0:T(8,128)(2,1)S(1)}, bf16[128,1024]{1,0:T(8,128)(2,1)S(1)}, u32[]{:S(2)}, u32[]{:S(2)}) collective-permute-start(bf16[128,1024]{1,0:T(8,128)(2,1)S(1)} %get-tuple-element.84), channel_id=1, source_target_pairs={{0,32},{1,33},{2,34},{3,35},{4,36},{5,37},{6,38},{7,39},{8,40},{9,... | collective-permute-start | bytes 786440 | tf_op jit(solution)/shard_map/ppermute | solution.py:31
  159.9 17.1 %copy-start.10 = (bf16[1024,256]{1,0:T(8,128)(2,1)S(1)}, bf16[1024,256]{1,0:T(8,128)(2,1)}, u32[]{:S(2)}) copy-start(bf16[1024,256]{1,0:T(8,128)(2,1)} %copy-done.9) | copy-start | bytes 1572868
  (5 other events, 21.6 us)
Sparse Core Ops, SparseCore 0:
  18.2 68.8 all-gather.1

commit v5 on v4

--- a/solution.py
+++ b/solution.py
@@ -253,10 +253,9 @@
     )[:4]
     up = move(up, z_up)
     down = move(down, z_down)
-    up, down, *raw = lax.optimization_barrier((up, down, *raw))
+    up, down, raw[0] = lax.optimization_barrier((up, down, raw[0]))
     up = add(block(1), up)
     down = add(block(-1), down)
-    up, down, *raw = lax.optimization_barrier((up, down, *raw))
     up = move(up, z_up)
     down = move(down, z_down)
     older = jnp.concatenate([older_first, older_second], axis=0)
@@ -280,7 +279,7 @@
     curve = jnp.where(mine, curve[0], curve[1])
     curve = jnp.broadcast_to(curve.reshape(1, N_T, OWN).astype(BF), (N_T, N_T, OWN))
     curve = lax.all_to_all(curve, "ts", 0, 0, tiled=True)
-    up, down, fresh_other = lax.optimization_barrier((up, down, fresh_other, curve))[:3]
+    up, down, fresh_other = lax.optimization_barrier((up, down, fresh_other, curve, late))[:3]
     fresh_rate = lax.rsqrt((squares[:2] + fresh_other) / WIDTH + eps)
     curve = jnp.sum(curve.astype(F32), axis=0).reshape(TOK)
     pull = older_rate * older_rate / WIDTH * curve

time: 195 us -> 184 us (0.944)
  waiting for transfers between devices: 53.1 us -> 44.4 us
  other arithmetic: 24.6 us -> 22.6 us
    ppermute x22, waiting for transfers between devices: 53.1 us -> 40.5 us  [move(): return lax.ppermute(value, AXES, pairs)]
    all_to_all x1, waiting for transfers between devices: 0.01 us -> 3.87 us  [shards(): curve = lax.all_to_all(curve, 'ts', 0, 0, tiled=True)]
    reduce_sum x1 -> x0, other arithmetic: 2.91 us -> none  [shards(): gain_grad = gain_grad + jnp.sum(grad * wide, axis=0)]
  transfers between devices with their start and end apart: 25 -> 25, of which waited for: 10 -> 10; matrix products, arithmetic and copies ran while one was open for 22% -> 24% of each run, Pallas kernels for 3% -> 3%
where the time goes in v5:
time: 184 us
  starting transfers between devices  66.8 us (36%)
  waiting for transfers between devices  44.4 us (24%)
  other arithmetic  22.6 us (12%)
  local copies, waits for them, and re-layouts  16.8 us (9%)
  between operations  15.2 us (8%)
  matrix products  12.7 us (7%)
  Pallas kernels  5.21 us (3%)
    ppermute x22, starting transfers between devices, move(): return lax.ppermute(value, AXES, pairs)  48.8 us
    ppermute x22, waiting for transfers between devices, move(): return lax.ppermute(value, AXES, pairs)  40.5 us
    all_to_all x1, starting transfers between devices, shards(): curve = lax.all_to_all(curve, 'ts', 0, 0, tiled=True)  9.31 us
    all_to_all x1, starting transfers between devices, shards(): lax.all_to_all(after(squares, packed), 'ts', 0, 0, axis_index_groups=halv...  8.59 us
    dot_general x2, matrix products, shards(): lax.dot_general(cot, weights, (((1,), (1,)), ((), ())), preferred_element...  6.77 us
    convert_element_type x1, other arithmetic, shards(): total.astype(BF)[None]  6.11 us
    dot_general x2, matrix products, shards(): lax.dot_general(left.astype(BF), cot, (((0,), (0,)), ((), ())), preferred...  5.92 us
    convert_element_type x3, other arithmetic, add(): return (a.astype(F32) + b.astype(F32)).astype(BF)  5.85 us
  transfers between devices with their start and end apart: 25, of which 10 were waited for; matrix products, arithmetic and copies ran while one was open for 24% of the time, Pallas kernels for 3%

profile of v5, /device:TPU:1, one launch (start us, length us, event | category | flops | bytes accessed | tf_op | source)
XLA Modules:
  0.0 183.8 jit_solution(17941553256365170537)
XLA Ops:
  7.2 3.7 %collective-permute-start.5 = (bf16[128,1024]{1,0:T(8,128)(2,1)}, bf16[128,1024]{1,0:T(8,128)(2,1)S(1)}, u32[]{:S(2)}, u32[]{:S(2)}) collective-permute-start(bf16[128,1024]{1,0:T(8,128)(2,1)} %bitcast.109), channel_id=1, source_target_pairs={{0,2},{1,3},{2,0},{3,1},{4,6},{5,7},{6,4},{7,5},{8,10},{9,11},{10,... | collective-permute-start | bytes 786440 | tf_op jit(solution)/shard_map/ppermute | solution.py:31
  10.9 5.3 %collective-permute-done.5 = bf16[128,1024]{1,0:T(8,128)(2,1)S(1)} collective-permute-done((bf16[128,1024]{1,0:T(8,128)(2,1)}, bf16[128,1024]{1,0:T(8,128)(2,1)S(1)}, u32[]{:S(2)}, u32[]{:S(2)}) %collective-permute-start.5) | collective-permute-done | bytes 262176 | tf_op jit(solution)/shard_map/ppermute | solution.py:31
  20.1 2.5 %collective-permute-start = (bf16[16,128,256]{2,1,0:T(8,128)(2,1)}, bf16[16,128,256]{2,1,0:T(8,128)(2,1)S(1)}, u32[]{:S(2)}, u32[]{:S(2)}) collective-permute-start(bf16[16,128,256]{2,1,0:T(8,128)(2,1)} %dynamic-slice_bitcast_fusion), channel_id=1, source_target_pairs={{0,1},{1,0},{2,3},{3,2},{4,5},{5,4},{6,7},{7,6},{8,9},{9,8},{10,11... | collective-permute-start | bytes 3145736 | tf_op jit(solution)/shard_map/ppermute | solution.py:31
  22.5 3.6 %collective-permute-start.1 = (bf16[272,1024]{1,0:T(8,128)(2,1)}, bf16[272,1024]{1,0:T(8,128)(2,1)}, u32[]{:S(2)}, u32[]{:S(2)}) collective-permute-start(bf16[272,1024]{1,0:T(8,128)(2,1)} %shard_map.102), channel_id=1, source_target_pairs={{0,224},{1,225},{2,226},{3,227},{4,228},{5,229},{6,230},{7,231},{8... | collective-permute-start | bytes 1671176 | tf_op jit(solution)/shard_map/ppermute | solution.py:31
  26.1 2.7 %slice_bitcast_fusion = bf16[3072,256]{1,0:T(8,128)(2,1)} fusion(bf16[1,4096,256]{2,1,0:T(8,128)(2,1)} %param.8), kind=kLoop, calls=%fused_computation.20 | loop fusion | bytes 3145728 | tf_op jit(solution)/shard_map/slice | solution.py:192
  29.5 2.4 %multiply_reduce_fusion = bf16[4096]{0:T(1024)(128)(2,1)S(1)} fusion(bf16[1,4096,256]{2,1,0:T(8,128)(2,1)} %param.8), kind=kLoop, calls=%fused_computation.1 | loop fusion | flops 3141632 | bytes 2105344 | tf_op jit(solution)/shard_map/reduce_sum | solution.py:203
  32.8 5.7 %collective-permute-done.1.packed_mine = bf16[272,1024]{1,0:T(8,128)(2,1)} collective-permute-done((bf16[272,1024]{1,0:T(8,128)(2,1)}, bf16[272,1024]{1,0:T(8,128)(2,1)}, u32[]{:S(2)}, u32[]{:S(2)}) %collective-permute-start.1) | collective-permute-done | bytes 557088 | tf_op jit(solution)/shard_map/ppermute | solution.py:31
  41.0 8.6 %all-to-all-start = ((bf16[16,34,128]{2,1,0:T(8,128)(2,1)}), bf16[16,34,128]{2,1,0:T(8,128)(2,1)S(1)}, u32[]{:S(2)}, u32[]{:S(2)}) async-start(bf16[16,34,128]{2,1,0:T(8,128)(2,1)} %pad_maximum_fusion.2), calls=%async_computation | async-start | bytes 327680 | tf_op jit(solution)/shard_map/all_to_all | solution.py:212
  49.6 4.3 %shard_map.103 = bf16[16,128,1024]{2,1,0:T(8,128)(2,1)S(1)} custom-call(s32[1]{0:T(128)} %bitcast.place, bf16[16,2,128,256]{3,2,1,0:T(8,128)(2,1)S(1)} %bitcast.97, bf16[16,128,256]{2,1,0:T(8,128)(2,1)S(1)} %collective-permute-done.rows_other, bf16[272,1024]{1,0:T(8,128)(2,1)} %collective-permute-done.1.packed_mine, ...), custom_call_target="tpu_custom_call" | custom-call | flops 2147483648 | bytes 7340032 | tf_op jit(solution)/shard_map/pallas_call | solution.py:142
  53.9 2.0 %copy-done = bf16[16,128,1024]{2,1,0:T(8,128)(2,1)} copy-done((bf16[16,128,1024]{2,1,0:T(8,128)(2,1)}, bf16[16,128,1024]{2,1,0:T(8,128)(2,1)S(1)}, u32[]{:S(2)}) %copy-start) | copy-done | bytes 4194328
  56.7 4.5 %collective-permute-start.4 = (bf16[2,128,1024]{2,1,0:T(8,128)(2,1)S(1)}, bf16[2,128,1024]{2,1,0:T(8,128)(2,1)}, u32[]{:S(2)}, u32[]{:S(2)}) collective-permute-start(bf16[2,128,1024]{2,1,0:T(8,128)(2,1)S(1)} %constant_dynamic-slice_fusion.6), channel_id=1, source_target_pairs={{1,29},{3,31},{5,1},{7,3},{9,5},{11,7},{13,9},{15,11},{17,13},{19,... | collective-permute-start | bytes 1572872 | tf_op jit(solution)/shard_map/ppermute | solution.py:31
  62.3 4.4 %collective-permute-start.7 = (f32[32,128]{1,0:T(8,128)S(1)}, f32[32,128]{1,0:T(8,128)S(1)}, u32[]{:S(2)}, u32[]{:S(2)}) collective-permute-start(f32[32,128]{1,0:T(8,128)S(1)} %slice.34), channel_id=1, source_target_pairs={{0,224},{1,225},{2,226},{3,227},{4,228},{5,229},{6,230},{7,231},{8... | collective-permute-start | bytes 49160 | tf_op jit(solution)/shard_map/ppermute | solution.py:31
  69.2 4.3 %collective-permute-done.7 = f32[32,128]{1,0:T(8,128)S(1)} collective-permute-done((f32[32,128]{1,0:T(8,128)S(1)}, f32[32,128]{1,0:T(8,128)S(1)}, u32[]{:S(2)}, u32[]{:S(2)}) %collective-permute-start.7) | collective-permute-done | bytes 16416 | tf_op jit(solution)/shard_map/ppermute | solution.py:31
  73.6 3.6 %collective-permute-start.11 = (bf16[1024,256]{1,0:T(8,128)(2,1)S(1)}, bf16[1024,256]{1,0:T(8,128)(2,1)S(1)}, u32[]{:S(2)}, u32[]{:S(2)}) collective-permute-start(bf16[1024,256]{1,0:T(8,128)(2,1)S(1)} %slice_bitcast_fusion.3), channel_id=1, source_target_pairs={{0,224},{1,225},{2,226},{3,227},{4,228},{5,229},{6,230},{7,231},{8... | collective-permute-start | bytes 1572872 | tf_op jit(solution)/shard_map/ppermute | solution.py:31
  78.2 1.8 add_convert_fusion.4
  81.4 3.5 %collective-permute-start.10 = (bf16[2,128,1024]{2,1,0:T(8,128)(2,1)S(1)}, bf16[2,128,1024]{2,1,0:T(8,128)(2,1)S(1)}, u32[]{:S(2)}, u32[]{:S(2)}) collective-permute-start(bf16[2,128,1024]{2,1,0:T(8,128)(2,1)S(1)} %get-tuple-element.68), channel_id=1, source_target_pairs={{0,28},{1,29},{2,30},{3,31},{4,0},{5,1},{6,2},{7,3},{8,4},{9,5},{1... | collective-permute-start | bytes 1572872 | tf_op jit(solution)/shard_map/ppermute | solution.py:31
  85.0 3.2 %collective-permute-done.11 = bf16[1024,256]{1,0:T(8,128)(2,1)S(1)} collective-permute-done((bf16[1024,256]{1,0:T(8,128)(2,1)S(1)}, bf16[1024,256]{1,0:T(8,128)(2,1)S(1)}, u32[]{:S(2)}, u32[]{:S(2)}) %collective-permute-start.11) | collective-permute-done | bytes 524320 | tf_op jit(solution)/shard_map/ppermute | solution.py:31
  88.2 10.8 %collective-permute-done.12 = bf16[1024,256]{1,0:T(8,128)(2,1)S(1)} collective-permute-done((bf16[1024,256]{1,0:T(8,128)(2,1)S(1)}, bf16[1024,256]{1,0:T(8,128)(2,1)S(1)}, u32[]{:S(2)}, u32[]{:S(2)}) %collective-permute-start.12) | collective-permute-done | bytes 524320 | tf_op jit(solution)/shard_map/ppermute | solution.py:31
  101.4 4.6 %collective-permute-start.19 = (bf16[3072,256]{1,0:T(8,128)(2,1)}, bf16[3072,256]{1,0:T(8,128)(2,1)}, u32[]{:S(2)}, u32[]{:S(2)}) collective-permute-start(bf16[3072,256]{1,0:T(8,128)(2,1)} %slice_bitcast_fusion.1), channel_id=1, source_target_pairs={{0,224},{1,225},{2,226},{3,227},{4,228},{5,229},{6,230},{7,231},{8... | collective-permute-start | bytes 4718600 | tf_op jit(solution)/shard_map/ppermute | solution.py:31
  107.7 1.7 collective-permute-start.13
  109.4 4.0 %collective-permute-start.14 = (bf16[2,128,1024]{2,1,0:T(8,128)(2,1)S(1)}, bf16[2,128,1024]{2,1,0:T(8,128)(2,1)S(1)}, u32[]{:S(2)}, u32[]{:S(2)}) collective-permute-start(bf16[2,128,1024]{2,1,0:T(8,128)(2,1)S(1)} %get-tuple-element.66), channel_id=1, source_target_pairs={{0,28},{1,29},{2,30},{3,31},{4,0},{5,1},{6,2},{7,3},{8,4},{9,5},{1... | collective-permute-start | bytes 1572872 | tf_op jit(solution)/shard_map/ppermute | solution.py:31
  117.7 7.6 %collective-permute-done.13 = bf16[2,128,1024]{2,1,0:T(8,128)(2,1)S(1)} collective-permute-done((bf16[2,128,1024]{2,1,0:T(8,128)(2,1)S(1)}, bf16[2,128,1024]{2,1,0:T(8,128)(2,1)S(1)}, u32[]{:S(2)}, u32[]{:S(2)}) %collective-permute-start.13) | collective-permute-done | bytes 524320 | tf_op jit(solution)/shard_map/ppermute | solution.py:31
  125.3 2.5 %add_convert_fusion = (bf16[2,128,1024]{2,1,0:T(8,128)(2,1)}, bf16[2,128,1024]{2,1,0:T(8,128)(2,1)}) fusion(bf16[2,128,1024]{2,1,0:T(8,128)(2,1)S(1)} %collective-permute-done.14, bf16[16,128,1024]{2,1,0:T(8,128)(2,1)} %copy-done, s32[]{:T(128)S(6)} %select_n.145, bf16[2,128,1024]{2,1,0:T(8,128)(2,1)S(1)} %collective-permute-done.13, s32[]{:T(128)S(6)} %select_n.128), kind=kLoop, calls=%fused_computation.31 | loop fusion | flops 2097152 | bytes 3145736 | tf_op jit(solution)/shard_map/convert_element_type | solution.py:79
  127.8 2.7 %collective-permute-start.16 = (bf16[2,128,1024]{2,1,0:T(8,128)(2,1)}, bf16[2,128,1024]{2,1,0:T(8,128)(2,1)}, u32[]{:S(2)}, u32[]{:S(2)}) collective-permute-start(bf16[2,128,1024]{2,1,0:T(8,128)(2,1)} %get-tuple-element.64), channel_id=1, source_target_pairs={{0,28},{1,29},{2,30},{3,31},{4,0},{5,1},{6,2},{7,3},{8,4},{9,5},{1... | collective-permute-start | bytes 1572872 | tf_op jit(solution)/shard_map/ppermute | solution.py:31
  130.5 5.5 %fusion.7 = (f32[256]{0:T(256)S(1)}, bf16[2048]{0:T(1024)(128)(2,1)S(1)}, f32[2048,256]{1,0:T(8,128)S(1)}, f32[2048,256]{1,0:T(8,128)}, bf16[2048]{0:T(1024)(128)(2,1)S(1)}, /*index=5*/f32[256]{0:T(256)S(1)}) fusion(bf16[16,1,128,256]{3,2,1,0:T(8,128)(2,1)S(1)} %get-tuple-element.72, f32[256]{0:T(256)S(1)} %bitcast.99, f32[2048,256]{1,0:T(8,128)S(1)} %fusion.22, ...), kind=kOutput, calls=%fused_computation.15 | convolution fusion | flops 1084222976 | bytes 13134848 | tf_op jit(solution)/shard_map/dot_general | solution.py:246
  136.8 9.3 %all-to-all-start.1 = ((bf16[32,32,128]{2,1,0:T(8,128)(2,1)}), bf16[32,32,128]{2,1,0:T(8,128)(2,1)S(1)}, u32[]{:S(2)}, u32[]{:S(2)}) async-start(bf16[32,32,128]{2,1,0:T(8,128)(2,1)} %broadcast_in_dim.83), calls=%async_computation.1 | async-start | bytes 524288 | tf_op jit(solution)/shard_map/all_to_all | solution.py:281
  146.2 3.0 %collective-permute-start.17 = (f32[2,128]{1,0:T(2,128)S(1)}, f32[2,128]{1,0:T(2,128)S(1)}, u32[]{:S(2)}, u32[]{:S(2)}) collective-permute-start(f32[2,128]{1,0:T(2,128)S(1)} %slice.35), channel_id=1, source_target_pairs={{0,2},{1,3},{2,0},{3,1},{4,6},{5,7},{6,4},{7,5},{8,10},{9,11},{10,... | collective-permute-start | bytes 3080 | tf_op jit(solution)/shard_map/ppermute | solution.py:31
  149.2 2.4 %broadcast_in_dim.72 = f32[16,2,128,256]{3,2,1,0:T(8,128)} broadcast(f32[]{:T(128)} %constant.138.clone.1), dimensions={} | broadcast | bytes 4194308 | tf_op jit(solution)/shard_map/broadcast_in_dim | solution.py:233
  155.2 3.9 %all-to-all-done.1 = bf16[32,32,128]{2,1,0:T(8,128)(2,1)S(1)} async-done(((bf16[32,32,128]{2,1,0:T(8,128)(2,1)}), bf16[32,32,128]{2,1,0:T(8,128)(2,1)S(1)}, u32[]{:S(2)}, u32[]{:S(2)}) %all-to-all-start.1) | async-done | bytes 262176 | tf_op jit(solution)/shard_map/all_to_all | solution.py:281
  161.4 3.5 %fusion.10 = f32[256,1024]{1,0:T(8,128)S(1)} fusion(bf16[2048,1024]{1,0:T(8,128)(2,1)} %collective-permute-done.18, bf16[2048,256]{1,0:T(8,128)(2,1)S(1)} %bitcast.107, f32[2048]{0:T(1024)S(1)} %bitcast.119, f32[256]{0:T(256)S(1)} %bitcast.100), kind=kOutput, calls=%fused_computation.24 | convolution fusion | flops 1075838976 | bytes 6300672 | tf_op jit(solution)/shard_map/dot_general | solution.py:296
  165.0 6.1 %subtract_convert_fusion = bf16[1,4096,256]{2,1,0:T(8,128)(2,1)} fusion(f32[1,4096,256]{2,1,0:T(8,128)} %bitcast.41, bf16[1,3072,256]{2,1,0:T(8,128)(2,1)} %bitcast.36, bf16[1,1024,256]{2,1,0:T(8,128)(2,1)S(1)} %bitcast.108, bf16[1,1024,256]{2,1,0:T(8,128)(2,1)S(1)} %bitcast.105, bf16[1,3072,256]{2,1,0:T(8,128)(2,1)} %bitcast.43, f32[4096]{0:T(1024)S(1)} %multiply_bitcast_fusion), kind=kLoop, calls=%fused_computation | loop fusion | flops 12582912 | bytes 10502144 | tf_op jit(solution)/shard_map/convert_element_type | solution.py:310
  171.1 2.4 %fusion.8 = f32[1,256,1024]{2,1,0:T(8,128)} fusion(f32[256,1024]{1,0:T(8,128)S(1)} %fusion.10, bf16[2048,1024]{1,0:T(8,128)(2,1)S(1)} %bitcast.125, bf16[2048,256]{1,0:T(8,128)(2,1)S(1)} %bitcast.106, f32[256]{0:T(256)S(1)} %bitcast.101, f32[2048]{0:T(1024)S(1)} %bitcast.117), kind=kOutput, calls=%fused_computation.23 | convolution fusion | flops 1076101120 | bytes 7349248 | tf_op jit(solution)/shard_map/dot_general | solution.py:296
  (95 shorter events, 32.6 us)
Async XLA Ops:
  7.2 11.0 %copy-start.2 = (bf16[1,256,1024]{2,1,0:T(8,128)(2,1)S(1)}, bf16[1,256,1024]{2,1,0:T(8,128)(2,1)}, u32[]{:S(2)}) copy-start(bf16[1,256,1024]{2,1,0:T(8,128)(2,1)} %param.11) | copy-start | bytes 1572868
  7.2 11.0 %copy-start.4 = (f32[1,256]{1,0:T(1,128)S(1)}, f32[1,256]{1,0:T(1,128)}, u32[]{:S(2)}) copy-start(f32[1,256]{1,0:T(1,128)} %gain.1) | copy-start | bytes 3076
  7.2 11.9 %copy-start.1 = (bf16[1,4096,256]{2,1,0:T(8,128)(2,1)S(1)}, bf16[1,4096,256]{2,1,0:T(8,128)(2,1)}, u32[]{:S(2)}) copy-start(bf16[1,4096,256]{2,1,0:T(8,128)(2,1)} %param.7) | copy-start | bytes 6291460
  7.2 91.8 %all-gather.2.cloned.1.call-start = ((), (), s32[]{:S(2)}) async-start(), calls=%async_computation.2 | async-start | bytes 4718592 | tf_op jit(solution)/shard_map/all_gather | solution.py:189
  7.2 8.9 %collective-permute-start.5 = (bf16[128,1024]{1,0:T(8,128)(2,1)}, bf16[128,1024]{1,0:T(8,128)(2,1)S(1)}, u32[]{:S(2)}, u32[]{:S(2)}) collective-permute-start(bf16[128,1024]{1,0:T(8,128)(2,1)} %bitcast.109), channel_id=1, source_target_pairs={{0,2},{1,3},{2,0},{3,1},{4,6},{5,7},{6,4},{7,5},{8,10},{9,11},{10,... | collective-permute-start | bytes 786440 | tf_op jit(solution)/shard_map/ppermute | solution.py:31
  20.1 29.5 %collective-permute-start = (bf16[16,128,256]{2,1,0:T(8,128)(2,1)}, bf16[16,128,256]{2,1,0:T(8,128)(2,1)S(1)}, u32[]{:S(2)}, u32[]{:S(2)}) collective-permute-start(bf16[16,128,256]{2,1,0:T(8,128)(2,1)} %dynamic-slice_bitcast_fusion), channel_id=1, source_target_pairs={{0,1},{1,0},{2,3},{3,2},{4,5},{5,4},{6,7},{7,6},{8,9},{9,8},{10,11... | collective-permute-start | bytes 3145736 | tf_op jit(solution)/shard_map/ppermute | solution.py:31
  22.5 16.0 %collective-permute-start.1 = (bf16[272,1024]{1,0:T(8,128)(2,1)}, bf16[272,1024]{1,0:T(8,128)(2,1)}, u32[]{:S(2)}, u32[]{:S(2)}) collective-permute-start(bf16[272,1024]{1,0:T(8,128)(2,1)} %shard_map.102), channel_id=1, source_target_pairs={{0,224},{1,225},{2,226},{3,227},{4,228},{5,229},{6,230},{7,231},{8... | collective-permute-start | bytes 1671176 | tf_op jit(solution)/shard_map/ppermute | solution.py:31
  29.5 10.2 %copy-start.5 = (bf16[1,4096,256]{2,1,0:T(8,128)(2,1)S(1)}, bf16[1,4096,256]{2,1,0:T(8,128)(2,1)}, u32[]{:S(2)}) copy-start(bf16[1,4096,256]{2,1,0:T(8,128)(2,1)} %param.9) | copy-start | bytes 6291460
  32.6 45.6 %collective-permute-start.6 = (bf16[3072,256]{1,0:T(8,128)(2,1)}, bf16[3072,256]{1,0:T(8,128)(2,1)}, u32[]{:S(2)}, u32[]{:S(2)}) collective-permute-start(bf16[3072,256]{1,0:T(8,128)(2,1)} %slice_bitcast_fusion), channel_id=1, source_target_pairs={{0,224},{1,225},{2,226},{3,227},{4,228},{5,229},{6,230},{7,231},{8... | collective-permute-start | bytes 4718600 | tf_op jit(solution)/shard_map/ppermute | solution.py:31
  38.5 11.0 %collective-permute-start.2 = (bf16[272,1024]{1,0:T(8,128)(2,1)}, bf16[272,1024]{1,0:T(8,128)(2,1)}, u32[]{:S(2)}, u32[]{:S(2)}) collective-permute-start(bf16[272,1024]{1,0:T(8,128)(2,1)} %collective-permute-done.1.packed_mine), channel_id=1, source_target_pairs={{0,1},{1,0},{2,3},{3,2},{4,5},{5,4},{6,7},{7,6},{8,9},{9,8},{10,11... | collective-permute-start | bytes 1671176 | tf_op jit(solution)/shard_map/ppermute | solution.py:31
  41.0 21.3 %all-to-all-start = ((bf16[16,34,128]{2,1,0:T(8,128)(2,1)}), bf16[16,34,128]{2,1,0:T(8,128)(2,1)S(1)}, u32[]{:S(2)}, u32[]{:S(2)}) async-start(bf16[16,34,128]{2,1,0:T(8,128)(2,1)} %pad_maximum_fusion.2), calls=%async_computation | async-start | bytes 327680 | tf_op jit(solution)/shard_map/all_to_all | solution.py:212
  56.0 21.3 %collective-permute-start.3 = (bf16[2,128,1024]{2,1,0:T(8,128)(2,1)S(1)}, bf16[2,128,1024]{2,1,0:T(8,128)(2,1)S(1)}, u32[]{:S(2)}, u32[]{:S(2)}) collective-permute-start(bf16[2,128,1024]{2,1,0:T(8,128)(2,1)S(1)} %constant_dynamic-slice_fusion.6), channel_id=1, source_target_pairs={{0,4},{2,6},{4,8},{6,10},{8,12},{10,14},{12,16},{14,18},{16,20},{1... | collective-permute-start | bytes 1572872 | tf_op jit(solution)/shard_map/ppermute | solution.py:31
  56.7 21.5 %collective-permute-start.4 = (bf16[2,128,1024]{2,1,0:T(8,128)(2,1)S(1)}, bf16[2,128,1024]{2,1,0:T(8,128)(2,1)}, u32[]{:S(2)}, u32[]{:S(2)}) collective-permute-start(bf16[2,128,1024]{2,1,0:T(8,128)(2,1)S(1)} %constant_dynamic-slice_fusion.6), channel_id=1, source_target_pairs={{1,29},{3,31},{5,1},{7,3},{9,5},{11,7},{13,9},{15,11},{17,13},{19,... | collective-permute-start | bytes 1572872 | tf_op jit(solution)/shard_map/ppermute | solution.py:31
  62.3 11.2 %collective-permute-start.7 = (f32[32,128]{1,0:T(8,128)S(1)}, f32[32,128]{1,0:T(8,128)S(1)}, u32[]{:S(2)}, u32[]{:S(2)}) collective-permute-start(f32[32,128]{1,0:T(8,128)S(1)} %slice.34), channel_id=1, source_target_pairs={{0,224},{1,225},{2,226},{3,227},{4,228},{5,229},{6,230},{7,231},{8... | collective-permute-start | bytes 49160 | tf_op jit(solution)/shard_map/ppermute | solution.py:31
  66.7 6.8 %collective-permute-start.8 = (f32[32,128]{1,0:T(8,128)S(1)}, f32[32,128]{1,0:T(8,128)S(1)}, u32[]{:S(2)}, u32[]{:S(2)}) collective-permute-start(f32[32,128]{1,0:T(8,128)S(1)} %slice.34), channel_id=1, source_target_pairs={{0,226},{1,227},{2,224},{3,225},{4,230},{5,231},{6,228},{7,229},{8... | collective-permute-start | bytes 49160 | tf_op jit(solution)/shard_map/ppermute | solution.py:31
  73.6 14.6 %collective-permute-start.11 = (bf16[1024,256]{1,0:T(8,128)(2,1)S(1)}, bf16[1024,256]{1,0:T(8,128)(2,1)S(1)}, u32[]{:S(2)}, u32[]{:S(2)}) collective-permute-start(bf16[1024,256]{1,0:T(8,128)(2,1)S(1)} %slice_bitcast_fusion.3), channel_id=1, source_target_pairs={{0,224},{1,225},{2,226},{3,227},{4,228},{5,229},{6,230},{7,231},{8... | collective-permute-start | bytes 1572872 | tf_op jit(solution)/shard_map/ppermute | solution.py:31
  77.2 21.8 %collective-permute-start.12 = (bf16[1024,256]{1,0:T(8,128)(2,1)S(1)}, bf16[1024,256]{1,0:T(8,128)(2,1)S(1)}, u32[]{:S(2)}, u32[]{:S(2)}) collective-permute-start(bf16[1024,256]{1,0:T(8,128)(2,1)S(1)} %slice_bitcast_fusion.2), channel_id=1, source_target_pairs={{0,224},{1,225},{2,226},{3,227},{4,228},{5,229},{6,230},{7,231},{8... | collective-permute-start | bytes 1572872 | tf_op jit(solution)/shard_map/ppermute | solution.py:31
  80.0 19.0 %collective-permute-start.9 = (bf16[2,128,1024]{2,1,0:T(8,128)(2,1)S(1)}, bf16[2,128,1024]{2,1,0:T(8,128)(2,1)S(1)}, u32[]{:S(2)}, u32[]{:S(2)}) collective-permute-start(bf16[2,128,1024]{2,1,0:T(8,128)(2,1)S(1)} %get-tuple-element.69), channel_id=1, source_target_pairs={{0,4},{1,5},{2,6},{3,7},{4,8},{5,9},{6,10},{7,11},{8,12},{9,13},{1... | collective-permute-start | bytes 1572872 | tf_op jit(solution)/shard_map/ppermute | solution.py:31
  81.4 17.5 %collective-permute-start.10 = (bf16[2,128,1024]{2,1,0:T(8,128)(2,1)S(1)}, bf16[2,128,1024]{2,1,0:T(8,128)(2,1)S(1)}, u32[]{:S(2)}, u32[]{:S(2)}) collective-permute-start(bf16[2,128,1024]{2,1,0:T(8,128)(2,1)S(1)} %get-tuple-element.68), channel_id=1, source_target_pairs={{0,28},{1,29},{2,30},{3,31},{4,0},{5,1},{6,2},{7,3},{8,4},{9,5},{1... | collective-permute-start | bytes 1572872 | tf_op jit(solution)/shard_map/ppermute | solution.py:31
  99.0 31.5 %collective-permute-start.18 = (bf16[2048,1024]{1,0:T(8,128)(2,1)}, bf16[2048,1024]{1,0:T(8,128)(2,1)}, u32[]{:S(2)}, u32[]{:S(2)}) collective-permute-start(bf16[2048,1024]{1,0:T(8,128)(2,1)} %bitcast.123), channel_id=1, source_target_pairs={{0,1},{1,0},{2,3},{3,2},{4,5},{5,4},{6,7},{7,6},{8,9},{9,8},{10,11... | collective-permute-start | bytes 12582920 | tf_op jit(solution)/shard_map/ppermute | solution.py:31
  101.4 53.7 %collective-permute-start.19 = (bf16[3072,256]{1,0:T(8,128)(2,1)}, bf16[3072,256]{1,0:T(8,128)(2,1)}, u32[]{:S(2)}, u32[]{:S(2)}) collective-permute-start(bf16[3072,256]{1,0:T(8,128)(2,1)} %slice_bitcast_fusion.1), channel_id=1, source_target_pairs={{0,224},{1,225},{2,226},{3,227},{4,228},{5,229},{6,230},{7,231},{8... | collective-permute-start | bytes 4718600 | tf_op jit(solution)/shard_map/ppermute | solution.py:31
  107.7 17.7 %collective-permute-start.13 = (bf16[2,128,1024]{2,1,0:T(8,128)(2,1)S(1)}, bf16[2,128,1024]{2,1,0:T(8,128)(2,1)S(1)}, u32[]{:S(2)}, u32[]{:S(2)}) collective-permute-start(bf16[2,128,1024]{2,1,0:T(8,128)(2,1)S(1)} %get-tuple-element.67), channel_id=1, source_target_pairs={{0,4},{1,5},{2,6},{3,7},{4,8},{5,9},{6,10},{7,11},{8,12},{9,13},{1... | collective-permute-start | bytes 1572872 | tf_op jit(solution)/shard_map/ppermute | solution.py:31
  109.4 15.9 %collective-permute-start.14 = (bf16[2,128,1024]{2,1,0:T(8,128)(2,1)S(1)}, bf16[2,128,1024]{2,1,0:T(8,128)(2,1)S(1)}, u32[]{:S(2)}, u32[]{:S(2)}) collective-permute-start(bf16[2,128,1024]{2,1,0:T(8,128)(2,1)S(1)} %get-tuple-element.66), channel_id=1, source_target_pairs={{0,28},{1,29},{2,30},{3,31},{4,0},{5,1},{6,2},{7,3},{8,4},{9,5},{1... | collective-permute-start | bytes 1572872 | tf_op jit(solution)/shard_map/ppermute | solution.py:31
  115.3 15.2 %copy-start.7 = (bf16[16,1,128,256]{3,2,1,0:T(8,128)(2,1)}, bf16[16,1,128,256]{3,2,1,0:T(8,128)(2,1)S(1)}, u32[]{:S(2)}) copy-start(bf16[16,1,128,256]{3,2,1,0:T(8,128)(2,1)S(1)} %get-tuple-element.73) | copy-start | bytes 3145732
  115.3 15.2 %copy-start.9 = (bf16[16,1,128,256]{3,2,1,0:T(8,128)(2,1)}, bf16[16,1,128,256]{3,2,1,0:T(8,128)(2,1)S(1)}, u32[]{:S(2)}) copy-start(bf16[16,1,128,256]{3,2,1,0:T(8,128)(2,1)S(1)} %get-tuple-element.72) | copy-start | bytes 3145732
  127.8 27.4 %collective-permute-start.15 = (bf16[2,128,1024]{2,1,0:T(8,128)(2,1)}, bf16[2,128,1024]{2,1,0:T(8,128)(2,1)}, u32[]{:S(2)}, u32[]{:S(2)}) collective-permute-start(bf16[2,128,1024]{2,1,0:T(8,128)(2,1)} %get-tuple-element.65), channel_id=1, source_target_pairs={{0,4},{1,5},{2,6},{3,7},{4,8},{5,9},{6,10},{7,11},{8,12},{9,13},{1... | collective-permute-start | bytes 1572872 | tf_op jit(solution)/shard_map/ppermute | solution.py:31
  127.8 27.4 %collective-permute-start.16 = (bf16[2,128,1024]{2,1,0:T(8,128)(2,1)}, bf16[2,128,1024]{2,1,0:T(8,128)(2,1)}, u32[]{:S(2)}, u32[]{:S(2)}) collective-permute-start(bf16[2,128,1024]{2,1,0:T(8,128)(2,1)} %get-tuple-element.64), channel_id=1, source_target_pairs={{0,28},{1,29},{2,30},{3,31},{4,0},{5,1},{6,2},{7,3},{8,4},{9,5},{1... | collective-permute-start | bytes 1572872 | tf_op jit(solution)/shard_map/ppermute | solution.py:31
  136.8 22.3 %all-to-all-start.1 = ((bf16[32,32,128]{2,1,0:T(8,128)(2,1)}), bf16[32,32,128]{2,1,0:T(8,128)(2,1)S(1)}, u32[]{:S(2)}, u32[]{:S(2)}) async-start(bf16[32,32,128]{2,1,0:T(8,128)(2,1)} %broadcast_in_dim.83), calls=%async_computation.1 | async-start | bytes 524288 | tf_op jit(solution)/shard_map/all_to_all | solution.py:281
  146.2 9.0 %collective-permute-start.17 = (f32[2,128]{1,0:T(2,128)S(1)}, f32[2,128]{1,0:T(2,128)S(1)}, u32[]{:S(2)}, u32[]{:S(2)}) collective-permute-start(f32[2,128]{1,0:T(2,128)S(1)} %slice.35), channel_id=1, source_target_pairs={{0,2},{1,3},{2,0},{3,1},{4,6},{5,7},{6,4},{7,5},{8,10},{9,11},{10,... | collective-permute-start | bytes 3080 | tf_op jit(solution)/shard_map/ppermute | solution.py:31
  161.0 14.0 %collective-permute-start.21 = (bf16[128,1024]{1,0:T(8,128)(2,1)S(1)}, bf16[128,1024]{1,0:T(8,128)(2,1)S(1)}, u32[]{:S(2)}, u32[]{:S(2)}) collective-permute-start(bf16[128,1024]{1,0:T(8,128)(2,1)S(1)} %get-tuple-element.75), channel_id=1, source_target_pairs={{0,34},{1,35},{2,32},{3,33},{4,38},{5,39},{6,36},{7,37},{8,42},{9,... | collective-permute-start | bytes 786440 | tf_op jit(solution)/shard_map/ppermute | solution.py:31
  161.0 15.1 %collective-permute-start.20 = (bf16[128,1024]{1,0:T(8,128)(2,1)S(1)}, bf16[128,1024]{1,0:T(8,128)(2,1)S(1)}, u32[]{:S(2)}, u32[]{:S(2)}) collective-permute-start(bf16[128,1024]{1,0:T(8,128)(2,1)S(1)} %get-tuple-element.74), channel_id=1, source_target_pairs={{0,32},{1,33},{2,34},{3,35},{4,36},{5,37},{6,38},{7,39},{8,40},{9,... | collective-permute-start | bytes 786440 | tf_op jit(solution)/shard_map/ppermute | solution.py:31
  165.0 6.1 %copy-start.8 = (bf16[16,1,128,256]{3,2,1,0:T(8,128)(2,1)S(1)}, bf16[16,1,128,256]{3,2,1,0:T(8,128)(2,1)}, u32[]{:S(2)}) copy-start(bf16[16,1,128,256]{3,2,1,0:T(8,128)(2,1)} %copy-done.7) | copy-start | bytes 3145732
  (6 other events, 16.9 us)
Sparse Core Ops, SparseCore 0:
  18.2 68.7 all-gather.1

commit v6 on v5

--- a/solution.py
+++ b/solution.py
@@ -17,6 +17,7 @@
 LANE = WIDTH // N_T
 KEYS = 1024
 PACK = LANE + 16
+ORDER = 4
 CUT = 3 * TOK // 4
 SPLIT = TOK // 4
 AXES = ("section", "ts")
@@ -156,6 +157,29 @@
     )(place, fresh, rows_other, packed_mine, packed_other)
 
 
+def order_kernel(place, mine, other, gain, out):
+    first = place[0] == 0
+    token = lax.broadcasted_iota(jnp.int32, (ORDER, OWN, LANE), 0) * 2 * OWN
+    token = token + lax.broadcasted_iota(jnp.int32, (ORDER, OWN, LANE), 1)
+    token = token + pl.program_id(0) * ORDER * 2 * OWN
+    left, right = mine[...] * gain[...], other[...] * gain[...]
+    out[:, 0] = jnp.where(token < place[1], jnp.where(first, left, right), 0)
+    out[:, 1] = jnp.where(token + OWN < place[1], jnp.where(first, right, left), 0)
+
+
+def order(place, mine, other, gain):
+    half = pl.BlockSpec((ORDER, OWN, LANE), lambda i, place: (i, 0, 0))
+    return call(
+        order_kernel,
+        (N_T // 2 // ORDER,),
+        [half, half, pl.BlockSpec((1, LANE), lambda i, place: (0, 0))],
+        pl.BlockSpec((ORDER, 2, OWN, LANE), lambda i, place: (i, 0, 0, 0)),
+        jax.ShapeDtypeStruct((N_T // 2, 2, OWN, LANE), F32),
+        200 * TOK * LANE * KEYS,
+        8 * TOK * LANE,
+    )(place, mine, other, gain)
+
+
 def shards(upstream, stashed, returning, key_cotangent, key_weight, norm_gain, lengths):
     lane = lax.axis_index("ts")
     core = lane % 2
@@ -197,114 +221,111 @@
         lax.dynamic_index_in_dim(rows_other, 1 - core, 1, keepdims=False), to_other_core
     )
 
-    fresh_wide = fresh.astype(F32)
-    saved_wide = saved.astype(F32)
-    fresh_part = jnp.sum(fresh_wide * fresh_wide, axis=1).reshape(N_Z, 2, 2, OWN)
-    saved_part = jnp.sum(saved_wide * saved_wide, axis=1).reshape(1, N_T, OWN)
-    squares = jnp.concatenate(
-        [
-            fresh_part.transpose(0, 2, 1, 3).reshape(N_T // 2, 2, OWN).astype(BF),
-            jnp.broadcast_to(saved_part.astype(BF), (N_T // 2, N_T, OWN)),
-        ],
-        axis=1,
-    )
-    halves = [[q * 4 + h * 2 + c for q in range(N_Z) for c in range(2)] for h in range(2)]
-    squares = lax.all_to_all(
-        after(squares, packed), "ts", 0, 0, axis_index_groups=halves, tiled=True
-    )
-    squares_raw = squares
-    squares = jnp.sum(squares.astype(F32), axis=0)
-    older_sq = [move(squares[2:], to_mirror), move(squares[2:], to_mirror_other_half)]
-    fresh_other = move(after(squares[:2], *older_sq), to_other_half)
-
-    older_second = move(after(saved[CUT:], *older_sq), to_mirror)
-
-    early = move(after(returning[0, :SPLIT], *older_sq), to_previous)
-    late = returning[0, SPLIT:]
-
     packed_other = move(packed, to_other_core)
     partial = forward(place, rows, rows_other, packed, packed_other)
 
     def block(distance):
         return lax.dynamic_slice_in_dim(partial, ((z + distance) % N_Z) * 2, 2, 0)
 
-    up = move(block(4), z_up, (0,))
-    down = move(block(4), z_down, (1,))
-    base = jnp.zeros((N_T // 2, 2, OWN, LANE), F32)
-    up, down, base, late = lax.optimization_barrier(
-        (up, down, base, late, squares_raw, older_first, *older_sq)
+    far = block(4)
+
+    older_second = move(after(saved[CUT:], partial), to_mirror)
+    early = move(after(returning[0, :SPLIT], older_first), to_previous)
+
+    up = move(far, z_up, (0,))
+    down = move(far, z_down, (1,))
+    fresh_wide = fresh.astype(F32)
+    fresh_part = jnp.sum(fresh_wide * fresh_wide, axis=1).astype(BF)
+    up, down, late, fresh_part = lax.optimization_barrier(
+        (up, down, returning[0, SPLIT:], fresh_part, older_first)
     )[:4]
-    late = move(after(late, early), to_previous)
-    up = add(block(3), up)
-    down = add(block(-3), down)
-    up = move(up, z_up)
-    down = move(down, z_down)
+    late = move(after(late, older_first), to_previous)
+    up = move(add(block(3), up), z_up)
+    down = move(add(block(-3), down), z_down)
     up, down, cot_mine = lax.optimization_barrier((up, down, cot_mine, older_second, early))[:3]
 
     cots = [cot_mine, move(cot_mine, to_other_core)]
-    raw = [
-        lax.dot_general(cot, weights, (((1,), (1,)), ((), ())), preferred_element_type=F32)
-        for cot in cots
-    ]
+    def times_weights(cot):
+        return lax.dot_general(cot, weights, (((1,), (1,)), ((), ())), preferred_element_type=F32)
+
+    raw = [times_weights(cots[0])]
     up = add(block(2), up)
     down = add(block(-2), down)
-    older_first, older_second, *older_sq = lax.optimization_barrier(
-        (older_first, older_second, *older_sq, up, down)
-    )[:4]
+    older_first, older_second = lax.optimization_barrier((older_first, older_second, up, down))[:2]
     up = move(up, z_up)
     down = move(down, z_down)
     up, down, raw[0] = lax.optimization_barrier((up, down, raw[0]))
     up = add(block(1), up)
     down = add(block(-1), down)
+    cots[1] = after(cots[1], up, down)
+    raw.append(times_weights(cots[1]))
     up = move(up, z_up)
     down = move(down, z_down)
+
     older = jnp.concatenate([older_first, older_second], axis=0)
-    older_rate = lax.rsqrt((older_sq[0] + older_sq[1]) / WIDTH + eps).reshape(TOK)
-    live = (jnp.arange(TOK, dtype=jnp.int32) < lengths[0]).astype(F32)
-    scales = by_core(live * older_rate)
-    grads = []
-    curves = []
-    lefts = []
-    gain_grad = jnp.zeros((LANE,), F32)
-    for cot, product, rows, scale in zip(cots, raw, by_core(older), scales):
-        wide = rows.astype(F32)
-        grad = scale[:, None] * product
-        grads.append(grad)
-        curves.append(jnp.sum(grad * (wide * gain).astype(BF).astype(F32), axis=1))
-        gain_grad = gain_grad + jnp.sum(grad * wide, axis=0)
-        lefts.append(wide * gain * scale[:, None])
-
+    wide = older.astype(F32)
+    part_sq = jnp.sum(wide * wide, axis=1).astype(BF)
+    part_rate = lax.rsqrt(part_sq.astype(F32) / LANE + eps)
     mine = (jnp.arange(2) == core)[None, :, None]
-    curve = [part.reshape(N_T // 2, 1, OWN) for part in curves]
-    curve = jnp.where(mine, curve[0], curve[1])
-    curve = jnp.broadcast_to(curve.reshape(1, N_T, OWN).astype(BF), (N_T, N_T, OWN))
-    curve = lax.all_to_all(curve, "ts", 0, 0, tiled=True)
-    up, down, fresh_other = lax.optimization_barrier((up, down, fresh_other, curve, late))[:3]
-    fresh_rate = lax.rsqrt((squares[:2] + fresh_other) / WIDTH + eps)
-    curve = jnp.sum(curve.astype(F32), axis=0).reshape(TOK)
-    pull = older_rate * older_rate / WIDTH * curve
+    curve = [
+        jnp.sum(
+            (scale[:, None] * product) * (rows.astype(F32) * gain).astype(BF).astype(F32), axis=1
+        ).reshape(N_T // 2, 1, OWN)
+        for product, rows, scale in zip(raw, by_core(older), by_core(part_rate))
+    ]
+    curve = jnp.where(mine, curve[0], curve[1]).reshape(1, N_T, OWN).astype(BF)
+    fresh_part = fresh_part.reshape(N_Z, 2, 2, OWN)
+    sent = jnp.concatenate(
+        [
+            jnp.broadcast_to(curve, (N_T, N_T, OWN)),
+            jnp.broadcast_to(part_sq.reshape(1, N_T, OWN), (N_T, N_T, OWN)),
+            fresh_part.reshape(N_T, 1, OWN),
+            fresh_part[:, ::-1].reshape(N_T, 1, OWN),
+        ],
+        axis=1,
+    )
+    ordered = order(
+        jnp.concatenate([place, lengths]),
+        *[product.reshape(N_T // 2, OWN, LANE) for product in raw],
+        norm_gain,
+    )
+    got = lax.all_to_all(sent, "ts", 0, 0, tiled=True)
+    up, down = lax.optimization_barrier((up, down, got, late))[:2]
+    got, ordered = lax.optimization_barrier((got, ordered))
+    got = got.astype(F32)
+    live = (jnp.arange(TOK, dtype=jnp.int32) < lengths[0]).reshape(N_T, OWN)
+    older_rate = lax.rsqrt(jnp.sum(got[:, N_T : 2 * N_T], axis=0) / WIDTH + eps)
+    curve = jnp.sum(
+        got[:, :N_T] * (older_rate * jnp.sqrt(got[:, N_T : 2 * N_T] / LANE + eps)), axis=0
+    )
+    pull = jnp.where(live, older_rate * older_rate / WIDTH * curve, 0).reshape(TOK)
+    scale = jnp.where(live, older_rate, 0).reshape(TOK)
+    fresh_rate = lax.rsqrt(jnp.sum(got[:, 2 * N_T :], axis=0) / WIDTH + eps)
 
     summed = block(0).astype(F32) + up.astype(F32) + down.astype(F32)
-    straight = (pick(summed, half) * pick(fresh_rate, half)[:, None]).astype(BF)
-    crossed = (pick(summed, 1 - half) * pick(fresh_rate, 1 - half)[:, None]).astype(BF)
-    *cots, pull = lax.optimization_barrier((*cots, pull, straight, crossed))[:3]
+    straight = (pick(summed, half) * fresh_rate[0][:, None]).astype(BF)
+    crossed = (pick(summed, 1 - half) * fresh_rate[1][:, None]).astype(BF)
+    *cots, pull, scale = lax.optimization_barrier((*cots, pull, scale, straight, crossed))[:4]
     straight = move(straight, to_next)
     crossed = move(crossed, to_next_other_half)
     new_keys = (straight.astype(F32) + crossed.astype(F32)).astype(BF)
 
     weight_total = sum(
         lax.dot_general(
-            left.astype(BF), cot, (((0,), (0,)), ((), ())), preferred_element_type=F32
+            (rows.astype(F32) * gain * row_scale[:, None]).astype(BF),
+            cot,
+            (((0,), (0,)), ((), ())),
+            preferred_element_type=F32,
         )
-        for left, cot in zip(lefts, cots)
-    )
-    for index, grad in zip((core, 1 - core), grads):
-        base = lax.dynamic_update_index_in_dim(
-            base, (gain * grad).reshape(N_T // 2, OWN, LANE), index, 1
-        )
-    base = base.reshape(TOK, LANE)
+        for cot, rows, row_scale in zip(cots, by_core(older), by_core(scale))
+    )
+    gain_grad = jnp.sum(weights.astype(F32) * weight_total, axis=1) / gain
     downstream = jnp.concatenate([early, late], axis=0)
-    total = downstream.astype(F32) + base - pull[:, None] * older.astype(F32)
+    total = (
+        downstream.astype(F32)
+        + scale[:, None] * ordered.reshape(TOK, LANE)
+        - pull[:, None] * wide
+    )
     return (
         new_keys[None],
         total.astype(BF)[None],

time: 184 us -> 192 us (1.043); the launches traced: 184 us -> 189 us
  waiting for transfers between devices: 44.4 us -> 65.9 us
  starting transfers between devices: 66.8 us -> 53.9 us
  other arithmetic: 22.6 us -> 20.3 us
  local copies, waits for them, and re-layouts: 16.8 us -> 14.7 us
    ppermute x22 -> x19, waiting for transfers between devices: 40.5 us -> 52 us  [move(): return lax.ppermute(value, AXES, pairs)]
    all_to_all x2 -> x1, starting transfers between devices: 17.9 us -> 7.68 us  [shards(): got = lax.all_to_all(sent, 'ts', 0, 0, tiled=True)]
    all_to_all x2 -> x1, waiting for transfers between devices: 3.87 us -> 13.8 us  [shards(): got = lax.all_to_all(sent, 'ts', 0, 0, tiled=True)]
    unnamed x26 -> x41, local copies, waits for them, and re-layouts: 3.14 us -> 9.75 us
    broadcast_in_dim x7 -> x6, local copies, waits for them, and re-layouts: 3.31 us -> 0.19 us  [the longest x4 0.12 us: shards(): curve = jnp.where(mine, curve[0], curve[1]).reshape(1, N_T, OWN).astype(BF)]
    dynamic_update_slice x2 -> x0, local copies, waits for them, and re-layouts: 3.01 us -> none  [shards(): lax.dynamic_update_index_in_dim(base, (gain * grad).reshape(N_T // 2, OWN...]
    ppermute x22 -> x19, starting transfers between devices: 48.8 us -> 46.1 us  [move(): return lax.ppermute(value, AXES, pairs)]
  transfers between devices with their start and end apart: 25 -> 21, of which waited for: 10 -> 9; matrix products, arithmetic and copies ran while one was open for 24% -> 18% of each run, Pallas kernels for 3% -> 3%
where the time goes in v6:
time: 192 us; the launch traced here: 189 us
  waiting for transfers between devices  65.9 us (34%)
  starting transfers between devices  53.9 us (28%)
  other arithmetic  20.3 us (11%)
  between operations  15.2 us (8%)
  local copies, waits for them, and re-layouts  14.7 us (8%)
  matrix products  12.5 us (7%)
  Pallas kernels  6.51 us (3%)
    ppermute x19, waiting for transfers between devices, move(): return lax.ppermute(value, AXES, pairs)  52 us
    ppermute x19, starting transfers between devices, move(): return lax.ppermute(value, AXES, pairs)  46.1 us
    all_to_all x1, waiting for transfers between devices, shards(): got = lax.all_to_all(sent, 'ts', 0, 0, tiled=True)  13.8 us
    unnamed x41, local copies, waits for them, and re-layouts  9.75 us
    all_to_all x1, starting transfers between devices, shards(): got = lax.all_to_all(sent, 'ts', 0, 0, tiled=True)  7.68 us
    convert_element_type x1, other arithmetic, shards(): total.astype(BF)[None]  7.13 us
    dot_general x2, matrix products, times_weights(): lax.dot_general(cot, weights, (((1,), (1,)), ((), ())), preferred_element...  6.58 us
    dot_general x2, matrix products, shards(): lax.dot_general((rows.astype(F32) * gain * row_scale[:, None]).astype(BF)...  5.93 us
  transfers between devices with their start and end apart: 21, of which 9 were waited for; matrix products, arithmetic and copies ran while one was open for 18% of the time, Pallas kernels for 3%

profile of v6, /device:TPU:1, one launch (start us, length us, event | category | flops | bytes accessed | tf_op | source)
XLA Modules:
  0.0 188.9 jit_solution(18033476707750883305)
XLA Ops:
  7.2 3.7 %collective-permute-start.5 = (bf16[128,1024]{1,0:T(8,128)(2,1)}, bf16[128,1024]{1,0:T(8,128)(2,1)S(1)}, u32[]{:S(2)}, u32[]{:S(2)}) collective-permute-start(bf16[128,1024]{1,0:T(8,128)(2,1)} %bitcast.114), channel_id=1, source_target_pairs={{0,2},{1,3},{2,0},{3,1},{4,6},{5,7},{6,4},{7,5},{8,10},{9,11},{10,... | collective-permute-start | bytes 786440 | tf_op jit(solution)/shard_map/ppermute | solution.py:32
  10.9 5.3 %collective-permute-done.5 = bf16[128,1024]{1,0:T(8,128)(2,1)S(1)} collective-permute-done((bf16[128,1024]{1,0:T(8,128)(2,1)}, bf16[128,1024]{1,0:T(8,128)(2,1)S(1)}, u32[]{:S(2)}, u32[]{:S(2)}) %collective-permute-start.5) | collective-permute-done | bytes 262176 | tf_op jit(solution)/shard_map/ppermute | solution.py:32
  19.0 4.5 %collective-permute-start.1 = (bf16[272,1024]{1,0:T(8,128)(2,1)}, bf16[272,1024]{1,0:T(8,128)(2,1)}, u32[]{:S(2)}, u32[]{:S(2)}) collective-permute-start(bf16[272,1024]{1,0:T(8,128)(2,1)} %shard_map.102), channel_id=1, source_target_pairs={{0,224},{1,225},{2,226},{3,227},{4,228},{5,229},{6,230},{7,231},{8... | collective-permute-start | bytes 1671176 | tf_op jit(solution)/shard_map/ppermute | solution.py:32
  24.5 1.8 collective-permute-start
  27.6 6.6 %collective-permute-done.1.packed_mine = bf16[272,1024]{1,0:T(8,128)(2,1)} collective-permute-done((bf16[272,1024]{1,0:T(8,128)(2,1)}, bf16[272,1024]{1,0:T(8,128)(2,1)}, u32[]{:S(2)}, u32[]{:S(2)}) %collective-permute-start.1) | collective-permute-done | bytes 557088 | tf_op jit(solution)/shard_map/ppermute | solution.py:32
  34.2 2.5 %collective-permute-start.2 = (bf16[272,1024]{1,0:T(8,128)(2,1)}, bf16[272,1024]{1,0:T(8,128)(2,1)}, u32[]{:S(2)}, u32[]{:S(2)}) collective-permute-start(bf16[272,1024]{1,0:T(8,128)(2,1)} %collective-permute-done.1.packed_mine), channel_id=1, source_target_pairs={{0,1},{1,0},{2,3},{3,2},{4,5},{5,4},{6,7},{7,6},{8,9},{9,8},{10,11... | collective-permute-start | bytes 1671176 | tf_op jit(solution)/shard_map/ppermute | solution.py:32
  37.5 4.3 %collective-permute-start.6 = (bf16[3072,256]{1,0:T(8,128)(2,1)}, bf16[3072,256]{1,0:T(8,128)(2,1)}, u32[]{:S(2)}, u32[]{:S(2)}) collective-permute-start(bf16[3072,256]{1,0:T(8,128)(2,1)} %slice_bitcast_fusion), channel_id=1, source_target_pairs={{0,224},{1,225},{2,226},{3,227},{4,228},{5,229},{6,230},{7,231},{8... | collective-permute-start | bytes 4718600 | tf_op jit(solution)/shard_map/ppermute | solution.py:32
  43.4 4.3 %shard_map.103 = bf16[16,128,1024]{2,1,0:T(8,128)(2,1)S(1)} custom-call(s32[1]{0:T(128)} %bitcast.place, bf16[16,2,128,256]{3,2,1,0:T(8,128)(2,1)S(1)} %bitcast.102, bf16[16,128,256]{2,1,0:T(8,128)(2,1)S(1)} %collective-permute-done.rows_other, bf16[272,1024]{1,0:T(8,128)(2,1)} %collective-permute-done.1.packed_mine, ...), custom_call_target="tpu_custom_call" | custom-call | flops 2147483648 | bytes 7340032 | tf_op jit(solution)/shard_map/pallas_call | solution.py:143
  47.8 7.6 %collective-permute-start.4 = (bf16[2,128,1024]{2,1,0:T(8,128)(2,1)S(1)}, bf16[2,128,1024]{2,1,0:T(8,128)(2,1)S(1)}, u32[]{:S(2)}, u32[]{:S(2)}) collective-permute-start(bf16[2,128,1024]{2,1,0:T(8,128)(2,1)S(1)} %constant_dynamic-slice_fusion.6), channel_id=1, source_target_pairs={{1,29},{3,31},{5,1},{7,3},{9,5},{11,7},{13,9},{15,11},{17,13},{19,... | collective-permute-start | bytes 1572872 | tf_op jit(solution)/shard_map/ppermute | solution.py:32
  57.5 19.4 %collective-permute-done.6 = bf16[3072,256]{1,0:T(8,128)(2,1)} collective-permute-done((bf16[3072,256]{1,0:T(8,128)(2,1)}, bf16[3072,256]{1,0:T(8,128)(2,1)}, u32[]{:S(2)}, u32[]{:S(2)}) %collective-permute-start.6) | collective-permute-done | bytes 1572896 | tf_op jit(solution)/shard_map/ppermute | solution.py:32
  76.9 3.4 %collective-permute-start.10 = (bf16[1024,256]{1,0:T(8,128)(2,1)S(1)}, bf16[1024,256]{1,0:T(8,128)(2,1)}, u32[]{:S(2)}, u32[]{:S(2)}) collective-permute-start(bf16[1024,256]{1,0:T(8,128)(2,1)S(1)} %slice_bitcast_fusion.2), channel_id=1, source_target_pairs={{0,224},{1,225},{2,226},{3,227},{4,228},{5,229},{6,230},{7,231},{8... | collective-permute-start | bytes 1572872 | tf_op jit(solution)/shard_map/ppermute | solution.py:32
  80.7 5.7 %collective-permute-start.8 = (bf16[2,128,1024]{2,1,0:T(8,128)(2,1)S(1)}, bf16[2,128,1024]{2,1,0:T(8,128)(2,1)S(1)}, u32[]{:S(2)}, u32[]{:S(2)}) collective-permute-start(bf16[2,128,1024]{2,1,0:T(8,128)(2,1)S(1)} %get-tuple-element.64), channel_id=1, source_target_pairs={{0,28},{1,29},{2,30},{3,31},{4,0},{5,1},{6,2},{7,3},{8,4},{9,5},{1... | collective-permute-start | bytes 1572872 | tf_op jit(solution)/shard_map/ppermute | solution.py:32
  86.3 1.7 collective-permute-done.9
  88.0 10.3 %collective-permute-done.10 = bf16[1024,256]{1,0:T(8,128)(2,1)} collective-permute-done((bf16[1024,256]{1,0:T(8,128)(2,1)S(1)}, bf16[1024,256]{1,0:T(8,128)(2,1)}, u32[]{:S(2)}, u32[]{:S(2)}) %collective-permute-start.10) | collective-permute-done | bytes 524320 | tf_op jit(solution)/shard_map/ppermute | solution.py:32
  99.2 2.6 %collective-permute-start.15 = (bf16[2048,1024]{1,0:T(8,128)(2,1)}, bf16[2048,1024]{1,0:T(8,128)(2,1)}, u32[]{:S(2)}, u32[]{:S(2)}) collective-permute-start(bf16[2048,1024]{1,0:T(8,128)(2,1)} %bitcast.130), channel_id=1, source_target_pairs={{0,1},{1,0},{2,3},{3,2},{4,5},{5,4},{6,7},{7,6},{8,9},{9,8},{10,11... | collective-permute-start | bytes 12582920 | tf_op jit(solution)/shard_map/ppermute | solution.py:32
  102.8 1.8 collective-permute-start.16
  104.6 1.5 add_convert_fusion.2
  106.1 5.7 %collective-permute-start.12 = (bf16[2,128,1024]{2,1,0:T(8,128)(2,1)S(1)}, bf16[2,128,1024]{2,1,0:T(8,128)(2,1)S(1)}, u32[]{:S(2)}, u32[]{:S(2)}) collective-permute-start(bf16[2,128,1024]{2,1,0:T(8,128)(2,1)S(1)} %get-tuple-element.62), channel_id=1, source_target_pairs={{0,28},{1,29},{2,30},{3,31},{4,0},{5,1},{6,2},{7,3},{8,4},{9,5},{1... | collective-permute-start | bytes 1572872 | tf_op jit(solution)/shard_map/ppermute | solution.py:32
  111.8 1.5 constant_dynamic-update-slice_fusion.1
  114.2 2.1 %copy-done.18 = bf16[16,128,1024]{2,1,0:T(8,128)(2,1)S(1)} copy-done((bf16[16,128,1024]{2,1,0:T(8,128)(2,1)S(1)}, bf16[16,128,1024]{2,1,0:T(8,128)(2,1)}, u32[]{:S(2)}) %copy-start.18) | copy-done | bytes 4194328
  117.9 4.8 %collective-permute-done.12 = bf16[2,128,1024]{2,1,0:T(8,128)(2,1)S(1)} collective-permute-done((bf16[2,128,1024]{2,1,0:T(8,128)(2,1)S(1)}, bf16[2,128,1024]{2,1,0:T(8,128)(2,1)S(1)}, u32[]{:S(2)}, u32[]{:S(2)}) %collective-permute-start.12) | collective-permute-done | bytes 524320 | tf_op jit(solution)/shard_map/ppermute | solution.py:32
  122.7 3.1 %collective-permute-done.11 = bf16[2,128,1024]{2,1,0:T(8,128)(2,1)S(1)} collective-permute-done((bf16[2,128,1024]{2,1,0:T(8,128)(2,1)S(1)}, bf16[2,128,1024]{2,1,0:T(8,128)(2,1)S(1)}, u32[]{:S(2)}, u32[]{:S(2)}) %collective-permute-start.11) | collective-permute-done | bytes 524320 | tf_op jit(solution)/shard_map/ppermute | solution.py:32
  125.8 2.5 %add_convert_fusion = (bf16[2,128,1024]{2,1,0:T(8,128)(2,1)}, bf16[2,128,1024]{2,1,0:T(8,128)(2,1)}) fusion(bf16[2,128,1024]{2,1,0:T(8,128)(2,1)S(1)} %collective-permute-done.12, bf16[16,128,1024]{2,1,0:T(8,128)(2,1)} %copy-done, s32[]{:T(128)S(6)} %select_n.149, bf16[2,128,1024]{2,1,0:T(8,128)(2,1)S(1)} %collective-permute-done.11, s32[]{:T(128)S(6)} %select_n.132), kind=kLoop, calls=%fused_computation.23 | loop fusion | flops 2097152 | bytes 3145736 | tf_op jit(solution)/shard_map/convert_element_type | solution.py:80
  129.7 5.3 %multiply_reduce_fusion.2 = (bf16[2048]{0:T(1024)(128)(2,1)S(1)}, bf16[2048]{0:T(1024)(128)(2,1)S(1)}, f32[2048,256]{1,0:T(8,128)}) fusion(bf16[16,1,128,256]{3,2,1,0:T(8,128)(2,1)S(1)} %get-tuple-element.67, f32[2048]{0:T(1024)S(1)} %bitcast.124, f32[256]{0:T(256)S(1)} %bitcast.105, bf16[16,1,128,256]{3,2,1,0:T(8,128)(2,1)S(1)} %get-tuple-element.66, ...), kind=kOutput, calls=%fused_computation.11 | convolution fusion | flops 1081077760 | bytes 11035648 | tf_op jit(solution)/shard_map/dot_general | solution.py:249
  136.0 7.7 %all-to-all-start = ((bf16[32,66,128]{2,1,0:T(8,128)(2,1)}), bf16[32,66,128]{2,1,0:T(8,128)(2,1)}, u32[]{:S(2)}, u32[]{:S(2)}) async-start(bf16[32,66,128]{2,1,0:T(8,128)(2,1)} %pad_maximum_fusion), calls=%async_computation | async-start | bytes 1179648 | tf_op jit(solution)/shard_map/all_to_all | solution.py:292
  143.7 1.6 copy-done.8
  146.7 1.9 %copy-done.2 = f32[16,2,128,256]{3,2,1,0:T(8,128)} copy-done((f32[16,2,128,256]{3,2,1,0:T(8,128)}, f32[16,2,128,256]{3,2,1,0:T(8,128)S(1)}, u32[]{:S(2)}) %copy-start.2) | copy-done | bytes 4194328
  148.6 13.8 %all-to-all-done = bf16[32,66,128]{2,1,0:T(8,128)(2,1)} async-done(((bf16[32,66,128]{2,1,0:T(8,128)(2,1)}), bf16[32,66,128]{2,1,0:T(8,128)(2,1)}, u32[]{:S(2)}, u32[]{:S(2)}) %all-to-all-start) | async-done | bytes 540704 | tf_op jit(solution)/shard_map/all_to_all | solution.py:292
  163.9 1.8 convert_add_fusion
  166.7 1.4 fusion.6
  169.0 7.1 %subtract_convert_fusion = bf16[1,4096,256]{2,1,0:T(8,128)(2,1)} fusion(f32[1,4096,256]{2,1,0:T(8,128)S(1)} %bitcast.103, bf16[1,3072,256]{2,1,0:T(8,128)(2,1)} %bitcast.37, bf16[1,1024,256]{2,1,0:T(8,128)(2,1)} %bitcast.36, bf16[1,1024,256]{2,1,0:T(8,128)(2,1)S(1)} %bitcast.111, bf16[1,3072,256]{2,1,0:T(8,128)(2,1)} %bitcast.42, ...), kind=kLoop, calls=%fused_computation | loop fusion | flops 13631488 | bytes 10518528 | tf_op jit(solution)/shard_map/convert_element_type | solution.py:331
  176.2 4.6 %multiply_reduce_fusion.4 = (f32[256]{0:T(256)S(1)}, f32[256,1024]{1,0:T(8,128)}) fusion(bf16[1,256,1024]{2,1,0:T(8,128)(2,1)S(1)} %copy-done.6, f32[256,1024]{1,0:T(8,128)S(1)} %fusion.6, bf16[2048,1024]{1,0:T(8,128)(2,1)} %collective-permute-done.15, bf16[2048,256]{1,0:T(8,128)(2,1)S(1)} %bitcast.112, f32[2048]{0:T(1024)S(1)} %bitcast.125, ...), kind=kOutput, calls=%fused_computation.17 | convolution fusion | flops 1076887296 | bytes 7874560 | tf_op jit(solution)/shard_map/dot_general | solution.py:314
  (103 shorter events, 22.1 us)
Async XLA Ops:
  7.2 10.9 %copy-start.7 = (f32[1,256]{1,0:T(1,128)S(1)}, f32[1,256]{1,0:T(1,128)}, u32[]{:S(2)}) copy-start(f32[1,256]{1,0:T(1,128)} %gain.3) | copy-start | bytes 3076
  7.2 10.9 %copy-start.4 = (bf16[1,256,1024]{2,1,0:T(8,128)(2,1)S(1)}, bf16[1,256,1024]{2,1,0:T(8,128)(2,1)}, u32[]{:S(2)}) copy-start(bf16[1,256,1024]{2,1,0:T(8,128)(2,1)} %param.11) | copy-start | bytes 1572868
  7.2 16.3 %copy-start.1 = (bf16[1,4096,256]{2,1,0:T(8,128)(2,1)S(1)}, bf16[1,4096,256]{2,1,0:T(8,128)(2,1)}, u32[]{:S(2)}) copy-start(bf16[1,4096,256]{2,1,0:T(8,128)(2,1)} %param.7) | copy-start | bytes 6291460
  7.2 92.0 %all-gather.2.cloned.1.call-start = ((), (), s32[]{:S(2)}) async-start(), calls=%async_computation.1 | async-start | bytes 4718592 | tf_op jit(solution)/shard_map/all_gather | solution.py:213
  7.2 8.9 %collective-permute-start.5 = (bf16[128,1024]{1,0:T(8,128)(2,1)}, bf16[128,1024]{1,0:T(8,128)(2,1)S(1)}, u32[]{:S(2)}, u32[]{:S(2)}) collective-permute-start(bf16[128,1024]{1,0:T(8,128)(2,1)} %bitcast.114), channel_id=1, source_target_pairs={{0,2},{1,3},{2,0},{3,1},{4,6},{5,7},{6,4},{7,5},{8,10},{9,11},{10,... | collective-permute-start | bytes 786440 | tf_op jit(solution)/shard_map/ppermute | solution.py:32
  19.0 15.2 %collective-permute-start.1 = (bf16[272,1024]{1,0:T(8,128)(2,1)}, bf16[272,1024]{1,0:T(8,128)(2,1)}, u32[]{:S(2)}, u32[]{:S(2)}) collective-permute-start(bf16[272,1024]{1,0:T(8,128)(2,1)} %shard_map.102), channel_id=1, source_target_pairs={{0,224},{1,225},{2,226},{3,227},{4,228},{5,229},{6,230},{7,231},{8... | collective-permute-start | bytes 1671176 | tf_op jit(solution)/shard_map/ppermute | solution.py:32
  24.5 18.9 %collective-permute-start = (bf16[16,128,256]{2,1,0:T(8,128)(2,1)}, bf16[16,128,256]{2,1,0:T(8,128)(2,1)S(1)}, u32[]{:S(2)}, u32[]{:S(2)}) collective-permute-start(bf16[16,128,256]{2,1,0:T(8,128)(2,1)} %dynamic-slice_bitcast_fusion), channel_id=1, source_target_pairs={{0,1},{1,0},{2,3},{3,2},{4,5},{5,4},{6,7},{7,6},{8,9},{9,8},{10,11... | collective-permute-start | bytes 3145736 | tf_op jit(solution)/shard_map/ppermute | solution.py:32
  34.2 9.3 %collective-permute-start.2 = (bf16[272,1024]{1,0:T(8,128)(2,1)}, bf16[272,1024]{1,0:T(8,128)(2,1)}, u32[]{:S(2)}, u32[]{:S(2)}) collective-permute-start(bf16[272,1024]{1,0:T(8,128)(2,1)} %collective-permute-done.1.packed_mine), channel_id=1, source_target_pairs={{0,1},{1,0},{2,3},{3,2},{4,5},{5,4},{6,7},{7,6},{8,9},{9,8},{10,11... | collective-permute-start | bytes 1671176 | tf_op jit(solution)/shard_map/ppermute | solution.py:32
  37.5 39.4 %collective-permute-start.6 = (bf16[3072,256]{1,0:T(8,128)(2,1)}, bf16[3072,256]{1,0:T(8,128)(2,1)}, u32[]{:S(2)}, u32[]{:S(2)}) collective-permute-start(bf16[3072,256]{1,0:T(8,128)(2,1)} %slice_bitcast_fusion), channel_id=1, source_target_pairs={{0,224},{1,225},{2,226},{3,227},{4,228},{5,229},{6,230},{7,231},{8... | collective-permute-start | bytes 4718600 | tf_op jit(solution)/shard_map/ppermute | solution.py:32
  47.8 32.5 %copy-start = (bf16[16,128,1024]{2,1,0:T(8,128)(2,1)}, bf16[16,128,1024]{2,1,0:T(8,128)(2,1)S(1)}, u32[]{:S(2)}) copy-start(bf16[16,128,1024]{2,1,0:T(8,128)(2,1)S(1)} %shard_map.103) | copy-start | bytes 12582916
  47.8 9.7 %copy-start.17 = (bf16[1024,256]{1,0:T(8,128)(2,1)S(1)}, bf16[1024,256]{1,0:T(8,128)(2,1)}, u32[]{:S(2)}) copy-start(bf16[1024,256]{1,0:T(8,128)(2,1)} %slice_bitcast_fusion.3) | copy-start | bytes 1572868
  47.8 32.4 %collective-permute-start.4 = (bf16[2,128,1024]{2,1,0:T(8,128)(2,1)S(1)}, bf16[2,128,1024]{2,1,0:T(8,128)(2,1)S(1)}, u32[]{:S(2)}, u32[]{:S(2)}) collective-permute-start(bf16[2,128,1024]{2,1,0:T(8,128)(2,1)S(1)} %constant_dynamic-slice_fusion.6), channel_id=1, source_target_pairs={{1,29},{3,31},{5,1},{7,3},{9,5},{11,7},{13,9},{15,11},{17,13},{19,... | collective-permute-start | bytes 1572872 | tf_op jit(solution)/shard_map/ppermute | solution.py:32
  55.5 24.8 %collective-permute-start.3 = (bf16[2,128,1024]{2,1,0:T(8,128)(2,1)S(1)}, bf16[2,128,1024]{2,1,0:T(8,128)(2,1)S(1)}, u32[]{:S(2)}, u32[]{:S(2)}) collective-permute-start(bf16[2,128,1024]{2,1,0:T(8,128)(2,1)S(1)} %constant_dynamic-slice_fusion.6), channel_id=1, source_target_pairs={{0,4},{2,6},{4,8},{6,10},{8,12},{10,14},{12,16},{14,18},{16,20},{1... | collective-permute-start | bytes 1572872 | tf_op jit(solution)/shard_map/ppermute | solution.py:32
  57.5 30.5 %collective-permute-start.9 = (bf16[1024,256]{1,0:T(8,128)(2,1)S(1)}, bf16[1024,256]{1,0:T(8,128)(2,1)S(1)}, u32[]{:S(2)}, u32[]{:S(2)}) collective-permute-start(bf16[1024,256]{1,0:T(8,128)(2,1)S(1)} %copy-done.17), channel_id=1, source_target_pairs={{0,224},{1,225},{2,226},{3,227},{4,228},{5,229},{6,230},{7,231},{8... | collective-permute-start | bytes 1572872 | tf_op jit(solution)/shard_map/ppermute | solution.py:32
  76.9 21.4 %collective-permute-start.10 = (bf16[1024,256]{1,0:T(8,128)(2,1)S(1)}, bf16[1024,256]{1,0:T(8,128)(2,1)}, u32[]{:S(2)}, u32[]{:S(2)}) collective-permute-start(bf16[1024,256]{1,0:T(8,128)(2,1)S(1)} %slice_bitcast_fusion.2), channel_id=1, source_target_pairs={{0,224},{1,225},{2,226},{3,227},{4,228},{5,229},{6,230},{7,231},{8... | collective-permute-start | bytes 1572872 | tf_op jit(solution)/shard_map/ppermute | solution.py:32
  80.7 17.6 %collective-permute-start.8 = (bf16[2,128,1024]{2,1,0:T(8,128)(2,1)S(1)}, bf16[2,128,1024]{2,1,0:T(8,128)(2,1)S(1)}, u32[]{:S(2)}, u32[]{:S(2)}) collective-permute-start(bf16[2,128,1024]{2,1,0:T(8,128)(2,1)S(1)} %get-tuple-element.64), channel_id=1, source_target_pairs={{0,28},{1,29},{2,30},{3,31},{4,0},{5,1},{6,2},{7,3},{8,4},{9,5},{1... | collective-permute-start | bytes 1572872 | tf_op jit(solution)/shard_map/ppermute | solution.py:32
  86.3 12.9 %collective-permute-start.7 = (bf16[2,128,1024]{2,1,0:T(8,128)(2,1)S(1)}, bf16[2,128,1024]{2,1,0:T(8,128)(2,1)S(1)}, u32[]{:S(2)}, u32[]{:S(2)}) collective-permute-start(bf16[2,128,1024]{2,1,0:T(8,128)(2,1)S(1)} %get-tuple-element.65), channel_id=1, source_target_pairs={{0,4},{1,5},{2,6},{3,7},{4,8},{5,9},{6,10},{7,11},{8,12},{9,13},{1... | collective-permute-start | bytes 1572872 | tf_op jit(solution)/shard_map/ppermute | solution.py:32
  88.0 25.3 %copy-start.9 = (bf16[1024,256]{1,0:T(8,128)(2,1)}, bf16[1024,256]{1,0:T(8,128)(2,1)S(1)}, u32[]{:S(2)}) copy-start(bf16[1024,256]{1,0:T(8,128)(2,1)S(1)} %collective-permute-done.9) | copy-start | bytes 1572868
  99.2 30.5 %collective-permute-start.15 = (bf16[2048,1024]{1,0:T(8,128)(2,1)}, bf16[2048,1024]{1,0:T(8,128)(2,1)}, u32[]{:S(2)}, u32[]{:S(2)}) collective-permute-start(bf16[2048,1024]{1,0:T(8,128)(2,1)} %bitcast.130), channel_id=1, source_target_pairs={{0,1},{1,0},{2,3},{3,2},{4,5},{5,4},{6,7},{7,6},{8,9},{9,8},{10,11... | collective-permute-start | bytes 12582920 | tf_op jit(solution)/shard_map/ppermute | solution.py:32
  102.8 60.8 %collective-permute-start.16 = (bf16[3072,256]{1,0:T(8,128)(2,1)}, bf16[3072,256]{1,0:T(8,128)(2,1)}, u32[]{:S(2)}, u32[]{:S(2)}) collective-permute-start(bf16[3072,256]{1,0:T(8,128)(2,1)} %slice_bitcast_fusion.1), channel_id=1, source_target_pairs={{0,224},{1,225},{2,226},{3,227},{4,228},{5,229},{6,230},{7,231},{8... | collective-permute-start | bytes 4718600 | tf_op jit(solution)/shard_map/ppermute | solution.py:32
  106.1 16.5 %collective-permute-start.12 = (bf16[2,128,1024]{2,1,0:T(8,128)(2,1)S(1)}, bf16[2,128,1024]{2,1,0:T(8,128)(2,1)S(1)}, u32[]{:S(2)}, u32[]{:S(2)}) collective-permute-start(bf16[2,128,1024]{2,1,0:T(8,128)(2,1)S(1)} %get-tuple-element.62), channel_id=1, source_target_pairs={{0,28},{1,29},{2,30},{3,31},{4,0},{5,1},{6,2},{7,3},{8,4},{9,5},{1... | collective-permute-start | bytes 1572872 | tf_op jit(solution)/shard_map/ppermute | solution.py:32
  111.8 14.0 %collective-permute-start.11 = (bf16[2,128,1024]{2,1,0:T(8,128)(2,1)S(1)}, bf16[2,128,1024]{2,1,0:T(8,128)(2,1)S(1)}, u32[]{:S(2)}, u32[]{:S(2)}) collective-permute-start(bf16[2,128,1024]{2,1,0:T(8,128)(2,1)S(1)} %get-tuple-element.63), channel_id=1, source_target_pairs={{0,4},{1,5},{2,6},{3,7},{4,8},{5,9},{6,10},{7,11},{8,12},{9,13},{1... | collective-permute-start | bytes 1572872 | tf_op jit(solution)/shard_map/ppermute | solution.py:32
  113.4 2.9 %copy-start.18 = (bf16[16,128,1024]{2,1,0:T(8,128)(2,1)S(1)}, bf16[16,128,1024]{2,1,0:T(8,128)(2,1)}, u32[]{:S(2)}) copy-start(bf16[16,128,1024]{2,1,0:T(8,128)(2,1)} %all-gather.2.cloned.1.call-done) | copy-start | bytes 12582916
  114.2 15.5 %copy-start.13 = (bf16[16,1,128,256]{3,2,1,0:T(8,128)(2,1)}, bf16[16,1,128,256]{3,2,1,0:T(8,128)(2,1)S(1)}, u32[]{:S(2)}) copy-start(bf16[16,1,128,256]{3,2,1,0:T(8,128)(2,1)S(1)} %get-tuple-element.67) | copy-start | bytes 3145732
  114.2 15.5 %copy-start.15 = (bf16[16,1,128,256]{3,2,1,0:T(8,128)(2,1)}, bf16[16,1,128,256]{3,2,1,0:T(8,128)(2,1)S(1)}, u32[]{:S(2)}) copy-start(bf16[16,1,128,256]{3,2,1,0:T(8,128)(2,1)S(1)} %get-tuple-element.66) | copy-start | bytes 3145732
  128.2 35.4 %collective-permute-start.14 = (bf16[2,128,1024]{2,1,0:T(8,128)(2,1)}, bf16[2,128,1024]{2,1,0:T(8,128)(2,1)}, u32[]{:S(2)}, u32[]{:S(2)}) collective-permute-start(bf16[2,128,1024]{2,1,0:T(8,128)(2,1)} %get-tuple-element.60), channel_id=1, source_target_pairs={{0,28},{1,29},{2,30},{3,31},{4,0},{5,1},{6,2},{7,3},{8,4},{9,5},{1... | collective-permute-start | bytes 1572872 | tf_op jit(solution)/shard_map/ppermute | solution.py:32
  128.5 35.1 %collective-permute-start.13 = (bf16[2,128,1024]{2,1,0:T(8,128)(2,1)}, bf16[2,128,1024]{2,1,0:T(8,128)(2,1)}, u32[]{:S(2)}, u32[]{:S(2)}) collective-permute-start(bf16[2,128,1024]{2,1,0:T(8,128)(2,1)} %get-tuple-element.61), channel_id=1, source_target_pairs={{0,4},{1,5},{2,6},{3,7},{4,8},{5,9},{6,10},{7,11},{8,12},{9,13},{1... | collective-permute-start | bytes 1572872 | tf_op jit(solution)/shard_map/ppermute | solution.py:32
  136.0 26.4 %all-to-all-start = ((bf16[32,66,128]{2,1,0:T(8,128)(2,1)}), bf16[32,66,128]{2,1,0:T(8,128)(2,1)}, u32[]{:S(2)}, u32[]{:S(2)}) async-start(bf16[32,66,128]{2,1,0:T(8,128)(2,1)} %pad_maximum_fusion), calls=%async_computation | async-start | bytes 1179648 | tf_op jit(solution)/shard_map/all_to_all | solution.py:292
  165.9 15.4 %collective-permute-start.17 = (bf16[128,1024]{1,0:T(8,128)(2,1)S(1)}, bf16[128,1024]{1,0:T(8,128)(2,1)S(1)}, u32[]{:S(2)}, u32[]{:S(2)}) collective-permute-start(bf16[128,1024]{1,0:T(8,128)(2,1)S(1)} %get-tuple-element.68), channel_id=1, source_target_pairs={{0,32},{1,33},{2,34},{3,35},{4,36},{5,37},{6,38},{7,39},{8,40},{9,... | collective-permute-start | bytes 786440 | tf_op jit(solution)/shard_map/ppermute | solution.py:32
  166.0 15.4 %collective-permute-start.18 = (bf16[128,1024]{1,0:T(8,128)(2,1)S(1)}, bf16[128,1024]{1,0:T(8,128)(2,1)S(1)}, u32[]{:S(2)}, u32[]{:S(2)}) collective-permute-start(bf16[128,1024]{1,0:T(8,128)(2,1)S(1)} %get-tuple-element.69), channel_id=1, source_target_pairs={{0,34},{1,35},{2,32},{3,33},{4,38},{5,39},{6,36},{7,37},{8,42},{9,... | collective-permute-start | bytes 786440 | tf_op jit(solution)/shard_map/ppermute | solution.py:32
  169.0 7.1 %copy-start.6 = (bf16[1,256,1024]{2,1,0:T(8,128)(2,1)S(1)}, bf16[1,256,1024]{2,1,0:T(8,128)(2,1)}, u32[]{:S(2)}) copy-start(bf16[1,256,1024]{2,1,0:T(8,128)(2,1)} %param.11) | copy-start | bytes 1572868
  169.0 7.1 %copy-start.14 = (bf16[16,1,128,256]{3,2,1,0:T(8,128)(2,1)S(1)}, bf16[16,1,128,256]{3,2,1,0:T(8,128)(2,1)}, u32[]{:S(2)}) copy-start(bf16[16,1,128,256]{3,2,1,0:T(8,128)(2,1)} %copy-done.13) | copy-start | bytes 3145732
  (9 other events, 20.5 us)
Sparse Core Ops, SparseCore 0:
  18.2 65.1 all-gather.1

commit v7 on v6

--- a/solution.py
+++ b/solution.py
@@ -18,8 +18,8 @@
 KEYS = 1024
 PACK = LANE + 16
 ORDER = 4
-CUT = 3 * TOK // 4
-SPLIT = TOK // 4
+CUT = TOK // 2
+SPLIT = 3 * TOK // 4
 AXES = ("section", "ts")
 
 
@@ -235,14 +235,13 @@
     up = move(far, z_up, (0,))
     down = move(far, z_down, (1,))
     fresh_wide = fresh.astype(F32)
-    fresh_part = jnp.sum(fresh_wide * fresh_wide, axis=1).astype(BF)
+    fresh_part = jnp.sum(fresh_wide * fresh_wide, axis=1)
     up, down, late, fresh_part = lax.optimization_barrier(
         (up, down, returning[0, SPLIT:], fresh_part, older_first)
     )[:4]
-    late = move(after(late, older_first), to_previous)
     up = move(add(block(3), up), z_up)
     down = move(add(block(-3), down), z_down)
-    up, down, cot_mine = lax.optimization_barrier((up, down, cot_mine, older_second, early))[:3]
+    up, down, cot_mine = lax.optimization_barrier((up, down, cot_mine, older_second))[:3]
 
     cots = [cot_mine, move(cot_mine, to_other_core)]
     def times_weights(cot):
@@ -264,8 +263,8 @@
 
     older = jnp.concatenate([older_first, older_second], axis=0)
     wide = older.astype(F32)
-    part_sq = jnp.sum(wide * wide, axis=1).astype(BF)
-    part_rate = lax.rsqrt(part_sq.astype(F32) / LANE + eps)
+    part_sq = jnp.sum(wide * wide, axis=1)
+    part_rate = lax.rsqrt(part_sq / LANE + eps)
     mine = (jnp.arange(2) == core)[None, :, None]
     curve = [
         jnp.sum(
@@ -273,39 +272,35 @@
         ).reshape(N_T // 2, 1, OWN)
         for product, rows, scale in zip(raw, by_core(older), by_core(part_rate))
     ]
-    curve = jnp.where(mine, curve[0], curve[1]).reshape(1, N_T, OWN).astype(BF)
+    curve = jnp.where(mine, curve[0], curve[1])
     fresh_part = fresh_part.reshape(N_Z, 2, 2, OWN)
-    sent = jnp.concatenate(
-        [
-            jnp.broadcast_to(curve, (N_T, N_T, OWN)),
-            jnp.broadcast_to(part_sq.reshape(1, N_T, OWN), (N_T, N_T, OWN)),
-            fresh_part.reshape(N_T, 1, OWN),
-            fresh_part[:, ::-1].reshape(N_T, 1, OWN),
-        ],
-        axis=1,
-    )
+    sent = [curve, part_sq, fresh_part, fresh_part[:, ::-1]]
+    sent = jnp.concatenate([value.reshape(N_T, 1, OWN) for value in sent], axis=1)
     ordered = order(
         jnp.concatenate([place, lengths]),
         *[product.reshape(N_T // 2, OWN, LANE) for product in raw],
         norm_gain,
     )
     got = lax.all_to_all(sent, "ts", 0, 0, tiled=True)
-    up, down = lax.optimization_barrier((up, down, got, late))[:2]
+    late = move(after(late, ordered), to_previous)
+    up, down = lax.optimization_barrier((up, down, got, early, late))[:2]
     got, ordered = lax.optimization_barrier((got, ordered))
-    got = got.astype(F32)
-    live = (jnp.arange(TOK, dtype=jnp.int32) < lengths[0]).reshape(N_T, OWN)
-    older_rate = lax.rsqrt(jnp.sum(got[:, N_T : 2 * N_T], axis=0) / WIDTH + eps)
-    curve = jnp.sum(
-        got[:, :N_T] * (older_rate * jnp.sqrt(got[:, N_T : 2 * N_T] / LANE + eps)), axis=0
-    )
-    pull = jnp.where(live, older_rate * older_rate / WIDTH * curve, 0).reshape(TOK)
-    scale = jnp.where(live, older_rate, 0).reshape(TOK)
-    fresh_rate = lax.rsqrt(jnp.sum(got[:, 2 * N_T :], axis=0) / WIDTH + eps)
+
+    live = lane * OWN + jnp.arange(OWN, dtype=jnp.int32) < lengths[0]
+    own_rate = lax.rsqrt(jnp.sum(got[:, 1], axis=0) / WIDTH + eps)
+    own_curve = jnp.sum(got[:, 0] * (own_rate * jnp.sqrt(got[:, 1] / LANE + eps)), axis=0)
+    factors = jnp.stack(
+        [jnp.where(live, own_rate, 0), jnp.where(live, own_rate * own_rate / WIDTH * own_curve, 0)]
+    )
+    factors = jnp.broadcast_to(factors[None], (N_T, 2, OWN))
+    factors = lax.all_to_all(factors, "ts", 0, 0, tiled=True)
+    fresh_rate = lax.rsqrt(jnp.sum(got[:, 2:], axis=0) / WIDTH + eps)
 
     summed = block(0).astype(F32) + up.astype(F32) + down.astype(F32)
     straight = (pick(summed, half) * fresh_rate[0][:, None]).astype(BF)
     crossed = (pick(summed, 1 - half) * fresh_rate[1][:, None]).astype(BF)
-    *cots, pull, scale = lax.optimization_barrier((*cots, pull, scale, straight, crossed))[:4]
+    *cots, factors = lax.optimization_barrier((*cots, factors, straight, crossed))[:3]
+    scale, pull = factors[:, 0].reshape(TOK), factors[:, 1].reshape(TOK)
     straight = move(straight, to_next)
     crossed = move(crossed, to_next_other_half)
     new_keys = (straight.astype(F32) + crossed.astype(F32)).astype(BF)

time: 192 us -> 192 us (level)
  waiting for transfers between devices: 65.9 us -> 54.7 us
  local copies, waits for them, and re-layouts: 14.7 us -> 20.2 us
  other arithmetic: 20.3 us -> 23.4 us
  matrix products: 12.5 us -> 14.8 us
  starting transfers between devices: 53.9 us -> 55.9 us
    all_to_all x1, waiting for transfers between devices: 13.8 us -> 5.08 us  [shards(): got = lax.all_to_all(sent, 'ts', 0, 0, tiled=True)]
    ppermute x19, waiting for transfers between devices: 52 us -> 45.8 us  [move(): return lax.ppermute(value, AXES, pairs)]
    all_to_all x0 -> x1, starting transfers between devices: none -> 5.54 us  [shards(): factors = lax.all_to_all(factors, 'ts', 0, 0, tiled=True)]
    ppermute x19, starting transfers between devices: 46.1 us -> 41.9 us  [move(): return lax.ppermute(value, AXES, pairs)]
    all_to_all x0 -> x1, waiting for transfers between devices: none -> 3.84 us  [shards(): factors = lax.all_to_all(factors, 'ts', 0, 0, tiled=True)]
    dot_general x2, matrix products: 5.93 us -> 8.29 us  [shards(): lax.dot_general((rows.astype(F32) * gain * row_scale[:, None]).astype(BF)...]
    convert_element_type x3, other arithmetic: 4.36 us -> 6.4 us  [add(): return (a.astype(F32) + b.astype(F32)).astype(BF)]
    unnamed x41 -> x43, local copies, waits for them, and re-layouts: 9.75 us -> 10.8 us
  transfers between devices with their start and end apart: 21 -> 22, of which waited for: 9 -> 8; matrix products, arithmetic and copies ran while one was open for 18% -> 24% of each run, Pallas kernels for 3% -> 3%
where the time goes in v7:
time: 192 us; the launch traced here: 191 us
  starting transfers between devices  55.9 us (29%)
  waiting for transfers between devices  54.7 us (28%)
  other arithmetic  23.4 us (12%)
  local copies, waits for them, and re-layouts  20.2 us (11%)
  between operations  15.2 us (8%)
  matrix products  14.8 us (8%)
  Pallas kernels  6.49 us (3%)
    ppermute x19, waiting for transfers between devices, move(): return lax.ppermute(value, AXES, pairs)  45.8 us
    ppermute x19, starting transfers between devices, move(): return lax.ppermute(value, AXES, pairs)  41.9 us
    unnamed x43, local copies, waits for them, and re-layouts  10.8 us
    convert_element_type x1, other arithmetic, shards(): total.astype(BF)[None]  8.86 us
    all_to_all x1, starting transfers between devices, shards(): got = lax.all_to_all(sent, 'ts', 0, 0, tiled=True)  8.41 us
    dot_general x2, matrix products, shards(): lax.dot_general((rows.astype(F32) * gain * row_scale[:, None]).astype(BF)...  8.29 us
    dot_general x2, matrix products, times_weights(): lax.dot_general(cot, weights, (((1,), (1,)), ((), ())), preferred_element...  6.54 us
    convert_element_type x3, other arithmetic, add(): return (a.astype(F32) + b.astype(F32)).astype(BF)  6.4 us
  transfers between devices with their start and end apart: 22, of which 8 were waited for; matrix products, arithmetic and copies ran while one was open for 24% of the time, Pallas kernels for 3%

profile of v7, /device:TPU:1, one launch (start us, length us, event | category | flops | bytes accessed | tf_op | source)
XLA Modules:
  0.0 190.8 jit_solution(10190404512040356172)
XLA Ops:
  7.2 3.7 %collective-permute-start.5 = (bf16[128,1024]{1,0:T(8,128)(2,1)}, bf16[128,1024]{1,0:T(8,128)(2,1)S(1)}, u32[]{:S(2)}, u32[]{:S(2)}) collective-permute-start(bf16[128,1024]{1,0:T(8,128)(2,1)} %bitcast.122), channel_id=1, source_target_pairs={{0,2},{1,3},{2,0},{3,1},{4,6},{5,7},{6,4},{7,5},{8,10},{9,11},{10,... | collective-permute-start | bytes 786440 | tf_op jit(solution)/shard_map/ppermute | solution.py:32
  10.9 5.3 %collective-permute-done.5 = bf16[128,1024]{1,0:T(8,128)(2,1)S(1)} collective-permute-done((bf16[128,1024]{1,0:T(8,128)(2,1)}, bf16[128,1024]{1,0:T(8,128)(2,1)S(1)}, u32[]{:S(2)}, u32[]{:S(2)}) %collective-permute-start.5) | collective-permute-done | bytes 262176 | tf_op jit(solution)/shard_map/ppermute | solution.py:32
  19.0 4.5 %collective-permute-start.1 = (bf16[272,1024]{1,0:T(8,128)(2,1)}, bf16[272,1024]{1,0:T(8,128)(2,1)}, u32[]{:S(2)}, u32[]{:S(2)}) collective-permute-start(bf16[272,1024]{1,0:T(8,128)(2,1)} %shard_map.102), channel_id=1, source_target_pairs={{0,224},{1,225},{2,226},{3,227},{4,228},{5,229},{6,230},{7,231},{8... | collective-permute-start | bytes 1671176 | tf_op jit(solution)/shard_map/ppermute | solution.py:32
  26.4 7.8 %collective-permute-done.1.packed_mine = bf16[272,1024]{1,0:T(8,128)(2,1)} collective-permute-done((bf16[272,1024]{1,0:T(8,128)(2,1)}, bf16[272,1024]{1,0:T(8,128)(2,1)}, u32[]{:S(2)}, u32[]{:S(2)}) %collective-permute-start.1) | collective-permute-done | bytes 557088 | tf_op jit(solution)/shard_map/ppermute | solution.py:32
  34.2 2.5 %collective-permute-start.2 = (bf16[272,1024]{1,0:T(8,128)(2,1)}, bf16[272,1024]{1,0:T(8,128)(2,1)}, u32[]{:S(2)}, u32[]{:S(2)}) collective-permute-start(bf16[272,1024]{1,0:T(8,128)(2,1)} %collective-permute-done.1.packed_mine), channel_id=1, source_target_pairs={{0,1},{1,0},{2,3},{3,2},{4,5},{5,4},{6,7},{7,6},{8,9},{9,8},{10,11... | collective-permute-start | bytes 1671176 | tf_op jit(solution)/shard_map/ppermute | solution.py:32
  38.1 4.3 %collective-permute-start.6 = (bf16[2048,256]{1,0:T(8,128)(2,1)}, bf16[2048,256]{1,0:T(8,128)(2,1)}, u32[]{:S(2)}, u32[]{:S(2)}) collective-permute-start(bf16[2048,256]{1,0:T(8,128)(2,1)} %get-tuple-element.32), channel_id=1, source_target_pairs={{0,224},{1,225},{2,226},{3,227},{4,228},{5,229},{6,230},{7,231},{8... | collective-permute-start | bytes 3145736 | tf_op jit(solution)/shard_map/ppermute | solution.py:32
  42.4 4.3 %shard_map.103 = bf16[16,128,1024]{2,1,0:T(8,128)(2,1)S(1)} custom-call(s32[1]{0:T(128)} %bitcast.place, bf16[16,2,128,256]{3,2,1,0:T(8,128)(2,1)S(1)} %bitcast.109, bf16[16,128,256]{2,1,0:T(8,128)(2,1)S(1)} %collective-permute-done.rows_other, bf16[272,1024]{1,0:T(8,128)(2,1)} %collective-permute-done.1.packed_mine, ...), custom_call_target="tpu_custom_call" | custom-call | flops 2147483648 | bytes 7340032 | tf_op jit(solution)/shard_map/pallas_call | solution.py:143
  46.8 2.0 %copy-done = bf16[16,128,1024]{2,1,0:T(8,128)(2,1)} copy-done((bf16[16,128,1024]{2,1,0:T(8,128)(2,1)}, bf16[16,128,1024]{2,1,0:T(8,128)(2,1)S(1)}, u32[]{:S(2)}) %copy-start) | copy-done | bytes 4194328
  51.1 7.5 %collective-permute-start.4 = (bf16[2,128,1024]{2,1,0:T(8,128)(2,1)}, bf16[2,128,1024]{2,1,0:T(8,128)(2,1)}, u32[]{:S(2)}, u32[]{:S(2)}) collective-permute-start(bf16[2,128,1024]{2,1,0:T(8,128)(2,1)} %constant_dynamic-slice_fusion.6), channel_id=1, source_target_pairs={{1,29},{3,31},{5,1},{7,3},{9,5},{11,7},{13,9},{15,11},{17,13},{19,... | collective-permute-start | bytes 1572872 | tf_op jit(solution)/shard_map/ppermute | solution.py:32
  59.7 2.0 %slice_bitcast_fusion.3 = bf16[1024,256]{1,0:T(8,128)(2,1)} fusion(bf16[1,4096,256]{2,1,0:T(8,128)(2,1)} %param.9), kind=kLoop, calls=%fused_computation.37 | loop fusion | bytes 1048576 | tf_op jit(solution)/shard_map/squeeze | solution.py:240
  61.8 4.5 %collective-permute-done.6 = bf16[2048,256]{1,0:T(8,128)(2,1)} collective-permute-done((bf16[2048,256]{1,0:T(8,128)(2,1)}, bf16[2048,256]{1,0:T(8,128)(2,1)}, u32[]{:S(2)}, u32[]{:S(2)}) %collective-permute-start.6) | collective-permute-done | bytes 1048608 | tf_op jit(solution)/shard_map/ppermute | solution.py:32
  66.3 9.7 %collective-permute-done.4 = bf16[2,128,1024]{2,1,0:T(8,128)(2,1)} collective-permute-done((bf16[2,128,1024]{2,1,0:T(8,128)(2,1)}, bf16[2,128,1024]{2,1,0:T(8,128)(2,1)}, u32[]{:S(2)}, u32[]{:S(2)}) %collective-permute-start.4) | collective-permute-done | bytes 524320 | tf_op jit(solution)/shard_map/ppermute | solution.py:32
  76.0 1.9 %add_convert_fusion.4 = (bf16[2,128,1024]{2,1,0:T(8,128)(2,1)S(1)}, bf16[2,128,1024]{2,1,0:T(8,128)(2,1)S(1)}) fusion(bf16[2,128,1024]{2,1,0:T(8,128)(2,1)} %collective-permute-done.4, bf16[16,128,1024]{2,1,0:T(8,128)(2,1)} %copy-done, s32[]{:T(128)S(6)} %select_n.154, bf16[2,128,1024]{2,1,0:T(8,128)(2,1)} %collective-permute-done.3, s32[]{:T(128)S(6)} %select_n.150), kind=kLoop, calls=%fused_computation.27 | loop fusion | flops 2097152 | bytes 3145736 | tf_op jit(solution)/shard_map/convert_element_type | solution.py:80
  78.1 3.5 %collective-permute-start.8 = (bf16[2,128,1024]{2,1,0:T(8,128)(2,1)S(1)}, bf16[2,128,1024]{2,1,0:T(8,128)(2,1)S(1)}, u32[]{:S(2)}, u32[]{:S(2)}) collective-permute-start(bf16[2,128,1024]{2,1,0:T(8,128)(2,1)S(1)} %get-tuple-element.62), channel_id=1, source_target_pairs={{0,28},{1,29},{2,30},{3,31},{4,0},{5,1},{6,2},{7,3},{8,4},{9,5},{1... | collective-permute-start | bytes 1572872 | tf_op jit(solution)/shard_map/ppermute | solution.py:32
  81.5 12.7 %collective-permute-done.7 = bf16[2,128,1024]{2,1,0:T(8,128)(2,1)S(1)} collective-permute-done((bf16[2,128,1024]{2,1,0:T(8,128)(2,1)S(1)}, bf16[2,128,1024]{2,1,0:T(8,128)(2,1)S(1)}, u32[]{:S(2)}, u32[]{:S(2)}) %collective-permute-start.7) | collective-permute-done | bytes 524320 | tf_op jit(solution)/shard_map/ppermute | solution.py:32
  98.4 3.4 %collective-permute-start.15 = (bf16[3072,256]{1,0:T(8,128)(2,1)}, bf16[3072,256]{1,0:T(8,128)(2,1)}, u32[]{:S(2)}, u32[]{:S(2)}) collective-permute-start(bf16[3072,256]{1,0:T(8,128)(2,1)} %slice_bitcast_fusion), channel_id=1, source_target_pairs={{0,224},{1,225},{2,226},{3,227},{4,228},{5,229},{6,230},{7,231},{8... | collective-permute-start | bytes 4718600 | tf_op jit(solution)/shard_map/ppermute | solution.py:32
  101.8 1.9 %add_convert_fusion.2 = (bf16[2,128,1024]{2,1,0:T(8,128)(2,1)S(1)}, bf16[2,128,1024]{2,1,0:T(8,128)(2,1)S(1)}) fusion(bf16[2,128,1024]{2,1,0:T(8,128)(2,1)} %copy-done.19, bf16[16,128,1024]{2,1,0:T(8,128)(2,1)} %copy-done, s32[]{:T(128)S(6)} %select_n.161, bf16[2,128,1024]{2,1,0:T(8,128)(2,1)} %copy-done.18, s32[]{:T(128)S(6)} %select_n.148), kind=kLoop, calls=%fused_computation.24 | loop fusion | flops 2097152 | bytes 3145736 | tf_op jit(solution)/shard_map/convert_element_type | solution.py:80
  103.8 2.7 %collective-permute-start.11 = (bf16[2,128,1024]{2,1,0:T(8,128)(2,1)S(1)}, bf16[2,128,1024]{2,1,0:T(8,128)(2,1)S(1)}, u32[]{:S(2)}, u32[]{:S(2)}) collective-permute-start(bf16[2,128,1024]{2,1,0:T(8,128)(2,1)S(1)} %get-tuple-element.60), channel_id=1, source_target_pairs={{0,28},{1,29},{2,30},{3,31},{4,0},{5,1},{6,2},{7,3},{8,4},{9,5},{1... | collective-permute-start | bytes 1572872 | tf_op jit(solution)/shard_map/ppermute | solution.py:32
  108.7 2.1 %copy-done.20 = bf16[16,128,1024]{2,1,0:T(8,128)(2,1)S(1)} copy-done((bf16[16,128,1024]{2,1,0:T(8,128)(2,1)S(1)}, bf16[16,128,1024]{2,1,0:T(8,128)(2,1)}, u32[]{:S(2)}) %copy-start.20) | copy-done | bytes 4194328
  112.4 5.7 %collective-permute-done.10 = bf16[2,128,1024]{2,1,0:T(8,128)(2,1)S(1)} collective-permute-done((bf16[2,128,1024]{2,1,0:T(8,128)(2,1)S(1)}, bf16[2,128,1024]{2,1,0:T(8,128)(2,1)S(1)}, u32[]{:S(2)}, u32[]{:S(2)}) %collective-permute-start.10) | collective-permute-done | bytes 524320 | tf_op jit(solution)/shard_map/ppermute | solution.py:32
  118.1 2.5 %add_convert_fusion = (bf16[2,128,1024]{2,1,0:T(8,128)(2,1)}, bf16[2,128,1024]{2,1,0:T(8,128)(2,1)}) fusion(bf16[2,128,1024]{2,1,0:T(8,128)(2,1)S(1)} %collective-permute-done.11, bf16[16,128,1024]{2,1,0:T(8,128)(2,1)} %copy-done, s32[]{:T(128)S(6)} %select_n.163, bf16[2,128,1024]{2,1,0:T(8,128)(2,1)S(1)} %collective-permute-done.10, s32[]{:T(128)S(6)} %select_n.146), kind=kLoop, calls=%fused_computation.22 | loop fusion | flops 2097152 | bytes 3145736 | tf_op jit(solution)/shard_map/convert_element_type | solution.py:80
  120.6 2.7 %collective-permute-start.13 = (bf16[2,128,1024]{2,1,0:T(8,128)(2,1)}, bf16[2,128,1024]{2,1,0:T(8,128)(2,1)}, u32[]{:S(2)}, u32[]{:S(2)}) collective-permute-start(bf16[2,128,1024]{2,1,0:T(8,128)(2,1)} %get-tuple-element.58), channel_id=1, source_target_pairs={{0,28},{1,29},{2,30},{3,31},{4,0},{5,1},{6,2},{7,3},{8,4},{9,5},{1... | collective-permute-start | bytes 1572872 | tf_op jit(solution)/shard_map/ppermute | solution.py:32
  123.3 5.2 %multiply_reduce_fusion.2 = (f32[2048]{0:T(1024)S(1)}, f32[2048]{0:T(1024)S(1)}, f32[2048,256]{1,0:T(8,128)}) fusion(bf16[16,1,128,256]{3,2,1,0:T(8,128)(2,1)S(1)} %get-tuple-element.65, f32[2048]{0:T(1024)S(1)} %bitcast.137, f32[256]{0:T(256)S(1)} %bitcast.112, bf16[16,1,128,256]{3,2,1,0:T(8,128)(2,1)S(1)} %get-tuple-element.64, ...), kind=kOutput, calls=%fused_computation.11 | convolution fusion | flops 1081077760 | bytes 11043840 | tf_op jit(solution)/shard_map/dot_general | solution.py:248
  129.3 8.4 %all-to-all-start = ((f32[32,4,128]{2,1,0:T(4,128)}), f32[32,4,128]{2,1,0:T(4,128)}, u32[]{:S(2)}, u32[]{:S(2)}) async-start(f32[32,4,128]{2,1,0:T(4,128)} %pad_maximum_fusion.1), calls=%async_computation | async-start | bytes 131072 | tf_op jit(solution)/shard_map/all_to_all | solution.py:284
  140.7 1.9 %copy-done.2 = f32[16,2,128,256]{3,2,1,0:T(8,128)} copy-done((f32[16,2,128,256]{3,2,1,0:T(8,128)}, f32[16,2,128,256]{3,2,1,0:T(8,128)S(1)}, u32[]{:S(2)}) %copy-start.2) | copy-done | bytes 4194328
  142.6 5.1 %all-to-all-done = f32[32,4,128]{2,1,0:T(4,128)} async-done(((f32[32,4,128]{2,1,0:T(4,128)}), f32[32,4,128]{2,1,0:T(4,128)}, u32[]{:S(2)}, u32[]{:S(2)}) %all-to-all-start) | async-done | bytes 65568 | tf_op jit(solution)/shard_map/all_to_all | solution.py:284
  150.1 5.5 %all-to-all-start.1 = ((f32[32,2,128]{2,1,0:T(2,128)}), f32[32,2,128]{2,1,0:T(2,128)S(1)}, u32[]{:S(2)}, u32[]{:S(2)}) async-start(f32[32,2,128]{2,1,0:T(2,128)} %broadcast_in_dim.72), calls=%async_computation.1 | async-start | bytes 65536 | tf_op jit(solution)/shard_map/all_to_all | solution.py:296
  158.8 2.6 %collective-permute-start.18 = (bf16[128,1024]{1,0:T(8,128)(2,1)S(1)}, bf16[128,1024]{1,0:T(8,128)(2,1)S(1)}, u32[]{:S(2)}, u32[]{:S(2)}) collective-permute-start(bf16[128,1024]{1,0:T(8,128)(2,1)S(1)} %get-tuple-element.69), channel_id=1, source_target_pairs={{0,34},{1,35},{2,32},{3,33},{4,38},{5,39},{6,36},{7,37},{8,42},{9,... | collective-permute-start | bytes 786440 | tf_op jit(solution)/shard_map/ppermute | solution.py:32
  161.4 3.8 %all-to-all-done.1 = f32[32,2,128]{2,1,0:T(2,128)S(1)} async-done(((f32[32,2,128]{2,1,0:T(2,128)}), f32[32,2,128]{2,1,0:T(2,128)S(1)}, u32[]{:S(2)}, u32[]{:S(2)}) %all-to-all-start.1) | async-done | bytes 32800 | tf_op jit(solution)/shard_map/all_to_all | solution.py:296
  165.4 3.7 %fusion.6 = f32[256,1024]{1,0:T(8,128)S(1)} fusion(bf16[2048,1024]{1,0:T(8,128)(2,1)} %bitcast.142, bf16[2048,256]{1,0:T(8,128)(2,1)S(1)} %bitcast.120, f32[2048]{0:T(1024)S(1)} %bitcast.139, f32[256]{0:T(256)S(1)} %bitcast.113), kind=kOutput, calls=%fused_computation.15 | convolution fusion | flops 1075838976 | bytes 6300672 | tf_op jit(solution)/shard_map/dot_general | solution.py:309
  169.2 8.9 %subtract_convert_fusion = bf16[1,4096,256]{2,1,0:T(8,128)(2,1)} fusion(f32[1,4096,256]{2,1,0:T(8,128)S(1)} %bitcast.110, bf16[1,1024,256]{2,1,0:T(8,128)(2,1)S(1)} %bitcast.121, bf16[1,3072,256]{2,1,0:T(8,128)(2,1)} %bitcast.36, bf16[1,2048,256]{2,1,0:T(8,128)(2,1)S(1)} %bitcast.118, bf16[1,2048,256]{2,1,0:T(8,128)(2,1)} %bitcast.46, f32[4096]{0:T(1024)S(1)} %bitcast.128, ...), kind=kLoop, calls=%fused_computation | loop fusion | flops 13631488 | bytes 10518528 | tf_op jit(solution)/shard_map/convert_element_type | solution.py:326
  178.0 4.6 %multiply_reduce_fusion.4 = (f32[256]{0:T(256)S(1)}, f32[256,1024]{1,0:T(8,128)}) fusion(bf16[1,256,1024]{2,1,0:T(8,128)(2,1)S(1)} %copy-done.6, f32[256,1024]{1,0:T(8,128)S(1)} %fusion.6, bf16[2048,1024]{1,0:T(8,128)(2,1)} %collective-permute-done.14, bf16[2048,256]{1,0:T(8,128)(2,1)S(1)} %bitcast.119, f32[2048]{0:T(1024)S(1)} %bitcast.138, ...), kind=kOutput, calls=%fused_computation.16 | convolution fusion | flops 1076887296 | bytes 7874560 | tf_op jit(solution)/shard_map/dot_general | solution.py:309
  (106 shorter events, 28.6 us)
Async XLA Ops:
  7.2 10.9 %copy-start.4 = (bf16[1,256,1024]{2,1,0:T(8,128)(2,1)S(1)}, bf16[1,256,1024]{2,1,0:T(8,128)(2,1)}, u32[]{:S(2)}) copy-start(bf16[1,256,1024]{2,1,0:T(8,128)(2,1)} %param.11) | copy-start | bytes 1572868
  7.2 10.9 %copy-start.7 = (f32[1,256]{1,0:T(1,128)S(1)}, f32[1,256]{1,0:T(1,128)}, u32[]{:S(2)}) copy-start(f32[1,256]{1,0:T(1,128)} %gain.3) | copy-start | bytes 3076
  7.2 16.3 %copy-start.1 = (bf16[1,4096,256]{2,1,0:T(8,128)(2,1)S(1)}, bf16[1,4096,256]{2,1,0:T(8,128)(2,1)}, u32[]{:S(2)}) copy-start(bf16[1,4096,256]{2,1,0:T(8,128)(2,1)} %param.7) | copy-start | bytes 6291460
  7.2 88.7 %all-gather.2.cloned.1.call-start = ((), (), s32[]{:S(2)}) async-start(), calls=%async_computation.2 | async-start | bytes 4718592 | tf_op jit(solution)/shard_map/all_gather | solution.py:213
  7.2 8.9 %collective-permute-start.5 = (bf16[128,1024]{1,0:T(8,128)(2,1)}, bf16[128,1024]{1,0:T(8,128)(2,1)S(1)}, u32[]{:S(2)}, u32[]{:S(2)}) collective-permute-start(bf16[128,1024]{1,0:T(8,128)(2,1)} %bitcast.122), channel_id=1, source_target_pairs={{0,2},{1,3},{2,0},{3,1},{4,6},{5,7},{6,4},{7,5},{8,10},{9,11},{10,... | collective-permute-start | bytes 786440 | tf_op jit(solution)/shard_map/ppermute | solution.py:32
  19.0 15.2 %collective-permute-start.1 = (bf16[272,1024]{1,0:T(8,128)(2,1)}, bf16[272,1024]{1,0:T(8,128)(2,1)}, u32[]{:S(2)}, u32[]{:S(2)}) collective-permute-start(bf16[272,1024]{1,0:T(8,128)(2,1)} %shard_map.102), channel_id=1, source_target_pairs={{0,224},{1,225},{2,226},{3,227},{4,228},{5,229},{6,230},{7,231},{8... | collective-permute-start | bytes 1671176 | tf_op jit(solution)/shard_map/ppermute | solution.py:32
  23.5 13.2 %copy-start.12 = (bf16[1,4096,256]{2,1,0:T(8,128)(2,1)S(1)}, bf16[1,4096,256]{2,1,0:T(8,128)(2,1)}, u32[]{:S(2)}) copy-start(bf16[1,4096,256]{2,1,0:T(8,128)(2,1)} %param.8) | copy-start | bytes 6291460
  24.5 17.9 %collective-permute-start = (bf16[16,128,256]{2,1,0:T(8,128)(2,1)}, bf16[16,128,256]{2,1,0:T(8,128)(2,1)S(1)}, u32[]{:S(2)}, u32[]{:S(2)}) collective-permute-start(bf16[16,128,256]{2,1,0:T(8,128)(2,1)} %dynamic-slice_bitcast_fusion), channel_id=1, source_target_pairs={{0,1},{1,0},{2,3},{3,2},{4,5},{5,4},{6,7},{7,6},{8,9},{9,8},{10,11... | collective-permute-start | bytes 3145736 | tf_op jit(solution)/shard_map/ppermute | solution.py:32
  34.2 8.3 %collective-permute-start.2 = (bf16[272,1024]{1,0:T(8,128)(2,1)}, bf16[272,1024]{1,0:T(8,128)(2,1)}, u32[]{:S(2)}, u32[]{:S(2)}) collective-permute-start(bf16[272,1024]{1,0:T(8,128)(2,1)} %collective-permute-done.1.packed_mine), channel_id=1, source_target_pairs={{0,1},{1,0},{2,3},{3,2},{4,5},{5,4},{6,7},{7,6},{8,9},{9,8},{10,11... | collective-permute-start | bytes 1671176 | tf_op jit(solution)/shard_map/ppermute | solution.py:32
  38.1 28.2 %collective-permute-start.6 = (bf16[2048,256]{1,0:T(8,128)(2,1)}, bf16[2048,256]{1,0:T(8,128)(2,1)}, u32[]{:S(2)}, u32[]{:S(2)}) collective-permute-start(bf16[2048,256]{1,0:T(8,128)(2,1)} %get-tuple-element.32), channel_id=1, source_target_pairs={{0,224},{1,225},{2,226},{3,227},{4,228},{5,229},{6,230},{7,231},{8... | collective-permute-start | bytes 3145736 | tf_op jit(solution)/shard_map/ppermute | solution.py:32
  49.6 16.7 %collective-permute-start.3 = (bf16[2,128,1024]{2,1,0:T(8,128)(2,1)}, bf16[2,128,1024]{2,1,0:T(8,128)(2,1)}, u32[]{:S(2)}, u32[]{:S(2)}) collective-permute-start(bf16[2,128,1024]{2,1,0:T(8,128)(2,1)} %constant_dynamic-slice_fusion.6), channel_id=1, source_target_pairs={{0,4},{2,6},{4,8},{6,10},{8,12},{10,14},{12,16},{14,18},{16,20},{1... | collective-permute-start | bytes 1572872 | tf_op jit(solution)/shard_map/ppermute | solution.py:32
  51.1 25.0 %collective-permute-start.4 = (bf16[2,128,1024]{2,1,0:T(8,128)(2,1)}, bf16[2,128,1024]{2,1,0:T(8,128)(2,1)}, u32[]{:S(2)}, u32[]{:S(2)}) collective-permute-start(bf16[2,128,1024]{2,1,0:T(8,128)(2,1)} %constant_dynamic-slice_fusion.6), channel_id=1, source_target_pairs={{1,29},{3,31},{5,1},{7,3},{9,5},{11,7},{13,9},{15,11},{17,13},{19,... | collective-permute-start | bytes 1572872 | tf_op jit(solution)/shard_map/ppermute | solution.py:32
  59.2 37.9 %copy-start.11 = (bf16[1,4096,256]{2,1,0:T(8,128)(2,1)S(1)}, bf16[1,4096,256]{2,1,0:T(8,128)(2,1)}, u32[]{:S(2)}) copy-start(bf16[1,4096,256]{2,1,0:T(8,128)(2,1)} %param.9) | copy-start | bytes 6291460
  59.2 36.6 %collective-permute-start.9 = (bf16[2048,256]{1,0:T(8,128)(2,1)}, bf16[2048,256]{1,0:T(8,128)(2,1)S(1)}, u32[]{:S(2)}, u32[]{:S(2)}) collective-permute-start(bf16[2048,256]{1,0:T(8,128)(2,1)} %get-tuple-element.35), channel_id=1, source_target_pairs={{0,224},{1,225},{2,226},{3,227},{4,228},{5,229},{6,230},{7,231},{8... | collective-permute-start | bytes 3145736 | tf_op jit(solution)/shard_map/ppermute | solution.py:32
  78.0 16.2 %collective-permute-start.7 = (bf16[2,128,1024]{2,1,0:T(8,128)(2,1)S(1)}, bf16[2,128,1024]{2,1,0:T(8,128)(2,1)S(1)}, u32[]{:S(2)}, u32[]{:S(2)}) collective-permute-start(bf16[2,128,1024]{2,1,0:T(8,128)(2,1)S(1)} %get-tuple-element.63), channel_id=1, source_target_pairs={{0,4},{1,5},{2,6},{3,7},{4,8},{5,9},{6,10},{7,11},{8,12},{9,13},{1... | collective-permute-start | bytes 1572872 | tf_op jit(solution)/shard_map/ppermute | solution.py:32
  78.1 17.0 %collective-permute-start.8 = (bf16[2,128,1024]{2,1,0:T(8,128)(2,1)S(1)}, bf16[2,128,1024]{2,1,0:T(8,128)(2,1)S(1)}, u32[]{:S(2)}, u32[]{:S(2)}) collective-permute-start(bf16[2,128,1024]{2,1,0:T(8,128)(2,1)S(1)} %get-tuple-element.62), channel_id=1, source_target_pairs={{0,28},{1,29},{2,30},{3,31},{4,0},{5,1},{6,2},{7,3},{8,4},{9,5},{1... | collective-permute-start | bytes 1572872 | tf_op jit(solution)/shard_map/ppermute | solution.py:32
  95.8 11.9 %copy-start.9 = (bf16[2048,256]{1,0:T(8,128)(2,1)}, bf16[2048,256]{1,0:T(8,128)(2,1)S(1)}, u32[]{:S(2)}) copy-start(bf16[2048,256]{1,0:T(8,128)(2,1)S(1)} %collective-permute-done.9) | copy-start | bytes 3145732
  95.8 27.4 %collective-permute-start.14 = (bf16[2048,1024]{1,0:T(8,128)(2,1)}, bf16[2048,1024]{1,0:T(8,128)(2,1)}, u32[]{:S(2)}, u32[]{:S(2)}) collective-permute-start(bf16[2048,1024]{1,0:T(8,128)(2,1)} %bitcast.141), channel_id=1, source_target_pairs={{0,1},{1,0},{2,3},{3,2},{4,5},{5,4},{6,7},{7,6},{8,9},{9,8},{10,11... | collective-permute-start | bytes 12582920 | tf_op jit(solution)/shard_map/ppermute | solution.py:32
  98.4 58.2 %collective-permute-start.15 = (bf16[3072,256]{1,0:T(8,128)(2,1)}, bf16[3072,256]{1,0:T(8,128)(2,1)}, u32[]{:S(2)}, u32[]{:S(2)}) collective-permute-start(bf16[3072,256]{1,0:T(8,128)(2,1)} %slice_bitcast_fusion), channel_id=1, source_target_pairs={{0,224},{1,225},{2,226},{3,227},{4,228},{5,229},{6,230},{7,231},{8... | collective-permute-start | bytes 4718600 | tf_op jit(solution)/shard_map/ppermute | solution.py:32
  103.7 14.3 %collective-permute-start.10 = (bf16[2,128,1024]{2,1,0:T(8,128)(2,1)S(1)}, bf16[2,128,1024]{2,1,0:T(8,128)(2,1)S(1)}, u32[]{:S(2)}, u32[]{:S(2)}) collective-permute-start(bf16[2,128,1024]{2,1,0:T(8,128)(2,1)S(1)} %get-tuple-element.61), channel_id=1, source_target_pairs={{0,4},{1,5},{2,6},{3,7},{4,8},{5,9},{6,10},{7,11},{8,12},{9,13},{1... | collective-permute-start | bytes 1572872 | tf_op jit(solution)/shard_map/ppermute | solution.py:32
  103.8 14.3 %collective-permute-start.11 = (bf16[2,128,1024]{2,1,0:T(8,128)(2,1)S(1)}, bf16[2,128,1024]{2,1,0:T(8,128)(2,1)S(1)}, u32[]{:S(2)}, u32[]{:S(2)}) collective-permute-start(bf16[2,128,1024]{2,1,0:T(8,128)(2,1)S(1)} %get-tuple-element.60), channel_id=1, source_target_pairs={{0,28},{1,29},{2,30},{3,31},{4,0},{5,1},{6,2},{7,3},{8,4},{9,5},{1... | collective-permute-start | bytes 1572872 | tf_op jit(solution)/shard_map/ppermute | solution.py:32
  108.7 14.6 %copy-start.13 = (bf16[16,1,128,256]{3,2,1,0:T(8,128)(2,1)}, bf16[16,1,128,256]{3,2,1,0:T(8,128)(2,1)S(1)}, u32[]{:S(2)}) copy-start(bf16[16,1,128,256]{3,2,1,0:T(8,128)(2,1)S(1)} %get-tuple-element.65) | copy-start | bytes 3145732
  108.7 14.6 %copy-start.15 = (bf16[16,1,128,256]{3,2,1,0:T(8,128)(2,1)}, bf16[16,1,128,256]{3,2,1,0:T(8,128)(2,1)S(1)}, u32[]{:S(2)}) copy-start(bf16[16,1,128,256]{3,2,1,0:T(8,128)(2,1)S(1)} %get-tuple-element.64) | copy-start | bytes 3145732
  120.6 36.0 %collective-permute-start.12 = (bf16[2,128,1024]{2,1,0:T(8,128)(2,1)}, bf16[2,128,1024]{2,1,0:T(8,128)(2,1)}, u32[]{:S(2)}, u32[]{:S(2)}) collective-permute-start(bf16[2,128,1024]{2,1,0:T(8,128)(2,1)} %get-tuple-element.59), channel_id=1, source_target_pairs={{0,4},{1,5},{2,6},{3,7},{4,8},{5,9},{6,10},{7,11},{8,12},{9,13},{1... | collective-permute-start | bytes 1572872 | tf_op jit(solution)/shard_map/ppermute | solution.py:32
  120.6 36.0 %collective-permute-start.13 = (bf16[2,128,1024]{2,1,0:T(8,128)(2,1)}, bf16[2,128,1024]{2,1,0:T(8,128)(2,1)}, u32[]{:S(2)}, u32[]{:S(2)}) collective-permute-start(bf16[2,128,1024]{2,1,0:T(8,128)(2,1)} %get-tuple-element.58), channel_id=1, source_target_pairs={{0,28},{1,29},{2,30},{3,31},{4,0},{5,1},{6,2},{7,3},{8,4},{9,5},{1... | collective-permute-start | bytes 1572872 | tf_op jit(solution)/shard_map/ppermute | solution.py:32
  129.3 18.3 %all-to-all-start = ((f32[32,4,128]{2,1,0:T(4,128)}), f32[32,4,128]{2,1,0:T(4,128)}, u32[]{:S(2)}, u32[]{:S(2)}) async-start(f32[32,4,128]{2,1,0:T(4,128)} %pad_maximum_fusion.1), calls=%async_computation | async-start | bytes 131072 | tf_op jit(solution)/shard_map/all_to_all | solution.py:284
  142.6 14.0 %collective-permute-start.16 = (bf16[1024,256]{1,0:T(8,128)(2,1)S(1)}, bf16[1024,256]{1,0:T(8,128)(2,1)S(1)}, u32[]{:S(2)}, u32[]{:S(2)}) collective-permute-start(bf16[1024,256]{1,0:T(8,128)(2,1)S(1)} %copy-done.17), channel_id=1, source_target_pairs={{0,224},{1,225},{2,226},{3,227},{4,228},{5,229},{6,230},{7,231},{8... | collective-permute-start | bytes 1572872 | tf_op jit(solution)/shard_map/ppermute | solution.py:32
  150.1 15.2 %all-to-all-start.1 = ((f32[32,2,128]{2,1,0:T(2,128)}), f32[32,2,128]{2,1,0:T(2,128)S(1)}, u32[]{:S(2)}, u32[]{:S(2)}) async-start(f32[32,2,128]{2,1,0:T(2,128)} %broadcast_in_dim.72), calls=%async_computation.1 | async-start | bytes 65536 | tf_op jit(solution)/shard_map/all_to_all | solution.py:296
  158.5 24.7 %collective-permute-start.17 = (bf16[128,1024]{1,0:T(8,128)(2,1)S(1)}, bf16[128,1024]{1,0:T(8,128)(2,1)S(1)}, u32[]{:S(2)}, u32[]{:S(2)}) collective-permute-start(bf16[128,1024]{1,0:T(8,128)(2,1)S(1)} %get-tuple-element.68), channel_id=1, source_target_pairs={{0,32},{1,33},{2,34},{3,35},{4,36},{5,37},{6,38},{7,39},{8,40},{9,... | collective-permute-start | bytes 786440 | tf_op jit(solution)/shard_map/ppermute | solution.py:32
  158.8 24.3 %collective-permute-start.18 = (bf16[128,1024]{1,0:T(8,128)(2,1)S(1)}, bf16[128,1024]{1,0:T(8,128)(2,1)S(1)}, u32[]{:S(2)}, u32[]{:S(2)}) collective-permute-start(bf16[128,1024]{1,0:T(8,128)(2,1)S(1)} %get-tuple-element.69), channel_id=1, source_target_pairs={{0,34},{1,35},{2,32},{3,33},{4,38},{5,39},{6,36},{7,37},{8,42},{9,... | collective-permute-start | bytes 786440 | tf_op jit(solution)/shard_map/ppermute | solution.py:32
  169.1 8.9 %copy-start.6 = (bf16[1,256,1024]{2,1,0:T(8,128)(2,1)S(1)}, bf16[1,256,1024]{2,1,0:T(8,128)(2,1)}, u32[]{:S(2)}) copy-start(bf16[1,256,1024]{2,1,0:T(8,128)(2,1)} %param.11) | copy-start | bytes 1572868
  169.1 8.9 %copy-start.14 = (bf16[16,1,128,256]{3,2,1,0:T(8,128)(2,1)S(1)}, bf16[16,1,128,256]{3,2,1,0:T(8,128)(2,1)}, u32[]{:S(2)}) copy-start(bf16[16,1,128,256]{3,2,1,0:T(8,128)(2,1)} %copy-done.13) | copy-start | bytes 3145732
  (11 other events, 32.2 us)
Sparse Core Ops, SparseCore 0:
  18.2 65.2 all-gather.1

commit v8 on v5

--- a/solution.py
+++ b/solution.py
@@ -17,8 +17,9 @@
 LANE = WIDTH // N_T
 KEYS = 1024
 PACK = LANE + 16
+ORDER = 4
 CUT = 3 * TOK // 4
-SPLIT = TOK // 4
+SPLIT = 3 * TOK // 16
 AXES = ("section", "ts")
 
 
@@ -156,6 +157,25 @@
     )(place, fresh, rows_other, packed_mine, packed_other)
 
 
+def order_kernel(place, mine, other, out):
+    first = place[0] == 0
+    out[:, 0] = jnp.where(first, mine[...], other[...])
+    out[:, 1] = jnp.where(first, other[...], mine[...])
+
+
+def order(place, mine, other):
+    half = pl.BlockSpec((ORDER, OWN, LANE), lambda i, place: (i, 0, 0))
+    return call(
+        order_kernel,
+        (N_T // 2 // ORDER,),
+        [half, half],
+        pl.BlockSpec((ORDER, 2, OWN, LANE), lambda i, place: (i, 0, 0, 0)),
+        jax.ShapeDtypeStruct((N_T // 2, 2, OWN, LANE), F32),
+        200 * TOK * LANE * KEYS,
+        8 * TOK * LANE,
+    )(place, mine, other)
+
+
 def shards(upstream, stashed, returning, key_cotangent, key_weight, norm_gain, lengths):
     lane = lax.axis_index("ts")
     core = lane % 2
@@ -230,16 +250,17 @@
 
     up = move(block(4), z_up, (0,))
     down = move(block(4), z_down, (1,))
-    base = jnp.zeros((N_T // 2, 2, OWN, LANE), F32)
-    up, down, base, late = lax.optimization_barrier(
-        (up, down, base, late, squares_raw, older_first, *older_sq)
-    )[:4]
+    up, down, late = lax.optimization_barrier(
+        (up, down, late, squares_raw, older_first, *older_sq)
+    )[:3]
     late = move(after(late, early), to_previous)
     up = add(block(3), up)
     down = add(block(-3), down)
     up = move(up, z_up)
     down = move(down, z_down)
-    up, down, cot_mine = lax.optimization_barrier((up, down, cot_mine, older_second, early))[:3]
+    up, down, cot_mine, fresh_other = lax.optimization_barrier(
+        (up, down, cot_mine, fresh_other, older_second, early)
+    )[:4]
 
     cots = [cot_mine, move(cot_mine, to_other_core)]
     raw = [
@@ -278,16 +299,17 @@
     curve = [part.reshape(N_T // 2, 1, OWN) for part in curves]
     curve = jnp.where(mine, curve[0], curve[1])
     curve = jnp.broadcast_to(curve.reshape(1, N_T, OWN).astype(BF), (N_T, N_T, OWN))
+    base = order(
+        place, *[(gain * grad).reshape(N_T // 2, OWN, LANE) for grad in grads]
+    ).reshape(TOK, LANE)
     curve = lax.all_to_all(curve, "ts", 0, 0, tiled=True)
-    up, down, fresh_other = lax.optimization_barrier((up, down, fresh_other, curve, late))[:3]
+    up, down, base = lax.optimization_barrier((up, down, base, late))[:3]
     fresh_rate = lax.rsqrt((squares[:2] + fresh_other) / WIDTH + eps)
-    curve = jnp.sum(curve.astype(F32), axis=0).reshape(TOK)
-    pull = older_rate * older_rate / WIDTH * curve
 
     summed = block(0).astype(F32) + up.astype(F32) + down.astype(F32)
     straight = (pick(summed, half) * pick(fresh_rate, half)[:, None]).astype(BF)
     crossed = (pick(summed, 1 - half) * pick(fresh_rate, 1 - half)[:, None]).astype(BF)
-    *cots, pull = lax.optimization_barrier((*cots, pull, straight, crossed))[:3]
+    cots = lax.optimization_barrier((*cots, straight, crossed))[:2]
     straight = move(straight, to_next)
     crossed = move(crossed, to_next_other_half)
     new_keys = (straight.astype(F32) + crossed.astype(F32)).astype(BF)
@@ -298,11 +320,9 @@
         )
         for left, cot in zip(lefts, cots)
     )
-    for index, grad in zip((core, 1 - core), grads):
-        base = lax.dynamic_update_index_in_dim(
-            base, (gain * grad).reshape(N_T // 2, OWN, LANE), index, 1
-        )
-    base = base.reshape(TOK, LANE)
+    curve, base, weight_total = lax.optimization_barrier((curve, base, weight_total))
+    curve = jnp.sum(curve.astype(F32), axis=0).reshape(TOK)
+    pull = older_rate * older_rate / WIDTH * curve
     downstream = jnp.concatenate([early, late], axis=0)
     total = downstream.astype(F32) + base - pull[:, None] * older.astype(F32)
     return (

time: 184 us -> 190 us (1.033); the launches traced: 184 us -> 188 us
  waiting for transfers between devices: 44.4 us -> 51.7 us
  other arithmetic: 22.6 us -> 20.4 us
    convert_element_type x1 -> x0, other arithmetic: 6.11 us -> none  [shards(): total.astype(BF)[None]]
    ppermute x22, waiting for transfers between devices: 40.5 us -> 46.3 us  [move(): return lax.ppermute(value, AXES, pairs)]
    broadcast_in_dim x0 -> x1, other arithmetic: none -> 4.33 us  [shards(): total.astype(BF)[None]]
    unnamed x26 -> x63, local copies, waits for them, and re-layouts: 3.14 us -> 7.34 us
    dynamic_update_slice x2 -> x0, local copies, waits for them, and re-layouts: 3.01 us -> none  [shards(): lax.dynamic_update_index_in_dim(base, (gain * grad).reshape(N_T // 2, OWN...]
    broadcast_in_dim x1 -> x0, local copies, waits for them, and re-layouts: 2.44 us -> none  [shards(): base = jnp.zeros((N_T // 2, 2, OWN, LANE), F32)]
  transfers between devices with their start and end apart: 25 -> 25, of which waited for: 10 -> 7; matrix products, arithmetic and copies ran while one was open for 24% -> 17% of each run, Pallas kernels for 3% -> 3%
where the time goes in v8:
time: 190 us; the launch traced here: 188 us
  starting transfers between devices  67.6 us (36%)
  waiting for transfers between devices  51.7 us (27%)
  other arithmetic  20.4 us (11%)
  local copies, waits for them, and re-layouts  15.3 us (8%)
  between operations  15.3 us (8%)
  matrix products  11.8 us (6%)
  Pallas kernels  5.81 us (3%)
    ppermute x22, starting transfers between devices, move(): return lax.ppermute(value, AXES, pairs)  48.2 us
    ppermute x22, waiting for transfers between devices, move(): return lax.ppermute(value, AXES, pairs)  46.3 us
    all_to_all x1, starting transfers between devices, shards(): curve = lax.all_to_all(curve, 'ts', 0, 0, tiled=True)  10.6 us
    all_to_all x1, starting transfers between devices, shards(): lax.all_to_all(after(squares, packed), 'ts', 0, 0, axis_index_groups=halv...  8.76 us
    unnamed x63, local copies, waits for them, and re-layouts  7.34 us
    dot_general x2, matrix products, shards(): lax.dot_general(left.astype(BF), cot, (((0,), (0,)), ((), ())), preferred...  6.12 us
    convert_element_type x3, other arithmetic, add(): return (a.astype(F32) + b.astype(F32)).astype(BF)  5.7 us
    dot_general x2, matrix products, shards(): lax.dot_general(cot, weights, (((1,), (1,)), ((), ())), preferred_element...  5.68 us
  transfers between devices with their start and end apart: 25, of which 7 were waited for; matrix products, arithmetic and copies ran while one was open for 17% of the time, Pallas kernels for 3%

profile of v8, /device:TPU:1, one launch (start us, length us, event | category | flops | bytes accessed | tf_op | source)
XLA Modules:
  0.0 187.8 jit_solution(16636927116180119769)
XLA Ops:
  7.2 3.7 %collective-permute-start.5 = (bf16[128,1024]{1,0:T(8,128)(2,1)}, bf16[128,1024]{1,0:T(8,128)(2,1)S(1)}, u32[]{:S(2)}, u32[]{:S(2)}) collective-permute-start(bf16[128,1024]{1,0:T(8,128)(2,1)} %bitcast.101), channel_id=1, source_target_pairs={{0,2},{1,3},{2,0},{3,1},{4,6},{5,7},{6,4},{7,5},{8,10},{9,11},{10,... | collective-permute-start | bytes 786440 | tf_op jit(solution)/shard_map/ppermute | solution.py:32
  10.9 5.3 %collective-permute-done.5 = bf16[128,1024]{1,0:T(8,128)(2,1)S(1)} collective-permute-done((bf16[128,1024]{1,0:T(8,128)(2,1)}, bf16[128,1024]{1,0:T(8,128)(2,1)S(1)}, u32[]{:S(2)}, u32[]{:S(2)}) %collective-permute-start.5) | collective-permute-done | bytes 262176 | tf_op jit(solution)/shard_map/ppermute | solution.py:32
  20.0 2.5 %collective-permute-start = (bf16[16,128,256]{2,1,0:T(8,128)(2,1)}, bf16[16,128,256]{2,1,0:T(8,128)(2,1)S(1)}, u32[]{:S(2)}, u32[]{:S(2)}) collective-permute-start(bf16[16,128,256]{2,1,0:T(8,128)(2,1)} %dynamic-slice_bitcast_fusion), channel_id=1, source_target_pairs={{0,1},{1,0},{2,3},{3,2},{4,5},{5,4},{6,7},{7,6},{8,9},{9,8},{10,11... | collective-permute-start | bytes 3145736 | tf_op jit(solution)/shard_map/ppermute | solution.py:32
  22.5 3.6 %collective-permute-start.1 = (bf16[272,1024]{1,0:T(8,128)(2,1)}, bf16[272,1024]{1,0:T(8,128)(2,1)}, u32[]{:S(2)}, u32[]{:S(2)}) collective-permute-start(bf16[272,1024]{1,0:T(8,128)(2,1)} %shard_map.102), channel_id=1, source_target_pairs={{0,224},{1,225},{2,226},{3,227},{4,228},{5,229},{6,230},{7,231},{8... | collective-permute-start | bytes 1671176 | tf_op jit(solution)/shard_map/ppermute | solution.py:32
  26.8 2.4 %multiply_reduce_fusion = bf16[4096]{0:T(1024)(128)(2,1)S(1)} fusion(bf16[1,4096,256]{2,1,0:T(8,128)(2,1)} %param.8), kind=kLoop, calls=%fused_computation.1 | loop fusion | flops 3141632 | bytes 2105344 | tf_op jit(solution)/shard_map/reduce_sum | solution.py:223
  29.9 8.6 %collective-permute-done.1.packed_mine = bf16[272,1024]{1,0:T(8,128)(2,1)} collective-permute-done((bf16[272,1024]{1,0:T(8,128)(2,1)}, bf16[272,1024]{1,0:T(8,128)(2,1)}, u32[]{:S(2)}, u32[]{:S(2)}) %collective-permute-start.1) | collective-permute-done | bytes 557088 | tf_op jit(solution)/shard_map/ppermute | solution.py:32
  40.5 4.3 %collective-permute-start.6 = (bf16[3072,256]{1,0:T(8,128)(2,1)}, bf16[3072,256]{1,0:T(8,128)(2,1)}, u32[]{:S(2)}, u32[]{:S(2)}) collective-permute-start(bf16[3072,256]{1,0:T(8,128)(2,1)} %slice_bitcast_fusion.1), channel_id=1, source_target_pairs={{0,224},{1,225},{2,226},{3,227},{4,228},{5,229},{6,230},{7,231},{8... | collective-permute-start | bytes 4718600 | tf_op jit(solution)/shard_map/ppermute | solution.py:32
  44.8 8.8 %all-to-all-start = ((bf16[16,34,128]{2,1,0:T(8,128)(2,1)}), bf16[16,34,128]{2,1,0:T(8,128)(2,1)S(1)}, u32[]{:S(2)}, u32[]{:S(2)}) async-start(bf16[16,34,128]{2,1,0:T(8,128)(2,1)} %pad_maximum_fusion.1), calls=%async_computation | async-start | bytes 327680 | tf_op jit(solution)/shard_map/all_to_all | solution.py:232
  53.6 4.5 %shard_map.103 = bf16[16,128,1024]{2,1,0:T(8,128)(2,1)S(1)} custom-call(s32[1]{0:T(128)} %bitcast.place, bf16[16,2,128,256]{3,2,1,0:T(8,128)(2,1)S(1)} %bitcast.90, bf16[16,128,256]{2,1,0:T(8,128)(2,1)S(1)} %collective-permute-done.rows_other, bf16[272,1024]{1,0:T(8,128)(2,1)} %collective-permute-done.1.packed_mine, ...), custom_call_target="tpu_custom_call" | custom-call | flops 2147483648 | bytes 7340032 | tf_op jit(solution)/shard_map/pallas_call | solution.py:143
  58.1 2.0 %copy-done = bf16[16,128,1024]{2,1,0:T(8,128)(2,1)} copy-done((bf16[16,128,1024]{2,1,0:T(8,128)(2,1)}, bf16[16,128,1024]{2,1,0:T(8,128)(2,1)S(1)}, u32[]{:S(2)}) %copy-start) | copy-done | bytes 4194328
  60.8 4.5 %collective-permute-start.4 = (bf16[2,128,1024]{2,1,0:T(8,128)(2,1)S(1)}, bf16[2,128,1024]{2,1,0:T(8,128)(2,1)S(1)}, u32[]{:S(2)}, u32[]{:S(2)}) collective-permute-start(bf16[2,128,1024]{2,1,0:T(8,128)(2,1)S(1)} %constant_dynamic-slice_fusion.6), channel_id=1, source_target_pairs={{1,29},{3,31},{5,1},{7,3},{9,5},{11,7},{13,9},{15,11},{17,13},{19,... | collective-permute-start | bytes 1572872 | tf_op jit(solution)/shard_map/ppermute | solution.py:32
  66.8 4.8 %collective-permute-start.8 = (f32[32,128]{1,0:T(8,128)S(1)}, f32[32,128]{1,0:T(8,128)S(1)}, u32[]{:S(2)}, u32[]{:S(2)}) collective-permute-start(f32[32,128]{1,0:T(8,128)S(1)} %slice.34), channel_id=1, source_target_pairs={{0,226},{1,227},{2,224},{3,225},{4,230},{5,231},{6,228},{7,229},{8... | collective-permute-start | bytes 49160 | tf_op jit(solution)/shard_map/ppermute | solution.py:32
  72.8 7.7 %collective-permute-done.7 = f32[32,128]{1,0:T(8,128)S(1)} collective-permute-done((f32[32,128]{1,0:T(8,128)S(1)}, f32[32,128]{1,0:T(8,128)S(1)}, u32[]{:S(2)}, u32[]{:S(2)}) %collective-permute-start.7) | collective-permute-done | bytes 16416 | tf_op jit(solution)/shard_map/ppermute | solution.py:32
  80.5 3.4 %collective-permute-start.12 = (bf16[1024,256]{1,0:T(8,128)(2,1)S(1)}, bf16[1024,256]{1,0:T(8,128)(2,1)S(1)}, u32[]{:S(2)}, u32[]{:S(2)}) collective-permute-start(bf16[1024,256]{1,0:T(8,128)(2,1)S(1)} %slice_bitcast_fusion.2), channel_id=1, source_target_pairs={{0,224},{1,225},{2,226},{3,227},{4,228},{5,229},{6,230},{7,231},{8... | collective-permute-start | bytes 1572872 | tf_op jit(solution)/shard_map/ppermute | solution.py:32
  85.5 5.7 %collective-permute-start.10 = (bf16[2,128,1024]{2,1,0:T(8,128)(2,1)S(1)}, bf16[2,128,1024]{2,1,0:T(8,128)(2,1)S(1)}, u32[]{:S(2)}, u32[]{:S(2)}) collective-permute-start(bf16[2,128,1024]{2,1,0:T(8,128)(2,1)S(1)} %get-tuple-element.72), channel_id=1, source_target_pairs={{0,28},{1,29},{2,30},{3,31},{4,0},{5,1},{6,2},{7,3},{8,4},{9,5},{1... | collective-permute-start | bytes 1572872 | tf_op jit(solution)/shard_map/ppermute | solution.py:32
  92.5 2.5 %collective-permute-start.11 = (f32[2,128]{1,0:T(2,128)S(1)}, f32[2,128]{1,0:T(2,128)S(1)}, u32[]{:S(2)}, u32[]{:S(2)}) collective-permute-start(f32[2,128]{1,0:T(2,128)S(1)} %slice.35), channel_id=1, source_target_pairs={{0,2},{1,3},{2,0},{3,1},{4,6},{5,7},{6,4},{7,5},{8,10},{9,11},{10,... | collective-permute-start | bytes 3080 | tf_op jit(solution)/shard_map/ppermute | solution.py:32
  94.9 10.8 %collective-permute-done.11 = f32[2,128]{1,0:T(2,128)S(1)} collective-permute-done((f32[2,128]{1,0:T(2,128)S(1)}, f32[2,128]{1,0:T(2,128)S(1)}, u32[]{:S(2)}, u32[]{:S(2)}) %collective-permute-start.11) | collective-permute-done | bytes 1056 | tf_op jit(solution)/shard_map/ppermute | solution.py:32
  106.5 1.9 %collective-permute-start.18 = (bf16[2048,1024]{1,0:T(8,128)(2,1)}, bf16[2048,1024]{1,0:T(8,128)(2,1)}, u32[]{:S(2)}, u32[]{:S(2)}) collective-permute-start(bf16[2048,1024]{1,0:T(8,128)(2,1)} %bitcast.115), channel_id=1, source_target_pairs={{0,1},{1,0},{2,3},{3,2},{4,5},{5,4},{6,7},{7,6},{8,9},{9,8},{10,11... | collective-permute-start | bytes 12582920 | tf_op jit(solution)/shard_map/ppermute | solution.py:32
  112.5 1.7 collective-permute-start.14
  114.2 4.0 %collective-permute-start.15 = (bf16[2,128,1024]{2,1,0:T(8,128)(2,1)S(1)}, bf16[2,128,1024]{2,1,0:T(8,128)(2,1)S(1)}, u32[]{:S(2)}, u32[]{:S(2)}) collective-permute-start(bf16[2,128,1024]{2,1,0:T(8,128)(2,1)S(1)} %get-tuple-element.70), channel_id=1, source_target_pairs={{0,28},{1,29},{2,30},{3,31},{4,0},{5,1},{6,2},{7,3},{8,4},{9,5},{1... | collective-permute-start | bytes 1572872 | tf_op jit(solution)/shard_map/ppermute | solution.py:32
  121.8 1.7 copy-done.29
  124.9 5.2 %collective-permute-done.14 = bf16[2,128,1024]{2,1,0:T(8,128)(2,1)S(1)} collective-permute-done((bf16[2,128,1024]{2,1,0:T(8,128)(2,1)S(1)}, bf16[2,128,1024]{2,1,0:T(8,128)(2,1)S(1)}, u32[]{:S(2)}, u32[]{:S(2)}) %collective-permute-start.14) | collective-permute-done | bytes 524320 | tf_op jit(solution)/shard_map/ppermute | solution.py:32
  130.1 2.5 %add_convert_fusion = (bf16[2,128,1024]{2,1,0:T(8,128)(2,1)}, bf16[2,128,1024]{2,1,0:T(8,128)(2,1)}) fusion(bf16[2,128,1024]{2,1,0:T(8,128)(2,1)S(1)} %collective-permute-done.15, bf16[16,128,1024]{2,1,0:T(8,128)(2,1)} %copy-done, s32[]{:T(128)S(6)} %select_n.142, bf16[2,128,1024]{2,1,0:T(8,128)(2,1)S(1)} %collective-permute-done.14, s32[]{:T(128)S(6)} %select_n.125), kind=kLoop, calls=%fused_computation.30 | loop fusion | flops 2097152 | bytes 3145736 | tf_op jit(solution)/shard_map/convert_element_type | solution.py:80
  132.6 2.7 %collective-permute-start.17 = (bf16[2,128,1024]{2,1,0:T(8,128)(2,1)}, bf16[2,128,1024]{2,1,0:T(8,128)(2,1)}, u32[]{:S(2)}, u32[]{:S(2)}) collective-permute-start(bf16[2,128,1024]{2,1,0:T(8,128)(2,1)} %get-tuple-element.68), channel_id=1, source_target_pairs={{0,28},{1,29},{2,30},{3,31},{4,0},{5,1},{6,2},{7,3},{8,4},{9,5},{1... | collective-permute-start | bytes 1572872 | tf_op jit(solution)/shard_map/ppermute | solution.py:32
  135.3 4.3 %fusion.7 = (f32[256]{0:T(256)}, bf16[2048]{0:T(1024)(128)(2,1)}, f32[2048,256]{1,0:T(8,128)S(1)}, f32[2048,256]{1,0:T(8,128)S(1)}, bf16[2048]{0:T(1024)(128)(2,1)}, /*index=5*/f32[256]{0:T(256)}) fusion(bf16[16,1,128,256]{3,2,1,0:T(8,128)(2,1)S(1)} %get-tuple-element.76, f32[256]{0:T(256)S(1)} %bitcast.93, f32[2048,256]{1,0:T(8,128)S(1)} %fusion.22, ...), kind=kOutput, calls=%fused_computation.15 | convolution fusion | flops 1084222976 | bytes 13134848 | tf_op jit(solution)/shard_map/dot_general | solution.py:267
  140.2 8.6 %collective-permute-done.19 = bf16[3328,256]{1,0:T(8,128)(2,1)} collective-permute-done((bf16[3328,256]{1,0:T(8,128)(2,1)}, bf16[3328,256]{1,0:T(8,128)(2,1)}, u32[]{:S(2)}, u32[]{:S(2)}) %collective-permute-start.19) | collective-permute-done | bytes 1703968 | tf_op jit(solution)/shard_map/ppermute | solution.py:32
  148.9 1.7 convert_add_fusion
  152.3 10.6 %all-to-all-start.1 = ((bf16[32,32,128]{2,1,0:T(8,128)(2,1)}), bf16[32,32,128]{2,1,0:T(8,128)(2,1)S(1)}, u32[]{:S(2)}, u32[]{:S(2)}) async-start(bf16[32,32,128]{2,1,0:T(8,128)(2,1)} %broadcast_in_dim.75), calls=%async_computation.1 | async-start | bytes 524288 | tf_op jit(solution)/shard_map/all_to_all | solution.py:305
  163.5 3.7 %fusion.10 = f32[256,1024]{1,0:T(8,128)S(1)} fusion(bf16[2048,1024]{1,0:T(8,128)(2,1)} %collective-permute-done.18, bf16[2048,256]{1,0:T(8,128)(2,1)S(1)} %bitcast.100, f32[2048]{0:T(1024)S(1)} %bitcast.111, f32[256]{0:T(256)S(1)} %bitcast.94), kind=kOutput, calls=%fused_computation.23 | convolution fusion | flops 1075838976 | bytes 6300672 | tf_op jit(solution)/shard_map/dot_general | solution.py:318
  167.3 2.4 %convolution_add_fusion = f32[256,1024]{1,0:T(8,128)} fusion(f32[256,1024]{1,0:T(8,128)S(1)} %fusion.10, bf16[2048,1024]{1,0:T(8,128)(2,1)S(1)} %bitcast.117, bf16[2048,256]{1,0:T(8,128)(2,1)S(1)} %bitcast.99, f32[2048]{0:T(1024)S(1)} %bitcast.109, f32[256]{0:T(256)S(1)} %bitcast.95), kind=kOutput, calls=%fused_computation.22 | convolution fusion | flops 1076101120 | bytes 7349248 | tf_op jit(solution)/shard_map/dot_general | solution.py:318
  170.5 5.4 %all-to-all-done.1 = bf16[32,32,128]{2,1,0:T(8,128)(2,1)S(1)} async-done(((bf16[32,32,128]{2,1,0:T(8,128)(2,1)}), bf16[32,32,128]{2,1,0:T(8,128)(2,1)S(1)}, u32[]{:S(2)}, u32[]{:S(2)}) %all-to-all-start.1) | async-done | bytes 262176 | tf_op jit(solution)/shard_map/all_to_all | solution.py:305
  176.6 4.3 %fusion.8 = bf16[1,4096,256]{2,1,0:T(8,128)(2,1)} fusion(bf16[4096,256]{1,0:T(8,128)(2,1)S(1)} %copy-done.8, f32[4096,256]{1,0:T(8,128)} %bitcast.91, bf16[3328,256]{1,0:T(8,128)(2,1)} %collective-permute-done.19, bf16[768,256]{1,0:T(8,128)(2,1)S(1)} %copy-done.16, f32[4096]{0:T(1024)S(1)} %multiply_bitcast_fusion), kind=kLoop, calls=%fused_computation.16 | loop fusion | flops 9437184 | bytes 10502144 | tf_op jit(solution)/shard_map/broadcast_in_dim | solution.py:330
  (130 shorter events, 26.8 us)
Async XLA Ops:
  7.2 99.3 %all-gather.2.cloned.1.call-start = ((), (), s32[]{:S(2)}) async-start(), calls=%async_computation.2 | async-start | bytes 4718592 | tf_op jit(solution)/shard_map/all_gather | solution.py:209
  7.2 8.9 %collective-permute-start.5 = (bf16[128,1024]{1,0:T(8,128)(2,1)}, bf16[128,1024]{1,0:T(8,128)(2,1)S(1)}, u32[]{:S(2)}, u32[]{:S(2)}) collective-permute-start(bf16[128,1024]{1,0:T(8,128)(2,1)} %bitcast.101), channel_id=1, source_target_pairs={{0,2},{1,3},{2,0},{3,1},{4,6},{5,7},{6,4},{7,5},{8,10},{9,11},{10,... | collective-permute-start | bytes 786440 | tf_op jit(solution)/shard_map/ppermute | solution.py:32
  20.0 33.5 %collective-permute-start = (bf16[16,128,256]{2,1,0:T(8,128)(2,1)}, bf16[16,128,256]{2,1,0:T(8,128)(2,1)S(1)}, u32[]{:S(2)}, u32[]{:S(2)}) collective-permute-start(bf16[16,128,256]{2,1,0:T(8,128)(2,1)} %dynamic-slice_bitcast_fusion), channel_id=1, source_target_pairs={{0,1},{1,0},{2,3},{3,2},{4,5},{5,4},{6,7},{7,6},{8,9},{9,8},{10,11... | collective-permute-start | bytes 3145736 | tf_op jit(solution)/shard_map/ppermute | solution.py:32
  22.5 16.0 %collective-permute-start.1 = (bf16[272,1024]{1,0:T(8,128)(2,1)}, bf16[272,1024]{1,0:T(8,128)(2,1)}, u32[]{:S(2)}, u32[]{:S(2)}) collective-permute-start(bf16[272,1024]{1,0:T(8,128)(2,1)} %shard_map.102), channel_id=1, source_target_pairs={{0,224},{1,225},{2,226},{3,227},{4,228},{5,229},{6,230},{7,231},{8... | collective-permute-start | bytes 1671176 | tf_op jit(solution)/shard_map/ppermute | solution.py:32
  38.5 15.1 %collective-permute-start.2 = (bf16[272,1024]{1,0:T(8,128)(2,1)}, bf16[272,1024]{1,0:T(8,128)(2,1)}, u32[]{:S(2)}, u32[]{:S(2)}) collective-permute-start(bf16[272,1024]{1,0:T(8,128)(2,1)} %collective-permute-done.1.packed_mine), channel_id=1, source_target_pairs={{0,1},{1,0},{2,3},{3,2},{4,5},{5,4},{6,7},{7,6},{8,9},{9,8},{10,11... | collective-permute-start | bytes 1671176 | tf_op jit(solution)/shard_map/ppermute | solution.py:32
  40.5 43.4 %collective-permute-start.6 = (bf16[3072,256]{1,0:T(8,128)(2,1)}, bf16[3072,256]{1,0:T(8,128)(2,1)}, u32[]{:S(2)}, u32[]{:S(2)}) collective-permute-start(bf16[3072,256]{1,0:T(8,128)(2,1)} %slice_bitcast_fusion.1), channel_id=1, source_target_pairs={{0,224},{1,225},{2,226},{3,227},{4,228},{5,229},{6,230},{7,231},{8... | collective-permute-start | bytes 4718600 | tf_op jit(solution)/shard_map/ppermute | solution.py:32
  44.8 21.9 %all-to-all-start = ((bf16[16,34,128]{2,1,0:T(8,128)(2,1)}), bf16[16,34,128]{2,1,0:T(8,128)(2,1)S(1)}, u32[]{:S(2)}, u32[]{:S(2)}) async-start(bf16[16,34,128]{2,1,0:T(8,128)(2,1)} %pad_maximum_fusion.1), calls=%async_computation | async-start | bytes 327680 | tf_op jit(solution)/shard_map/all_to_all | solution.py:232
  60.1 23.8 %collective-permute-start.3 = (bf16[2,128,1024]{2,1,0:T(8,128)(2,1)S(1)}, bf16[2,128,1024]{2,1,0:T(8,128)(2,1)S(1)}, u32[]{:S(2)}, u32[]{:S(2)}) collective-permute-start(bf16[2,128,1024]{2,1,0:T(8,128)(2,1)S(1)} %constant_dynamic-slice_fusion.6), channel_id=1, source_target_pairs={{0,4},{2,6},{4,8},{6,10},{8,12},{10,14},{12,16},{14,18},{16,20},{1... | collective-permute-start | bytes 1572872 | tf_op jit(solution)/shard_map/ppermute | solution.py:32
  60.8 23.1 %collective-permute-start.4 = (bf16[2,128,1024]{2,1,0:T(8,128)(2,1)S(1)}, bf16[2,128,1024]{2,1,0:T(8,128)(2,1)S(1)}, u32[]{:S(2)}, u32[]{:S(2)}) collective-permute-start(bf16[2,128,1024]{2,1,0:T(8,128)(2,1)S(1)} %constant_dynamic-slice_fusion.6), channel_id=1, source_target_pairs={{1,29},{3,31},{5,1},{7,3},{9,5},{11,7},{13,9},{15,11},{17,13},{19,... | collective-permute-start | bytes 1572872 | tf_op jit(solution)/shard_map/ppermute | solution.py:32
  66.7 13.8 %collective-permute-start.7 = (f32[32,128]{1,0:T(8,128)S(1)}, f32[32,128]{1,0:T(8,128)S(1)}, u32[]{:S(2)}, u32[]{:S(2)}) collective-permute-start(f32[32,128]{1,0:T(8,128)S(1)} %slice.34), channel_id=1, source_target_pairs={{0,224},{1,225},{2,226},{3,227},{4,228},{5,229},{6,230},{7,231},{8... | collective-permute-start | bytes 49160 | tf_op jit(solution)/shard_map/ppermute | solution.py:32
  66.8 13.7 %collective-permute-start.8 = (f32[32,128]{1,0:T(8,128)S(1)}, f32[32,128]{1,0:T(8,128)S(1)}, u32[]{:S(2)}, u32[]{:S(2)}) collective-permute-start(f32[32,128]{1,0:T(8,128)S(1)} %slice.34), channel_id=1, source_target_pairs={{0,226},{1,227},{2,224},{3,225},{4,230},{5,231},{6,228},{7,229},{8... | collective-permute-start | bytes 49160 | tf_op jit(solution)/shard_map/ppermute | solution.py:32
  80.5 25.2 %collective-permute-start.12 = (bf16[1024,256]{1,0:T(8,128)(2,1)S(1)}, bf16[1024,256]{1,0:T(8,128)(2,1)S(1)}, u32[]{:S(2)}, u32[]{:S(2)}) collective-permute-start(bf16[1024,256]{1,0:T(8,128)(2,1)S(1)} %slice_bitcast_fusion.2), channel_id=1, source_target_pairs={{0,224},{1,225},{2,226},{3,227},{4,228},{5,229},{6,230},{7,231},{8... | collective-permute-start | bytes 1572872 | tf_op jit(solution)/shard_map/ppermute | solution.py:32
  85.5 20.2 %collective-permute-start.10 = (bf16[2,128,1024]{2,1,0:T(8,128)(2,1)S(1)}, bf16[2,128,1024]{2,1,0:T(8,128)(2,1)S(1)}, u32[]{:S(2)}, u32[]{:S(2)}) collective-permute-start(bf16[2,128,1024]{2,1,0:T(8,128)(2,1)S(1)} %get-tuple-element.72), channel_id=1, source_target_pairs={{0,28},{1,29},{2,30},{3,31},{4,0},{5,1},{6,2},{7,3},{8,4},{9,5},{1... | collective-permute-start | bytes 1572872 | tf_op jit(solution)/shard_map/ppermute | solution.py:32
  91.2 15.3 %collective-permute-start.9 = (bf16[2,128,1024]{2,1,0:T(8,128)(2,1)S(1)}, bf16[2,128,1024]{2,1,0:T(8,128)(2,1)S(1)}, u32[]{:S(2)}, u32[]{:S(2)}) collective-permute-start(bf16[2,128,1024]{2,1,0:T(8,128)(2,1)S(1)} %get-tuple-element.73), channel_id=1, source_target_pairs={{0,4},{1,5},{2,6},{3,7},{4,8},{5,9},{6,10},{7,11},{8,12},{9,13},{1... | collective-permute-start | bytes 1572872 | tf_op jit(solution)/shard_map/ppermute | solution.py:32
  92.2 13.5 %collective-permute-start.13 = (bf16[768,256]{1,0:T(8,128)(2,1)S(1)}, bf16[768,256]{1,0:T(8,128)(2,1)S(1)}, u32[]{:S(2)}, u32[]{:S(2)}) collective-permute-start(bf16[768,256]{1,0:T(8,128)(2,1)S(1)} %slice_bitcast_fusion.3), channel_id=1, source_target_pairs={{0,224},{1,225},{2,226},{3,227},{4,228},{5,229},{6,230},{7,231},{8... | collective-permute-start | bytes 1179656 | tf_op jit(solution)/shard_map/ppermute | solution.py:32
  92.5 13.3 %collective-permute-start.11 = (f32[2,128]{1,0:T(2,128)S(1)}, f32[2,128]{1,0:T(2,128)S(1)}, u32[]{:S(2)}, u32[]{:S(2)}) collective-permute-start(f32[2,128]{1,0:T(2,128)S(1)} %slice.35), channel_id=1, source_target_pairs={{0,2},{1,3},{2,0},{3,1},{4,6},{5,7},{6,4},{7,5},{8,10},{9,11},{10,... | collective-permute-start | bytes 3080 | tf_op jit(solution)/shard_map/ppermute | solution.py:32
  106.5 28.8 %collective-permute-start.18 = (bf16[2048,1024]{1,0:T(8,128)(2,1)}, bf16[2048,1024]{1,0:T(8,128)(2,1)}, u32[]{:S(2)}, u32[]{:S(2)}) collective-permute-start(bf16[2048,1024]{1,0:T(8,128)(2,1)} %bitcast.115), channel_id=1, source_target_pairs={{0,1},{1,0},{2,3},{3,2},{4,5},{5,4},{6,7},{7,6},{8,9},{9,8},{10,11... | collective-permute-start | bytes 12582920 | tf_op jit(solution)/shard_map/ppermute | solution.py:32
  109.7 39.1 %collective-permute-start.19 = (bf16[3328,256]{1,0:T(8,128)(2,1)}, bf16[3328,256]{1,0:T(8,128)(2,1)}, u32[]{:S(2)}, u32[]{:S(2)}) collective-permute-start(bf16[3328,256]{1,0:T(8,128)(2,1)} %slice_bitcast_fusion), channel_id=1, source_target_pairs={{0,224},{1,225},{2,226},{3,227},{4,228},{5,229},{6,230},{7,231},{8... | collective-permute-start | bytes 5111816 | tf_op jit(solution)/shard_map/ppermute | solution.py:32
  112.5 17.7 %collective-permute-start.14 = (bf16[2,128,1024]{2,1,0:T(8,128)(2,1)S(1)}, bf16[2,128,1024]{2,1,0:T(8,128)(2,1)S(1)}, u32[]{:S(2)}, u32[]{:S(2)}) collective-permute-start(bf16[2,128,1024]{2,1,0:T(8,128)(2,1)S(1)} %get-tuple-element.71), channel_id=1, source_target_pairs={{0,4},{1,5},{2,6},{3,7},{4,8},{5,9},{6,10},{7,11},{8,12},{9,13},{1... | collective-permute-start | bytes 1572872 | tf_op jit(solution)/shard_map/ppermute | solution.py:32
  114.2 15.9 %collective-permute-start.15 = (bf16[2,128,1024]{2,1,0:T(8,128)(2,1)S(1)}, bf16[2,128,1024]{2,1,0:T(8,128)(2,1)S(1)}, u32[]{:S(2)}, u32[]{:S(2)}) collective-permute-start(bf16[2,128,1024]{2,1,0:T(8,128)(2,1)S(1)} %get-tuple-element.70), channel_id=1, source_target_pairs={{0,28},{1,29},{2,30},{3,31},{4,0},{5,1},{6,2},{7,3},{8,4},{9,5},{1... | collective-permute-start | bytes 1572872 | tf_op jit(solution)/shard_map/ppermute | solution.py:32
  121.1 14.2 %copy-start.11 = (bf16[16,1,128,256]{3,2,1,0:T(8,128)(2,1)}, bf16[16,1,128,256]{3,2,1,0:T(8,128)(2,1)S(1)}, u32[]{:S(2)}) copy-start(bf16[16,1,128,256]{3,2,1,0:T(8,128)(2,1)S(1)} %get-tuple-element.77) | copy-start | bytes 3145732
  121.1 14.2 %copy-start.13 = (bf16[16,1,128,256]{3,2,1,0:T(8,128)(2,1)}, bf16[16,1,128,256]{3,2,1,0:T(8,128)(2,1)S(1)}, u32[]{:S(2)}) copy-start(bf16[16,1,128,256]{3,2,1,0:T(8,128)(2,1)S(1)} %get-tuple-element.76) | copy-start | bytes 3145732
  121.1 14.2 %copy-start.17 = (f32[32,128]{1,0:T(8,128)}, f32[32,128]{1,0:T(8,128)S(1)}, u32[]{:S(2)}) copy-start(f32[32,128]{1,0:T(8,128)S(1)} %add_rsqrt_fusion) | copy-start | bytes 49156
  132.6 16.2 %collective-permute-start.16 = (bf16[2,128,1024]{2,1,0:T(8,128)(2,1)}, bf16[2,128,1024]{2,1,0:T(8,128)(2,1)}, u32[]{:S(2)}, u32[]{:S(2)}) collective-permute-start(bf16[2,128,1024]{2,1,0:T(8,128)(2,1)} %get-tuple-element.69), channel_id=1, source_target_pairs={{0,4},{1,5},{2,6},{3,7},{4,8},{5,9},{6,10},{7,11},{8,12},{9,13},{1... | collective-permute-start | bytes 1572872 | tf_op jit(solution)/shard_map/ppermute | solution.py:32
  132.6 16.2 %collective-permute-start.17 = (bf16[2,128,1024]{2,1,0:T(8,128)(2,1)}, bf16[2,128,1024]{2,1,0:T(8,128)(2,1)}, u32[]{:S(2)}, u32[]{:S(2)}) collective-permute-start(bf16[2,128,1024]{2,1,0:T(8,128)(2,1)} %get-tuple-element.68), channel_id=1, source_target_pairs={{0,28},{1,29},{2,30},{3,31},{4,0},{5,1},{6,2},{7,3},{8,4},{9,5},{1... | collective-permute-start | bytes 1572872 | tf_op jit(solution)/shard_map/ppermute | solution.py:32
  148.8 14.1 %copy-start.27 = (f32[256]{0:T(256)S(1)}, f32[256]{0:T(256)}, u32[]{:S(2)}) copy-start(f32[256]{0:T(256)} %get-tuple-element.66) | copy-start | bytes 3076
  148.9 14.6 %copy-start.6 = (f32[1,256]{1,0:T(1,128)S(1)}, f32[1,256]{1,0:T(1,128)}, u32[]{:S(2)}) copy-start(f32[1,256]{1,0:T(1,128)} %gain.1) | copy-start | bytes 3076
  148.9 14.6 %copy-start.14 = (bf16[16,1,128,256]{3,2,1,0:T(8,128)(2,1)S(1)}, bf16[16,1,128,256]{3,2,1,0:T(8,128)(2,1)}, u32[]{:S(2)}) copy-start(bf16[16,1,128,256]{3,2,1,0:T(8,128)(2,1)} %copy-done.13) | copy-start | bytes 3145732
  148.9 14.6 %copy-start.21 = (f32[16,1,128]{2,1,0:T(1,128)S(1)}, f32[16,1,128]{2,1,0:T(1,128)}, u32[]{:S(2)}) copy-start(f32[16,1,128]{2,1,0:T(1,128)} %copy-done.20) | copy-start | bytes 24580
  151.4 18.3 %collective-permute-start.20 = (bf16[128,1024]{1,0:T(8,128)(2,1)}, bf16[128,1024]{1,0:T(8,128)(2,1)S(1)}, u32[]{:S(2)}, u32[]{:S(2)}) collective-permute-start(bf16[128,1024]{1,0:T(8,128)(2,1)} %get-tuple-element.78), channel_id=1, source_target_pairs={{0,32},{1,33},{2,34},{3,35},{4,36},{5,37},{6,38},{7,39},{8,40},{9,... | collective-permute-start | bytes 786440 | tf_op jit(solution)/shard_map/ppermute | solution.py:32
  151.4 18.3 %collective-permute-start.21 = (bf16[128,1024]{1,0:T(8,128)(2,1)S(1)}, bf16[128,1024]{1,0:T(8,128)(2,1)S(1)}, u32[]{:S(2)}, u32[]{:S(2)}) collective-permute-start(bf16[128,1024]{1,0:T(8,128)(2,1)S(1)} %get-tuple-element.79), channel_id=1, source_target_pairs={{0,34},{1,35},{2,32},{3,33},{4,38},{5,39},{6,36},{7,37},{8,42},{9,... | collective-permute-start | bytes 786440 | tf_op jit(solution)/shard_map/ppermute | solution.py:32
  152.3 23.5 %all-to-all-start.1 = ((bf16[32,32,128]{2,1,0:T(8,128)(2,1)}), bf16[32,32,128]{2,1,0:T(8,128)(2,1)S(1)}, u32[]{:S(2)}, u32[]{:S(2)}) async-start(bf16[32,32,128]{2,1,0:T(8,128)(2,1)} %broadcast_in_dim.75), calls=%async_computation.1 | async-start | bytes 524288 | tf_op jit(solution)/shard_map/all_to_all | solution.py:305
  (24 other events, 177.2 us)
Sparse Core Ops, SparseCore 0:
  18.2 68.6 all-gather.1

commit v9 on v5

--- a/solution.py
+++ b/solution.py
@@ -17,8 +17,7 @@
 LANE = WIDTH // N_T
 KEYS = 1024
 PACK = LANE + 16
-CUT = 3 * TOK // 4
-SPLIT = TOK // 4
+CUT = TOK // 2
 AXES = ("section", "ts")
 
 
@@ -197,6 +196,14 @@
         lax.dynamic_index_in_dim(rows_other, 1 - core, 1, keepdims=False), to_other_core
     )
 
+    packed_other = move(packed, to_other_core)
+    partial = forward(place, rows, rows_other, packed, packed_other)
+
+    def block(distance):
+        return lax.dynamic_slice_in_dim(partial, ((z + distance) % N_Z) * 2, 2, 0)
+
+    older_second = move(after(saved[CUT:], partial), to_mirror)
+
     fresh_wide = fresh.astype(F32)
     saved_wide = saved.astype(F32)
     fresh_part = jnp.sum(fresh_wide * fresh_wide, axis=1).reshape(N_Z, 2, 2, OWN)
@@ -210,36 +217,25 @@
     )
     halves = [[q * 4 + h * 2 + c for q in range(N_Z) for c in range(2)] for h in range(2)]
     squares = lax.all_to_all(
-        after(squares, packed), "ts", 0, 0, axis_index_groups=halves, tiled=True
+        after(squares, older_first), "ts", 0, 0, axis_index_groups=halves, tiled=True
     )
     squares_raw = squares
     squares = jnp.sum(squares.astype(F32), axis=0)
     older_sq = [move(squares[2:], to_mirror), move(squares[2:], to_mirror_other_half)]
     fresh_other = move(after(squares[:2], *older_sq), to_other_half)
 
-    older_second = move(after(saved[CUT:], *older_sq), to_mirror)
-
-    early = move(after(returning[0, :SPLIT], *older_sq), to_previous)
-    late = returning[0, SPLIT:]
-
-    packed_other = move(packed, to_other_core)
-    partial = forward(place, rows, rows_other, packed, packed_other)
-
-    def block(distance):
-        return lax.dynamic_slice_in_dim(partial, ((z + distance) % N_Z) * 2, 2, 0)
+    downstream = move(after(returning[0], *older_sq), to_previous)
 
     up = move(block(4), z_up, (0,))
     down = move(block(4), z_down, (1,))
-    base = jnp.zeros((N_T // 2, 2, OWN, LANE), F32)
-    up, down, base, late = lax.optimization_barrier(
-        (up, down, base, late, squares_raw, older_first, *older_sq)
-    )[:4]
-    late = move(after(late, early), to_previous)
+    up, down = lax.optimization_barrier((up, down, older_first, squares_raw))[:2]
     up = add(block(3), up)
     down = add(block(-3), down)
     up = move(up, z_up)
     down = move(down, z_down)
-    up, down, cot_mine = lax.optimization_barrier((up, down, cot_mine, older_second, early))[:3]
+    up, down, cot_mine = lax.optimization_barrier(
+        (up, down, cot_mine, older_second, *older_sq)
+    )[:3]
 
     cots = [cot_mine, move(cot_mine, to_other_core)]
     raw = [
@@ -253,7 +249,7 @@
     )[:4]
     up = move(up, z_up)
     down = move(down, z_down)
-    up, down, raw[0] = lax.optimization_barrier((up, down, raw[0]))
+    up, down, raw[0], fresh_other = lax.optimization_barrier((up, down, raw[0], fresh_other))
     up = add(block(1), up)
     down = add(block(-1), down)
     up = move(up, z_up)
@@ -279,7 +275,7 @@
     curve = jnp.where(mine, curve[0], curve[1])
     curve = jnp.broadcast_to(curve.reshape(1, N_T, OWN).astype(BF), (N_T, N_T, OWN))
     curve = lax.all_to_all(curve, "ts", 0, 0, tiled=True)
-    up, down, fresh_other = lax.optimization_barrier((up, down, fresh_other, curve, late))[:3]
+    up, down = lax.optimization_barrier((up, down, curve, downstream))[:2]
     fresh_rate = lax.rsqrt((squares[:2] + fresh_other) / WIDTH + eps)
     curve = jnp.sum(curve.astype(F32), axis=0).reshape(TOK)
     pull = older_rate * older_rate / WIDTH * curve
@@ -298,12 +294,12 @@
         )
         for left, cot in zip(lefts, cots)
     )
+    base = jnp.zeros((N_T // 2, 2, OWN, LANE), F32)
     for index, grad in zip((core, 1 - core), grads):
         base = lax.dynamic_update_index_in_dim(
             base, (gain * grad).reshape(N_T // 2, OWN, LANE), index, 1
         )
     base = base.reshape(TOK, LANE)
-    downstream = jnp.concatenate([early, late], axis=0)
     total = downstream.astype(F32) + base - pull[:, None] * older.astype(F32)
     return (
         new_keys[None],

time: 184 us -> 186 us (1.011)
  waiting for transfers between devices: 44.4 us -> 50.7 us
  other arithmetic: 22.6 us -> 17.7 us
    all_to_all x1, waiting for transfers between devices: 0.01 us -> 7.93 us  [shards(): lax.all_to_all(after(squares, older_first), 'ts', 0, 0, axis_index_groups...]
    ppermute x22 -> x21, waiting for transfers between devices: 40.5 us -> 35.4 us  [move(): return lax.ppermute(value, AXES, pairs)]
    all_to_all x1, waiting for transfers between devices: 3.87 us -> 7.35 us  [shards(): curve = lax.all_to_all(curve, 'ts', 0, 0, tiled=True)]
    unnamed x26 -> x33, local copies, waits for them, and re-layouts: 3.14 us -> 6.38 us
    squeeze x2 -> x0, local copies, waits for them, and re-layouts: 2.34 us -> none  [the longest x1 1.26 us: shards(): late = returning[0, SPLIT:]]
    slice x2 -> x1, local copies, waits for them, and re-layouts: 3.73 us -> 1.53 us  [shards(): older_second = move(after(saved[CUT:], partial), to_mirror)]
    ppermute x22 -> x21, starting transfers between devices: 48.8 us -> 49.6 us  [move(): return lax.ppermute(value, AXES, pairs)]
  transfers between devices with their start and end apart: 25 -> 24, of which waited for: 10 -> 10; matrix products, arithmetic and copies ran while one was open for 24% -> 20% of each run, Pallas kernels for 3% -> 3%
where the time goes in v9:
time: 186 us
  starting transfers between devices  68.6 us (37%)
  waiting for transfers between devices  50.7 us (27%)
  other arithmetic  17.7 us (10%)
  local copies, waits for them, and re-layouts  15.6 us (8%)
  between operations  15.2 us (8%)
  matrix products  12.7 us (7%)
  Pallas kernels  5.31 us (3%)
    ppermute x21, starting transfers between devices, move(): return lax.ppermute(value, AXES, pairs)  49.6 us
    ppermute x21, waiting for transfers between devices, move(): return lax.ppermute(value, AXES, pairs)  35.4 us
    all_to_all x1, starting transfers between devices, shards(): curve = lax.all_to_all(curve, 'ts', 0, 0, tiled=True)  9.88 us
    all_to_all x1, starting transfers between devices, shards(): lax.all_to_all(after(squares, older_first), 'ts', 0, 0, axis_index_groups...  9.06 us
    all_to_all x1, waiting for transfers between devices, shards(): lax.all_to_all(after(squares, older_first), 'ts', 0, 0, axis_index_groups...  7.93 us
    all_to_all x1, waiting for transfers between devices, shards(): curve = lax.all_to_all(curve, 'ts', 0, 0, tiled=True)  7.35 us
    dot_general x2, matrix products, shards(): lax.dot_general(cot, weights, (((1,), (1,)), ((), ())), preferred_element...  6.73 us
    unnamed x33, local copies, waits for them, and re-layouts  6.38 us
  transfers between devices with their start and end apart: 24, of which 10 were waited for; matrix products, arithmetic and copies ran while one was open for 20% of the time, Pallas kernels for 3%

profile of v9, /device:TPU:1, one launch (start us, length us, event | category | flops | bytes accessed | tf_op | source)
XLA Modules:
  0.0 185.7 jit_solution(12570506385716421403)
XLA Ops:
  7.2 3.7 %collective-permute-start.5 = (bf16[128,1024]{1,0:T(8,128)(2,1)}, bf16[128,1024]{1,0:T(8,128)(2,1)S(1)}, u32[]{:S(2)}, u32[]{:S(2)}) collective-permute-start(bf16[128,1024]{1,0:T(8,128)(2,1)} %bitcast.107), channel_id=1, source_target_pairs={{0,2},{1,3},{2,0},{3,1},{4,6},{5,7},{6,4},{7,5},{8,10},{9,11},{10,... | collective-permute-start | bytes 786440 | tf_op jit(solution)/shard_map/ppermute | solution.py:30
  10.9 5.3 %collective-permute-done.5 = bf16[128,1024]{1,0:T(8,128)(2,1)S(1)} collective-permute-done((bf16[128,1024]{1,0:T(8,128)(2,1)}, bf16[128,1024]{1,0:T(8,128)(2,1)S(1)}, u32[]{:S(2)}, u32[]{:S(2)}) %collective-permute-start.5) | collective-permute-done | bytes 262176 | tf_op jit(solution)/shard_map/ppermute | solution.py:30
  19.0 4.5 %collective-permute-start.1 = (bf16[272,1024]{1,0:T(8,128)(2,1)}, bf16[272,1024]{1,0:T(8,128)(2,1)}, u32[]{:S(2)}, u32[]{:S(2)}) collective-permute-start(bf16[272,1024]{1,0:T(8,128)(2,1)} %shard_map.102), channel_id=1, source_target_pairs={{0,224},{1,225},{2,226},{3,227},{4,228},{5,229},{6,230},{7,231},{8... | collective-permute-start | bytes 1671176 | tf_op jit(solution)/shard_map/ppermute | solution.py:30
  26.3 7.8 %collective-permute-done.1.packed_mine = bf16[272,1024]{1,0:T(8,128)(2,1)} collective-permute-done((bf16[272,1024]{1,0:T(8,128)(2,1)}, bf16[272,1024]{1,0:T(8,128)(2,1)}, u32[]{:S(2)}, u32[]{:S(2)}) %collective-permute-start.1) | collective-permute-done | bytes 557088 | tf_op jit(solution)/shard_map/ppermute | solution.py:30
  34.2 2.5 %collective-permute-start.2 = (bf16[272,1024]{1,0:T(8,128)(2,1)}, bf16[272,1024]{1,0:T(8,128)(2,1)}, u32[]{:S(2)}, u32[]{:S(2)}) collective-permute-start(bf16[272,1024]{1,0:T(8,128)(2,1)} %collective-permute-done.1.packed_mine), channel_id=1, source_target_pairs={{0,1},{1,0},{2,3},{3,2},{4,5},{5,4},{6,7},{7,6},{8,9},{9,8},{10,11... | collective-permute-start | bytes 1671176 | tf_op jit(solution)/shard_map/ppermute | solution.py:30
  38.2 4.3 %collective-permute-start.6 = (bf16[2048,256]{1,0:T(8,128)(2,1)}, bf16[2048,256]{1,0:T(8,128)(2,1)}, u32[]{:S(2)}, u32[]{:S(2)}) collective-permute-start(bf16[2048,256]{1,0:T(8,128)(2,1)} %get-tuple-element.31), channel_id=1, source_target_pairs={{0,224},{1,225},{2,226},{3,227},{4,228},{5,229},{6,230},{7,231},{8... | collective-permute-start | bytes 3145736 | tf_op jit(solution)/shard_map/ppermute | solution.py:30
  43.2 4.5 %shard_map.103 = bf16[16,128,1024]{2,1,0:T(8,128)(2,1)S(1)} custom-call(s32[1]{0:T(128)} %bitcast.place, bf16[16,2,128,256]{3,2,1,0:T(8,128)(2,1)S(1)} %bitcast.96, bf16[16,128,256]{2,1,0:T(8,128)(2,1)S(1)} %collective-permute-done.rows_other, bf16[272,1024]{1,0:T(8,128)(2,1)} %collective-permute-done.1.packed_mine, ...), custom_call_target="tpu_custom_call" | custom-call | flops 2147483648 | bytes 7340032 | tf_op jit(solution)/shard_map/pallas_call | solution.py:141
  47.6 2.0 %copy-done = bf16[16,128,1024]{2,1,0:T(8,128)(2,1)} copy-done((bf16[16,128,1024]{2,1,0:T(8,128)(2,1)}, bf16[16,128,1024]{2,1,0:T(8,128)(2,1)S(1)}, u32[]{:S(2)}) %copy-start) | copy-done | bytes 4194328
  51.3 7.5 %collective-permute-start.4 = (bf16[2,128,1024]{2,1,0:T(8,128)(2,1)S(1)}, bf16[2,128,1024]{2,1,0:T(8,128)(2,1)}, u32[]{:S(2)}, u32[]{:S(2)}) collective-permute-start(bf16[2,128,1024]{2,1,0:T(8,128)(2,1)S(1)} %constant_dynamic-slice_fusion.6), channel_id=1, source_target_pairs={{1,29},{3,31},{5,1},{7,3},{9,5},{11,7},{13,9},{15,11},{17,13},{19,... | collective-permute-start | bytes 1572872 | tf_op jit(solution)/shard_map/ppermute | solution.py:30
  60.2 6.1 %collective-permute-done.6 = bf16[2048,256]{1,0:T(8,128)(2,1)} collective-permute-done((bf16[2048,256]{1,0:T(8,128)(2,1)}, bf16[2048,256]{1,0:T(8,128)(2,1)}, u32[]{:S(2)}, u32[]{:S(2)}) %collective-permute-start.6) | collective-permute-done | bytes 1048608 | tf_op jit(solution)/shard_map/ppermute | solution.py:30
  66.3 9.1 %all-to-all-start = ((bf16[16,34,128]{2,1,0:T(8,128)(2,1)}), bf16[16,34,128]{2,1,0:T(8,128)(2,1)S(1)}, u32[]{:S(2)}, u32[]{:S(2)}) async-start(bf16[16,34,128]{2,1,0:T(8,128)(2,1)} %pad_maximum_fusion.1), calls=%async_computation | async-start | bytes 327680 | tf_op jit(solution)/shard_map/all_to_all | solution.py:219
  75.4 3.7 %collective-permute-start.9 = (bf16[2048,256]{1,0:T(8,128)(2,1)S(1)}, bf16[2048,256]{1,0:T(8,128)(2,1)S(1)}, u32[]{:S(2)}, u32[]{:S(2)}) collective-permute-start(bf16[2048,256]{1,0:T(8,128)(2,1)S(1)} %copy-done.13), channel_id=1, source_target_pairs={{0,224},{1,225},{2,226},{3,227},{4,228},{5,229},{6,230},{7,231},{8... | collective-permute-start | bytes 3145736 | tf_op jit(solution)/shard_map/ppermute | solution.py:30
  79.1 7.9 %all-to-all-done = bf16[16,34,128]{2,1,0:T(8,128)(2,1)S(1)} async-done(((bf16[16,34,128]{2,1,0:T(8,128)(2,1)}), bf16[16,34,128]{2,1,0:T(8,128)(2,1)S(1)}, u32[]{:S(2)}, u32[]{:S(2)}) %all-to-all-start) | async-done | bytes 139296 | tf_op jit(solution)/shard_map/all_to_all | solution.py:219
  87.0 1.9 %add_convert_fusion.4 = (bf16[2,128,1024]{2,1,0:T(8,128)(2,1)S(1)}, bf16[2,128,1024]{2,1,0:T(8,128)(2,1)S(1)}) fusion(bf16[2,128,1024]{2,1,0:T(8,128)(2,1)} %collective-permute-done.4, bf16[16,128,1024]{2,1,0:T(8,128)(2,1)} %copy-done, s32[]{:T(128)S(6)} %select_n.136, bf16[2,128,1024]{2,1,0:T(8,128)(2,1)} %collective-permute-done.3, s32[]{:T(128)S(6)} %select_n.132), kind=kLoop, calls=%fused_computation.35 | loop fusion | flops 2097152 | bytes 3145736 | tf_op jit(solution)/shard_map/convert_element_type | solution.py:78
  89.0 2.7 %collective-permute-start.8 = (bf16[2,128,1024]{2,1,0:T(8,128)(2,1)S(1)}, bf16[2,128,1024]{2,1,0:T(8,128)(2,1)}, u32[]{:S(2)}, u32[]{:S(2)}) collective-permute-start(bf16[2,128,1024]{2,1,0:T(8,128)(2,1)S(1)} %get-tuple-element.62), channel_id=1, source_target_pairs={{0,28},{1,29},{2,30},{3,31},{4,0},{5,1},{6,2},{7,3},{8,4},{9,5},{1... | collective-permute-start | bytes 1572872 | tf_op jit(solution)/shard_map/ppermute | solution.py:30
  91.7 3.7 %collective-permute-start.10 = (f32[32,128]{1,0:T(8,128)S(1)}, f32[32,128]{1,0:T(8,128)S(1)}, u32[]{:S(2)}, u32[]{:S(2)}) collective-permute-start(f32[32,128]{1,0:T(8,128)S(1)} %slice.26), channel_id=1, source_target_pairs={{0,224},{1,225},{2,226},{3,227},{4,228},{5,229},{6,230},{7,231},{8... | collective-permute-start | bytes 49160 | tf_op jit(solution)/shard_map/ppermute | solution.py:30
  96.8 6.0 %collective-permute-done.10 = f32[32,128]{1,0:T(8,128)S(1)} collective-permute-done((f32[32,128]{1,0:T(8,128)S(1)}, f32[32,128]{1,0:T(8,128)S(1)}, u32[]{:S(2)}, u32[]{:S(2)}) %collective-permute-start.10) | collective-permute-done | bytes 16416 | tf_op jit(solution)/shard_map/ppermute | solution.py:30
  105.5 2.5 %collective-permute-start.14 = (f32[2,128]{1,0:T(2,128)S(1)}, f32[2,128]{1,0:T(2,128)S(1)}, u32[]{:S(2)}, u32[]{:S(2)}) collective-permute-start(f32[2,128]{1,0:T(2,128)S(1)} %slice.27), channel_id=1, source_target_pairs={{0,2},{1,3},{2,0},{3,1},{4,6},{5,7},{6,4},{7,5},{8,10},{9,11},{10,... | collective-permute-start | bytes 3080 | tf_op jit(solution)/shard_map/ppermute | solution.py:30
  108.0 3.0 %collective-permute-start.18 = (bf16[4096,256]{1,0:T(8,128)(2,1)}, bf16[4096,256]{1,0:T(8,128)(2,1)}, u32[]{:S(2)}, u32[]{:S(2)}) collective-permute-start(bf16[4096,256]{1,0:T(8,128)(2,1)} %bitcast.124), channel_id=1, source_target_pairs={{0,224},{1,225},{2,226},{3,227},{4,228},{5,229},{6,230},{7,231},{8... | collective-permute-start | bytes 6291464 | tf_op jit(solution)/shard_map/ppermute | solution.py:30
  113.5 2.1 %collective-permute-start.13 = (bf16[2,128,1024]{2,1,0:T(8,128)(2,1)S(1)}, bf16[2,128,1024]{2,1,0:T(8,128)(2,1)S(1)}, u32[]{:S(2)}, u32[]{:S(2)}) collective-permute-start(bf16[2,128,1024]{2,1,0:T(8,128)(2,1)S(1)} %get-tuple-element.60), channel_id=1, source_target_pairs={{0,28},{1,29},{2,30},{3,31},{4,0},{5,1},{6,2},{7,3},{8,4},{9,5},{1... | collective-permute-start | bytes 1572872 | tf_op jit(solution)/shard_map/ppermute | solution.py:30
  117.1 1.9 %copy-done.14 = bf16[16,128,1024]{2,1,0:T(8,128)(2,1)S(1)} copy-done((bf16[16,128,1024]{2,1,0:T(8,128)(2,1)S(1)}, bf16[16,128,1024]{2,1,0:T(8,128)(2,1)}, u32[]{:S(2)}) %copy-start.14) | copy-done | bytes 4194328
  120.5 6.3 %collective-permute-done.12 = bf16[2,128,1024]{2,1,0:T(8,128)(2,1)S(1)} collective-permute-done((bf16[2,128,1024]{2,1,0:T(8,128)(2,1)S(1)}, bf16[2,128,1024]{2,1,0:T(8,128)(2,1)S(1)}, u32[]{:S(2)}, u32[]{:S(2)}) %collective-permute-start.12) | collective-permute-done | bytes 524320 | tf_op jit(solution)/shard_map/ppermute | solution.py:30
  126.8 2.5 %add_convert_fusion = (bf16[2,128,1024]{2,1,0:T(8,128)(2,1)}, bf16[2,128,1024]{2,1,0:T(8,128)(2,1)}) fusion(bf16[2,128,1024]{2,1,0:T(8,128)(2,1)S(1)} %collective-permute-done.13, bf16[16,128,1024]{2,1,0:T(8,128)(2,1)} %copy-done, s32[]{:T(128)S(6)} %select_n.145, bf16[2,128,1024]{2,1,0:T(8,128)(2,1)S(1)} %collective-permute-done.12, s32[]{:T(128)S(6)} %select_n.128), kind=kLoop, calls=%fused_computation.30 | loop fusion | flops 2097152 | bytes 3145736 | tf_op jit(solution)/shard_map/convert_element_type | solution.py:78
  129.7 2.3 %collective-permute-start.16 = (bf16[2,128,1024]{2,1,0:T(8,128)(2,1)}, bf16[2,128,1024]{2,1,0:T(8,128)(2,1)}, u32[]{:S(2)}, u32[]{:S(2)}) collective-permute-start(bf16[2,128,1024]{2,1,0:T(8,128)(2,1)} %get-tuple-element.58), channel_id=1, source_target_pairs={{0,28},{1,29},{2,30},{3,31},{4,0},{5,1},{6,2},{7,3},{8,4},{9,5},{1... | collective-permute-start | bytes 1572872 | tf_op jit(solution)/shard_map/ppermute | solution.py:30
  131.9 5.4 %fusion.9 = (f32[256]{0:T(256)S(1)}, bf16[2048]{0:T(1024)(128)(2,1)S(1)}, f32[2048,256]{1,0:T(8,128)}, f32[2048,256]{1,0:T(8,128)}, bf16[2048]{0:T(1024)(128)(2,1)S(1)}, /*index=5*/f32[256]{0:T(256)S(1)}) fusion(bf16[16,1,128,256]{3,2,1,0:T(8,128)(2,1)S(1)} %get-tuple-element.66, f32[256]{0:T(256)S(1)} %bitcast.98, f32[2048,256]{1,0:T(8,128)S(1)} %fusion.24, ...), kind=kOutput, calls=%fused_computation.17 | convolution fusion | flops 1084222976 | bytes 13134848 | tf_op jit(solution)/shard_map/dot_general | solution.py:242
  138.2 9.9 %all-to-all-start.1 = ((bf16[32,32,128]{2,1,0:T(8,128)(2,1)}), bf16[32,32,128]{2,1,0:T(8,128)(2,1)S(1)}, u32[]{:S(2)}, u32[]{:S(2)}) async-start(bf16[32,32,128]{2,1,0:T(8,128)(2,1)} %broadcast_in_dim.84), calls=%async_computation.1 | async-start | bytes 524288 | tf_op jit(solution)/shard_map/all_to_all | solution.py:277
  148.2 2.4 %broadcast_in_dim.86 = f32[16,2,128,256]{3,2,1,0:T(8,128)} broadcast(f32[]{:T(128)} %constant.138.clone.1), dimensions={} | broadcast | bytes 4194308 | tf_op jit(solution)/shard_map/broadcast_in_dim | solution.py:297
  154.5 7.4 %all-to-all-done.1 = bf16[32,32,128]{2,1,0:T(8,128)(2,1)S(1)} async-done(((bf16[32,32,128]{2,1,0:T(8,128)(2,1)}), bf16[32,32,128]{2,1,0:T(8,128)(2,1)S(1)}, u32[]{:S(2)}, u32[]{:S(2)}) %all-to-all-start.1) | async-done | bytes 262176 | tf_op jit(solution)/shard_map/all_to_all | solution.py:277
  164.2 3.6 %fusion.12 = f32[256,1024]{1,0:T(8,128)S(1)} fusion(bf16[2048,1024]{1,0:T(8,128)(2,1)} %collective-permute-done.17, bf16[2048,256]{1,0:T(8,128)(2,1)S(1)} %bitcast.106, f32[2048]{0:T(1024)S(1)} %bitcast.117, f32[256]{0:T(256)S(1)} %bitcast.99), kind=kOutput, calls=%fused_computation.23 | convolution fusion | flops 1075838976 | bytes 6300672 | tf_op jit(solution)/shard_map/dot_general | solution.py:292
  167.8 4.4 %fusion.1 = bf16[4096,256]{1,0:T(8,128)(2,1)} fusion(f32[16,2,128,256]{3,2,1,0:T(8,128)} %constant_dynamic-update-slice_fusion.2, bf16[4096,256]{1,0:T(8,128)(2,1)S(1)} %constant_dynamic-update-slice_fusion, bf16[4096,256]{1,0:T(8,128)(2,1)} %collective-permute-done.18, f32[4096]{0:T(1024)S(1)} %multiply_bitcast_fusion), kind=kLoop, calls=%fused_computation.2 | loop fusion | flops 6291456 | bytes 10502144 | tf_op jit(solution)/shard_map/convert_element_type | solution.py:306
  172.9 2.4 %fusion.10 = f32[1,256,1024]{2,1,0:T(8,128)} fusion(f32[256,1024]{1,0:T(8,128)S(1)} %fusion.12, bf16[2048,1024]{1,0:T(8,128)(2,1)S(1)} %bitcast.123, bf16[2048,256]{1,0:T(8,128)(2,1)S(1)} %bitcast.105, f32[256]{0:T(256)S(1)} %bitcast.100, f32[2048]{0:T(1024)S(1)} %bitcast.115), kind=kOutput, calls=%fused_computation.22 | convolution fusion | flops 1076101120 | bytes 7349248 | tf_op jit(solution)/shard_map/dot_general | solution.py:292
  175.3 2.4 %collective-permute-done.19 = bf16[128,1024]{1,0:T(8,128)(2,1)S(1)} collective-permute-done((bf16[128,1024]{1,0:T(8,128)(2,1)S(1)}, bf16[128,1024]{1,0:T(8,128)(2,1)S(1)}, u32[]{:S(2)}, u32[]{:S(2)}) %collective-permute-start.19) | collective-permute-done | bytes 262176 | tf_op jit(solution)/shard_map/ppermute | solution.py:30
  (97 shorter events, 29.1 us)
Async XLA Ops:
  7.2 10.9 %copy-start.2 = (bf16[1,256,1024]{2,1,0:T(8,128)(2,1)S(1)}, bf16[1,256,1024]{2,1,0:T(8,128)(2,1)}, u32[]{:S(2)}) copy-start(bf16[1,256,1024]{2,1,0:T(8,128)(2,1)} %param.11) | copy-start | bytes 1572868
  7.2 10.9 %copy-start.4 = (f32[1,256]{1,0:T(1,128)S(1)}, f32[1,256]{1,0:T(1,128)}, u32[]{:S(2)}) copy-start(f32[1,256]{1,0:T(1,128)} %gain.1) | copy-start | bytes 3076
  7.2 16.3 %copy-start.1 = (bf16[1,4096,256]{2,1,0:T(8,128)(2,1)S(1)}, bf16[1,4096,256]{2,1,0:T(8,128)(2,1)}, u32[]{:S(2)}) copy-start(bf16[1,4096,256]{2,1,0:T(8,128)(2,1)} %param.7) | copy-start | bytes 6291460
  7.2 96.6 %all-gather.2.cloned.1.call-start = ((), (), s32[]{:S(2)}) async-start(), calls=%async_computation.2 | async-start | bytes 4718592 | tf_op jit(solution)/shard_map/all_gather | solution.py:188
  7.2 8.9 %collective-permute-start.5 = (bf16[128,1024]{1,0:T(8,128)(2,1)}, bf16[128,1024]{1,0:T(8,128)(2,1)S(1)}, u32[]{:S(2)}, u32[]{:S(2)}) collective-permute-start(bf16[128,1024]{1,0:T(8,128)(2,1)} %bitcast.107), channel_id=1, source_target_pairs={{0,2},{1,3},{2,0},{3,1},{4,6},{5,7},{6,4},{7,5},{8,10},{9,11},{10,... | collective-permute-start | bytes 786440 | tf_op jit(solution)/shard_map/ppermute | solution.py:30
  19.0 15.2 %collective-permute-start.1 = (bf16[272,1024]{1,0:T(8,128)(2,1)}, bf16[272,1024]{1,0:T(8,128)(2,1)}, u32[]{:S(2)}, u32[]{:S(2)}) collective-permute-start(bf16[272,1024]{1,0:T(8,128)(2,1)} %shard_map.102), channel_id=1, source_target_pairs={{0,224},{1,225},{2,226},{3,227},{4,228},{5,229},{6,230},{7,231},{8... | collective-permute-start | bytes 1671176 | tf_op jit(solution)/shard_map/ppermute | solution.py:30
  23.5 13.2 %copy-start.5 = (bf16[1,4096,256]{2,1,0:T(8,128)(2,1)S(1)}, bf16[1,4096,256]{2,1,0:T(8,128)(2,1)}, u32[]{:S(2)}) copy-start(bf16[1,4096,256]{2,1,0:T(8,128)(2,1)} %param.8) | copy-start | bytes 6291460
  24.5 18.6 %collective-permute-start = (bf16[16,128,256]{2,1,0:T(8,128)(2,1)}, bf16[16,128,256]{2,1,0:T(8,128)(2,1)S(1)}, u32[]{:S(2)}, u32[]{:S(2)}) collective-permute-start(bf16[16,128,256]{2,1,0:T(8,128)(2,1)} %dynamic-slice_bitcast_fusion), channel_id=1, source_target_pairs={{0,1},{1,0},{2,3},{3,2},{4,5},{5,4},{6,7},{7,6},{8,9},{9,8},{10,11... | collective-permute-start | bytes 3145736 | tf_op jit(solution)/shard_map/ppermute | solution.py:30
  34.2 9.0 %collective-permute-start.2 = (bf16[272,1024]{1,0:T(8,128)(2,1)}, bf16[272,1024]{1,0:T(8,128)(2,1)}, u32[]{:S(2)}, u32[]{:S(2)}) collective-permute-start(bf16[272,1024]{1,0:T(8,128)(2,1)} %collective-permute-done.1.packed_mine), channel_id=1, source_target_pairs={{0,1},{1,0},{2,3},{3,2},{4,5},{5,4},{6,7},{7,6},{8,9},{9,8},{10,11... | collective-permute-start | bytes 1671176 | tf_op jit(solution)/shard_map/ppermute | solution.py:30
  38.2 28.2 %collective-permute-start.6 = (bf16[2048,256]{1,0:T(8,128)(2,1)}, bf16[2048,256]{1,0:T(8,128)(2,1)}, u32[]{:S(2)}, u32[]{:S(2)}) collective-permute-start(bf16[2048,256]{1,0:T(8,128)(2,1)} %get-tuple-element.31), channel_id=1, source_target_pairs={{0,224},{1,225},{2,226},{3,227},{4,228},{5,229},{6,230},{7,231},{8... | collective-permute-start | bytes 3145736 | tf_op jit(solution)/shard_map/ppermute | solution.py:30
  43.2 15.6 %copy-start.6 = (bf16[1,4096,256]{2,1,0:T(8,128)(2,1)S(1)}, bf16[1,4096,256]{2,1,0:T(8,128)(2,1)}, u32[]{:S(2)}) copy-start(bf16[1,4096,256]{2,1,0:T(8,128)(2,1)} %param.8) | copy-start | bytes 6291460
  49.6 25.7 %copy-start.13 = (bf16[2048,256]{1,0:T(8,128)(2,1)S(1)}, bf16[2048,256]{1,0:T(8,128)(2,1)}, u32[]{:S(2)}) copy-start(bf16[2048,256]{1,0:T(8,128)(2,1)} %get-tuple-element.35) | copy-start | bytes 3145732
  49.7 37.3 %collective-permute-start.3 = (bf16[2,128,1024]{2,1,0:T(8,128)(2,1)S(1)}, bf16[2,128,1024]{2,1,0:T(8,128)(2,1)}, u32[]{:S(2)}, u32[]{:S(2)}) collective-permute-start(bf16[2,128,1024]{2,1,0:T(8,128)(2,1)S(1)} %constant_dynamic-slice_fusion.6), channel_id=1, source_target_pairs={{0,4},{2,6},{4,8},{6,10},{8,12},{10,14},{12,16},{14,18},{16,20},{1... | collective-permute-start | bytes 1572872 | tf_op jit(solution)/shard_map/ppermute | solution.py:30
  51.3 35.7 %collective-permute-start.4 = (bf16[2,128,1024]{2,1,0:T(8,128)(2,1)S(1)}, bf16[2,128,1024]{2,1,0:T(8,128)(2,1)}, u32[]{:S(2)}, u32[]{:S(2)}) collective-permute-start(bf16[2,128,1024]{2,1,0:T(8,128)(2,1)S(1)} %constant_dynamic-slice_fusion.6), channel_id=1, source_target_pairs={{1,29},{3,31},{5,1},{7,3},{9,5},{11,7},{13,9},{15,11},{17,13},{19,... | collective-permute-start | bytes 1572872 | tf_op jit(solution)/shard_map/ppermute | solution.py:30
  66.3 20.7 %all-to-all-start = ((bf16[16,34,128]{2,1,0:T(8,128)(2,1)}), bf16[16,34,128]{2,1,0:T(8,128)(2,1)S(1)}, u32[]{:S(2)}, u32[]{:S(2)}) async-start(bf16[16,34,128]{2,1,0:T(8,128)(2,1)} %pad_maximum_fusion.1), calls=%async_computation | async-start | bytes 327680 | tf_op jit(solution)/shard_map/all_to_all | solution.py:219
  75.4 28.4 %collective-permute-start.9 = (bf16[2048,256]{1,0:T(8,128)(2,1)S(1)}, bf16[2048,256]{1,0:T(8,128)(2,1)S(1)}, u32[]{:S(2)}, u32[]{:S(2)}) collective-permute-start(bf16[2048,256]{1,0:T(8,128)(2,1)S(1)} %copy-done.13), channel_id=1, source_target_pairs={{0,224},{1,225},{2,226},{3,227},{4,228},{5,229},{6,230},{7,231},{8... | collective-permute-start | bytes 3145736 | tf_op jit(solution)/shard_map/ppermute | solution.py:30
  88.9 14.9 %collective-permute-start.7 = (bf16[2,128,1024]{2,1,0:T(8,128)(2,1)S(1)}, bf16[2,128,1024]{2,1,0:T(8,128)(2,1)S(1)}, u32[]{:S(2)}, u32[]{:S(2)}) collective-permute-start(bf16[2,128,1024]{2,1,0:T(8,128)(2,1)S(1)} %get-tuple-element.63), channel_id=1, source_target_pairs={{0,4},{1,5},{2,6},{3,7},{4,8},{5,9},{6,10},{7,11},{8,12},{9,13},{1... | collective-permute-start | bytes 1572872 | tf_op jit(solution)/shard_map/ppermute | solution.py:30
  89.0 14.8 %collective-permute-start.8 = (bf16[2,128,1024]{2,1,0:T(8,128)(2,1)S(1)}, bf16[2,128,1024]{2,1,0:T(8,128)(2,1)}, u32[]{:S(2)}, u32[]{:S(2)}) collective-permute-start(bf16[2,128,1024]{2,1,0:T(8,128)(2,1)S(1)} %get-tuple-element.62), channel_id=1, source_target_pairs={{0,28},{1,29},{2,30},{3,31},{4,0},{5,1},{6,2},{7,3},{8,4},{9,5},{1... | collective-permute-start | bytes 1572872 | tf_op jit(solution)/shard_map/ppermute | solution.py:30
  91.7 11.0 %collective-permute-start.10 = (f32[32,128]{1,0:T(8,128)S(1)}, f32[32,128]{1,0:T(8,128)S(1)}, u32[]{:S(2)}, u32[]{:S(2)}) collective-permute-start(f32[32,128]{1,0:T(8,128)S(1)} %slice.26), channel_id=1, source_target_pairs={{0,224},{1,225},{2,226},{3,227},{4,228},{5,229},{6,230},{7,231},{8... | collective-permute-start | bytes 49160 | tf_op jit(solution)/shard_map/ppermute | solution.py:30
  95.4 7.4 %collective-permute-start.11 = (f32[32,128]{1,0:T(8,128)S(1)}, f32[32,128]{1,0:T(8,128)S(1)}, u32[]{:S(2)}, u32[]{:S(2)}) collective-permute-start(f32[32,128]{1,0:T(8,128)S(1)} %slice.26), channel_id=1, source_target_pairs={{0,226},{1,227},{2,224},{3,225},{4,230},{5,231},{6,228},{7,229},{8... | collective-permute-start | bytes 49160 | tf_op jit(solution)/shard_map/ppermute | solution.py:30
  103.8 28.1 %collective-permute-start.17 = (bf16[2048,1024]{1,0:T(8,128)(2,1)}, bf16[2048,1024]{1,0:T(8,128)(2,1)}, u32[]{:S(2)}, u32[]{:S(2)}) collective-permute-start(bf16[2048,1024]{1,0:T(8,128)(2,1)} %bitcast.121), channel_id=1, source_target_pairs={{0,1},{1,0},{2,3},{3,2},{4,5},{5,4},{6,7},{7,6},{8,9},{9,8},{10,11... | collective-permute-start | bytes 12582920 | tf_op jit(solution)/shard_map/ppermute | solution.py:30
  105.5 15.0 %collective-permute-start.14 = (f32[2,128]{1,0:T(2,128)S(1)}, f32[2,128]{1,0:T(2,128)S(1)}, u32[]{:S(2)}, u32[]{:S(2)}) collective-permute-start(f32[2,128]{1,0:T(2,128)S(1)} %slice.27), channel_id=1, source_target_pairs={{0,2},{1,3},{2,0},{3,1},{4,6},{5,7},{6,4},{7,5},{8,10},{9,11},{10,... | collective-permute-start | bytes 3080 | tf_op jit(solution)/shard_map/ppermute | solution.py:30
  108.0 53.9 %collective-permute-start.18 = (bf16[4096,256]{1,0:T(8,128)(2,1)}, bf16[4096,256]{1,0:T(8,128)(2,1)}, u32[]{:S(2)}, u32[]{:S(2)}) collective-permute-start(bf16[4096,256]{1,0:T(8,128)(2,1)} %bitcast.124), channel_id=1, source_target_pairs={{0,224},{1,225},{2,226},{3,227},{4,228},{5,229},{6,230},{7,231},{8... | collective-permute-start | bytes 6291464 | tf_op jit(solution)/shard_map/ppermute | solution.py:30
  112.7 14.1 %collective-permute-start.12 = (bf16[2,128,1024]{2,1,0:T(8,128)(2,1)S(1)}, bf16[2,128,1024]{2,1,0:T(8,128)(2,1)S(1)}, u32[]{:S(2)}, u32[]{:S(2)}) collective-permute-start(bf16[2,128,1024]{2,1,0:T(8,128)(2,1)S(1)} %get-tuple-element.61), channel_id=1, source_target_pairs={{0,4},{1,5},{2,6},{3,7},{4,8},{5,9},{6,10},{7,11},{8,12},{9,13},{1... | collective-permute-start | bytes 1572872 | tf_op jit(solution)/shard_map/ppermute | solution.py:30
  113.5 13.3 %collective-permute-start.13 = (bf16[2,128,1024]{2,1,0:T(8,128)(2,1)S(1)}, bf16[2,128,1024]{2,1,0:T(8,128)(2,1)S(1)}, u32[]{:S(2)}, u32[]{:S(2)}) collective-permute-start(bf16[2,128,1024]{2,1,0:T(8,128)(2,1)S(1)} %get-tuple-element.60), channel_id=1, source_target_pairs={{0,28},{1,29},{2,30},{3,31},{4,0},{5,1},{6,2},{7,3},{8,4},{9,5},{1... | collective-permute-start | bytes 1572872 | tf_op jit(solution)/shard_map/ppermute | solution.py:30
  119.2 12.7 %copy-start.9 = (bf16[16,1,128,256]{3,2,1,0:T(8,128)(2,1)}, bf16[16,1,128,256]{3,2,1,0:T(8,128)(2,1)S(1)}, u32[]{:S(2)}) copy-start(bf16[16,1,128,256]{3,2,1,0:T(8,128)(2,1)S(1)} %get-tuple-element.67) | copy-start | bytes 3145732
  119.2 12.7 %copy-start.11 = (bf16[16,1,128,256]{3,2,1,0:T(8,128)(2,1)}, bf16[16,1,128,256]{3,2,1,0:T(8,128)(2,1)S(1)}, u32[]{:S(2)}) copy-start(bf16[16,1,128,256]{3,2,1,0:T(8,128)(2,1)S(1)} %get-tuple-element.66) | copy-start | bytes 3145732
  129.3 32.7 %collective-permute-start.15 = (bf16[2,128,1024]{2,1,0:T(8,128)(2,1)}, bf16[2,128,1024]{2,1,0:T(8,128)(2,1)}, u32[]{:S(2)}, u32[]{:S(2)}) collective-permute-start(bf16[2,128,1024]{2,1,0:T(8,128)(2,1)} %get-tuple-element.59), channel_id=1, source_target_pairs={{0,4},{1,5},{2,6},{3,7},{4,8},{5,9},{6,10},{7,11},{8,12},{9,13},{1... | collective-permute-start | bytes 1572872 | tf_op jit(solution)/shard_map/ppermute | solution.py:30
  129.7 32.3 %collective-permute-start.16 = (bf16[2,128,1024]{2,1,0:T(8,128)(2,1)}, bf16[2,128,1024]{2,1,0:T(8,128)(2,1)}, u32[]{:S(2)}, u32[]{:S(2)}) collective-permute-start(bf16[2,128,1024]{2,1,0:T(8,128)(2,1)} %get-tuple-element.58), channel_id=1, source_target_pairs={{0,28},{1,29},{2,30},{3,31},{4,0},{5,1},{6,2},{7,3},{8,4},{9,5},{1... | collective-permute-start | bytes 1572872 | tf_op jit(solution)/shard_map/ppermute | solution.py:30
  138.2 23.6 %all-to-all-start.1 = ((bf16[32,32,128]{2,1,0:T(8,128)(2,1)}), bf16[32,32,128]{2,1,0:T(8,128)(2,1)S(1)}, u32[]{:S(2)}, u32[]{:S(2)}) async-start(bf16[32,32,128]{2,1,0:T(8,128)(2,1)} %broadcast_in_dim.84), calls=%async_computation.1 | async-start | bytes 524288 | tf_op jit(solution)/shard_map/all_to_all | solution.py:277
  163.8 13.9 %collective-permute-start.19 = (bf16[128,1024]{1,0:T(8,128)(2,1)S(1)}, bf16[128,1024]{1,0:T(8,128)(2,1)S(1)}, u32[]{:S(2)}, u32[]{:S(2)}) collective-permute-start(bf16[128,1024]{1,0:T(8,128)(2,1)S(1)} %get-tuple-element.70), channel_id=1, source_target_pairs={{0,32},{1,33},{2,34},{3,35},{4,36},{5,37},{6,38},{7,39},{8,40},{9,... | collective-permute-start | bytes 786440 | tf_op jit(solution)/shard_map/ppermute | solution.py:30
  163.9 14.2 %collective-permute-start.20 = (bf16[128,1024]{1,0:T(8,128)(2,1)S(1)}, bf16[128,1024]{1,0:T(8,128)(2,1)S(1)}, u32[]{:S(2)}, u32[]{:S(2)}) collective-permute-start(bf16[128,1024]{1,0:T(8,128)(2,1)S(1)} %get-tuple-element.71), channel_id=1, source_target_pairs={{0,34},{1,35},{2,32},{3,33},{4,38},{5,39},{6,36},{7,37},{8,42},{9,... | collective-permute-start | bytes 786440 | tf_op jit(solution)/shard_map/ppermute | solution.py:30
  (8 other events, 23.1 us)
Sparse Core Ops, SparseCore 0:
  18.2 68.4 all-gather.1

commit v10 on v8

--- a/solution.py
+++ b/solution.py
@@ -17,9 +17,9 @@
 LANE = WIDTH // N_T
 KEYS = 1024
 PACK = LANE + 16
+CUT = 3 * TOK // 4
+SPLIT = TOK // 4
 ORDER = 4
-CUT = 3 * TOK // 4
-SPLIT = 3 * TOK // 16
 AXES = ("section", "ts")
 
 
@@ -250,17 +250,14 @@
 
     up = move(block(4), z_up, (0,))
     down = move(block(4), z_down, (1,))
-    up, down, late = lax.optimization_barrier(
-        (up, down, late, squares_raw, older_first, *older_sq)
-    )[:3]
-    late = move(after(late, early), to_previous)
+    up, down, late, fresh_other = lax.optimization_barrier(
+        (up, down, late, fresh_other, squares_raw, older_first, *older_sq)
+    )[:4]
     up = add(block(3), up)
     down = add(block(-3), down)
     up = move(up, z_up)
     down = move(down, z_down)
-    up, down, cot_mine, fresh_other = lax.optimization_barrier(
-        (up, down, cot_mine, fresh_other, older_second, early)
-    )[:4]
+    up, down, cot_mine = lax.optimization_barrier((up, down, cot_mine, older_second, early))[:3]
 
     cots = [cot_mine, move(cot_mine, to_other_core)]
     raw = [
@@ -272,11 +269,16 @@
     older_first, older_second, *older_sq = lax.optimization_barrier(
         (older_first, older_second, *older_sq, up, down)
     )[:4]
+    late = move(after(late, up, down), to_previous)
     up = move(up, z_up)
     down = move(down, z_down)
     up, down, raw[0] = lax.optimization_barrier((up, down, raw[0]))
     up = add(block(1), up)
     down = add(block(-1), down)
+    cots[1] = after(cots[1], up, down)
+    raw[1] = lax.dot_general(
+        cots[1], weights, (((1,), (1,)), ((), ())), preferred_element_type=F32
+    )
     up = move(up, z_up)
     down = move(down, z_down)
     older = jnp.concatenate([older_first, older_second], axis=0)
@@ -303,13 +305,16 @@
         place, *[(gain * grad).reshape(N_T // 2, OWN, LANE) for grad in grads]
     ).reshape(TOK, LANE)
     curve = lax.all_to_all(curve, "ts", 0, 0, tiled=True)
-    up, down, base = lax.optimization_barrier((up, down, base, late))[:3]
+    curve, base = lax.optimization_barrier((curve, base))
+    up, down = lax.optimization_barrier((up, down, curve, late))[:2]
     fresh_rate = lax.rsqrt((squares[:2] + fresh_other) / WIDTH + eps)
+    curve = jnp.sum(curve.astype(F32), axis=0).reshape(TOK)
+    pull = older_rate * older_rate / WIDTH * curve
 
     summed = block(0).astype(F32) + up.astype(F32) + down.astype(F32)
     straight = (pick(summed, half) * pick(fresh_rate, half)[:, None]).astype(BF)
     crossed = (pick(summed, 1 - half) * pick(fresh_rate, 1 - half)[:, None]).astype(BF)
-    cots = lax.optimization_barrier((*cots, straight, crossed))[:2]
+    *cots, pull = lax.optimization_barrier((*cots, pull, straight, crossed))[:3]
     straight = move(straight, to_next)
     crossed = move(crossed, to_next_other_half)
     new_keys = (straight.astype(F32) + crossed.astype(F32)).astype(BF)
@@ -320,9 +325,6 @@
         )
         for left, cot in zip(lefts, cots)
     )
-    curve, base, weight_total = lax.optimization_barrier((curve, base, weight_total))
-    curve = jnp.sum(curve.astype(F32), axis=0).reshape(TOK)
-    pull = older_rate * older_rate / WIDTH * curve
     downstream = jnp.concatenate([early, late], axis=0)
     total = downstream.astype(F32) + base - pull[:, None] * older.astype(F32)
     return (

time: 190 us -> 179 us (0.942)
  waiting for transfers between devices: 51.7 us -> 40.5 us
  starting transfers between devices: 67.6 us -> 62.2 us
  local copies, waits for them, and re-layouts: 15.3 us -> 19.9 us
  matrix products: 11.8 us -> 15.7 us
    ppermute x22, waiting for transfers between devices: 46.3 us -> 32.1 us  [move(): return lax.ppermute(value, AXES, pairs)]
    dot_general x0 -> x1, matrix products: none -> 6.14 us  [shards(): lax.dot_general(cots[1], weights, (((1,), (1,)), ((), ())), preferred_ele...]
    all_to_all x1, starting transfers between devices: 10.6 us -> 6 us  [shards(): curve = lax.all_to_all(curve, 'ts', 0, 0, tiled=True)]
    dot_general x2 -> x1, matrix products: 5.68 us -> 1.32 us  [shards(): lax.dot_general(cot, weights, (((1,), (1,)), ((), ())), preferred_element...]
    unnamed x63 -> x55, local copies, waits for them, and re-layouts: 7.34 us -> 11.1 us
    all_to_all x1, waiting for transfers between devices: 5.35 us -> 8.41 us  [shards(): curve = lax.all_to_all(curve, 'ts', 0, 0, tiled=True)]
    dot_general x2, matrix products: 6.12 us -> 8.25 us  [shards(): lax.dot_general(left.astype(BF), cot, (((0,), (0,)), ((), ())), preferred...]
  transfers between devices with their start and end apart: 25 -> 25, of which waited for: 7 -> 12; matrix products, arithmetic and copies ran while one was open for 17% -> 23% of each run, Pallas kernels for 3% -> 3%
where the time goes in v10:
time: 179 us; the launch traced here: 178 us
  starting transfers between devices  62.2 us (35%)
  waiting for transfers between devices  40.5 us (23%)
  local copies, waits for them, and re-layouts  19.9 us (11%)
  other arithmetic  19.1 us (11%)
  matrix products  15.7 us (9%)
  between operations  15.3 us (9%)
  Pallas kernels  5.69 us (3%)
    ppermute x22, starting transfers between devices, move(): return lax.ppermute(value, AXES, pairs)  47.5 us
    ppermute x22, waiting for transfers between devices, move(): return lax.ppermute(value, AXES, pairs)  32.1 us
    unnamed x55, local copies, waits for them, and re-layouts  11.1 us
    all_to_all x1, starting transfers between devices, shards(): lax.all_to_all(after(squares, packed), 'ts', 0, 0, axis_index_groups=halv...  8.59 us
    all_to_all x1, waiting for transfers between devices, shards(): curve = lax.all_to_all(curve, 'ts', 0, 0, tiled=True)  8.41 us
    dot_general x2, matrix products, shards(): lax.dot_general(left.astype(BF), cot, (((0,), (0,)), ((), ())), preferred...  8.25 us
    dot_general x1, matrix products, shards(): lax.dot_general(cots[1], weights, (((1,), (1,)), ((), ())), preferred_ele...  6.14 us
    all_to_all x1, starting transfers between devices, shards(): curve = lax.all_to_all(curve, 'ts', 0, 0, tiled=True)  6 us
  transfers between devices with their start and end apart: 25, of which 12 were waited for; matrix products, arithmetic and copies ran while one was open for 23% of the time, Pallas kernels for 3%

profile of v10, /device:TPU:1, one launch (start us, length us, event | category | flops | bytes accessed | tf_op | source)
XLA Modules:
  0.0 178.3 jit_solution(1130449577878971216)
XLA Ops:
  7.2 3.7 %collective-permute-start.8 = (bf16[128,1024]{1,0:T(8,128)(2,1)}, bf16[128,1024]{1,0:T(8,128)(2,1)S(1)}, u32[]{:S(2)}, u32[]{:S(2)}) collective-permute-start(bf16[128,1024]{1,0:T(8,128)(2,1)} %bitcast.102), channel_id=1, source_target_pairs={{0,2},{1,3},{2,0},{3,1},{4,6},{5,7},{6,4},{7,5},{8,10},{9,11},{10,... | collective-permute-start | bytes 786440 | tf_op jit(solution)/shard_map/ppermute | solution.py:32
  10.9 5.3 %collective-permute-done.8 = bf16[128,1024]{1,0:T(8,128)(2,1)S(1)} collective-permute-done((bf16[128,1024]{1,0:T(8,128)(2,1)}, bf16[128,1024]{1,0:T(8,128)(2,1)S(1)}, u32[]{:S(2)}, u32[]{:S(2)}) %collective-permute-start.8) | collective-permute-done | bytes 262176 | tf_op jit(solution)/shard_map/ppermute | solution.py:32
  19.0 4.5 %collective-permute-start.1 = (bf16[272,1024]{1,0:T(8,128)(2,1)}, bf16[272,1024]{1,0:T(8,128)(2,1)}, u32[]{:S(2)}, u32[]{:S(2)}) collective-permute-start(bf16[272,1024]{1,0:T(8,128)(2,1)} %shard_map.102), channel_id=1, source_target_pairs={{0,224},{1,225},{2,226},{3,227},{4,228},{5,229},{6,230},{7,231},{8... | collective-permute-start | bytes 1671176 | tf_op jit(solution)/shard_map/ppermute | solution.py:32
  24.5 1.8 %collective-permute-start = (bf16[16,128,256]{2,1,0:T(8,128)(2,1)}, bf16[16,128,256]{2,1,0:T(8,128)(2,1)S(1)}, u32[]{:S(2)}, u32[]{:S(2)}) collective-permute-start(bf16[16,128,256]{2,1,0:T(8,128)(2,1)} %dynamic-slice_bitcast_fusion), channel_id=1, source_target_pairs={{0,1},{1,0},{2,3},{3,2},{4,5},{5,4},{6,7},{7,6},{8,9},{9,8},{10,11... | collective-permute-start | bytes 3145736 | tf_op jit(solution)/shard_map/ppermute | solution.py:32
  26.3 2.7 %slice_bitcast_fusion = bf16[3072,256]{1,0:T(8,128)(2,1)} fusion(bf16[1,4096,256]{2,1,0:T(8,128)(2,1)} %param.8), kind=kLoop, calls=%fused_computation.20 | loop fusion | bytes 3145728 | tf_op jit(solution)/shard_map/slice | solution.py:212
  29.7 2.4 %multiply_reduce_fusion = bf16[4096]{0:T(1024)(128)(2,1)S(1)} fusion(bf16[1,4096,256]{2,1,0:T(8,128)(2,1)} %param.8), kind=kLoop, calls=%fused_computation.1 | loop fusion | flops 3141632 | bytes 2105344 | tf_op jit(solution)/shard_map/reduce_sum | solution.py:223
  34.2 4.5 %collective-permute-start.2 = (bf16[272,1024]{1,0:T(8,128)(2,1)}, bf16[272,1024]{1,0:T(8,128)(2,1)}, u32[]{:S(2)}, u32[]{:S(2)}) collective-permute-start(bf16[272,1024]{1,0:T(8,128)(2,1)} %collective-permute-done.1.packed_mine), channel_id=1, source_target_pairs={{0,1},{1,0},{2,3},{3,2},{4,5},{5,4},{6,7},{7,6},{8,9},{9,8},{10,11... | collective-permute-start | bytes 1671176 | tf_op jit(solution)/shard_map/ppermute | solution.py:32
  40.0 8.6 %all-to-all-start = ((bf16[16,34,128]{2,1,0:T(8,128)(2,1)}), bf16[16,34,128]{2,1,0:T(8,128)(2,1)S(1)}, u32[]{:S(2)}, u32[]{:S(2)}) async-start(bf16[16,34,128]{2,1,0:T(8,128)(2,1)} %pad_maximum_fusion.1), calls=%async_computation | async-start | bytes 327680 | tf_op jit(solution)/shard_map/all_to_all | solution.py:232
  48.6 4.3 %shard_map.103 = bf16[16,128,1024]{2,1,0:T(8,128)(2,1)S(1)} custom-call(s32[1]{0:T(128)} %bitcast.place, bf16[16,2,128,256]{3,2,1,0:T(8,128)(2,1)S(1)} %bitcast.91, bf16[16,128,256]{2,1,0:T(8,128)(2,1)S(1)} %collective-permute-done.rows_other, bf16[272,1024]{1,0:T(8,128)(2,1)} %collective-permute-done.1.packed_mine, ...), custom_call_target="tpu_custom_call" | custom-call | flops 2147483648 | bytes 7340032 | tf_op jit(solution)/shard_map/pallas_call | solution.py:143
  52.9 2.0 %copy-done = bf16[16,128,1024]{2,1,0:T(8,128)(2,1)} copy-done((bf16[16,128,1024]{2,1,0:T(8,128)(2,1)}, bf16[16,128,1024]{2,1,0:T(8,128)(2,1)S(1)}, u32[]{:S(2)}) %copy-start) | copy-done | bytes 4194328
  55.0 4.5 %collective-permute-start.4 = (bf16[2,128,1024]{2,1,0:T(8,128)(2,1)S(1)}, bf16[2,128,1024]{2,1,0:T(8,128)(2,1)S(1)}, u32[]{:S(2)}, u32[]{:S(2)}) collective-permute-start(bf16[2,128,1024]{2,1,0:T(8,128)(2,1)S(1)} %constant_dynamic-slice_fusion.6), channel_id=1, source_target_pairs={{1,29},{3,31},{5,1},{7,3},{9,5},{11,7},{13,9},{15,11},{17,13},{19,... | collective-permute-start | bytes 1572872 | tf_op jit(solution)/shard_map/ppermute | solution.py:32
  61.3 5.7 %collective-permute-start.6 = (f32[32,128]{1,0:T(8,128)S(1)}, f32[32,128]{1,0:T(8,128)S(1)}, u32[]{:S(2)}, u32[]{:S(2)}) collective-permute-start(f32[32,128]{1,0:T(8,128)S(1)} %slice.35), channel_id=1, source_target_pairs={{0,226},{1,227},{2,224},{3,225},{4,230},{5,231},{6,228},{7,229},{8... | collective-permute-start | bytes 49160 | tf_op jit(solution)/shard_map/ppermute | solution.py:32
  68.5 3.5 %collective-permute-done.5 = f32[32,128]{1,0:T(8,128)S(1)} collective-permute-done((f32[32,128]{1,0:T(8,128)S(1)}, f32[32,128]{1,0:T(8,128)S(1)}, u32[]{:S(2)}, u32[]{:S(2)}) %collective-permute-start.5) | collective-permute-done | bytes 16416 | tf_op jit(solution)/shard_map/ppermute | solution.py:32
  72.0 2.3 %collective-permute-start.7 = (f32[2,128]{1,0:T(2,128)S(1)}, f32[2,128]{1,0:T(2,128)S(1)}, u32[]{:S(2)}, u32[]{:S(2)}) collective-permute-start(f32[2,128]{1,0:T(2,128)S(1)} %slice.34), channel_id=1, source_target_pairs={{0,2},{1,3},{2,0},{3,1},{4,6},{5,7},{6,4},{7,5},{8,10},{9,11},{10,... | collective-permute-start | bytes 3080 | tf_op jit(solution)/shard_map/ppermute | solution.py:32
  76.0 1.9 %collective-permute-start.13 = (bf16[1024,256]{1,0:T(8,128)(2,1)S(1)}, bf16[1024,256]{1,0:T(8,128)(2,1)}, u32[]{:S(2)}, u32[]{:S(2)}) collective-permute-start(bf16[1024,256]{1,0:T(8,128)(2,1)S(1)} %slice_bitcast_fusion.2), channel_id=1, source_target_pairs={{0,224},{1,225},{2,226},{3,227},{4,228},{5,229},{6,230},{7,231},{8... | collective-permute-start | bytes 1572872 | tf_op jit(solution)/shard_map/ppermute | solution.py:32
  79.6 5.6 %collective-permute-start.11 = (bf16[2,128,1024]{2,1,0:T(8,128)(2,1)S(1)}, bf16[2,128,1024]{2,1,0:T(8,128)(2,1)S(1)}, u32[]{:S(2)}, u32[]{:S(2)}) collective-permute-start(bf16[2,128,1024]{2,1,0:T(8,128)(2,1)S(1)} %get-tuple-element.72), channel_id=1, source_target_pairs={{0,28},{1,29},{2,30},{3,31},{4,0},{5,1},{6,2},{7,3},{8,4},{9,5},{1... | collective-permute-start | bytes 1572872 | tf_op jit(solution)/shard_map/ppermute | solution.py:32
  85.2 3.7 %collective-permute-done.12 = bf16[1024,256]{1,0:T(8,128)(2,1)S(1)} collective-permute-done((bf16[1024,256]{1,0:T(8,128)(2,1)S(1)}, bf16[1024,256]{1,0:T(8,128)(2,1)S(1)}, u32[]{:S(2)}, u32[]{:S(2)}) %collective-permute-start.12) | collective-permute-done | bytes 524320 | tf_op jit(solution)/shard_map/ppermute | solution.py:32
  88.8 9.4 %collective-permute-done.13 = bf16[1024,256]{1,0:T(8,128)(2,1)} collective-permute-done((bf16[1024,256]{1,0:T(8,128)(2,1)S(1)}, bf16[1024,256]{1,0:T(8,128)(2,1)}, u32[]{:S(2)}, u32[]{:S(2)}) %collective-permute-start.13) | collective-permute-done | bytes 524320 | tf_op jit(solution)/shard_map/ppermute | solution.py:32
  98.3 2.5 %collective-permute-start.18 = (bf16[2048,1024]{1,0:T(8,128)(2,1)}, bf16[2048,1024]{1,0:T(8,128)(2,1)}, u32[]{:S(2)}, u32[]{:S(2)}) collective-permute-start(bf16[2048,1024]{1,0:T(8,128)(2,1)} %bitcast.116), channel_id=1, source_target_pairs={{0,1},{1,0},{2,3},{3,2},{4,5},{5,4},{6,7},{7,6},{8,9},{9,8},{10,11... | collective-permute-start | bytes 12582920 | tf_op jit(solution)/shard_map/ppermute | solution.py:32
  103.7 5.4 %collective-permute-start.15 = (bf16[2,128,1024]{2,1,0:T(8,128)(2,1)S(1)}, bf16[2,128,1024]{2,1,0:T(8,128)(2,1)S(1)}, u32[]{:S(2)}, u32[]{:S(2)}) collective-permute-start(bf16[2,128,1024]{2,1,0:T(8,128)(2,1)S(1)} %get-tuple-element.70), channel_id=1, source_target_pairs={{0,28},{1,29},{2,30},{3,31},{4,0},{5,1},{6,2},{7,3},{8,4},{9,5},{1... | collective-permute-start | bytes 1572872 | tf_op jit(solution)/shard_map/ppermute | solution.py:32
  109.1 2.3 %collective-permute-start.19 = (bf16[3072,256]{1,0:T(8,128)(2,1)}, bf16[3072,256]{1,0:T(8,128)(2,1)}, u32[]{:S(2)}, u32[]{:S(2)}) collective-permute-start(bf16[3072,256]{1,0:T(8,128)(2,1)} %slice_bitcast_fusion.1), channel_id=1, source_target_pairs={{0,224},{1,225},{2,226},{3,227},{4,228},{5,229},{6,230},{7,231},{8... | collective-permute-start | bytes 4718600 | tf_op jit(solution)/shard_map/ppermute | solution.py:32
  114.3 2.3 %copy-done.26 = bf16[16,128,1024]{2,1,0:T(8,128)(2,1)S(1)} copy-done((bf16[16,128,1024]{2,1,0:T(8,128)(2,1)S(1)}, bf16[16,128,1024]{2,1,0:T(8,128)(2,1)}, u32[]{:S(2)}) %copy-start.26) | copy-done | bytes 4194328
  118.1 2.2 %collective-permute-done.15 = bf16[2,128,1024]{2,1,0:T(8,128)(2,1)S(1)} collective-permute-done((bf16[2,128,1024]{2,1,0:T(8,128)(2,1)S(1)}, bf16[2,128,1024]{2,1,0:T(8,128)(2,1)S(1)}, u32[]{:S(2)}, u32[]{:S(2)}) %collective-permute-start.15) | collective-permute-done | bytes 524320 | tf_op jit(solution)/shard_map/ppermute | solution.py:32
  120.3 3.1 %collective-permute-done.14 = bf16[2,128,1024]{2,1,0:T(8,128)(2,1)S(1)} collective-permute-done((bf16[2,128,1024]{2,1,0:T(8,128)(2,1)S(1)}, bf16[2,128,1024]{2,1,0:T(8,128)(2,1)S(1)}, u32[]{:S(2)}, u32[]{:S(2)}) %collective-permute-start.14) | collective-permute-done | bytes 524320 | tf_op jit(solution)/shard_map/ppermute | solution.py:32
  123.4 2.5 %add_convert_fusion = (bf16[2,128,1024]{2,1,0:T(8,128)(2,1)}, bf16[2,128,1024]{2,1,0:T(8,128)(2,1)}) fusion(bf16[2,128,1024]{2,1,0:T(8,128)(2,1)S(1)} %collective-permute-done.15, bf16[16,128,1024]{2,1,0:T(8,128)(2,1)} %copy-done, s32[]{:T(128)S(6)} %select_n.142, bf16[2,128,1024]{2,1,0:T(8,128)(2,1)S(1)} %collective-permute-done.14, s32[]{:T(128)S(6)} %select_n.125), kind=kLoop, calls=%fused_computation.31 | loop fusion | flops 2097152 | bytes 3145736 | tf_op jit(solution)/shard_map/convert_element_type | solution.py:80
  127.4 6.1 %fusion.7 = (f32[256]{0:T(256)}, bf16[2048]{0:T(1024)(128)(2,1)S(1)}, f32[2048,256]{1,0:T(8,128)S(1)}, f32[2048,256]{1,0:T(8,128)}, bf16[2048]{0:T(1024)(128)(2,1)S(1)}, /*index=5*/f32[256]{0:T(256)}) fusion(bf16[16,1,128,256]{3,2,1,0:T(8,128)(2,1)S(1)} %get-tuple-element.76, f32[256]{0:T(256)S(1)} %bitcast.94, f32[2048,256]{1,0:T(8,128)S(1)} %fusion.23, ...), kind=kOutput, calls=%fused_computation.15 | convolution fusion | flops 1084222976 | bytes 13134848 | tf_op jit(solution)/shard_map/dot_general | solution.py:279
  134.4 6.0 %all-to-all-start.1 = ((bf16[32,32,128]{2,1,0:T(8,128)(2,1)}), bf16[32,32,128]{2,1,0:T(8,128)(2,1)}, u32[]{:S(2)}, u32[]{:S(2)}) async-start(bf16[32,32,128]{2,1,0:T(8,128)(2,1)} %broadcast_in_dim.74), calls=%async_computation.1 | async-start | bytes 524288 | tf_op jit(solution)/shard_map/all_to_all | solution.py:307
  142.5 1.9 %copy-done.2 = f32[16,2,128,256]{3,2,1,0:T(8,128)} copy-done((f32[16,2,128,256]{3,2,1,0:T(8,128)}, f32[16,2,128,256]{3,2,1,0:T(8,128)S(1)}, u32[]{:S(2)}) %copy-start.2) | copy-done | bytes 4194328
  145.0 8.4 %all-to-all-done.1 = bf16[32,32,128]{2,1,0:T(8,128)(2,1)} async-done(((bf16[32,32,128]{2,1,0:T(8,128)(2,1)}), bf16[32,32,128]{2,1,0:T(8,128)(2,1)}, u32[]{:S(2)}, u32[]{:S(2)}) %all-to-all-start.1) | async-done | bytes 262176 | tf_op jit(solution)/shard_map/all_to_all | solution.py:307
  156.8 3.7 %fusion.10 = f32[256,1024]{1,0:T(8,128)S(1)} fusion(bf16[2048,1024]{1,0:T(8,128)(2,1)} %bitcast.117, bf16[2048,256]{1,0:T(8,128)(2,1)S(1)} %bitcast.101, f32[256]{0:T(256)S(1)} %bitcast.95, f32[2048]{0:T(1024)S(1)} %bitcast.112), kind=kOutput, calls=%fused_computation.24 | convolution fusion | flops 1075838976 | bytes 6300672 | tf_op jit(solution)/shard_map/dot_general | solution.py:323
  160.9 3.5 %fusion.8 = bf16[1,4096,256]{2,1,0:T(8,128)(2,1)} fusion(bf16[4096,256]{1,0:T(8,128)(2,1)S(1)} %copy-done.10, f32[4096,256]{1,0:T(8,128)S(1)} %bitcast.92, bf16[3072,256]{1,0:T(8,128)(2,1)} %collective-permute-done.19, bf16[1024,256]{1,0:T(8,128)(2,1)} %collective-permute-done.13, f32[4096]{0:T(1024)S(1)} %multiply_bitcast_fusion), kind=kLoop, calls=%fused_computation.16 | loop fusion | flops 9437184 | bytes 10502144 | tf_op jit(solution)/shard_map/broadcast_in_dim | solution.py:332
  164.4 4.6 %fusion.9 = f32[1,256,1024]{2,1,0:T(8,128)} fusion(f32[256,1024]{1,0:T(8,128)S(1)} %fusion.10, bf16[2048,1024]{1,0:T(8,128)(2,1)} %collective-permute-done.18, bf16[2048,256]{1,0:T(8,128)(2,1)S(1)} %bitcast.100, f32[2048]{0:T(1024)S(1)} %bitcast.110, f32[256]{0:T(256)S(1)} %bitcast.96), kind=kOutput, calls=%fused_computation.23 | convolution fusion | flops 1076101120 | bytes 7349248 | tf_op jit(solution)/shard_map/dot_general | solution.py:323
  (122 shorter events, 32.2 us)
Async XLA Ops:
  7.2 10.9 %copy-start.6 = (f32[1,256]{1,0:T(1,128)S(1)}, f32[1,256]{1,0:T(1,128)}, u32[]{:S(2)}) copy-start(f32[1,256]{1,0:T(1,128)} %gain.1) | copy-start | bytes 3076
  7.2 16.3 %copy-start.1 = (bf16[1,4096,256]{2,1,0:T(8,128)(2,1)S(1)}, bf16[1,4096,256]{2,1,0:T(8,128)(2,1)}, u32[]{:S(2)}) copy-start(bf16[1,4096,256]{2,1,0:T(8,128)(2,1)} %param.7) | copy-start | bytes 6291460
  7.2 91.1 %all-gather.2.cloned.1.call-start = ((), (), s32[]{:S(2)}) async-start(), calls=%async_computation.2 | async-start | bytes 4718592 | tf_op jit(solution)/shard_map/all_gather | solution.py:209
  7.2 8.9 %collective-permute-start.8 = (bf16[128,1024]{1,0:T(8,128)(2,1)}, bf16[128,1024]{1,0:T(8,128)(2,1)S(1)}, u32[]{:S(2)}, u32[]{:S(2)}) collective-permute-start(bf16[128,1024]{1,0:T(8,128)(2,1)} %bitcast.102), channel_id=1, source_target_pairs={{0,2},{1,3},{2,0},{3,1},{4,6},{5,7},{6,4},{7,5},{8,10},{9,11},{10,... | collective-permute-start | bytes 786440 | tf_op jit(solution)/shard_map/ppermute | solution.py:32
  19.0 15.2 %collective-permute-start.1 = (bf16[272,1024]{1,0:T(8,128)(2,1)}, bf16[272,1024]{1,0:T(8,128)(2,1)}, u32[]{:S(2)}, u32[]{:S(2)}) collective-permute-start(bf16[272,1024]{1,0:T(8,128)(2,1)} %shard_map.102), channel_id=1, source_target_pairs={{0,224},{1,225},{2,226},{3,227},{4,228},{5,229},{6,230},{7,231},{8... | collective-permute-start | bytes 1671176 | tf_op jit(solution)/shard_map/ppermute | solution.py:32
  24.5 24.0 %collective-permute-start = (bf16[16,128,256]{2,1,0:T(8,128)(2,1)}, bf16[16,128,256]{2,1,0:T(8,128)(2,1)S(1)}, u32[]{:S(2)}, u32[]{:S(2)}) collective-permute-start(bf16[16,128,256]{2,1,0:T(8,128)(2,1)} %dynamic-slice_bitcast_fusion), channel_id=1, source_target_pairs={{0,1},{1,0},{2,3},{3,2},{4,5},{5,4},{6,7},{7,6},{8,9},{9,8},{10,11... | collective-permute-start | bytes 3145736 | tf_op jit(solution)/shard_map/ppermute | solution.py:32
  32.8 45.1 %collective-permute-start.9 = (bf16[3072,256]{1,0:T(8,128)(2,1)}, bf16[3072,256]{1,0:T(8,128)(2,1)}, u32[]{:S(2)}, u32[]{:S(2)}) collective-permute-start(bf16[3072,256]{1,0:T(8,128)(2,1)} %slice_bitcast_fusion), channel_id=1, source_target_pairs={{0,224},{1,225},{2,226},{3,227},{4,228},{5,229},{6,230},{7,231},{8... | collective-permute-start | bytes 4718600 | tf_op jit(solution)/shard_map/ppermute | solution.py:32
  34.2 14.4 %collective-permute-start.2 = (bf16[272,1024]{1,0:T(8,128)(2,1)}, bf16[272,1024]{1,0:T(8,128)(2,1)}, u32[]{:S(2)}, u32[]{:S(2)}) collective-permute-start(bf16[272,1024]{1,0:T(8,128)(2,1)} %collective-permute-done.1.packed_mine), channel_id=1, source_target_pairs={{0,1},{1,0},{2,3},{3,2},{4,5},{5,4},{6,7},{7,6},{8,9},{9,8},{10,11... | collective-permute-start | bytes 1671176 | tf_op jit(solution)/shard_map/ppermute | solution.py:32
  40.0 21.3 %all-to-all-start = ((bf16[16,34,128]{2,1,0:T(8,128)(2,1)}), bf16[16,34,128]{2,1,0:T(8,128)(2,1)S(1)}, u32[]{:S(2)}, u32[]{:S(2)}) async-start(bf16[16,34,128]{2,1,0:T(8,128)(2,1)} %pad_maximum_fusion.1), calls=%async_computation | async-start | bytes 327680 | tf_op jit(solution)/shard_map/all_to_all | solution.py:232
  55.0 23.0 %collective-permute-start.4 = (bf16[2,128,1024]{2,1,0:T(8,128)(2,1)S(1)}, bf16[2,128,1024]{2,1,0:T(8,128)(2,1)S(1)}, u32[]{:S(2)}, u32[]{:S(2)}) collective-permute-start(bf16[2,128,1024]{2,1,0:T(8,128)(2,1)S(1)} %constant_dynamic-slice_fusion.6), channel_id=1, source_target_pairs={{1,29},{3,31},{5,1},{7,3},{9,5},{11,7},{13,9},{15,11},{17,13},{19,... | collective-permute-start | bytes 1572872 | tf_op jit(solution)/shard_map/ppermute | solution.py:32
  59.5 18.4 %collective-permute-start.3 = (bf16[2,128,1024]{2,1,0:T(8,128)(2,1)S(1)}, bf16[2,128,1024]{2,1,0:T(8,128)(2,1)S(1)}, u32[]{:S(2)}, u32[]{:S(2)}) collective-permute-start(bf16[2,128,1024]{2,1,0:T(8,128)(2,1)S(1)} %constant_dynamic-slice_fusion.6), channel_id=1, source_target_pairs={{0,4},{2,6},{4,8},{6,10},{8,12},{10,14},{12,16},{14,18},{16,20},{1... | collective-permute-start | bytes 1572872 | tf_op jit(solution)/shard_map/ppermute | solution.py:32
  61.3 7.2 %collective-permute-start.6 = (f32[32,128]{1,0:T(8,128)S(1)}, f32[32,128]{1,0:T(8,128)S(1)}, u32[]{:S(2)}, u32[]{:S(2)}) collective-permute-start(f32[32,128]{1,0:T(8,128)S(1)} %slice.35), channel_id=1, source_target_pairs={{0,226},{1,227},{2,224},{3,225},{4,230},{5,231},{6,228},{7,229},{8... | collective-permute-start | bytes 49160 | tf_op jit(solution)/shard_map/ppermute | solution.py:32
  67.0 5.0 %collective-permute-start.5 = (f32[32,128]{1,0:T(8,128)S(1)}, f32[32,128]{1,0:T(8,128)S(1)}, u32[]{:S(2)}, u32[]{:S(2)}) collective-permute-start(f32[32,128]{1,0:T(8,128)S(1)} %slice.35), channel_id=1, source_target_pairs={{0,224},{1,225},{2,226},{3,227},{4,228},{5,229},{6,230},{7,231},{8... | collective-permute-start | bytes 49160 | tf_op jit(solution)/shard_map/ppermute | solution.py:32
  72.0 4.0 %collective-permute-start.7 = (f32[2,128]{1,0:T(2,128)S(1)}, f32[2,128]{1,0:T(2,128)S(1)}, u32[]{:S(2)}, u32[]{:S(2)}) collective-permute-start(f32[2,128]{1,0:T(2,128)S(1)} %slice.34), channel_id=1, source_target_pairs={{0,2},{1,3},{2,0},{3,1},{4,6},{5,7},{6,4},{7,5},{8,10},{9,11},{10,... | collective-permute-start | bytes 3080 | tf_op jit(solution)/shard_map/ppermute | solution.py:32
  74.3 14.5 %collective-permute-start.12 = (bf16[1024,256]{1,0:T(8,128)(2,1)S(1)}, bf16[1024,256]{1,0:T(8,128)(2,1)S(1)}, u32[]{:S(2)}, u32[]{:S(2)}) collective-permute-start(bf16[1024,256]{1,0:T(8,128)(2,1)S(1)} %slice_bitcast_fusion.3), channel_id=1, source_target_pairs={{0,224},{1,225},{2,226},{3,227},{4,228},{5,229},{6,230},{7,231},{8... | collective-permute-start | bytes 1572872 | tf_op jit(solution)/shard_map/ppermute | solution.py:32
  76.0 22.2 %collective-permute-start.13 = (bf16[1024,256]{1,0:T(8,128)(2,1)S(1)}, bf16[1024,256]{1,0:T(8,128)(2,1)}, u32[]{:S(2)}, u32[]{:S(2)}) collective-permute-start(bf16[1024,256]{1,0:T(8,128)(2,1)S(1)} %slice_bitcast_fusion.2), channel_id=1, source_target_pairs={{0,224},{1,225},{2,226},{3,227},{4,228},{5,229},{6,230},{7,231},{8... | collective-permute-start | bytes 1572872 | tf_op jit(solution)/shard_map/ppermute | solution.py:32
  79.6 18.7 %collective-permute-start.11 = (bf16[2,128,1024]{2,1,0:T(8,128)(2,1)S(1)}, bf16[2,128,1024]{2,1,0:T(8,128)(2,1)S(1)}, u32[]{:S(2)}, u32[]{:S(2)}) collective-permute-start(bf16[2,128,1024]{2,1,0:T(8,128)(2,1)S(1)} %get-tuple-element.72), channel_id=1, source_target_pairs={{0,28},{1,29},{2,30},{3,31},{4,0},{5,1},{6,2},{7,3},{8,4},{9,5},{1... | collective-permute-start | bytes 1572872 | tf_op jit(solution)/shard_map/ppermute | solution.py:32
  85.2 13.1 %collective-permute-start.10 = (bf16[2,128,1024]{2,1,0:T(8,128)(2,1)S(1)}, bf16[2,128,1024]{2,1,0:T(8,128)(2,1)S(1)}, u32[]{:S(2)}, u32[]{:S(2)}) collective-permute-start(bf16[2,128,1024]{2,1,0:T(8,128)(2,1)S(1)} %get-tuple-element.73), channel_id=1, source_target_pairs={{0,4},{1,5},{2,6},{3,7},{4,8},{5,9},{6,10},{7,11},{8,12},{9,13},{1... | collective-permute-start | bytes 1572872 | tf_op jit(solution)/shard_map/ppermute | solution.py:32
  98.3 29.1 %collective-permute-start.18 = (bf16[2048,1024]{1,0:T(8,128)(2,1)}, bf16[2048,1024]{1,0:T(8,128)(2,1)}, u32[]{:S(2)}, u32[]{:S(2)}) collective-permute-start(bf16[2048,1024]{1,0:T(8,128)(2,1)} %bitcast.116), channel_id=1, source_target_pairs={{0,1},{1,0},{2,3},{3,2},{4,5},{5,4},{6,7},{7,6},{8,9},{9,8},{10,11... | collective-permute-start | bytes 12582920 | tf_op jit(solution)/shard_map/ppermute | solution.py:32
  103.7 16.6 %collective-permute-start.15 = (bf16[2,128,1024]{2,1,0:T(8,128)(2,1)S(1)}, bf16[2,128,1024]{2,1,0:T(8,128)(2,1)S(1)}, u32[]{:S(2)}, u32[]{:S(2)}) collective-permute-start(bf16[2,128,1024]{2,1,0:T(8,128)(2,1)S(1)} %get-tuple-element.70), channel_id=1, source_target_pairs={{0,28},{1,29},{2,30},{3,31},{4,0},{5,1},{6,2},{7,3},{8,4},{9,5},{1... | collective-permute-start | bytes 1572872 | tf_op jit(solution)/shard_map/ppermute | solution.py:32
  109.1 14.3 %collective-permute-start.14 = (bf16[2,128,1024]{2,1,0:T(8,128)(2,1)S(1)}, bf16[2,128,1024]{2,1,0:T(8,128)(2,1)S(1)}, u32[]{:S(2)}, u32[]{:S(2)}) collective-permute-start(bf16[2,128,1024]{2,1,0:T(8,128)(2,1)S(1)} %get-tuple-element.71), channel_id=1, source_target_pairs={{0,4},{1,5},{2,6},{3,7},{4,8},{5,9},{6,10},{7,11},{8,12},{9,13},{1... | collective-permute-start | bytes 1572872 | tf_op jit(solution)/shard_map/ppermute | solution.py:32
  109.1 45.3 %collective-permute-start.19 = (bf16[3072,256]{1,0:T(8,128)(2,1)}, bf16[3072,256]{1,0:T(8,128)(2,1)}, u32[]{:S(2)}, u32[]{:S(2)}) collective-permute-start(bf16[3072,256]{1,0:T(8,128)(2,1)} %slice_bitcast_fusion.1), channel_id=1, source_target_pairs={{0,224},{1,225},{2,226},{3,227},{4,228},{5,229},{6,230},{7,231},{8... | collective-permute-start | bytes 4718600 | tf_op jit(solution)/shard_map/ppermute | solution.py:32
  114.3 13.1 %copy-start.12 = (bf16[16,1,128,256]{3,2,1,0:T(8,128)(2,1)}, bf16[16,1,128,256]{3,2,1,0:T(8,128)(2,1)S(1)}, u32[]{:S(2)}) copy-start(bf16[16,1,128,256]{3,2,1,0:T(8,128)(2,1)S(1)} %get-tuple-element.76) | copy-start | bytes 3145732
  114.3 13.1 %copy-start.14 = (bf16[16,1,128,256]{3,2,1,0:T(8,128)(2,1)}, bf16[16,1,128,256]{3,2,1,0:T(8,128)(2,1)S(1)}, u32[]{:S(2)}) copy-start(bf16[16,1,128,256]{3,2,1,0:T(8,128)(2,1)S(1)} %get-tuple-element.77) | copy-start | bytes 3145732
  125.9 28.5 %collective-permute-start.17 = (bf16[2,128,1024]{2,1,0:T(8,128)(2,1)}, bf16[2,128,1024]{2,1,0:T(8,128)(2,1)}, u32[]{:S(2)}, u32[]{:S(2)}) collective-permute-start(bf16[2,128,1024]{2,1,0:T(8,128)(2,1)} %get-tuple-element.68), channel_id=1, source_target_pairs={{0,28},{1,29},{2,30},{3,31},{4,0},{5,1},{6,2},{7,3},{8,4},{9,5},{1... | collective-permute-start | bytes 1572872 | tf_op jit(solution)/shard_map/ppermute | solution.py:32
  126.2 28.2 %collective-permute-start.16 = (bf16[2,128,1024]{2,1,0:T(8,128)(2,1)}, bf16[2,128,1024]{2,1,0:T(8,128)(2,1)}, u32[]{:S(2)}, u32[]{:S(2)}) collective-permute-start(bf16[2,128,1024]{2,1,0:T(8,128)(2,1)} %get-tuple-element.69), channel_id=1, source_target_pairs={{0,4},{1,5},{2,6},{3,7},{4,8},{5,9},{6,10},{7,11},{8,12},{9,13},{1... | collective-permute-start | bytes 1572872 | tf_op jit(solution)/shard_map/ppermute | solution.py:32
  134.4 19.0 %all-to-all-start.1 = ((bf16[32,32,128]{2,1,0:T(8,128)(2,1)}), bf16[32,32,128]{2,1,0:T(8,128)(2,1)}, u32[]{:S(2)}, u32[]{:S(2)}) async-start(bf16[32,32,128]{2,1,0:T(8,128)(2,1)} %broadcast_in_dim.74), calls=%async_computation.1 | async-start | bytes 524288 | tf_op jit(solution)/shard_map/all_to_all | solution.py:307
  142.0 12.5 %copy-start.17 = (f32[32,128]{1,0:T(8,128)S(1)}, f32[32,128]{1,0:T(8,128)}, u32[]{:S(2)}) copy-start(f32[32,128]{1,0:T(8,128)} %copy-done.16) | copy-start | bytes 49156
  144.4 11.8 %copy-start.22 = (f32[128]{0:T(128)S(1)}, f32[128]{0:T(128)}, u32[]{:S(2)}) copy-start(f32[128]{0:T(128)} %get-tuple-element.84) | copy-start | bytes 1540
  144.4 11.8 %copy-start.23 = (f32[128]{0:T(128)S(1)}, f32[128]{0:T(128)}, u32[]{:S(2)}) copy-start(f32[128]{0:T(128)} %get-tuple-element.85) | copy-start | bytes 1540
  156.4 13.9 %collective-permute-start.20 = (bf16[128,1024]{1,0:T(8,128)(2,1)S(1)}, bf16[128,1024]{1,0:T(8,128)(2,1)S(1)}, u32[]{:S(2)}, u32[]{:S(2)}) collective-permute-start(bf16[128,1024]{1,0:T(8,128)(2,1)S(1)} %get-tuple-element.78), channel_id=1, source_target_pairs={{0,32},{1,33},{2,34},{3,35},{4,36},{5,37},{6,38},{7,39},{8,40},{9,... | collective-permute-start | bytes 786440 | tf_op jit(solution)/shard_map/ppermute | solution.py:32
  156.5 14.2 %collective-permute-start.21 = (bf16[128,1024]{1,0:T(8,128)(2,1)S(1)}, bf16[128,1024]{1,0:T(8,128)(2,1)S(1)}, u32[]{:S(2)}, u32[]{:S(2)}) collective-permute-start(bf16[128,1024]{1,0:T(8,128)(2,1)S(1)} %get-tuple-element.79), channel_id=1, source_target_pairs={{0,34},{1,35},{2,32},{3,33},{4,38},{5,39},{6,36},{7,37},{8,42},{9,... | collective-permute-start | bytes 786440 | tf_op jit(solution)/shard_map/ppermute | solution.py:32
  (20 other events, 82.2 us)
Sparse Core Ops, SparseCore 0:
  18.2 68.6 all-gather.1

commit v11 on v10

--- a/solution.py
+++ b/solution.py
@@ -305,19 +305,17 @@
         place, *[(gain * grad).reshape(N_T // 2, OWN, LANE) for grad in grads]
     ).reshape(TOK, LANE)
     curve = lax.all_to_all(curve, "ts", 0, 0, tiled=True)
-    curve, base = lax.optimization_barrier((curve, base))
-    up, down = lax.optimization_barrier((up, down, curve, late))[:2]
+    up, down, base = lax.optimization_barrier((up, down, base, late))[:3]
     fresh_rate = lax.rsqrt((squares[:2] + fresh_other) / WIDTH + eps)
-    curve = jnp.sum(curve.astype(F32), axis=0).reshape(TOK)
-    pull = older_rate * older_rate / WIDTH * curve
 
     summed = block(0).astype(F32) + up.astype(F32) + down.astype(F32)
     straight = (pick(summed, half) * pick(fresh_rate, half)[:, None]).astype(BF)
     crossed = (pick(summed, 1 - half) * pick(fresh_rate, 1 - half)[:, None]).astype(BF)
-    *cots, pull = lax.optimization_barrier((*cots, pull, straight, crossed))[:3]
+    *cots, curve = lax.optimization_barrier((*cots, curve, straight, crossed))[:3]
+    curve = jnp.sum(curve.astype(F32), axis=0).reshape(TOK)
+    pull = older_rate * older_rate / WIDTH * curve
     straight = move(straight, to_next)
     crossed = move(crossed, to_next_other_half)
-    new_keys = (straight.astype(F32) + crossed.astype(F32)).astype(BF)
 
     weight_total = sum(
         lax.dot_general(
@@ -327,6 +325,8 @@
     )
     downstream = jnp.concatenate([early, late], axis=0)
     total = downstream.astype(F32) + base - pull[:, None] * older.astype(F32)
+    straight, crossed = lax.optimization_barrier((straight, crossed, weight_total, total))[:2]
+    new_keys = (straight.astype(F32) + crossed.astype(F32)).astype(BF)
     return (
         new_keys[None],
         total.astype(BF)[None],

time: 179 us -> 175 us (0.978)
  waiting for transfers between devices: 40.5 us -> 38.4 us
  local copies, waits for them, and re-layouts: 19.9 us -> 17.9 us
    all_to_all x1, waiting for transfers between devices: 8.41 us -> 3.83 us  [shards(): curve = lax.all_to_all(curve, 'ts', 0, 0, tiled=True)]
    broadcast_in_dim x1 -> x0, other arithmetic: 3.49 us -> none  [shards(): total.astype(BF)[None]]
    sub x0 -> x1, other arithmetic: none -> 3.49 us  [shards(): total = downstream.astype(F32) + base - pull[:, None] * older.astype(F32)]
    ppermute x22, waiting for transfers between devices: 32.1 us -> 34.5 us  [move(): return lax.ppermute(value, AXES, pairs)]
    unnamed x55, local copies, waits for them, and re-layouts: 11.1 us -> 9.12 us
  transfers between devices with their start and end apart: 25 -> 25, of which waited for: 12 -> 11; matrix products, arithmetic and copies ran while one was open for 23% -> 24% of each run, Pallas kernels for 3% -> 3%
where the time goes in v11:
time: 175 us; the launch traced here: 174 us
  starting transfers between devices  62.2 us (36%)
  waiting for transfers between devices  38.4 us (22%)
  other arithmetic  19.1 us (11%)
  local copies, waits for them, and re-layouts  17.9 us (10%)
  matrix products  15.7 us (9%)
  between operations  15.3 us (9%)
  Pallas kernels  5.69 us (3%)
    ppermute x22, starting transfers between devices, move(): return lax.ppermute(value, AXES, pairs)  47.5 us
    ppermute x22, waiting for transfers between devices, move(): return lax.ppermute(value, AXES, pairs)  34.5 us
    unnamed x55, local copies, waits for them, and re-layouts  9.12 us
    all_to_all x1, starting transfers between devices, shards(): lax.all_to_all(after(squares, packed), 'ts', 0, 0, axis_index_groups=halv...  8.59 us
    dot_general x2, matrix products, shards(): lax.dot_general(left.astype(BF), cot, (((0,), (0,)), ((), ())), preferred...  8.27 us
    dot_general x1, matrix products, shards(): lax.dot_general(cots[1], weights, (((1,), (1,)), ((), ())), preferred_ele...  6.14 us
    all_to_all x1, starting transfers between devices, shards(): curve = lax.all_to_all(curve, 'ts', 0, 0, tiled=True)  6 us
    convert_element_type x3, other arithmetic, add(): return (a.astype(F32) + b.astype(F32)).astype(BF)  5.73 us
  transfers between devices with their start and end apart: 25, of which 11 were waited for; matrix products, arithmetic and copies ran while one was open for 24% of the time, Pallas kernels for 3%

profile of v11, /device:TPU:1, one launch (start us, length us, event | category | flops | bytes accessed | tf_op | source)
XLA Modules:
  0.0 174.3 jit_solution(17809115172926041247)
XLA Ops:
  7.2 3.7 %collective-permute-start.8 = (bf16[128,1024]{1,0:T(8,128)(2,1)}, bf16[128,1024]{1,0:T(8,128)(2,1)S(1)}, u32[]{:S(2)}, u32[]{:S(2)}) collective-permute-start(bf16[128,1024]{1,0:T(8,128)(2,1)} %bitcast.103), channel_id=1, source_target_pairs={{0,2},{1,3},{2,0},{3,1},{4,6},{5,7},{6,4},{7,5},{8,10},{9,11},{10,... | collective-permute-start | bytes 786440 | tf_op jit(solution)/shard_map/ppermute | solution.py:32
  10.9 5.3 %collective-permute-done.8 = bf16[128,1024]{1,0:T(8,128)(2,1)S(1)} collective-permute-done((bf16[128,1024]{1,0:T(8,128)(2,1)}, bf16[128,1024]{1,0:T(8,128)(2,1)S(1)}, u32[]{:S(2)}, u32[]{:S(2)}) %collective-permute-start.8) | collective-permute-done | bytes 262176 | tf_op jit(solution)/shard_map/ppermute | solution.py:32
  19.0 4.5 %collective-permute-start.1 = (bf16[272,1024]{1,0:T(8,128)(2,1)}, bf16[272,1024]{1,0:T(8,128)(2,1)}, u32[]{:S(2)}, u32[]{:S(2)}) collective-permute-start(bf16[272,1024]{1,0:T(8,128)(2,1)} %shard_map.102), channel_id=1, source_target_pairs={{0,224},{1,225},{2,226},{3,227},{4,228},{5,229},{6,230},{7,231},{8... | collective-permute-start | bytes 1671176 | tf_op jit(solution)/shard_map/ppermute | solution.py:32
  24.5 1.8 %collective-permute-start = (bf16[16,128,256]{2,1,0:T(8,128)(2,1)}, bf16[16,128,256]{2,1,0:T(8,128)(2,1)S(1)}, u32[]{:S(2)}, u32[]{:S(2)}) collective-permute-start(bf16[16,128,256]{2,1,0:T(8,128)(2,1)} %dynamic-slice_bitcast_fusion), channel_id=1, source_target_pairs={{0,1},{1,0},{2,3},{3,2},{4,5},{5,4},{6,7},{7,6},{8,9},{9,8},{10,11... | collective-permute-start | bytes 3145736 | tf_op jit(solution)/shard_map/ppermute | solution.py:32
  26.3 2.7 %slice_bitcast_fusion = bf16[3072,256]{1,0:T(8,128)(2,1)} fusion(bf16[1,4096,256]{2,1,0:T(8,128)(2,1)} %param.8), kind=kLoop, calls=%fused_computation.20 | loop fusion | bytes 3145728 | tf_op jit(solution)/shard_map/slice | solution.py:212
  29.7 2.4 %multiply_reduce_fusion = bf16[4096]{0:T(1024)(128)(2,1)S(1)} fusion(bf16[1,4096,256]{2,1,0:T(8,128)(2,1)} %param.8), kind=kLoop, calls=%fused_computation.1 | loop fusion | flops 3141632 | bytes 2105344 | tf_op jit(solution)/shard_map/reduce_sum | solution.py:223
  34.2 4.5 %collective-permute-start.2 = (bf16[272,1024]{1,0:T(8,128)(2,1)}, bf16[272,1024]{1,0:T(8,128)(2,1)}, u32[]{:S(2)}, u32[]{:S(2)}) collective-permute-start(bf16[272,1024]{1,0:T(8,128)(2,1)} %collective-permute-done.1.packed_mine), channel_id=1, source_target_pairs={{0,1},{1,0},{2,3},{3,2},{4,5},{5,4},{6,7},{7,6},{8,9},{9,8},{10,11... | collective-permute-start | bytes 1671176 | tf_op jit(solution)/shard_map/ppermute | solution.py:32
  40.0 8.6 %all-to-all-start = ((bf16[16,34,128]{2,1,0:T(8,128)(2,1)}), bf16[16,34,128]{2,1,0:T(8,128)(2,1)S(1)}, u32[]{:S(2)}, u32[]{:S(2)}) async-start(bf16[16,34,128]{2,1,0:T(8,128)(2,1)} %pad_maximum_fusion.1), calls=%async_computation | async-start | bytes 327680 | tf_op jit(solution)/shard_map/all_to_all | solution.py:232
  48.6 4.3 %shard_map.103 = bf16[16,128,1024]{2,1,0:T(8,128)(2,1)S(1)} custom-call(s32[1]{0:T(128)} %bitcast.place, bf16[16,2,128,256]{3,2,1,0:T(8,128)(2,1)S(1)} %bitcast.91, bf16[16,128,256]{2,1,0:T(8,128)(2,1)S(1)} %collective-permute-done.rows_other, bf16[272,1024]{1,0:T(8,128)(2,1)} %collective-permute-done.1.packed_mine, ...), custom_call_target="tpu_custom_call" | custom-call | flops 2147483648 | bytes 7340032 | tf_op jit(solution)/shard_map/pallas_call | solution.py:143
  52.9 2.0 %copy-done = bf16[16,128,1024]{2,1,0:T(8,128)(2,1)} copy-done((bf16[16,128,1024]{2,1,0:T(8,128)(2,1)}, bf16[16,128,1024]{2,1,0:T(8,128)(2,1)S(1)}, u32[]{:S(2)}) %copy-start) | copy-done | bytes 4194328
  55.0 4.5 %collective-permute-start.4 = (bf16[2,128,1024]{2,1,0:T(8,128)(2,1)S(1)}, bf16[2,128,1024]{2,1,0:T(8,128)(2,1)S(1)}, u32[]{:S(2)}, u32[]{:S(2)}) collective-permute-start(bf16[2,128,1024]{2,1,0:T(8,128)(2,1)S(1)} %constant_dynamic-slice_fusion.6), channel_id=1, source_target_pairs={{1,29},{3,31},{5,1},{7,3},{9,5},{11,7},{13,9},{15,11},{17,13},{19,... | collective-permute-start | bytes 1572872 | tf_op jit(solution)/shard_map/ppermute | solution.py:32
  61.3 5.7 %collective-permute-start.6 = (f32[32,128]{1,0:T(8,128)S(1)}, f32[32,128]{1,0:T(8,128)S(1)}, u32[]{:S(2)}, u32[]{:S(2)}) collective-permute-start(f32[32,128]{1,0:T(8,128)S(1)} %slice.35), channel_id=1, source_target_pairs={{0,226},{1,227},{2,224},{3,225},{4,230},{5,231},{6,228},{7,229},{8... | collective-permute-start | bytes 49160 | tf_op jit(solution)/shard_map/ppermute | solution.py:32
  68.5 3.5 %collective-permute-done.5 = f32[32,128]{1,0:T(8,128)S(1)} collective-permute-done((f32[32,128]{1,0:T(8,128)S(1)}, f32[32,128]{1,0:T(8,128)S(1)}, u32[]{:S(2)}, u32[]{:S(2)}) %collective-permute-start.5) | collective-permute-done | bytes 16416 | tf_op jit(solution)/shard_map/ppermute | solution.py:32
  72.0 2.3 %collective-permute-start.7 = (f32[2,128]{1,0:T(2,128)S(1)}, f32[2,128]{1,0:T(2,128)S(1)}, u32[]{:S(2)}, u32[]{:S(2)}) collective-permute-start(f32[2,128]{1,0:T(2,128)S(1)} %slice.34), channel_id=1, source_target_pairs={{0,2},{1,3},{2,0},{3,1},{4,6},{5,7},{6,4},{7,5},{8,10},{9,11},{10,... | collective-permute-start | bytes 3080 | tf_op jit(solution)/shard_map/ppermute | solution.py:32
  76.0 1.9 %collective-permute-start.13 = (bf16[1024,256]{1,0:T(8,128)(2,1)S(1)}, bf16[1024,256]{1,0:T(8,128)(2,1)}, u32[]{:S(2)}, u32[]{:S(2)}) collective-permute-start(bf16[1024,256]{1,0:T(8,128)(2,1)S(1)} %slice_bitcast_fusion.2), channel_id=1, source_target_pairs={{0,224},{1,225},{2,226},{3,227},{4,228},{5,229},{6,230},{7,231},{8... | collective-permute-start | bytes 1572872 | tf_op jit(solution)/shard_map/ppermute | solution.py:32
  79.6 5.6 %collective-permute-start.11 = (bf16[2,128,1024]{2,1,0:T(8,128)(2,1)S(1)}, bf16[2,128,1024]{2,1,0:T(8,128)(2,1)S(1)}, u32[]{:S(2)}, u32[]{:S(2)}) collective-permute-start(bf16[2,128,1024]{2,1,0:T(8,128)(2,1)S(1)} %get-tuple-element.74), channel_id=1, source_target_pairs={{0,28},{1,29},{2,30},{3,31},{4,0},{5,1},{6,2},{7,3},{8,4},{9,5},{1... | collective-permute-start | bytes 1572872 | tf_op jit(solution)/shard_map/ppermute | solution.py:32
  85.2 3.7 %collective-permute-done.12 = bf16[1024,256]{1,0:T(8,128)(2,1)S(1)} collective-permute-done((bf16[1024,256]{1,0:T(8,128)(2,1)S(1)}, bf16[1024,256]{1,0:T(8,128)(2,1)S(1)}, u32[]{:S(2)}, u32[]{:S(2)}) %collective-permute-start.12) | collective-permute-done | bytes 524320 | tf_op jit(solution)/shard_map/ppermute | solution.py:32
  88.8 9.4 %collective-permute-done.13 = bf16[1024,256]{1,0:T(8,128)(2,1)} collective-permute-done((bf16[1024,256]{1,0:T(8,128)(2,1)S(1)}, bf16[1024,256]{1,0:T(8,128)(2,1)}, u32[]{:S(2)}, u32[]{:S(2)}) %collective-permute-start.13) | collective-permute-done | bytes 524320 | tf_op jit(solution)/shard_map/ppermute | solution.py:32
  98.3 2.5 %collective-permute-start.18 = (bf16[2048,1024]{1,0:T(8,128)(2,1)}, bf16[2048,1024]{1,0:T(8,128)(2,1)}, u32[]{:S(2)}, u32[]{:S(2)}) collective-permute-start(bf16[2048,1024]{1,0:T(8,128)(2,1)} %bitcast.117), channel_id=1, source_target_pairs={{0,1},{1,0},{2,3},{3,2},{4,5},{5,4},{6,7},{7,6},{8,9},{9,8},{10,11... | collective-permute-start | bytes 12582920 | tf_op jit(solution)/shard_map/ppermute | solution.py:32
  103.7 5.4 %collective-permute-start.15 = (bf16[2,128,1024]{2,1,0:T(8,128)(2,1)S(1)}, bf16[2,128,1024]{2,1,0:T(8,128)(2,1)S(1)}, u32[]{:S(2)}, u32[]{:S(2)}) collective-permute-start(bf16[2,128,1024]{2,1,0:T(8,128)(2,1)S(1)} %get-tuple-element.72), channel_id=1, source_target_pairs={{0,28},{1,29},{2,30},{3,31},{4,0},{5,1},{6,2},{7,3},{8,4},{9,5},{1... | collective-permute-start | bytes 1572872 | tf_op jit(solution)/shard_map/ppermute | solution.py:32
  109.1 2.3 %collective-permute-start.19 = (bf16[3072,256]{1,0:T(8,128)(2,1)}, bf16[3072,256]{1,0:T(8,128)(2,1)}, u32[]{:S(2)}, u32[]{:S(2)}) collective-permute-start(bf16[3072,256]{1,0:T(8,128)(2,1)} %slice_bitcast_fusion.1), channel_id=1, source_target_pairs={{0,224},{1,225},{2,226},{3,227},{4,228},{5,229},{6,230},{7,231},{8... | collective-permute-start | bytes 4718600 | tf_op jit(solution)/shard_map/ppermute | solution.py:32
  114.3 2.3 %copy-done.26 = bf16[16,128,1024]{2,1,0:T(8,128)(2,1)S(1)} copy-done((bf16[16,128,1024]{2,1,0:T(8,128)(2,1)S(1)}, bf16[16,128,1024]{2,1,0:T(8,128)(2,1)}, u32[]{:S(2)}) %copy-start.26) | copy-done | bytes 4194328
  118.1 2.2 %collective-permute-done.15 = bf16[2,128,1024]{2,1,0:T(8,128)(2,1)S(1)} collective-permute-done((bf16[2,128,1024]{2,1,0:T(8,128)(2,1)S(1)}, bf16[2,128,1024]{2,1,0:T(8,128)(2,1)S(1)}, u32[]{:S(2)}, u32[]{:S(2)}) %collective-permute-start.15) | collective-permute-done | bytes 524320 | tf_op jit(solution)/shard_map/ppermute | solution.py:32
  120.3 3.1 %collective-permute-done.14 = bf16[2,128,1024]{2,1,0:T(8,128)(2,1)S(1)} collective-permute-done((bf16[2,128,1024]{2,1,0:T(8,128)(2,1)S(1)}, bf16[2,128,1024]{2,1,0:T(8,128)(2,1)S(1)}, u32[]{:S(2)}, u32[]{:S(2)}) %collective-permute-start.14) | collective-permute-done | bytes 524320 | tf_op jit(solution)/shard_map/ppermute | solution.py:32
  123.4 2.5 %add_convert_fusion = (bf16[2,128,1024]{2,1,0:T(8,128)(2,1)}, bf16[2,128,1024]{2,1,0:T(8,128)(2,1)}) fusion(bf16[2,128,1024]{2,1,0:T(8,128)(2,1)S(1)} %collective-permute-done.15, bf16[16,128,1024]{2,1,0:T(8,128)(2,1)} %copy-done, s32[]{:T(128)S(6)} %select_n.142, bf16[2,128,1024]{2,1,0:T(8,128)(2,1)S(1)} %collective-permute-done.14, s32[]{:T(128)S(6)} %select_n.125), kind=kLoop, calls=%fused_computation.30 | loop fusion | flops 2097152 | bytes 3145736 | tf_op jit(solution)/shard_map/convert_element_type | solution.py:80
  127.4 6.1 %fusion.7 = (f32[256]{0:T(256)}, bf16[2048]{0:T(1024)(128)(2,1)S(1)}, f32[2048,256]{1,0:T(8,128)S(1)}, f32[2048,256]{1,0:T(8,128)}, bf16[2048]{0:T(1024)(128)(2,1)S(1)}, /*index=5*/f32[256]{0:T(256)}) fusion(bf16[16,1,128,256]{3,2,1,0:T(8,128)(2,1)S(1)} %get-tuple-element.78, f32[256]{0:T(256)S(1)} %bitcast.94, f32[2048,256]{1,0:T(8,128)S(1)} %fusion.21, ...), kind=kOutput, calls=%fused_computation.15 | convolution fusion | flops 1084222976 | bytes 13134848 | tf_op jit(solution)/shard_map/dot_general | solution.py:279
  134.4 6.0 %all-to-all-start.1 = ((bf16[32,32,128]{2,1,0:T(8,128)(2,1)}), bf16[32,32,128]{2,1,0:T(8,128)(2,1)}, u32[]{:S(2)}, u32[]{:S(2)}) async-start(bf16[32,32,128]{2,1,0:T(8,128)(2,1)} %broadcast_in_dim.74), calls=%async_computation.1 | async-start | bytes 524288 | tf_op jit(solution)/shard_map/all_to_all | solution.py:307
  142.5 4.1 %collective-permute-done.19 = bf16[3072,256]{1,0:T(8,128)(2,1)} collective-permute-done((bf16[3072,256]{1,0:T(8,128)(2,1)}, bf16[3072,256]{1,0:T(8,128)(2,1)}, u32[]{:S(2)}, u32[]{:S(2)}) %collective-permute-start.19) | collective-permute-done | bytes 1572896 | tf_op jit(solution)/shard_map/ppermute | solution.py:32
  149.6 3.8 %all-to-all-done.1 = bf16[32,32,128]{2,1,0:T(8,128)(2,1)} async-done(((bf16[32,32,128]{2,1,0:T(8,128)(2,1)}), bf16[32,32,128]{2,1,0:T(8,128)(2,1)}, u32[]{:S(2)}, u32[]{:S(2)}) %all-to-all-start.1) | async-done | bytes 262176 | tf_op jit(solution)/shard_map/all_to_all | solution.py:307
  154.5 3.7 %fusion.8 = f32[256,1024]{1,0:T(8,128)S(1)} fusion(bf16[2048,1024]{1,0:T(8,128)(2,1)} %bitcast.118, bf16[2048,256]{1,0:T(8,128)(2,1)S(1)} %bitcast.102, f32[2048]{0:T(1024)S(1)} %bitcast.113, f32[256]{0:T(256)S(1)} %bitcast.95), kind=kOutput, calls=%fused_computation.23 | convolution fusion | flops 1075838976 | bytes 6300672 | tf_op jit(solution)/shard_map/dot_general | solution.py:321
  158.6 3.5 %multiply_subtract_fusion = bf16[4096,256]{1,0:T(8,128)(2,1)} fusion(bf16[4096,256]{1,0:T(8,128)(2,1)S(1)} %copy-done.10, f32[4096,256]{1,0:T(8,128)S(1)} %bitcast.92, bf16[3072,256]{1,0:T(8,128)(2,1)} %collective-permute-done.19, bf16[1024,256]{1,0:T(8,128)(2,1)} %collective-permute-done.13, f32[4096]{0:T(1024)S(1)} %multiply_bitcast_fusion), kind=kLoop, calls=%fused_computation | loop fusion | flops 9437184 | bytes 10502144 | tf_op jit(solution)/shard_map/sub | solution.py:327
  162.1 4.6 %convolution_add_fusion = f32[256,1024]{1,0:T(8,128)} fusion(f32[256,1024]{1,0:T(8,128)S(1)} %fusion.8, bf16[2048,1024]{1,0:T(8,128)(2,1)} %collective-permute-done.18, bf16[2048,256]{1,0:T(8,128)(2,1)S(1)} %bitcast.101, f32[2048]{0:T(1024)S(1)} %bitcast.111, f32[256]{0:T(256)S(1)} %bitcast.96), kind=kOutput, calls=%fused_computation.22 | convolution fusion | flops 1076101120 | bytes 7349248 | tf_op jit(solution)/shard_map/dot_general | solution.py:321
  (122 shorter events, 30.5 us)
Async XLA Ops:
  7.2 10.9 %copy-start.6 = (f32[1,256]{1,0:T(1,128)S(1)}, f32[1,256]{1,0:T(1,128)}, u32[]{:S(2)}) copy-start(f32[1,256]{1,0:T(1,128)} %gain.1) | copy-start | bytes 3076
  7.2 10.9 %copy-start.4 = (bf16[1,256,1024]{2,1,0:T(8,128)(2,1)S(1)}, bf16[1,256,1024]{2,1,0:T(8,128)(2,1)}, u32[]{:S(2)}) copy-start(bf16[1,256,1024]{2,1,0:T(8,128)(2,1)} %param.11) | copy-start | bytes 1572868
  7.2 16.3 %copy-start.1 = (bf16[1,4096,256]{2,1,0:T(8,128)(2,1)S(1)}, bf16[1,4096,256]{2,1,0:T(8,128)(2,1)}, u32[]{:S(2)}) copy-start(bf16[1,4096,256]{2,1,0:T(8,128)(2,1)} %param.7) | copy-start | bytes 6291460
  7.2 91.1 %all-gather.2.cloned.1.call-start = ((), (), s32[]{:S(2)}) async-start(), calls=%async_computation.2 | async-start | bytes 4718592 | tf_op jit(solution)/shard_map/all_gather | solution.py:209
  7.2 8.9 %collective-permute-start.8 = (bf16[128,1024]{1,0:T(8,128)(2,1)}, bf16[128,1024]{1,0:T(8,128)(2,1)S(1)}, u32[]{:S(2)}, u32[]{:S(2)}) collective-permute-start(bf16[128,1024]{1,0:T(8,128)(2,1)} %bitcast.103), channel_id=1, source_target_pairs={{0,2},{1,3},{2,0},{3,1},{4,6},{5,7},{6,4},{7,5},{8,10},{9,11},{10,... | collective-permute-start | bytes 786440 | tf_op jit(solution)/shard_map/ppermute | solution.py:32
  19.0 15.2 %collective-permute-start.1 = (bf16[272,1024]{1,0:T(8,128)(2,1)}, bf16[272,1024]{1,0:T(8,128)(2,1)}, u32[]{:S(2)}, u32[]{:S(2)}) collective-permute-start(bf16[272,1024]{1,0:T(8,128)(2,1)} %shard_map.102), channel_id=1, source_target_pairs={{0,224},{1,225},{2,226},{3,227},{4,228},{5,229},{6,230},{7,231},{8... | collective-permute-start | bytes 1671176 | tf_op jit(solution)/shard_map/ppermute | solution.py:32
  24.5 24.0 %collective-permute-start = (bf16[16,128,256]{2,1,0:T(8,128)(2,1)}, bf16[16,128,256]{2,1,0:T(8,128)(2,1)S(1)}, u32[]{:S(2)}, u32[]{:S(2)}) collective-permute-start(bf16[16,128,256]{2,1,0:T(8,128)(2,1)} %dynamic-slice_bitcast_fusion), channel_id=1, source_target_pairs={{0,1},{1,0},{2,3},{3,2},{4,5},{5,4},{6,7},{7,6},{8,9},{9,8},{10,11... | collective-permute-start | bytes 3145736 | tf_op jit(solution)/shard_map/ppermute | solution.py:32
  32.8 45.1 %collective-permute-start.9 = (bf16[3072,256]{1,0:T(8,128)(2,1)}, bf16[3072,256]{1,0:T(8,128)(2,1)}, u32[]{:S(2)}, u32[]{:S(2)}) collective-permute-start(bf16[3072,256]{1,0:T(8,128)(2,1)} %slice_bitcast_fusion), channel_id=1, source_target_pairs={{0,224},{1,225},{2,226},{3,227},{4,228},{5,229},{6,230},{7,231},{8... | collective-permute-start | bytes 4718600 | tf_op jit(solution)/shard_map/ppermute | solution.py:32
  34.2 14.4 %collective-permute-start.2 = (bf16[272,1024]{1,0:T(8,128)(2,1)}, bf16[272,1024]{1,0:T(8,128)(2,1)}, u32[]{:S(2)}, u32[]{:S(2)}) collective-permute-start(bf16[272,1024]{1,0:T(8,128)(2,1)} %collective-permute-done.1.packed_mine), channel_id=1, source_target_pairs={{0,1},{1,0},{2,3},{3,2},{4,5},{5,4},{6,7},{7,6},{8,9},{9,8},{10,11... | collective-permute-start | bytes 1671176 | tf_op jit(solution)/shard_map/ppermute | solution.py:32
  40.0 21.3 %all-to-all-start = ((bf16[16,34,128]{2,1,0:T(8,128)(2,1)}), bf16[16,34,128]{2,1,0:T(8,128)(2,1)S(1)}, u32[]{:S(2)}, u32[]{:S(2)}) async-start(bf16[16,34,128]{2,1,0:T(8,128)(2,1)} %pad_maximum_fusion.1), calls=%async_computation | async-start | bytes 327680 | tf_op jit(solution)/shard_map/all_to_all | solution.py:232
  55.0 23.0 %collective-permute-start.4 = (bf16[2,128,1024]{2,1,0:T(8,128)(2,1)S(1)}, bf16[2,128,1024]{2,1,0:T(8,128)(2,1)S(1)}, u32[]{:S(2)}, u32[]{:S(2)}) collective-permute-start(bf16[2,128,1024]{2,1,0:T(8,128)(2,1)S(1)} %constant_dynamic-slice_fusion.6), channel_id=1, source_target_pairs={{1,29},{3,31},{5,1},{7,3},{9,5},{11,7},{13,9},{15,11},{17,13},{19,... | collective-permute-start | bytes 1572872 | tf_op jit(solution)/shard_map/ppermute | solution.py:32
  59.5 18.4 %collective-permute-start.3 = (bf16[2,128,1024]{2,1,0:T(8,128)(2,1)S(1)}, bf16[2,128,1024]{2,1,0:T(8,128)(2,1)S(1)}, u32[]{:S(2)}, u32[]{:S(2)}) collective-permute-start(bf16[2,128,1024]{2,1,0:T(8,128)(2,1)S(1)} %constant_dynamic-slice_fusion.6), channel_id=1, source_target_pairs={{0,4},{2,6},{4,8},{6,10},{8,12},{10,14},{12,16},{14,18},{16,20},{1... | collective-permute-start | bytes 1572872 | tf_op jit(solution)/shard_map/ppermute | solution.py:32
  61.3 7.2 %collective-permute-start.6 = (f32[32,128]{1,0:T(8,128)S(1)}, f32[32,128]{1,0:T(8,128)S(1)}, u32[]{:S(2)}, u32[]{:S(2)}) collective-permute-start(f32[32,128]{1,0:T(8,128)S(1)} %slice.35), channel_id=1, source_target_pairs={{0,226},{1,227},{2,224},{3,225},{4,230},{5,231},{6,228},{7,229},{8... | collective-permute-start | bytes 49160 | tf_op jit(solution)/shard_map/ppermute | solution.py:32
  67.0 5.0 %collective-permute-start.5 = (f32[32,128]{1,0:T(8,128)S(1)}, f32[32,128]{1,0:T(8,128)S(1)}, u32[]{:S(2)}, u32[]{:S(2)}) collective-permute-start(f32[32,128]{1,0:T(8,128)S(1)} %slice.35), channel_id=1, source_target_pairs={{0,224},{1,225},{2,226},{3,227},{4,228},{5,229},{6,230},{7,231},{8... | collective-permute-start | bytes 49160 | tf_op jit(solution)/shard_map/ppermute | solution.py:32
  72.0 4.0 %collective-permute-start.7 = (f32[2,128]{1,0:T(2,128)S(1)}, f32[2,128]{1,0:T(2,128)S(1)}, u32[]{:S(2)}, u32[]{:S(2)}) collective-permute-start(f32[2,128]{1,0:T(2,128)S(1)} %slice.34), channel_id=1, source_target_pairs={{0,2},{1,3},{2,0},{3,1},{4,6},{5,7},{6,4},{7,5},{8,10},{9,11},{10,... | collective-permute-start | bytes 3080 | tf_op jit(solution)/shard_map/ppermute | solution.py:32
  74.3 14.5 %collective-permute-start.12 = (bf16[1024,256]{1,0:T(8,128)(2,1)S(1)}, bf16[1024,256]{1,0:T(8,128)(2,1)S(1)}, u32[]{:S(2)}, u32[]{:S(2)}) collective-permute-start(bf16[1024,256]{1,0:T(8,128)(2,1)S(1)} %slice_bitcast_fusion.3), channel_id=1, source_target_pairs={{0,224},{1,225},{2,226},{3,227},{4,228},{5,229},{6,230},{7,231},{8... | collective-permute-start | bytes 1572872 | tf_op jit(solution)/shard_map/ppermute | solution.py:32
  76.0 22.2 %collective-permute-start.13 = (bf16[1024,256]{1,0:T(8,128)(2,1)S(1)}, bf16[1024,256]{1,0:T(8,128)(2,1)}, u32[]{:S(2)}, u32[]{:S(2)}) collective-permute-start(bf16[1024,256]{1,0:T(8,128)(2,1)S(1)} %slice_bitcast_fusion.2), channel_id=1, source_target_pairs={{0,224},{1,225},{2,226},{3,227},{4,228},{5,229},{6,230},{7,231},{8... | collective-permute-start | bytes 1572872 | tf_op jit(solution)/shard_map/ppermute | solution.py:32
  79.6 18.7 %collective-permute-start.11 = (bf16[2,128,1024]{2,1,0:T(8,128)(2,1)S(1)}, bf16[2,128,1024]{2,1,0:T(8,128)(2,1)S(1)}, u32[]{:S(2)}, u32[]{:S(2)}) collective-permute-start(bf16[2,128,1024]{2,1,0:T(8,128)(2,1)S(1)} %get-tuple-element.74), channel_id=1, source_target_pairs={{0,28},{1,29},{2,30},{3,31},{4,0},{5,1},{6,2},{7,3},{8,4},{9,5},{1... | collective-permute-start | bytes 1572872 | tf_op jit(solution)/shard_map/ppermute | solution.py:32
  85.2 13.1 %collective-permute-start.10 = (bf16[2,128,1024]{2,1,0:T(8,128)(2,1)S(1)}, bf16[2,128,1024]{2,1,0:T(8,128)(2,1)S(1)}, u32[]{:S(2)}, u32[]{:S(2)}) collective-permute-start(bf16[2,128,1024]{2,1,0:T(8,128)(2,1)S(1)} %get-tuple-element.75), channel_id=1, source_target_pairs={{0,4},{1,5},{2,6},{3,7},{4,8},{5,9},{6,10},{7,11},{8,12},{9,13},{1... | collective-permute-start | bytes 1572872 | tf_op jit(solution)/shard_map/ppermute | solution.py:32
  98.3 29.1 %collective-permute-start.18 = (bf16[2048,1024]{1,0:T(8,128)(2,1)}, bf16[2048,1024]{1,0:T(8,128)(2,1)}, u32[]{:S(2)}, u32[]{:S(2)}) collective-permute-start(bf16[2048,1024]{1,0:T(8,128)(2,1)} %bitcast.117), channel_id=1, source_target_pairs={{0,1},{1,0},{2,3},{3,2},{4,5},{5,4},{6,7},{7,6},{8,9},{9,8},{10,11... | collective-permute-start | bytes 12582920 | tf_op jit(solution)/shard_map/ppermute | solution.py:32
  103.7 16.6 %collective-permute-start.15 = (bf16[2,128,1024]{2,1,0:T(8,128)(2,1)S(1)}, bf16[2,128,1024]{2,1,0:T(8,128)(2,1)S(1)}, u32[]{:S(2)}, u32[]{:S(2)}) collective-permute-start(bf16[2,128,1024]{2,1,0:T(8,128)(2,1)S(1)} %get-tuple-element.72), channel_id=1, source_target_pairs={{0,28},{1,29},{2,30},{3,31},{4,0},{5,1},{6,2},{7,3},{8,4},{9,5},{1... | collective-permute-start | bytes 1572872 | tf_op jit(solution)/shard_map/ppermute | solution.py:32
  109.1 14.3 %collective-permute-start.14 = (bf16[2,128,1024]{2,1,0:T(8,128)(2,1)S(1)}, bf16[2,128,1024]{2,1,0:T(8,128)(2,1)S(1)}, u32[]{:S(2)}, u32[]{:S(2)}) collective-permute-start(bf16[2,128,1024]{2,1,0:T(8,128)(2,1)S(1)} %get-tuple-element.73), channel_id=1, source_target_pairs={{0,4},{1,5},{2,6},{3,7},{4,8},{5,9},{6,10},{7,11},{8,12},{9,13},{1... | collective-permute-start | bytes 1572872 | tf_op jit(solution)/shard_map/ppermute | solution.py:32
  109.1 37.5 %collective-permute-start.19 = (bf16[3072,256]{1,0:T(8,128)(2,1)}, bf16[3072,256]{1,0:T(8,128)(2,1)}, u32[]{:S(2)}, u32[]{:S(2)}) collective-permute-start(bf16[3072,256]{1,0:T(8,128)(2,1)} %slice_bitcast_fusion.1), channel_id=1, source_target_pairs={{0,224},{1,225},{2,226},{3,227},{4,228},{5,229},{6,230},{7,231},{8... | collective-permute-start | bytes 4718600 | tf_op jit(solution)/shard_map/ppermute | solution.py:32
  114.3 13.1 %copy-start.12 = (bf16[16,1,128,256]{3,2,1,0:T(8,128)(2,1)}, bf16[16,1,128,256]{3,2,1,0:T(8,128)(2,1)S(1)}, u32[]{:S(2)}) copy-start(bf16[16,1,128,256]{3,2,1,0:T(8,128)(2,1)S(1)} %get-tuple-element.78) | copy-start | bytes 3145732
  114.3 13.1 %copy-start.14 = (bf16[16,1,128,256]{3,2,1,0:T(8,128)(2,1)}, bf16[16,1,128,256]{3,2,1,0:T(8,128)(2,1)S(1)}, u32[]{:S(2)}) copy-start(bf16[16,1,128,256]{3,2,1,0:T(8,128)(2,1)S(1)} %get-tuple-element.79) | copy-start | bytes 3145732
  116.8 10.6 %copy-start.18 = (f32[16,1,128]{2,1,0:T(1,128)}, f32[16,1,128]{2,1,0:T(1,128)S(1)}, u32[]{:S(2)}) copy-start(f32[16,1,128]{2,1,0:T(1,128)S(1)} %get-tuple-element.84) | copy-start | bytes 24580
  116.8 10.6 %copy-start.20 = (f32[16,1,128]{2,1,0:T(1,128)}, f32[16,1,128]{2,1,0:T(1,128)S(1)}, u32[]{:S(2)}) copy-start(f32[16,1,128]{2,1,0:T(1,128)S(1)} %get-tuple-element.85) | copy-start | bytes 24580
  125.9 16.6 %collective-permute-start.17 = (bf16[2,128,1024]{2,1,0:T(8,128)(2,1)}, bf16[2,128,1024]{2,1,0:T(8,128)(2,1)}, u32[]{:S(2)}, u32[]{:S(2)}) collective-permute-start(bf16[2,128,1024]{2,1,0:T(8,128)(2,1)} %get-tuple-element.70), channel_id=1, source_target_pairs={{0,28},{1,29},{2,30},{3,31},{4,0},{5,1},{6,2},{7,3},{8,4},{9,5},{1... | collective-permute-start | bytes 1572872 | tf_op jit(solution)/shard_map/ppermute | solution.py:32
  126.2 16.3 %collective-permute-start.16 = (bf16[2,128,1024]{2,1,0:T(8,128)(2,1)}, bf16[2,128,1024]{2,1,0:T(8,128)(2,1)}, u32[]{:S(2)}, u32[]{:S(2)}) collective-permute-start(bf16[2,128,1024]{2,1,0:T(8,128)(2,1)} %get-tuple-element.71), channel_id=1, source_target_pairs={{0,4},{1,5},{2,6},{3,7},{4,8},{5,9},{6,10},{7,11},{8,12},{9,13},{1... | collective-permute-start | bytes 1572872 | tf_op jit(solution)/shard_map/ppermute | solution.py:32
  134.4 19.0 %all-to-all-start.1 = ((bf16[32,32,128]{2,1,0:T(8,128)(2,1)}), bf16[32,32,128]{2,1,0:T(8,128)(2,1)}, u32[]{:S(2)}, u32[]{:S(2)}) async-start(bf16[32,32,128]{2,1,0:T(8,128)(2,1)} %broadcast_in_dim.74), calls=%async_computation.1 | async-start | bytes 524288 | tf_op jit(solution)/shard_map/all_to_all | solution.py:307
  148.6 18.1 %collective-permute-start.21 = (bf16[128,1024]{1,0:T(8,128)(2,1)S(1)}, bf16[128,1024]{1,0:T(8,128)(2,1)S(1)}, u32[]{:S(2)}, u32[]{:S(2)}) collective-permute-start(bf16[128,1024]{1,0:T(8,128)(2,1)S(1)} %get-tuple-element.80), channel_id=1, source_target_pairs={{0,34},{1,35},{2,32},{3,33},{4,38},{5,39},{6,36},{7,37},{8,42},{9,... | collective-permute-start | bytes 786440 | tf_op jit(solution)/shard_map/ppermute | solution.py:32
  148.7 18.0 %collective-permute-start.20 = (bf16[128,1024]{1,0:T(8,128)(2,1)S(1)}, bf16[128,1024]{1,0:T(8,128)(2,1)S(1)}, u32[]{:S(2)}, u32[]{:S(2)}) collective-permute-start(bf16[128,1024]{1,0:T(8,128)(2,1)S(1)} %get-tuple-element.81), channel_id=1, source_target_pairs={{0,32},{1,33},{2,34},{3,35},{4,36},{5,37},{6,38},{7,39},{8,40},{9,... | collective-permute-start | bytes 786440 | tf_op jit(solution)/shard_map/ppermute | solution.py:32
  (20 other events, 89.9 us)
Sparse Core Ops, SparseCore 0:
  18.2 68.6 all-gather.1

commit v12 on v11

--- a/solution.py
+++ b/solution.py
@@ -305,7 +305,7 @@
         place, *[(gain * grad).reshape(N_T // 2, OWN, LANE) for grad in grads]
     ).reshape(TOK, LANE)
     curve = lax.all_to_all(curve, "ts", 0, 0, tiled=True)
-    up, down, base = lax.optimization_barrier((up, down, base, late))[:3]
+    up, down, base = lax.optimization_barrier((up, down, base))
     fresh_rate = lax.rsqrt((squares[:2] + fresh_other) / WIDTH + eps)
 
     summed = block(0).astype(F32) + up.astype(F32) + down.astype(F32)

time: 175 us -> 175 us (level)
  waiting for transfers between devices: 38.4 us -> 35.9 us
    ppermute x22, waiting for transfers between devices: 34.5 us -> 30.4 us  [move(): return lax.ppermute(value, AXES, pairs)]
  transfers between devices with their start and end apart: 25 -> 25, of which waited for: 11 -> 10; matrix products, arithmetic and copies ran while one was open for 24% -> 25% of each run, Pallas kernels for 3% -> 3%
where the time goes in v12:
time: 175 us; the launch traced here: 174 us
  starting transfers between devices  63.3 us (36%)
  waiting for transfers between devices  35.9 us (21%)
  other arithmetic  20.4 us (12%)
  local copies, waits for them, and re-layouts  17.9 us (10%)
  matrix products  15.7 us (9%)
  between operations  15.3 us (9%)
  Pallas kernels  5.69 us (3%)
    ppermute x22, starting transfers between devices, move(): return lax.ppermute(value, AXES, pairs)  48.7 us
    ppermute x22, waiting for transfers between devices, move(): return lax.ppermute(value, AXES, pairs)  30.4 us
    unnamed x55, local copies, waits for them, and re-layouts  9.1 us
    all_to_all x1, starting transfers between devices, shards(): lax.all_to_all(after(squares, packed), 'ts', 0, 0, axis_index_groups=halv...  8.59 us
    dot_general x2, matrix products, shards(): lax.dot_general(left.astype(BF), cot, (((0,), (0,)), ((), ())), preferred...  8.28 us
    dot_general x1, matrix products, shards(): lax.dot_general(cots[1], weights, (((1,), (1,)), ((), ())), preferred_ele...  6.14 us
    all_to_all x1, starting transfers between devices, shards(): curve = lax.all_to_all(curve, 'ts', 0, 0, tiled=True)  6 us
    convert_element_type x3, other arithmetic, add(): return (a.astype(F32) + b.astype(F32)).astype(BF)  5.73 us
  transfers between devices with their start and end apart: 25, of which 10 were waited for; matrix products, arithmetic and copies ran while one was open for 25% of the time, Pallas kernels for 3%

profile of v12, /device:TPU:1, one launch (start us, length us, event | category | flops | bytes accessed | tf_op | source)
XLA Modules:
  0.0 174.3 jit_solution(16621449797865890368)
XLA Ops:
  7.2 3.7 %collective-permute-start.8 = (bf16[128,1024]{1,0:T(8,128)(2,1)}, bf16[128,1024]{1,0:T(8,128)(2,1)S(1)}, u32[]{:S(2)}, u32[]{:S(2)}) collective-permute-start(bf16[128,1024]{1,0:T(8,128)(2,1)} %bitcast.103), channel_id=1, source_target_pairs={{0,2},{1,3},{2,0},{3,1},{4,6},{5,7},{6,4},{7,5},{8,10},{9,11},{10,... | collective-permute-start | bytes 786440 | tf_op jit(solution)/shard_map/ppermute | solution.py:32
  10.9 5.3 %collective-permute-done.8 = bf16[128,1024]{1,0:T(8,128)(2,1)S(1)} collective-permute-done((bf16[128,1024]{1,0:T(8,128)(2,1)}, bf16[128,1024]{1,0:T(8,128)(2,1)S(1)}, u32[]{:S(2)}, u32[]{:S(2)}) %collective-permute-start.8) | collective-permute-done | bytes 262176 | tf_op jit(solution)/shard_map/ppermute | solution.py:32
  19.0 4.5 %collective-permute-start.1 = (bf16[272,1024]{1,0:T(8,128)(2,1)}, bf16[272,1024]{1,0:T(8,128)(2,1)}, u32[]{:S(2)}, u32[]{:S(2)}) collective-permute-start(bf16[272,1024]{1,0:T(8,128)(2,1)} %shard_map.102), channel_id=1, source_target_pairs={{0,224},{1,225},{2,226},{3,227},{4,228},{5,229},{6,230},{7,231},{8... | collective-permute-start | bytes 1671176 | tf_op jit(solution)/shard_map/ppermute | solution.py:32
  24.6 1.8 %collective-permute-start = (bf16[16,128,256]{2,1,0:T(8,128)(2,1)}, bf16[16,128,256]{2,1,0:T(8,128)(2,1)S(1)}, u32[]{:S(2)}, u32[]{:S(2)}) collective-permute-start(bf16[16,128,256]{2,1,0:T(8,128)(2,1)} %dynamic-slice_bitcast_fusion), channel_id=1, source_target_pairs={{0,1},{1,0},{2,3},{3,2},{4,5},{5,4},{6,7},{7,6},{8,9},{9,8},{10,11... | collective-permute-start | bytes 3145736 | tf_op jit(solution)/shard_map/ppermute | solution.py:32
  26.4 2.7 %slice_bitcast_fusion = bf16[3072,256]{1,0:T(8,128)(2,1)} fusion(bf16[1,4096,256]{2,1,0:T(8,128)(2,1)} %param.8), kind=kLoop, calls=%fused_computation.20 | loop fusion | bytes 3145728 | tf_op jit(solution)/shard_map/slice | solution.py:212
  29.7 2.4 %multiply_reduce_fusion = bf16[4096]{0:T(1024)(128)(2,1)S(1)} fusion(bf16[1,4096,256]{2,1,0:T(8,128)(2,1)} %param.8), kind=kLoop, calls=%fused_computation.1 | loop fusion | flops 3141632 | bytes 2105344 | tf_op jit(solution)/shard_map/reduce_sum | solution.py:223
  34.2 4.5 %collective-permute-start.2 = (bf16[272,1024]{1,0:T(8,128)(2,1)}, bf16[272,1024]{1,0:T(8,128)(2,1)}, u32[]{:S(2)}, u32[]{:S(2)}) collective-permute-start(bf16[272,1024]{1,0:T(8,128)(2,1)} %collective-permute-done.1.packed_mine), channel_id=1, source_target_pairs={{0,1},{1,0},{2,3},{3,2},{4,5},{5,4},{6,7},{7,6},{8,9},{9,8},{10,11... | collective-permute-start | bytes 1671176 | tf_op jit(solution)/shard_map/ppermute | solution.py:32
  40.0 8.6 %all-to-all-start = ((bf16[16,34,128]{2,1,0:T(8,128)(2,1)}), bf16[16,34,128]{2,1,0:T(8,128)(2,1)S(1)}, u32[]{:S(2)}, u32[]{:S(2)}) async-start(bf16[16,34,128]{2,1,0:T(8,128)(2,1)} %pad_maximum_fusion.1), calls=%async_computation | async-start | bytes 327680 | tf_op jit(solution)/shard_map/all_to_all | solution.py:232
  48.6 4.3 %shard_map.103 = bf16[16,128,1024]{2,1,0:T(8,128)(2,1)S(1)} custom-call(s32[1]{0:T(128)} %bitcast.place, bf16[16,2,128,256]{3,2,1,0:T(8,128)(2,1)S(1)} %bitcast.91, bf16[16,128,256]{2,1,0:T(8,128)(2,1)S(1)} %collective-permute-done.rows_other, bf16[272,1024]{1,0:T(8,128)(2,1)} %collective-permute-done.1.packed_mine, ...), custom_call_target="tpu_custom_call" | custom-call | flops 2147483648 | bytes 7340032 | tf_op jit(solution)/shard_map/pallas_call | solution.py:143
  53.0 2.0 %copy-done = bf16[16,128,1024]{2,1,0:T(8,128)(2,1)} copy-done((bf16[16,128,1024]{2,1,0:T(8,128)(2,1)}, bf16[16,128,1024]{2,1,0:T(8,128)(2,1)S(1)}, u32[]{:S(2)}) %copy-start) | copy-done | bytes 4194328
  55.0 4.5 %collective-permute-start.4 = (bf16[2,128,1024]{2,1,0:T(8,128)(2,1)S(1)}, bf16[2,128,1024]{2,1,0:T(8,128)(2,1)S(1)}, u32[]{:S(2)}, u32[]{:S(2)}) collective-permute-start(bf16[2,128,1024]{2,1,0:T(8,128)(2,1)S(1)} %constant_dynamic-slice_fusion.6), channel_id=1, source_target_pairs={{1,29},{3,31},{5,1},{7,3},{9,5},{11,7},{13,9},{15,11},{17,13},{19,... | collective-permute-start | bytes 1572872 | tf_op jit(solution)/shard_map/ppermute | solution.py:32
  61.4 5.7 %collective-permute-start.6 = (f32[32,128]{1,0:T(8,128)S(1)}, f32[32,128]{1,0:T(8,128)S(1)}, u32[]{:S(2)}, u32[]{:S(2)}) collective-permute-start(f32[32,128]{1,0:T(8,128)S(1)} %slice.35), channel_id=1, source_target_pairs={{0,226},{1,227},{2,224},{3,225},{4,230},{5,231},{6,228},{7,229},{8... | collective-permute-start | bytes 49160 | tf_op jit(solution)/shard_map/ppermute | solution.py:32
  68.6 3.5 %collective-permute-done.5 = f32[32,128]{1,0:T(8,128)S(1)} collective-permute-done((f32[32,128]{1,0:T(8,128)S(1)}, f32[32,128]{1,0:T(8,128)S(1)}, u32[]{:S(2)}, u32[]{:S(2)}) %collective-permute-start.5) | collective-permute-done | bytes 16416 | tf_op jit(solution)/shard_map/ppermute | solution.py:32
  72.1 2.3 %collective-permute-start.7 = (f32[2,128]{1,0:T(2,128)S(1)}, f32[2,128]{1,0:T(2,128)S(1)}, u32[]{:S(2)}, u32[]{:S(2)}) collective-permute-start(f32[2,128]{1,0:T(2,128)S(1)} %slice.34), channel_id=1, source_target_pairs={{0,2},{1,3},{2,0},{3,1},{4,6},{5,7},{6,4},{7,5},{8,10},{9,11},{10,... | collective-permute-start | bytes 3080 | tf_op jit(solution)/shard_map/ppermute | solution.py:32
  76.1 1.9 %collective-permute-start.13 = (bf16[1024,256]{1,0:T(8,128)(2,1)S(1)}, bf16[1024,256]{1,0:T(8,128)(2,1)}, u32[]{:S(2)}, u32[]{:S(2)}) collective-permute-start(bf16[1024,256]{1,0:T(8,128)(2,1)S(1)} %slice_bitcast_fusion.2), channel_id=1, source_target_pairs={{0,224},{1,225},{2,226},{3,227},{4,228},{5,229},{6,230},{7,231},{8... | collective-permute-start | bytes 1572872 | tf_op jit(solution)/shard_map/ppermute | solution.py:32
  79.6 5.6 %collective-permute-start.11 = (bf16[2,128,1024]{2,1,0:T(8,128)(2,1)S(1)}, bf16[2,128,1024]{2,1,0:T(8,128)(2,1)S(1)}, u32[]{:S(2)}, u32[]{:S(2)}) collective-permute-start(bf16[2,128,1024]{2,1,0:T(8,128)(2,1)S(1)} %get-tuple-element.74), channel_id=1, source_target_pairs={{0,28},{1,29},{2,30},{3,31},{4,0},{5,1},{6,2},{7,3},{8,4},{9,5},{1... | collective-permute-start | bytes 1572872 | tf_op jit(solution)/shard_map/ppermute | solution.py:32
  85.2 3.7 %collective-permute-done.12 = bf16[1024,256]{1,0:T(8,128)(2,1)S(1)} collective-permute-done((bf16[1024,256]{1,0:T(8,128)(2,1)S(1)}, bf16[1024,256]{1,0:T(8,128)(2,1)S(1)}, u32[]{:S(2)}, u32[]{:S(2)}) %collective-permute-start.12) | collective-permute-done | bytes 524320 | tf_op jit(solution)/shard_map/ppermute | solution.py:32
  88.9 9.4 %collective-permute-done.13 = bf16[1024,256]{1,0:T(8,128)(2,1)} collective-permute-done((bf16[1024,256]{1,0:T(8,128)(2,1)S(1)}, bf16[1024,256]{1,0:T(8,128)(2,1)}, u32[]{:S(2)}, u32[]{:S(2)}) %collective-permute-start.13) | collective-permute-done | bytes 524320 | tf_op jit(solution)/shard_map/ppermute | solution.py:32
  98.3 2.5 %collective-permute-start.18 = (bf16[2048,1024]{1,0:T(8,128)(2,1)}, bf16[2048,1024]{1,0:T(8,128)(2,1)}, u32[]{:S(2)}, u32[]{:S(2)}) collective-permute-start(bf16[2048,1024]{1,0:T(8,128)(2,1)} %bitcast.117), channel_id=1, source_target_pairs={{0,1},{1,0},{2,3},{3,2},{4,5},{5,4},{6,7},{7,6},{8,9},{9,8},{10,11... | collective-permute-start | bytes 12582920 | tf_op jit(solution)/shard_map/ppermute | solution.py:32
  103.8 5.4 %collective-permute-start.15 = (bf16[2,128,1024]{2,1,0:T(8,128)(2,1)S(1)}, bf16[2,128,1024]{2,1,0:T(8,128)(2,1)S(1)}, u32[]{:S(2)}, u32[]{:S(2)}) collective-permute-start(bf16[2,128,1024]{2,1,0:T(8,128)(2,1)S(1)} %get-tuple-element.72), channel_id=1, source_target_pairs={{0,28},{1,29},{2,30},{3,31},{4,0},{5,1},{6,2},{7,3},{8,4},{9,5},{1... | collective-permute-start | bytes 1572872 | tf_op jit(solution)/shard_map/ppermute | solution.py:32
  109.2 2.3 %collective-permute-start.21 = (bf16[3072,256]{1,0:T(8,128)(2,1)}, bf16[3072,256]{1,0:T(8,128)(2,1)}, u32[]{:S(2)}, u32[]{:S(2)}) collective-permute-start(bf16[3072,256]{1,0:T(8,128)(2,1)} %slice_bitcast_fusion.1), channel_id=1, source_target_pairs={{0,224},{1,225},{2,226},{3,227},{4,228},{5,229},{6,230},{7,231},{8... | collective-permute-start | bytes 4718600 | tf_op jit(solution)/shard_map/ppermute | solution.py:32
  114.4 2.3 %copy-done.26 = bf16[16,128,1024]{2,1,0:T(8,128)(2,1)S(1)} copy-done((bf16[16,128,1024]{2,1,0:T(8,128)(2,1)S(1)}, bf16[16,128,1024]{2,1,0:T(8,128)(2,1)}, u32[]{:S(2)}) %copy-start.26) | copy-done | bytes 4194328
  118.1 2.2 %collective-permute-done.15 = bf16[2,128,1024]{2,1,0:T(8,128)(2,1)S(1)} collective-permute-done((bf16[2,128,1024]{2,1,0:T(8,128)(2,1)S(1)}, bf16[2,128,1024]{2,1,0:T(8,128)(2,1)S(1)}, u32[]{:S(2)}, u32[]{:S(2)}) %collective-permute-start.15) | collective-permute-done | bytes 524320 | tf_op jit(solution)/shard_map/ppermute | solution.py:32
  120.4 3.1 %collective-permute-done.14 = bf16[2,128,1024]{2,1,0:T(8,128)(2,1)S(1)} collective-permute-done((bf16[2,128,1024]{2,1,0:T(8,128)(2,1)S(1)}, bf16[2,128,1024]{2,1,0:T(8,128)(2,1)S(1)}, u32[]{:S(2)}, u32[]{:S(2)}) %collective-permute-start.14) | collective-permute-done | bytes 524320 | tf_op jit(solution)/shard_map/ppermute | solution.py:32
  123.5 2.5 %add_convert_fusion = (bf16[2,128,1024]{2,1,0:T(8,128)(2,1)}, bf16[2,128,1024]{2,1,0:T(8,128)(2,1)}) fusion(bf16[2,128,1024]{2,1,0:T(8,128)(2,1)S(1)} %collective-permute-done.15, bf16[16,128,1024]{2,1,0:T(8,128)(2,1)} %copy-done, s32[]{:T(128)S(6)} %select_n.142, bf16[2,128,1024]{2,1,0:T(8,128)(2,1)S(1)} %collective-permute-done.14, s32[]{:T(128)S(6)} %select_n.125), kind=kLoop, calls=%fused_computation.30 | loop fusion | flops 2097152 | bytes 3145736 | tf_op jit(solution)/shard_map/convert_element_type | solution.py:80
  127.5 6.1 %fusion.7 = (f32[256]{0:T(256)}, bf16[2048]{0:T(1024)(128)(2,1)S(1)}, f32[2048,256]{1,0:T(8,128)S(1)}, f32[2048,256]{1,0:T(8,128)}, bf16[2048]{0:T(1024)(128)(2,1)S(1)}, /*index=5*/f32[256]{0:T(256)}) fusion(bf16[16,1,128,256]{3,2,1,0:T(8,128)(2,1)S(1)} %get-tuple-element.78, f32[256]{0:T(256)S(1)} %bitcast.94, f32[2048,256]{1,0:T(8,128)S(1)} %fusion.21, ...), kind=kOutput, calls=%fused_computation.15 | convolution fusion | flops 1084222976 | bytes 13134848 | tf_op jit(solution)/shard_map/dot_general | solution.py:279
  134.4 6.0 %all-to-all-start.1 = ((bf16[32,32,128]{2,1,0:T(8,128)(2,1)}), bf16[32,32,128]{2,1,0:T(8,128)(2,1)}, u32[]{:S(2)}, u32[]{:S(2)}) async-start(bf16[32,32,128]{2,1,0:T(8,128)(2,1)} %broadcast_in_dim.74), calls=%async_computation.1 | async-start | bytes 524288 | tf_op jit(solution)/shard_map/all_to_all | solution.py:307
  142.7 3.1 %convert_add_fusion = f32[2,128,1024]{2,1,0:T(8,128)S(1)} fusion(bf16[2,128,1024]{2,1,0:T(8,128)(2,1)} %collective-permute-done.17, bf16[2,128,1024]{2,1,0:T(8,128)(2,1)} %collective-permute-done.16, bf16[16,128,1024]{2,1,0:T(8,128)(2,1)} %copy-done, s32[]{:T(128)S(6)} %select_n.123), kind=kLoop, calls=%fused_computation.24 | loop fusion | flops 1310720 | bytes 2621444 | tf_op jit(solution)/shard_map/add | solution.py:311
  148.0 5.5 %all-to-all-done.1 = bf16[32,32,128]{2,1,0:T(8,128)(2,1)} async-done(((bf16[32,32,128]{2,1,0:T(8,128)(2,1)}), bf16[32,32,128]{2,1,0:T(8,128)(2,1)}, u32[]{:S(2)}, u32[]{:S(2)}) %all-to-all-start.1) | async-done | bytes 262176 | tf_op jit(solution)/shard_map/all_to_all | solution.py:307
  154.6 3.7 %fusion.8 = f32[256,1024]{1,0:T(8,128)S(1)} fusion(bf16[2048,1024]{1,0:T(8,128)(2,1)} %bitcast.118, bf16[2048,256]{1,0:T(8,128)(2,1)S(1)} %bitcast.102, f32[2048]{0:T(1024)S(1)} %bitcast.113, f32[256]{0:T(256)S(1)} %bitcast.95), kind=kOutput, calls=%fused_computation.23 | convolution fusion | flops 1075838976 | bytes 6300672 | tf_op jit(solution)/shard_map/dot_general | solution.py:321
  158.7 3.4 %multiply_subtract_fusion = bf16[4096,256]{1,0:T(8,128)(2,1)} fusion(bf16[4096,256]{1,0:T(8,128)(2,1)S(1)} %copy-done.10, f32[4096,256]{1,0:T(8,128)S(1)} %bitcast.92, bf16[3072,256]{1,0:T(8,128)(2,1)} %collective-permute-done.21, bf16[1024,256]{1,0:T(8,128)(2,1)} %collective-permute-done.13, f32[4096]{0:T(1024)S(1)} %multiply_bitcast_fusion), kind=kLoop, calls=%fused_computation | loop fusion | flops 9437184 | bytes 10502144 | tf_op jit(solution)/shard_map/sub | solution.py:327
  162.1 4.6 %convolution_add_fusion = f32[256,1024]{1,0:T(8,128)} fusion(f32[256,1024]{1,0:T(8,128)S(1)} %fusion.8, bf16[2048,1024]{1,0:T(8,128)(2,1)} %collective-permute-done.18, bf16[2048,256]{1,0:T(8,128)(2,1)S(1)} %bitcast.101, f32[2048]{0:T(1024)S(1)} %bitcast.111, f32[256]{0:T(256)S(1)} %bitcast.96), kind=kOutput, calls=%fused_computation.22 | convolution fusion | flops 1076101120 | bytes 7349248 | tf_op jit(solution)/shard_map/dot_general | solution.py:321
  (122 shorter events, 29.9 us)
Async XLA Ops:
  7.2 16.3 %copy-start.1 = (bf16[1,4096,256]{2,1,0:T(8,128)(2,1)S(1)}, bf16[1,4096,256]{2,1,0:T(8,128)(2,1)}, u32[]{:S(2)}) copy-start(bf16[1,4096,256]{2,1,0:T(8,128)(2,1)} %param.7) | copy-start | bytes 6291460
  7.2 91.1 %all-gather.2.cloned.1.call-start = ((), (), s32[]{:S(2)}) async-start(), calls=%async_computation.2 | async-start | bytes 4718592 | tf_op jit(solution)/shard_map/all_gather | solution.py:209
  7.2 8.9 %collective-permute-start.8 = (bf16[128,1024]{1,0:T(8,128)(2,1)}, bf16[128,1024]{1,0:T(8,128)(2,1)S(1)}, u32[]{:S(2)}, u32[]{:S(2)}) collective-permute-start(bf16[128,1024]{1,0:T(8,128)(2,1)} %bitcast.103), channel_id=1, source_target_pairs={{0,2},{1,3},{2,0},{3,1},{4,6},{5,7},{6,4},{7,5},{8,10},{9,11},{10,... | collective-permute-start | bytes 786440 | tf_op jit(solution)/shard_map/ppermute | solution.py:32
  19.0 15.2 %collective-permute-start.1 = (bf16[272,1024]{1,0:T(8,128)(2,1)}, bf16[272,1024]{1,0:T(8,128)(2,1)}, u32[]{:S(2)}, u32[]{:S(2)}) collective-permute-start(bf16[272,1024]{1,0:T(8,128)(2,1)} %shard_map.102), channel_id=1, source_target_pairs={{0,224},{1,225},{2,226},{3,227},{4,228},{5,229},{6,230},{7,231},{8... | collective-permute-start | bytes 1671176 | tf_op jit(solution)/shard_map/ppermute | solution.py:32
  24.6 24.1 %collective-permute-start = (bf16[16,128,256]{2,1,0:T(8,128)(2,1)}, bf16[16,128,256]{2,1,0:T(8,128)(2,1)S(1)}, u32[]{:S(2)}, u32[]{:S(2)}) collective-permute-start(bf16[16,128,256]{2,1,0:T(8,128)(2,1)} %dynamic-slice_bitcast_fusion), channel_id=1, source_target_pairs={{0,1},{1,0},{2,3},{3,2},{4,5},{5,4},{6,7},{7,6},{8,9},{9,8},{10,11... | collective-permute-start | bytes 3145736 | tf_op jit(solution)/shard_map/ppermute | solution.py:32
  32.8 45.1 %collective-permute-start.9 = (bf16[3072,256]{1,0:T(8,128)(2,1)}, bf16[3072,256]{1,0:T(8,128)(2,1)}, u32[]{:S(2)}, u32[]{:S(2)}) collective-permute-start(bf16[3072,256]{1,0:T(8,128)(2,1)} %slice_bitcast_fusion), channel_id=1, source_target_pairs={{0,224},{1,225},{2,226},{3,227},{4,228},{5,229},{6,230},{7,231},{8... | collective-permute-start | bytes 4718600 | tf_op jit(solution)/shard_map/ppermute | solution.py:32
  34.2 14.4 %collective-permute-start.2 = (bf16[272,1024]{1,0:T(8,128)(2,1)}, bf16[272,1024]{1,0:T(8,128)(2,1)}, u32[]{:S(2)}, u32[]{:S(2)}) collective-permute-start(bf16[272,1024]{1,0:T(8,128)(2,1)} %collective-permute-done.1.packed_mine), channel_id=1, source_target_pairs={{0,1},{1,0},{2,3},{3,2},{4,5},{5,4},{6,7},{7,6},{8,9},{9,8},{10,11... | collective-permute-start | bytes 1671176 | tf_op jit(solution)/shard_map/ppermute | solution.py:32
  40.0 21.3 %all-to-all-start = ((bf16[16,34,128]{2,1,0:T(8,128)(2,1)}), bf16[16,34,128]{2,1,0:T(8,128)(2,1)S(1)}, u32[]{:S(2)}, u32[]{:S(2)}) async-start(bf16[16,34,128]{2,1,0:T(8,128)(2,1)} %pad_maximum_fusion.1), calls=%async_computation | async-start | bytes 327680 | tf_op jit(solution)/shard_map/all_to_all | solution.py:232
  55.0 22.9 %collective-permute-start.4 = (bf16[2,128,1024]{2,1,0:T(8,128)(2,1)S(1)}, bf16[2,128,1024]{2,1,0:T(8,128)(2,1)S(1)}, u32[]{:S(2)}, u32[]{:S(2)}) collective-permute-start(bf16[2,128,1024]{2,1,0:T(8,128)(2,1)S(1)} %constant_dynamic-slice_fusion.6), channel_id=1, source_target_pairs={{1,29},{3,31},{5,1},{7,3},{9,5},{11,7},{13,9},{15,11},{17,13},{19,... | collective-permute-start | bytes 1572872 | tf_op jit(solution)/shard_map/ppermute | solution.py:32
  59.5 18.4 %collective-permute-start.3 = (bf16[2,128,1024]{2,1,0:T(8,128)(2,1)S(1)}, bf16[2,128,1024]{2,1,0:T(8,128)(2,1)S(1)}, u32[]{:S(2)}, u32[]{:S(2)}) collective-permute-start(bf16[2,128,1024]{2,1,0:T(8,128)(2,1)S(1)} %constant_dynamic-slice_fusion.6), channel_id=1, source_target_pairs={{0,4},{2,6},{4,8},{6,10},{8,12},{10,14},{12,16},{14,18},{16,20},{1... | collective-permute-start | bytes 1572872 | tf_op jit(solution)/shard_map/ppermute | solution.py:32
  61.4 7.2 %collective-permute-start.6 = (f32[32,128]{1,0:T(8,128)S(1)}, f32[32,128]{1,0:T(8,128)S(1)}, u32[]{:S(2)}, u32[]{:S(2)}) collective-permute-start(f32[32,128]{1,0:T(8,128)S(1)} %slice.35), channel_id=1, source_target_pairs={{0,226},{1,227},{2,224},{3,225},{4,230},{5,231},{6,228},{7,229},{8... | collective-permute-start | bytes 49160 | tf_op jit(solution)/shard_map/ppermute | solution.py:32
  67.1 5.0 %collective-permute-start.5 = (f32[32,128]{1,0:T(8,128)S(1)}, f32[32,128]{1,0:T(8,128)S(1)}, u32[]{:S(2)}, u32[]{:S(2)}) collective-permute-start(f32[32,128]{1,0:T(8,128)S(1)} %slice.35), channel_id=1, source_target_pairs={{0,224},{1,225},{2,226},{3,227},{4,228},{5,229},{6,230},{7,231},{8... | collective-permute-start | bytes 49160 | tf_op jit(solution)/shard_map/ppermute | solution.py:32
  72.1 4.0 %collective-permute-start.7 = (f32[2,128]{1,0:T(2,128)S(1)}, f32[2,128]{1,0:T(2,128)S(1)}, u32[]{:S(2)}, u32[]{:S(2)}) collective-permute-start(f32[2,128]{1,0:T(2,128)S(1)} %slice.34), channel_id=1, source_target_pairs={{0,2},{1,3},{2,0},{3,1},{4,6},{5,7},{6,4},{7,5},{8,10},{9,11},{10,... | collective-permute-start | bytes 3080 | tf_op jit(solution)/shard_map/ppermute | solution.py:32
  74.4 14.5 %collective-permute-start.12 = (bf16[1024,256]{1,0:T(8,128)(2,1)S(1)}, bf16[1024,256]{1,0:T(8,128)(2,1)S(1)}, u32[]{:S(2)}, u32[]{:S(2)}) collective-permute-start(bf16[1024,256]{1,0:T(8,128)(2,1)S(1)} %slice_bitcast_fusion.3), channel_id=1, source_target_pairs={{0,224},{1,225},{2,226},{3,227},{4,228},{5,229},{6,230},{7,231},{8... | collective-permute-start | bytes 1572872 | tf_op jit(solution)/shard_map/ppermute | solution.py:32
  76.1 22.2 %collective-permute-start.13 = (bf16[1024,256]{1,0:T(8,128)(2,1)S(1)}, bf16[1024,256]{1,0:T(8,128)(2,1)}, u32[]{:S(2)}, u32[]{:S(2)}) collective-permute-start(bf16[1024,256]{1,0:T(8,128)(2,1)S(1)} %slice_bitcast_fusion.2), channel_id=1, source_target_pairs={{0,224},{1,225},{2,226},{3,227},{4,228},{5,229},{6,230},{7,231},{8... | collective-permute-start | bytes 1572872 | tf_op jit(solution)/shard_map/ppermute | solution.py:32
  79.6 18.7 %collective-permute-start.11 = (bf16[2,128,1024]{2,1,0:T(8,128)(2,1)S(1)}, bf16[2,128,1024]{2,1,0:T(8,128)(2,1)S(1)}, u32[]{:S(2)}, u32[]{:S(2)}) collective-permute-start(bf16[2,128,1024]{2,1,0:T(8,128)(2,1)S(1)} %get-tuple-element.74), channel_id=1, source_target_pairs={{0,28},{1,29},{2,30},{3,31},{4,0},{5,1},{6,2},{7,3},{8,4},{9,5},{1... | collective-permute-start | bytes 1572872 | tf_op jit(solution)/shard_map/ppermute | solution.py:32
  85.2 13.1 %collective-permute-start.10 = (bf16[2,128,1024]{2,1,0:T(8,128)(2,1)S(1)}, bf16[2,128,1024]{2,1,0:T(8,128)(2,1)S(1)}, u32[]{:S(2)}, u32[]{:S(2)}) collective-permute-start(bf16[2,128,1024]{2,1,0:T(8,128)(2,1)S(1)} %get-tuple-element.75), channel_id=1, source_target_pairs={{0,4},{1,5},{2,6},{3,7},{4,8},{5,9},{6,10},{7,11},{8,12},{9,13},{1... | collective-permute-start | bytes 1572872 | tf_op jit(solution)/shard_map/ppermute | solution.py:32
  98.3 29.1 %collective-permute-start.18 = (bf16[2048,1024]{1,0:T(8,128)(2,1)}, bf16[2048,1024]{1,0:T(8,128)(2,1)}, u32[]{:S(2)}, u32[]{:S(2)}) collective-permute-start(bf16[2048,1024]{1,0:T(8,128)(2,1)} %bitcast.117), channel_id=1, source_target_pairs={{0,1},{1,0},{2,3},{3,2},{4,5},{5,4},{6,7},{7,6},{8,9},{9,8},{10,11... | collective-permute-start | bytes 12582920 | tf_op jit(solution)/shard_map/ppermute | solution.py:32
  103.8 16.6 %collective-permute-start.15 = (bf16[2,128,1024]{2,1,0:T(8,128)(2,1)S(1)}, bf16[2,128,1024]{2,1,0:T(8,128)(2,1)S(1)}, u32[]{:S(2)}, u32[]{:S(2)}) collective-permute-start(bf16[2,128,1024]{2,1,0:T(8,128)(2,1)S(1)} %get-tuple-element.72), channel_id=1, source_target_pairs={{0,28},{1,29},{2,30},{3,31},{4,0},{5,1},{6,2},{7,3},{8,4},{9,5},{1... | collective-permute-start | bytes 1572872 | tf_op jit(solution)/shard_map/ppermute | solution.py:32
  109.2 14.3 %collective-permute-start.14 = (bf16[2,128,1024]{2,1,0:T(8,128)(2,1)S(1)}, bf16[2,128,1024]{2,1,0:T(8,128)(2,1)S(1)}, u32[]{:S(2)}, u32[]{:S(2)}) collective-permute-start(bf16[2,128,1024]{2,1,0:T(8,128)(2,1)S(1)} %get-tuple-element.73), channel_id=1, source_target_pairs={{0,4},{1,5},{2,6},{3,7},{4,8},{5,9},{6,10},{7,11},{8,12},{9,13},{1... | collective-permute-start | bytes 1572872 | tf_op jit(solution)/shard_map/ppermute | solution.py:32
  109.2 49.1 %collective-permute-start.21 = (bf16[3072,256]{1,0:T(8,128)(2,1)}, bf16[3072,256]{1,0:T(8,128)(2,1)}, u32[]{:S(2)}, u32[]{:S(2)}) collective-permute-start(bf16[3072,256]{1,0:T(8,128)(2,1)} %slice_bitcast_fusion.1), channel_id=1, source_target_pairs={{0,224},{1,225},{2,226},{3,227},{4,228},{5,229},{6,230},{7,231},{8... | collective-permute-start | bytes 4718600 | tf_op jit(solution)/shard_map/ppermute | solution.py:32
  114.4 13.1 %copy-start.12 = (bf16[16,1,128,256]{3,2,1,0:T(8,128)(2,1)}, bf16[16,1,128,256]{3,2,1,0:T(8,128)(2,1)S(1)}, u32[]{:S(2)}) copy-start(bf16[16,1,128,256]{3,2,1,0:T(8,128)(2,1)S(1)} %get-tuple-element.78) | copy-start | bytes 3145732
  114.4 13.1 %copy-start.14 = (bf16[16,1,128,256]{3,2,1,0:T(8,128)(2,1)}, bf16[16,1,128,256]{3,2,1,0:T(8,128)(2,1)S(1)}, u32[]{:S(2)}) copy-start(bf16[16,1,128,256]{3,2,1,0:T(8,128)(2,1)S(1)} %get-tuple-element.79) | copy-start | bytes 3145732
  126.0 16.6 %collective-permute-start.17 = (bf16[2,128,1024]{2,1,0:T(8,128)(2,1)}, bf16[2,128,1024]{2,1,0:T(8,128)(2,1)}, u32[]{:S(2)}, u32[]{:S(2)}) collective-permute-start(bf16[2,128,1024]{2,1,0:T(8,128)(2,1)} %get-tuple-element.70), channel_id=1, source_target_pairs={{0,28},{1,29},{2,30},{3,31},{4,0},{5,1},{6,2},{7,3},{8,4},{9,5},{1... | collective-permute-start | bytes 1572872 | tf_op jit(solution)/shard_map/ppermute | solution.py:32
  126.3 16.3 %collective-permute-start.16 = (bf16[2,128,1024]{2,1,0:T(8,128)(2,1)}, bf16[2,128,1024]{2,1,0:T(8,128)(2,1)}, u32[]{:S(2)}, u32[]{:S(2)}) collective-permute-start(bf16[2,128,1024]{2,1,0:T(8,128)(2,1)} %get-tuple-element.71), channel_id=1, source_target_pairs={{0,4},{1,5},{2,6},{3,7},{4,8},{5,9},{6,10},{7,11},{8,12},{9,13},{1... | collective-permute-start | bytes 1572872 | tf_op jit(solution)/shard_map/ppermute | solution.py:32
  134.4 19.0 %all-to-all-start.1 = ((bf16[32,32,128]{2,1,0:T(8,128)(2,1)}), bf16[32,32,128]{2,1,0:T(8,128)(2,1)}, u32[]{:S(2)}, u32[]{:S(2)}) async-start(bf16[32,32,128]{2,1,0:T(8,128)(2,1)} %broadcast_in_dim.74), calls=%async_computation.1 | async-start | bytes 524288 | tf_op jit(solution)/shard_map/all_to_all | solution.py:307
  142.6 11.9 %copy-start.17 = (f32[32,128]{1,0:T(8,128)S(1)}, f32[32,128]{1,0:T(8,128)}, u32[]{:S(2)}) copy-start(f32[32,128]{1,0:T(8,128)} %copy-done.16) | copy-start | bytes 49156
  142.6 11.9 %copy-start.7 = (f32[1,256]{1,0:T(1,128)S(1)}, f32[1,256]{1,0:T(1,128)}, u32[]{:S(2)}) copy-start(f32[1,256]{1,0:T(1,128)} %gain.1) | copy-start | bytes 3076
  142.6 11.9 %copy-start.15 = (bf16[16,1,128,256]{3,2,1,0:T(8,128)(2,1)S(1)}, bf16[16,1,128,256]{3,2,1,0:T(8,128)(2,1)}, u32[]{:S(2)}) copy-start(bf16[16,1,128,256]{3,2,1,0:T(8,128)(2,1)} %copy-done.14) | copy-start | bytes 3145732
  142.6 11.9 %copy-start.21 = (f32[16,1,128]{2,1,0:T(1,128)S(1)}, f32[16,1,128]{2,1,0:T(1,128)}, u32[]{:S(2)}) copy-start(f32[16,1,128]{2,1,0:T(1,128)} %copy-done.20) | copy-start | bytes 24580
  145.9 20.7 %collective-permute-start.20 = (bf16[128,1024]{1,0:T(8,128)(2,1)S(1)}, bf16[128,1024]{1,0:T(8,128)(2,1)S(1)}, u32[]{:S(2)}, u32[]{:S(2)}) collective-permute-start(bf16[128,1024]{1,0:T(8,128)(2,1)S(1)} %get-tuple-element.80), channel_id=1, source_target_pairs={{0,34},{1,35},{2,32},{3,33},{4,38},{5,39},{6,36},{7,37},{8,42},{9,... | collective-permute-start | bytes 786440 | tf_op jit(solution)/shard_map/ppermute | solution.py:32
  147.4 19.2 %collective-permute-start.19 = (bf16[128,1024]{1,0:T(8,128)(2,1)S(1)}, bf16[128,1024]{1,0:T(8,128)(2,1)S(1)}, u32[]{:S(2)}, u32[]{:S(2)}) collective-permute-start(bf16[128,1024]{1,0:T(8,128)(2,1)S(1)} %get-tuple-element.81), channel_id=1, source_target_pairs={{0,32},{1,33},{2,34},{3,35},{4,36},{5,37},{6,38},{7,39},{8,40},{9,... | collective-permute-start | bytes 786440 | tf_op jit(solution)/shard_map/ppermute | solution.py:32
  (20 other events, 99.4 us)
Sparse Core Ops, SparseCore 0:
  18.2 68.6 all-gather.1
